TPU v7x, 32 devices: a whole 2x2x4 slice. The times are simulated.
32 devices in a mesh: dp: 4 (over z), feat: 8 (over y, x, core).
Axes of the slice: x: 2, y: 2, z: 4, core: 2. Of those that a mesh axis runs over, the one named last changes fastest.
Arguments:
- earlier: bfloat16 [3, 16384, 2560], P(None, 'feat', 'dp'), may hold values from -6 to 6
- mix_weights: float32 [3], replicated, may hold values from 0.3 to 1
- destinations: int32 [2560], replicated, may hold values from -1 to 2047, as said below
- cotangent: bfloat16 [16384, 2048], P('feat', 'dp'), may hold values from -6 to 6
- right_gate: bfloat16 [128, 128, 128], P('feat'), may hold values from -0.5 to 0.5
- left_gate: bfloat16 [128, 128, 128], P('feat'), may hold values from -0.5 to 0.5
- right_up: bfloat16 [128, 128, 128], P('feat'), may hold values from -0.5 to 0.5
- left_up: bfloat16 [128, 128, 128], P('feat'), may hold values from -0.5 to 0.5
- right_down: bfloat16 [128, 128, 128], P('feat'), may hold values from -0.5 to 0.5
- left_down: bfloat16 [128, 128, 128], P('feat'), may hold values from -0.5 to 0.5
Outputs:
- output: bfloat16 [16384, 2048], P('feat', 'dp')
- mixed_grad: bfloat16 [16384, 2560], P('feat', 'dp')
- grad_right_gate: float32 [128, 128, 128], P('feat', 'dp')
- grad_left_gate: float32 [128, 128, 128], P('feat', 'dp')
- grad_right_up: float32 [128, 128, 128], P('feat', 'dp')
- grad_left_up: float32 [128, 128, 128], P('feat', 'dp')
- grad_right_down: float32 [128, 128, 128], P('feat', 'dp')
- grad_left_down: float32 [128, 128, 128], P('feat', 'dp')
Inputs may be any that keep to these rules, and one draw needn't show every extreme that they name: `destinations`: every packed row 0 to 2047 is named by exactly one slot; other slots hold -1. Among the 640 slots of one index of dp, at most 160 name rows of any one index of dp (packed rows of index g are g * 512 to (g + 1) * 512 - 1). In every draw one index of dp fills all its 640 slots, sending exactly 160 rows to every index.
All inputs are finite; a program needn't handle non-finite values.
Results may differ from a plain program's by a relative error of at most 0.0092.
Values may be sent and summed in bfloat16 or wider, within the bound.
No kernel may reach another device: no remote copies, remote signals or barrier semaphores. Data moves between devices by JAX's collectives and lax.ppermute only.
A program may use at most 128 MiB of HBM per device.

v0:
```python
import jax
import jax.numpy as jnp
from jax import lax
from jax.sharding import PartitionSpec as P


def right_apply(values, right_factor):
    return jnp.einsum(
        "ijt,ijo->iot", values, right_factor, preferred_element_type=jnp.float32
    ).astype(jnp.bfloat16)


def left_apply(spread, left_factor):
    return jnp.einsum(
        "iot,oip->pot", spread, left_factor, preferred_element_type=jnp.float32
    ).astype(jnp.bfloat16)


def left_back(out_grad, left_factor):
    return jnp.einsum(
        "pot,oip->iot", out_grad, left_factor, preferred_element_type=jnp.float32
    ).astype(jnp.bfloat16)


def right_back(spread_grad, right_factor):
    return jnp.einsum("iot,ijo->ijt", spread_grad, right_factor, preferred_element_type=jnp.float32)


def left_grad(spread, out_grad):
    return jnp.einsum("iot,pot->oip", spread, out_grad, preferred_element_type=jnp.float32)


def right_grad(values, spread_grad):
    return jnp.einsum("ijt,iot->ijo", values, spread_grad, preferred_element_type=jnp.float32)


def gelu_slope(values):
    return jax.vjp(jax.nn.gelu, values)[1](jnp.ones_like(values))[0]


def mixer_block(inputs, out_grads, factors):
    right_gate, left_gate, right_up, left_up, right_down, left_down = factors
    gate_start = right_apply(inputs, right_gate)
    up_start = right_apply(inputs, right_up)
    pieces = (
        lax.all_to_all(gate_start, "feat", split_axis=1, concat_axis=0, tiled=True),
        lax.all_to_all(up_start, "feat", split_axis=1, concat_axis=0, tiled=True),
    )
    gate_spread = pieces[0]
    up_spread = pieces[1]
    gate_mixed = left_apply(pieces[0], left_gate)
    up_mixed = left_apply(pieces[1], left_up)
    gate_out, up_out = (
        lax.all_to_all(gate_mixed, "feat", split_axis=0, concat_axis=1, tiled=True),
        lax.all_to_all(up_mixed, "feat", split_axis=0, concat_axis=1, tiled=True),
    )
    gate_f = gate_out.astype(jnp.float32)
    up_f = up_out.astype(jnp.float32)
    activated = jax.nn.gelu(gate_f)
    hidden = (activated * up_f).astype(jnp.bfloat16)
    down_start = right_apply(hidden, right_down)
    portion = lax.all_to_all(down_start, "feat", split_axis=1, concat_axis=0, tiled=True)
    down_spread = portion
    down_mixed = left_apply(portion, left_down)
    output = lax.all_to_all(down_mixed, "feat", split_axis=0, concat_axis=1, tiled=True)
    portion = lax.all_to_all(out_grads, "feat", split_axis=1, concat_axis=0, tiled=True)
    down_outgrad = portion
    down_spread_grad = left_back(portion, left_down)
    grad_left_down = left_grad(down_spread, down_outgrad)
    portion = lax.all_to_all(down_spread_grad, "feat", split_axis=0, concat_axis=1, tiled=True)
    hidden_grad = right_back(portion, right_down)
    grad_right_down = right_grad(hidden, portion)
    gate_grad = (hidden_grad * up_f * gelu_slope(gate_f)).astype(jnp.bfloat16)
    up_grad = (hidden_grad * activated).astype(jnp.bfloat16)
    pieces = (
        lax.all_to_all(gate_grad, "feat", split_axis=1, concat_axis=0, tiled=True),
        lax.all_to_all(up_grad, "feat", split_axis=1, concat_axis=0, tiled=True),
    )
    gate_outgrad = pieces[0]
    up_outgrad = pieces[1]
    gate_spread_grad = left_back(pieces[0], left_gate)
    up_spread_grad = left_back(pieces[1], left_up)
    grad_left_gate = left_grad(gate_spread, gate_outgrad)
    grad_left_up = left_grad(up_spread, up_outgrad)
    pieces = (
        lax.all_to_all(gate_spread_grad, "feat", split_axis=0, concat_axis=1, tiled=True),
        lax.all_to_all(up_spread_grad, "feat", split_axis=0, concat_axis=1, tiled=True),
    )
    gate_start_grad = pieces[0]
    up_start_grad = pieces[1]
    input_grad = right_back(pieces[0], right_gate) + right_back(pieces[1], right_up)
    grad_right_gate = right_grad(inputs, gate_start_grad)
    grad_right_up = right_grad(inputs, up_start_grad)
    grads = (
        grad_right_gate,
        grad_left_gate,
        grad_right_up,
        grad_left_up,
        grad_right_down,
        grad_left_down,
    )
    return (output, input_grad.astype(jnp.bfloat16), grads)


def body(
    earlier,
    mix_weights,
    destinations,
    cotangent,
    right_gate,
    left_gate,
    right_up,
    left_up,
    right_down,
    left_down,
):
    factors = (right_gate, left_gate, right_up, left_up, right_down, left_down)
    block_count = right_gate.shape[0]
    block_width = right_gate.shape[1]
    feat_count = earlier.shape[1]
    slot_count = earlier.shape[2]
    tok_rows = cotangent.shape[1]
    groups = lax.axis_size("dp")
    own_index = lax.axis_index("dp")
    cap_rows = 5 * tok_rows // (4 * groups)
    lane_count = groups * cap_rows
    route_table = destinations.reshape(groups, slot_count)
    target = jnp.where(route_table >= 0, route_table // tok_rows, -1)
    members = (target[:, :, None] == jnp.arange(groups, dtype=jnp.int32)[None, None, :]).astype(
        jnp.int32
    )
    places = jnp.sum((jnp.cumsum(members, axis=1) - 1) * members, axis=2)
    mine_target = lax.dynamic_index_in_dim(target, own_index, 0, keepdims=False)
    mine_place = lax.dynamic_index_in_dim(places, own_index, 0, keepdims=False)
    home_index = jnp.where(mine_target >= 0, mine_target * cap_rows + mine_place, lane_count)
    outgoing = (
        jnp.full((lane_count,), slot_count, jnp.int32)
        .at[home_index]
        .set(jnp.arange(slot_count, dtype=jnp.int32), mode="drop")
    )
    arriving = target == own_index
    lane_of = jnp.arange(groups, dtype=jnp.int32)[:, None] * cap_rows + places
    slot_here = route_table - own_index * tok_rows
    incoming = (
        jnp.zeros((tok_rows,), jnp.int32)
        .at[jnp.where(arriving, slot_here, tok_rows)]
        .set(lane_of, mode="drop")
    )
    returning = (
        jnp.full((lane_count,), tok_rows, jnp.int32)
        .at[jnp.where(arriving, lane_of, lane_count)]
        .set(slot_here, mode="drop")
    )
    averaged = jnp.zeros((feat_count, slot_count), jnp.float32)
    for depth_index in range(earlier.shape[0]):
        averaged = averaged + mix_weights[depth_index] * earlier[depth_index].astype(jnp.float32)
    mixed = averaged.astype(jnp.bfloat16)
    lane_data = jnp.take(mixed, outgoing, axis=1, mode="fill", fill_value=0)
    received = lax.all_to_all(lane_data, "dp", split_axis=1, concat_axis=1, tiled=True)
    packed = jnp.take(received, incoming, axis=1)
    result, input_grad, grads = mixer_block(
        packed.reshape(block_count, block_width, tok_rows),
        cotangent.reshape(block_count, block_width, tok_rows),
        factors,
    )
    output = result.reshape(feat_count, tok_rows)
    lane_data = jnp.take(
        input_grad.reshape(feat_count, tok_rows), returning, axis=1, mode="fill", fill_value=0
    )
    received = lax.all_to_all(lane_data, "dp", split_axis=1, concat_axis=1, tiled=True)
    mixed_grad = jnp.take(received, home_index, axis=1, mode="fill", fill_value=0)
    summed = (
        lax.psum_scatter(grads[0], "dp", scatter_dimension=1, tiled=True),
        lax.psum_scatter(grads[1], "dp", scatter_dimension=1, tiled=True),
        lax.psum_scatter(grads[2], "dp", scatter_dimension=1, tiled=True),
        lax.psum_scatter(grads[3], "dp", scatter_dimension=1, tiled=True),
        lax.psum_scatter(grads[4], "dp", scatter_dimension=1, tiled=True),
        lax.psum_scatter(grads[5], "dp", scatter_dimension=1, tiled=True),
    )
    grad_scale = (tok_rows * groups) ** (-0.5)
    return (
        output,
        mixed_grad,
        summed[0] * grad_scale,
        summed[1] * grad_scale,
        summed[2] * grad_scale,
        summed[3] * grad_scale,
        summed[4] * grad_scale,
        summed[5] * grad_scale,
    )


def solution(mesh):
    return jax.shard_map(
        body,
        mesh=mesh,
        in_specs=(
            P(None, "feat", "dp"),
            P(),
            P(),
            P("feat", "dp"),
            P("feat", None, None),
            P("feat", None, None),
            P("feat", None, None),
            P("feat", None, None),
            P("feat", None, None),
            P("feat", None, None),
        ),
        out_specs=(
            P("feat", "dp"),
            P("feat", "dp"),
            P("feat", "dp", None),
            P("feat", "dp", None),
            P("feat", "dp", None),
            P("feat", "dp", None),
            P("feat", "dp", None),
            P("feat", "dp", None),
        ),
        check_vma=False,
    )
```

profile of v0, /device:TPU:0, one launch (start us, length us, event | category | flops | bytes accessed | tf_op | source)
XLA Modules:
  0.0 591.6 jit_solution(17118959811074789341)
XLA Ops:
  7.2 4.1 copy.229
  11.3 5.3 all-to-all-start.7
  16.7 4.5 reduce-window.6
  22.6 5.1 fusion.55
  27.7 4.1 scatter_custom_fusion.1
  31.8 4.5 copy.268
  36.3 4.5 copy.269
  44.1 7.1 %fusion.9 = bf16[2048,640]{0,1:T(8,128)(2,1)S(1)} fusion(bf16[1,2048,640]{1,2,0:T(8,128)(2,1)} %copy.270, bf16[1,2048,640]{1,2,0:T(8,128)(2,1)} %copy.269, bf16[1,2048,640]{1,2,0:T(8,128)(2,1)} %copy.268, f32[]{:T(128)} %bitcast.4, f32[]{:T(128)} %bitcast.3, f32[]{:T(128)} %bitcast.2), kind=kLoop, calls=%fused_computation.26 | loop fusion | flops 11796480 | bytes 10485772 | tf_op jit(solution)/shard_map/add | solution.py:156
  51.2 4.1 gather_fusion.2
  58.7 5.5 all-to-all-start
  69.9 54.3 %all-to-all-done = bf16[2048,4,160]{0,2,1:T(8,128)(2,1)S(1)} async-done(((bf16[2048,4,160]{0,2,1:T(8,128)(2,1)}), bf16[2048,4,160]{0,2,1:T(8,128)(2,1)S(1)}, u32[]{:S(2)}, u32[]{:S(2)}) %all-to-all-start) | async-done | bytes 2621472 | tf_op jit(solution)/shard_map/all_to_all | solution.py:159
  124.2 4.4 all-to-all-start.8
  128.8 10.1 %scatter_custom_fusion = s32[512]{0:T(512)S(1)} fusion(s32[2560]{0:T(1024)S(1)} %reshape.389, s32[2560]{0:T(1024)S(1)} %reshape.391, s32[]{:T(128)} %constant.46.clone.1), kind=kCustom, calls=%fused_computation.122 | custom fusion | bytes 2052 | tf_op jit(solution)/shard_map/scatter | solution.py:147
  147.3 4.6 copy.216
  155.2 4.3 all-to-all-start.3
  161.7 4.5 copy.204
  166.2 20.0 %all-to-all-done.3 = bf16[16,128,512]{2,0,1:T(8,128)(2,1)} async-done(((bf16[16,128,512]{2,0,1:T(8,128)(2,1)}), bf16[16,128,512]{2,0,1:T(8,128)(2,1)}, u32[]{:S(2)}, u32[]{:S(2)}) %all-to-all-start.3) | async-done | bytes 2097184 | tf_op jit(solution)/shard_map/all_to_all | solution.py:47
  197.7 4.5 copy.220
  202.3 14.1 %all-to-all-done.1 = bf16[16,128,512]{2,0,1:T(8,128)(2,1)S(1)} async-done(((bf16[16,128,512]{2,0,1:T(8,128)(2,1)}), bf16[16,128,512]{2,0,1:T(8,128)(2,1)S(1)}, u32[]{:S(2)}, u32[]{:S(2)}) %all-to-all-start.1) | async-done | bytes 2097184 | tf_op jit(solution)/shard_map/all_to_all | solution.py:46
  229.7 4.5 copy.208
  234.1 14.2 %all-to-all-done.4 = bf16[128,16,512]{2,1,0:T(8,128)(2,1)S(1)} async-done(((bf16[128,16,512]{2,1,0:T(8,128)(2,1)}), bf16[128,16,512]{2,1,0:T(8,128)(2,1)S(1)}, u32[]{:S(2)}, u32[]{:S(2)}) %all-to-all-start.4) | async-done | bytes 2097184 | tf_op jit(solution)/shard_map/all_to_all | solution.py:55
  248.3 4.4 all-to-all-start.2
  258.9 5.3 copy.222
  264.3 15.1 %all-to-all-done.2 = bf16[128,16,512]{2,1,0:T(8,128)(2,1)} async-done(((bf16[128,16,512]{2,1,0:T(8,128)(2,1)}), bf16[128,16,512]{2,1,0:T(8,128)(2,1)}, u32[]{:S(2)}, u32[]{:S(2)}) %all-to-all-start.2) | async-done | bytes 2097184 | tf_op jit(solution)/shard_map/all_to_all | solution.py:54
  284.0 5.6 copy.214
  289.6 8.0 %fusion.8 = (bf16[16,128,512]{1,2,0:T(8,128)(2,1)}, bf16[16,128,512]{1,2,0:T(8,128)(2,1)}, bf16[16,128,512]{1,2,0:T(8,128)(2,1)}) fusion(f32[16,128,512]{1,2,0:T(8,128)} %copy.214, f32[16,128,512]{1,2,0:T(8,128)} %copy.222, bf16[16,128,512]{2,1,0:T(8,128)(2,1)S(1)} %bitcast.165, bf16[16,128,128]{2,1,0:T(8,128)(2,1)S(1)} %copy-done), kind=kOutput, calls=%fused_computation.22 | convolution fusion | flops 294649856 | bytes 17301504 | tf_op jit(solution)/shard_map/iot,ijo->ijt/dot_general | solution.py:26
  297.6 4.6 copy.243
  305.8 4.6 copy.237
  310.4 22.0 %all-to-all-done.11 = bf16[16,128,512]{2,0,1:T(8,128)(2,1)S(1)} async-done(((bf16[16,128,512]{2,0,1:T(8,128)(2,1)}), bf16[16,128,512]{2,0,1:T(8,128)(2,1)S(1)}, u32[]{:S(2)}, u32[]{:S(2)}) %all-to-all-start.11) | async-done | bytes 2097184 | tf_op jit(solution)/shard_map/all_to_all | solution.py:77
  345.1 4.5 copy.223
  349.6 14.4 %all-to-all-done.9 = bf16[16,128,512]{2,0,1:T(8,128)(2,1)S(1)} async-done(((bf16[16,128,512]{2,0,1:T(8,128)(2,1)}), bf16[16,128,512]{2,0,1:T(8,128)(2,1)S(1)}, u32[]{:S(2)}, u32[]{:S(2)}) %all-to-all-start.9) | async-done | bytes 2097184 | tf_op jit(solution)/shard_map/all_to_all | solution.py:76
  376.8 5.3 convert_bitcast_fusion.2
  382.1 4.5 copy.247
  386.6 9.0 %all-to-all-done.5 = bf16[16,128,512]{2,0,1:T(8,128)(2,1)S(1)} async-done(((bf16[16,128,512]{2,0,1:T(8,128)(2,1)}), bf16[16,128,512]{2,0,1:T(8,128)(2,1)S(1)}, u32[]{:S(2)}, u32[]{:S(2)}) %all-to-all-start.5) | async-done | bytes 2097184 | tf_op jit(solution)/shard_map/all_to_all | solution.py:62
  408.6 5.3 convert_bitcast_fusion.3
  413.8 4.5 copy.241
  418.3 8.8 %all-to-all-done.12 = bf16[128,16,512]{2,1,0:T(8,128)(2,1)S(1)} async-done(((bf16[128,16,512]{2,1,0:T(8,128)(2,1)}), bf16[128,16,512]{2,1,0:T(8,128)(2,1)S(1)}, u32[]{:S(2)}, u32[]{:S(2)}) %all-to-all-start.12) | async-done | bytes 2097184 | tf_op jit(solution)/shard_map/all_to_all | solution.py:87
  428.6 4.4 all-to-all-start.10
  433.0 10.2 %scatter_custom_fusion.2 = s32[640]{0:T(1024)S(1)} fusion(s32[2560]{0:T(1024)S(1)} %reshape.405, s32[2560]{0:T(1024)S(1)} %reshape.407, s32[]{:T(128)} %constant.58.clone.1), kind=kCustom, calls=%fused_computation.117 | custom fusion | bytes 2564 | tf_op jit(solution)/shard_map/scatter | solution.py:152
  452.4 4.6 copy.227
  459.6 4.4 all-to-all-start.6
  477.3 4.1 gather_fusion.1
  485.0 5.7 all-to-all-done.6
  494.6 4.0 fusion.24
  508.6 10.1 %reduce-scatter.11.cloned.1.call-done = f32[16,32,128]{2,1,0:T(8,128)} async-done(((f32[16,128,128]{2,1,0:T(8,128)}), f32[16,32,128]{2,1,0:T(8,128)}) %reduce-scatter.11.cloned.1.call-update) | async-done | bytes 262160 | tf_op jit(solution)/shard_map/reduce_scatter | solution.py:175
  520.4 47.5 %reduce-scatter.7.cloned.1.call-done = f32[16,32,128]{2,1,0:T(8,128)} async-done(((f32[16,128,128]{2,1,0:T(8,128)}), f32[16,32,128]{2,1,0:T(8,128)}) %reduce-scatter.7.cloned.1.call-update) | async-done | bytes 262160 | tf_op jit(solution)/shard_map/reduce_scatter | solution.py:173
  569.6 6.1 %all-to-all-done.13 = bf16[2048,4,160]{0,2,1:T(8,128)(2,1)S(1)} async-done(((bf16[2048,4,160]{0,2,1:T(8,128)(2,1)}), bf16[2048,4,160]{0,2,1:T(8,128)(2,1)S(1)}, u32[]{:S(2)}, u32[]{:S(2)}) %all-to-all-start.13) | async-done | bytes 2621472 | tf_op jit(solution)/shard_map/all_to_all | solution.py:170
  575.7 4.1 gather_fusion.3
  (165 shorter events, 157.0 us)
Async XLA Ops:
  7.2 282.4 %copy-start = (bf16[16,128,128]{2,1,0:T(8,128)(2,1)S(1)}, bf16[16,128,128]{2,1,0:T(8,128)(2,1)}, u32[]{:S(2)}) copy-start(bf16[16,128,128]{2,1,0:T(8,128)(2,1)} %param.20) | copy-start | bytes 1572868
  11.3 5.3 copy-start.28
  11.3 47.4 %all-to-all-start.7 = ((bf16[16,128,512]{2,0,1:T(8,128)(2,1)}), bf16[16,128,512]{2,0,1:T(8,128)(2,1)}, u32[]{:S(2)}, u32[]{:S(2)}) async-start(bf16[16,128,512]{2,0,1:T(8,128)(2,1)} %copy.229), calls=%async_computation.7 | async-start | bytes 4194304 | tf_op jit(solution)/shard_map/all_to_all | solution.py:66
  40.8 2.6 copy-start.29
  58.7 65.5 %all-to-all-start = ((bf16[2048,4,160]{0,2,1:T(8,128)(2,1)}), bf16[2048,4,160]{0,2,1:T(8,128)(2,1)S(1)}, u32[]{:S(2)}, u32[]{:S(2)}) async-start(bf16[2048,4,160]{0,2,1:T(8,128)(2,1)} %bitcast.150), calls=%async_computation | async-start | bytes 5242880 | tf_op jit(solution)/shard_map/all_to_all | solution.py:159
  64.3 1.9 copy-start.22
  124.2 31.0 %all-to-all-start.8 = ((bf16[128,16,512]{2,1,0:T(8,128)(2,1)}), bf16[128,16,512]{2,1,0:T(8,128)(2,1)}, u32[]{:S(2)}, u32[]{:S(2)}) async-start(bf16[128,16,512]{2,1,0:T(8,128)(2,1)} %copy.232), calls=%async_computation.8 | async-start | bytes 4194304 | tf_op jit(solution)/shard_map/all_to_all | solution.py:70
  142.2 2.9 copy-start.24
  145.1 14.4 %copy-start.1 = (bf16[2048,512]{1,0:T(8,128)(2,1)}, bf16[2048,512]{1,0:T(8,128)(2,1)S(1)}, u32[]{:S(2)}) copy-start(bf16[2048,512]{1,0:T(8,128)(2,1)S(1)} %copy.261) | copy-start | bytes 6291460
  151.9 7.7 %copy-start.26 = (bf16[16,128,128]{2,1,0:T(8,128)(2,1)S(1)}, bf16[16,128,128]{2,1,0:T(8,128)(2,1)}, u32[]{:S(2)}) copy-start(bf16[16,128,128]{2,1,0:T(8,128)(2,1)} %param.16) | copy-start | bytes 1572868
  155.2 31.0 %all-to-all-start.3 = ((bf16[16,128,512]{2,0,1:T(8,128)(2,1)}), bf16[16,128,512]{2,0,1:T(8,128)(2,1)}, u32[]{:S(2)}, u32[]{:S(2)}) async-start(bf16[16,128,512]{2,0,1:T(8,128)(2,1)} %copy.216), calls=%async_computation.3 | async-start | bytes 4194304 | tf_op jit(solution)/shard_map/all_to_all | solution.py:47
  186.2 30.2 %all-to-all-start.1 = ((bf16[16,128,512]{2,0,1:T(8,128)(2,1)}), bf16[16,128,512]{2,0,1:T(8,128)(2,1)S(1)}, u32[]{:S(2)}, u32[]{:S(2)}) async-start(bf16[16,128,512]{2,0,1:T(8,128)(2,1)} %copy.204), calls=%async_computation.1 | async-start | bytes 4194304 | tf_op jit(solution)/shard_map/all_to_all | solution.py:46
  189.8 4.2 copy-start.19
  192.7 1.3 copy-start.7
  217.7 30.6 %all-to-all-start.4 = ((bf16[128,16,512]{2,1,0:T(8,128)(2,1)}), bf16[128,16,512]{2,1,0:T(8,128)(2,1)S(1)}, u32[]{:S(2)}, u32[]{:S(2)}) async-start(bf16[128,16,512]{2,1,0:T(8,128)(2,1)} %copy.220), calls=%async_computation.4 | async-start | bytes 4194304 | tf_op jit(solution)/shard_map/all_to_all | solution.py:55
  221.7 4.3 copy-start.20
  224.6 1.4 copy-start.5
  248.3 31.0 %all-to-all-start.2 = ((bf16[128,16,512]{2,1,0:T(8,128)(2,1)}), bf16[128,16,512]{2,1,0:T(8,128)(2,1)}, u32[]{:S(2)}, u32[]{:S(2)}) async-start(bf16[128,16,512]{2,1,0:T(8,128)(2,1)} %copy.208), calls=%async_computation.2 | async-start | bytes 4194304 | tf_op jit(solution)/shard_map/all_to_all | solution.py:54
  284.0 5.6 copy-start.13
  302.2 30.2 %all-to-all-start.11 = ((bf16[16,128,512]{2,0,1:T(8,128)(2,1)}), bf16[16,128,512]{2,0,1:T(8,128)(2,1)S(1)}, u32[]{:S(2)}, u32[]{:S(2)}) async-start(bf16[16,128,512]{2,0,1:T(8,128)(2,1)} %copy.243), calls=%async_computation.11 | async-start | bytes 4194304 | tf_op jit(solution)/shard_map/all_to_all | solution.py:77
  332.4 1.3 copy-start.14
  333.8 30.2 %all-to-all-start.9 = ((bf16[16,128,512]{2,0,1:T(8,128)(2,1)}), bf16[16,128,512]{2,0,1:T(8,128)(2,1)S(1)}, u32[]{:S(2)}, u32[]{:S(2)}) async-start(bf16[16,128,512]{2,0,1:T(8,128)(2,1)} %copy.237), calls=%async_computation.9 | async-start | bytes 4194304 | tf_op jit(solution)/shard_map/all_to_all | solution.py:76
  337.4 161.4 %reduce-scatter.15.cloned.1.call-start = ((), (), s32[]{:S(2)}) async-start(), calls=%async_computation.24 | async-start | bytes 1310720 | tf_op jit(solution)/shard_map/reduce_scatter | solution.py:177
  363.9 1.4 copy-start.12
  365.3 30.4 %all-to-all-start.5 = ((bf16[16,128,512]{2,0,1:T(8,128)(2,1)}), bf16[16,128,512]{2,0,1:T(8,128)(2,1)S(1)}, u32[]{:S(2)}, u32[]{:S(2)}) async-start(bf16[16,128,512]{2,0,1:T(8,128)(2,1)} %copy.223), calls=%async_computation.5 | async-start | bytes 4194304 | tf_op jit(solution)/shard_map/all_to_all | solution.py:62
  369.1 134.5 %reduce-scatter.13.cloned.1.call-start = ((), (), s32[]{:S(2)}) async-start(), calls=%async_computation.23 | async-start | bytes 1310720 | tf_op jit(solution)/shard_map/reduce_scatter | solution.py:176
  369.1 4.3 copy-start.8
  372.1 1.3 copy-start.17
  395.7 1.3 copy-start.11
  397.0 30.2 %all-to-all-start.12 = ((bf16[128,16,512]{2,1,0:T(8,128)(2,1)}), bf16[128,16,512]{2,1,0:T(8,128)(2,1)S(1)}, u32[]{:S(2)}, u32[]{:S(2)}) async-start(bf16[128,16,512]{2,1,0:T(8,128)(2,1)} %copy.247), calls=%async_computation.12 | async-start | bytes 4194304 | tf_op jit(solution)/shard_map/all_to_all | solution.py:87
  400.6 104.7 %reduce-scatter.9.cloned.1.call-start = ((), (), s32[]{:S(2)}) async-start(), calls=%async_computation.21 | async-start | bytes 1310720 | tf_op jit(solution)/shard_map/reduce_scatter | solution.py:174
  400.9 4.3 copy-start.6
  403.9 1.3 copy-start.18
  405.2 3.4 copy-start.21
  427.2 1.4 copy-start.9
  428.6 31.0 %all-to-all-start.10 = ((bf16[128,16,512]{2,1,0:T(8,128)(2,1)}), bf16[128,16,512]{2,1,0:T(8,128)(2,1)}, u32[]{:S(2)}, u32[]{:S(2)}) async-start(bf16[128,16,512]{2,1,0:T(8,128)(2,1)} %copy.241), calls=%async_computation.10 | async-start | bytes 4194304 | tf_op jit(solution)/shard_map/all_to_all | solution.py:86
  432.9 74.0 %reduce-scatter.17.cloned.1.call-start = ((), (), s32[]{:S(2)}) async-start(), calls=%async_computation.25 | async-start | bytes 1310720 | tf_op jit(solution)/shard_map/reduce_scatter | solution.py:178
  443.2 3.0 copy-start.3
  446.2 2.5 copy-start.23
  457.0 7.1 %copy-start.10 = (bf16[128,16,512]{2,1,0:T(8,128)(2,1)S(1)}, bf16[128,16,512]{2,1,0:T(8,128)(2,1)}, u32[]{:S(2)}) copy-start(bf16[128,16,512]{2,1,0:T(8,128)(2,1)} %copy-done.9) | copy-start | bytes 6291460
  459.6 31.0 %all-to-all-start.6 = ((bf16[128,16,512]{2,1,0:T(8,128)(2,1)}), bf16[128,16,512]{2,1,0:T(8,128)(2,1)}, u32[]{:S(2)}, u32[]{:S(2)}) async-start(bf16[128,16,512]{2,1,0:T(8,128)(2,1)} %copy.227), calls=%async_computation.6 | async-start | bytes 4194304 | tf_op jit(solution)/shard_map/all_to_all | solution.py:65
  464.0 54.7 %reduce-scatter.11.cloned.1.call-start = ((), (), s32[]{:S(2)}) async-start(), calls=%async_computation.22 | async-start | bytes 1310720 | tf_op jit(solution)/shard_map/reduce_scatter | solution.py:175
  464.3 3.9 copy-start.4
  464.3 2.6 copy-start.27
  466.9 1.3 copy-start.15
  466.9 1.5 copy-start.25
  490.6 85.1 %all-to-all-start.13 = ((bf16[2048,4,160]{0,2,1:T(8,128)(2,1)}), bf16[2048,4,160]{0,2,1:T(8,128)(2,1)S(1)}, u32[]{:S(2)}, u32[]{:S(2)}) async-start(bf16[2048,4,160]{0,2,1:T(8,128)(2,1)} %broadcast_select_fusion.1), calls=%async_computation.13 | async-start | bytes 5242880 | tf_op jit(solution)/shard_map/all_to_all | solution.py:170
  494.3 73.6 %reduce-scatter.7.cloned.1.call-start = ((), (), s32[]{:S(2)}) async-start(), calls=%async_computation.20 | async-start | bytes 1310720 | tf_op jit(solution)/shard_map/reduce_scatter | solution.py:173
  (2 other events, 2.6 us)
Sparse Core Ops, SparseCore 0:
  341.6 26.6 reduce-scatter.14
  376.9 26.5 reduce-scatter.12
  408.7 26.6 reduce-scatter.8
  448.8 26.5 reduce-scatter.16
  477.6 41.1 reduce-scatter.10
  521.0 46.8 reduce-scatter.6
where the time goes:
time: 603 us; the launch traced here: 592 us
  waiting for transfers between devices  247 us (41%)
  local copies, waits for them, and re-layouts  173 us (29%)
  matrix products  61.9 us (10%)
  starting transfers between devices  59.3 us (10%)
  other arithmetic  34.6 us (6%)
  between operations  15.3 us (3%)
    all_to_all x2, waiting for transfers between devices, body(): lax.all_to_all(lane_data, 'dp', split_axis=1, concat_axis=1, tiled=True)  60.4 us
    reduce_scatter x1, waiting for transfers between devices, body(): lax.psum_scatter(grads[0], 'dp', scatter_dimension=1, tiled=True)  47.5 us
    unnamed x64, local copies, waits for them, and re-layouts  27.7 us
    all_to_all x1, waiting for transfers between devices, mixer_block(): lax.all_to_all(up_grad, 'feat', split_axis=1, concat_axis=0, tiled=True)  22 us
    all_to_all x1, waiting for transfers between devices, mixer_block(): lax.all_to_all(up_start, 'feat', split_axis=1, concat_axis=0, tiled=True)  20 us
    all_to_all x1, waiting for transfers between devices, mixer_block(): lax.all_to_all(gate_mixed, 'feat', split_axis=0, concat_axis=1, tiled=True)  15.1 us
    all_to_all x1, waiting for transfers between devices, mixer_block(): lax.all_to_all(gate_grad, 'feat', split_axis=1, concat_axis=0, tiled=True)  14.4 us
    all_to_all x1, waiting for transfers between devices, mixer_block(): lax.all_to_all(up_mixed, 'feat', split_axis=0, concat_axis=1, tiled=True)  14.2 us
  transfers between devices with their start and end apart: 20, of which 15 were waited for; matrix products, arithmetic and copies ran while one was open for 37% of the time, Pallas kernels for 0%

commit v1 on v0

v1 whole, which is shorter than its diff:
```python
import functools

import jax
import jax.numpy as jnp
from jax import lax
from jax.experimental import pallas as pl
from jax.experimental.pallas import tpu as pltpu
from jax.sharding import PartitionSpec as P

F32 = jnp.float32
BF16 = jnp.bfloat16
VMEM_LIMIT = 48 * 1024 * 1024


def params(steps=1):
    return pltpu.CompilerParams(
        vmem_limit_bytes=VMEM_LIMIT, dimension_semantics=("arbitrary",) * steps
    )


def dot(a, b, over):
    return lax.dot_general(a, b, (over, ((), ())), preferred_element_type=F32)


NN = ((1,), (0,))
NT = ((1,), (1,))
TN = ((0,), (0,))


def routing_kernel(sizes, own_ref, dest_ref, home_ref, back_ref, back_t_ref):
    groups, tok, cap, lanes = sizes
    rows, slots = dest_ref.shape
    own = own_ref[0]
    dest = dest_ref[...]
    group = lax.broadcasted_iota(jnp.int32, (rows, slots), 0)
    if groups & (groups - 1) == 0:
        relative = group ^ own
    else:
        relative = jnp.where(group >= own, group - own, group - own + groups)
    before = lax.broadcasted_iota(jnp.int32, (slots, slots), 0) < lax.broadcasted_iota(
        jnp.int32, (slots, slots), 1
    )
    before = jnp.where(before, 1.0, 0.0).astype(BF16)
    lane = lax.broadcasted_iota(jnp.int32, (lanes, slots), 0)

    def place(members):
        return dot(jnp.where(members, 1.0, 0.0).astype(BF16), before, NN).astype(jnp.int32)

    mine = jnp.sum(jnp.where(group == own, dest, 0), axis=0, keepdims=True)
    local = mine - group * tok
    leaving = (local >= 0) & (local < tok) & (group < groups) & (mine >= 0)
    index = jnp.where(leaving, relative * cap + place(leaving) + 1, 0)
    home = jnp.sum(index, axis=0, keepdims=True) - 1
    home_ref[...] = jnp.where(lane == home, 1.0, 0.0).astype(BF16)
    local = dest - own * tok
    arriving = (local >= 0) & (local < tok) & (dest >= 0)
    index = jnp.where(arriving, relative * cap + place(arriving), -1)
    total = jnp.zeros((lanes, slots), jnp.int32)
    for source in range(groups):
        total = total + jnp.where(
            lane == index[source : source + 1], local[source : source + 1] + 1, 0
        )
    row = jnp.sum(total.astype(F32), axis=1, keepdims=True).astype(jnp.int32) - 1
    taken = lax.broadcasted_iota(jnp.int32, (lanes, tok), 1) == row
    taken = jnp.where(taken, 1.0, 0.0)
    back_ref[...] = taken.astype(BF16)
    back_t_ref[...] = taken.T.astype(BF16)


def routing(destinations, own, groups, tok, cap):
    slots = destinations.shape[0] // groups
    lanes = groups * cap
    rows = -(-groups // 16) * 16
    table = destinations.reshape(groups, slots)
    table = jnp.pad(table, ((0, rows - groups), (0, 0)), constant_values=-1)
    return pl.pallas_call(
        functools.partial(routing_kernel, (groups, tok, cap, lanes)),
        in_specs=[
            pl.BlockSpec(memory_space=pltpu.SMEM),
            pl.BlockSpec(memory_space=pltpu.VMEM),
        ],
        out_specs=[pl.BlockSpec(memory_space=pltpu.VMEM)] * 3,
        out_shape=[
            jax.ShapeDtypeStruct((lanes, slots), BF16),
            jax.ShapeDtypeStruct((lanes, tok), BF16),
            jax.ShapeDtypeStruct((tok, lanes), BF16),
        ],
        compiler_params=pltpu.CompilerParams(vmem_limit_bytes=VMEM_LIMIT),
        name="routing",
    )(own, table)


def mix_kernel(weights_ref, earlier_ref, home_ref, *out_refs):
    total = weights_ref[0] * earlier_ref[0].astype(F32)
    for k in range(1, earlier_ref.shape[0]):
        total = total + weights_ref[k] * earlier_ref[k].astype(F32)
    sent = dot(home_ref[...], total.astype(BF16), NT).astype(BF16)
    cap = out_refs[0].shape[0]
    for k, ref in enumerate(out_refs):
        ref[...] = sent[k * cap : (k + 1) * cap]


def mix_and_sort(earlier, mix_weights, home, groups, width):
    depth, feats, slots = earlier.shape
    lanes = home.shape[0]
    cap = lanes // groups
    step = 2 * width
    return pl.pallas_call(
        mix_kernel,
        grid=(feats // step,),
        in_specs=[
            pl.BlockSpec(memory_space=pltpu.SMEM),
            pl.BlockSpec((depth, step, slots), lambda i: (0, i, 0)),
            pl.BlockSpec((lanes, slots), lambda i: (0, 0)),
        ],
        out_specs=[pl.BlockSpec((cap, step), lambda i: (0, i))] * groups,
        out_shape=[jax.ShapeDtypeStruct((cap, feats), BF16)] * groups,
        compiler_params=params(),
        name="mix_and_sort",
    )(mix_weights, earlier, home)


def exchange_rows(slabs, groups):
    received = [slabs[0]]
    for k in range(1, groups):
        if groups & (groups - 1) == 0:
            pairs = [(i, i ^ k) for i in range(groups)]
        else:
            pairs = [(i, (i + k) % groups) for i in range(groups)]
        received.append(lax.ppermute(slabs[k], "dp", pairs))
    return received


def unsort_kernel(home_ref, *refs):
    in_refs, out_ref = refs[:-1], refs[-1]
    rows = jnp.concatenate([ref[...] for ref in in_refs], axis=0)
    out_ref[...] = dot(rows, home_ref[...], TN).astype(BF16)


def unsort(slabs, home, width):
    lanes, slots = home.shape
    cap, feats = slabs[0].shape
    step = 2 * width
    return pl.pallas_call(
        unsort_kernel,
        grid=(feats // step,),
        in_specs=[pl.BlockSpec((lanes, slots), lambda i: (0, 0))]
        + [pl.BlockSpec((cap, step), lambda i: (0, i))] * len(slabs),
        out_specs=pl.BlockSpec((step, slots), lambda i: (i, 0)),
        out_shape=jax.ShapeDtypeStruct((feats, slots), BF16),
        compiler_params=params(),
        name="unsort",
    )(home, *slabs)


class Plan:
    def __init__(self, peers, held, width, tok):
        self.peers, self.held, self.width, self.tok = peers, held, width, tok
        self.piece = held * held
        self.direct = held % 16 == 0

    def sent_shape(self, parts):
        return jax.ShapeDtypeStruct((self.peers, parts * self.piece, self.tok), BF16)

    def sent_spec(self, parts, step):
        return pl.BlockSpec((self.peers, parts * self.piece, step), lambda t: (0, 0, t))

    def arranged(self, array):
        if self.direct:
            return array
        parts = array.shape[1] // self.piece
        array = array.reshape(self.peers, parts, self.held, self.held, self.tok)
        array = array.transpose(1, 2, 0, 3, 4)
        return array.reshape(parts * self.held, self.width, self.tok)

    def arrived_spec(self, parts, step):
        if self.direct:
            return self.sent_spec(parts, step)
        return pl.BlockSpec((parts * self.held, self.width, step), lambda t: (0, 0, t))

    def block(self, ref, part, b):
        if not self.direct:
            return ref[part * self.held + b]
        base = part * self.piece + b * self.held
        return jnp.concatenate(
            [ref[s, base : base + self.held, :] for s in range(self.peers)], axis=0
        )

    def put(self, scratch, b, value):
        for at in range(scratch.shape[0]):
            scratch[at, pl.ds(b, self.width, stride=self.held), :] = value[
                :, at * 128 : (at + 1) * 128
            ]

    def store(self, out_ref, part, scratch):
        rows = slice(part * self.piece, (part + 1) * self.piece)
        for at in range(scratch.shape[0]):
            out_ref[:, rows, at * 128 : (at + 1) * 128] = (
                scratch[at].reshape(self.peers, self.piece, 128).astype(BF16)
            )


def step_of(tok):
    return 256 if tok % 256 == 0 else 128


def scratch_for(plan, step):
    return pltpu.VMEM((step // 128, plan.width * plan.held, 128), F32)


def whole(array):
    return pl.BlockSpec(array.shape, lambda t: (0,) * array.ndim)


def sum_over_steps(ref, b, value, scale):
    step = pl.program_id(0)

    @pl.when(step == 0)
    def _():
        ref[b] = value * scale

    @pl.when(step > 0)
    def _():
        ref[b] += value * scale


def cotangent_kernel(plan, in_ref, out_ref, scratch):
    for b in range(plan.held):
        plan.put(scratch, b, in_ref[b * plan.width : (b + 1) * plan.width, :].astype(F32))
    plan.store(out_ref, 0, scratch)


def send_cotangent(plan, cotangent):
    step = step_of(plan.tok)
    return pl.pallas_call(
        functools.partial(cotangent_kernel, plan),
        grid=(plan.tok // step,),
        in_specs=[pl.BlockSpec((plan.width * plan.held, step), lambda t: (0, t))],
        out_specs=plan.sent_spec(1, step),
        out_shape=plan.sent_shape(1),
        scratch_shapes=[scratch_for(plan, step)],
        compiler_params=params(),
        name="send_cotangent",
    )(cotangent)


def product_kernel(plan, over, in_ref, factor_ref, out_ref, scratch):
    for b in range(plan.held):
        plan.put(scratch, b, dot(factor_ref[b], plan.block(in_ref, 0, b), over))
    plan.store(out_ref, 0, scratch)


def product(plan, arrived, factor, over, name):
    step = step_of(plan.tok)
    return pl.pallas_call(
        functools.partial(product_kernel, plan, over),
        grid=(plan.tok // step,),
        in_specs=[plan.arrived_spec(1, step), whole(factor)],
        out_specs=plan.sent_spec(1, step),
        out_shape=plan.sent_shape(1),
        scratch_shapes=[scratch_for(plan, step)],
        compiler_params=params(),
        name=name,
    )(arrived, factor)


def product_and_grad_kernel(
    plan, scale, values_first, in_ref, other_ref, factor_ref, out_ref, grad_ref, scratch, sums
):
    for b in range(plan.held):
        values = plan.block(in_ref, 0, b)
        others = plan.block(other_ref, 0, b)
        plan.put(scratch, b, dot(factor_ref[b], values, TN))
        sum_over_steps(sums, b, dot(values, others, NT), scale)
    plan.store(out_ref, 0, scratch)
    grad_ref[...] = sums[...].astype(BF16)


def product_and_grad(plan, arrived, other, factor, scale, name):
    step = step_of(plan.tok)
    return pl.pallas_call(
        functools.partial(product_and_grad_kernel, plan, scale, True),
        grid=(plan.tok // step,),
        in_specs=[plan.arrived_spec(1, step), plan.arrived_spec(1, step), whole(factor)],
        out_specs=[plan.sent_spec(1, step), whole(factor)],
        out_shape=[plan.sent_shape(1), jax.ShapeDtypeStruct(factor.shape, BF16)],
        scratch_shapes=[scratch_for(plan, step), pltpu.VMEM(factor.shape, F32)],
        compiler_params=params(),
        name=name,
    )(arrived, other, factor)


def first_kernel(plan, groups, *refs):
    slab_refs, (back_t_ref, gate_ref, up_ref, packed_ref, out_ref, gates, ups) = (
        refs[:groups],
        refs[groups:],
    )
    step = pl.program_id(0)
    count = gate_ref.shape[0]
    rows = jnp.concatenate([ref[...] for ref in slab_refs], axis=0)
    packed = dot(back_t_ref[...], rows, NN).astype(BF16)
    packed_ref[...] = packed
    for at in range(count):
        values = packed[:, at * plan.width : (at + 1) * plan.width]
        b = step * count + at
        plan.put(gates, b, dot(gate_ref[at], values, ((0,), (1,))))
        plan.put(ups, b, dot(up_ref[at], values, ((0,), (1,))))

    @pl.when(step == pl.num_programs(0) - 1)
    def _():
        plan.store(out_ref, 0, gates)
        plan.store(out_ref, 1, ups)


def first_products(plan, slabs, back_t, right_gate, right_up):
    count = 4
    cap, feats = slabs[0].shape
    width = plan.width
    steps = plan.held // count
    factor_spec = pl.BlockSpec((count,) + right_gate.shape[1:], lambda i: (i, 0, 0))
    return pl.pallas_call(
        functools.partial(first_kernel, plan, len(slabs)),
        grid=(steps,),
        in_specs=[pl.BlockSpec((cap, count * width), lambda i: (0, i))] * len(slabs)
        + [whole(back_t), factor_spec, factor_spec],
        out_specs=[
            pl.BlockSpec((plan.tok, count * width), lambda i: (0, i)),
            pl.BlockSpec(plan.sent_shape(2).shape, lambda i: (0, 0, 0)),
        ],
        out_shape=[jax.ShapeDtypeStruct((plan.tok, feats), BF16), plan.sent_shape(2)],
        scratch_shapes=[scratch_for(plan, plan.tok)] * 2,
        compiler_params=params(),
        name="first_products",
    )(*slabs, back_t, right_gate, right_up)


ROOT = 0.7978845608028654
CUBE = 0.044715


def gelu_and_slope(x):
    square = x * x
    wave = jnp.tanh(ROOT * (x + CUBE * (square * x)))
    half = 0.5 * (1.0 + wave)
    slope = half + 0.5 * x * (1.0 - wave * wave) * (ROOT * (1.0 + 3.0 * CUBE * square))
    return x * half, slope


def middle_kernel(
    plan,
    scale,
    spread_ref,
    hidden_grad_ref,
    gate_ref,
    up_ref,
    hidden_ref,
    out_ref,
    gate_grad_ref,
    up_grad_ref,
    hiddens,
    gates,
    ups,
    gate_sums,
    up_sums,
):
    for b in range(plan.held):
        gate_in = plan.block(spread_ref, 0, b)
        up_in = plan.block(spread_ref, 1, b)
        gate_out = dot(gate_ref[b], gate_in, TN).astype(BF16).astype(F32)
        up_out = dot(up_ref[b], up_in, TN).astype(BF16).astype(F32)
        back = plan.block(hidden_grad_ref, 0, b).astype(F32)
        active, slope = gelu_and_slope(gate_out)
        plan.put(hiddens, b, active * up_out)
        gate_back = (back * up_out * slope).astype(BF16)
        up_back = (back * active).astype(BF16)
        plan.put(gates, b, dot(gate_ref[b], gate_back, NN))
        plan.put(ups, b, dot(up_ref[b], up_back, NN))
        sum_over_steps(gate_sums, b, dot(gate_in, gate_back, NT), scale)
        sum_over_steps(up_sums, b, dot(up_in, up_back, NT), scale)
    plan.store(hidden_ref, 0, hiddens)
    plan.store(out_ref, 0, gates)
    plan.store(out_ref, 1, ups)
    gate_grad_ref[...] = gate_sums[...].astype(BF16)
    up_grad_ref[...] = up_sums[...].astype(BF16)


def middle(plan, spreads, hidden_grad, left_gate, left_up, scale):
    step = step_of(plan.tok)
    grad_shape = jax.ShapeDtypeStruct(left_gate.shape, BF16)
    return pl.pallas_call(
        functools.partial(middle_kernel, plan, scale),
        grid=(plan.tok // step,),
        in_specs=[
            plan.arrived_spec(2, step),
            plan.arrived_spec(1, step),
            whole(left_gate),
            whole(left_up),
        ],
        out_specs=[
            plan.sent_spec(1, step),
            plan.sent_spec(2, step),
            whole(left_gate),
            whole(left_up),
        ],
        out_shape=[plan.sent_shape(1), plan.sent_shape(2), grad_shape, grad_shape],
        scratch_shapes=[scratch_for(plan, step)] * 3 + [pltpu.VMEM(left_gate.shape, F32)] * 2,
        compiler_params=params(),
        name="middle",
    )(spreads, hidden_grad, left_gate, left_up)


def last_kernel(plan, scale, groups, in_ref, packed_ref, back_ref, gate_ref, up_ref, *out_refs):
    slab_refs, (gate_grad_ref, up_grad_ref) = out_refs[:groups], out_refs[groups:]
    count = gate_ref.shape[0]
    width = plan.width
    cap = slab_refs[0].shape[0]
    for at in range(count):
        if plan.direct:
            parts = [
                jnp.concatenate(
                    [
                        in_ref[s, part, at * plan.held : (at + 1) * plan.held, :]
                        for s in range(plan.peers)
                    ],
                    axis=0,
                )
                for part in range(2)
            ]
        else:
            parts = [in_ref[part, at] for part in range(2)]
        gate_back, up_back = parts
        back = dot(gate_ref[at], gate_back, NN) + dot(up_ref[at], up_back, NN)
        columns = slice(at * width, (at + 1) * width)
        sent = dot(back_ref[...], back.astype(BF16), NT).astype(BF16)
        for k, ref in enumerate(slab_refs):
            ref[:, columns] = sent[k * cap : (k + 1) * cap]
        values = packed_ref[:, columns]
        gate_grad_ref[at] = (dot(values, gate_back, ((0,), (1,))) * scale).astype(BF16)
        up_grad_ref[at] = (dot(values, up_back, ((0,), (1,))) * scale).astype(BF16)


def last_products(plan, arrived, packed, back, right_gate, right_up, groups, scale):
    count = 4
    lanes = back.shape[0]
    cap = lanes // groups
    feats = packed.shape[1]
    width = plan.width
    if plan.direct:
        arrived = arrived.reshape(plan.peers, 2, plan.piece, plan.tok)
        arrived_spec = pl.BlockSpec(
            (plan.peers, 2, count * plan.held, plan.tok), lambda i: (0, 0, i, 0)
        )
    else:
        arrived = arrived.reshape(2, plan.held, width, plan.tok)
        arrived_spec = pl.BlockSpec((2, count, width, plan.tok), lambda i: (0, i, 0, 0))
    factor_spec = pl.BlockSpec((count,) + right_gate.shape[1:], lambda i: (i, 0, 0))
    grad_shape = jax.ShapeDtypeStruct(right_gate.shape, BF16)
    outs = pl.pallas_call(
        functools.partial(last_kernel, plan, scale, groups),
        grid=(plan.held // count,),
        in_specs=[
            arrived_spec,
            pl.BlockSpec((plan.tok, count * width), lambda i: (0, i)),
            whole(back),
            factor_spec,
            factor_spec,
        ],
        out_specs=[pl.BlockSpec((cap, count * width), lambda i: (0, i))] * groups
        + [factor_spec] * 2,
        out_shape=[jax.ShapeDtypeStruct((cap, feats), BF16)] * groups + [grad_shape] * 2,
        compiler_params=params(),
        name="last_products",
    )(arrived, packed, back, right_gate, right_up)
    return outs[:groups], outs[groups], outs[groups + 1]


def body(
    earlier,
    mix_weights,
    destinations,
    cotangent,
    right_gate,
    left_gate,
    right_up,
    left_up,
    right_down,
    left_down,
):
    held, width = right_gate.shape[0], right_gate.shape[1]
    feats = earlier.shape[1]
    tok = cotangent.shape[1]
    groups = lax.axis_size("dp")
    peers = lax.axis_size("feat")
    cap = 5 * tok // (4 * groups)
    scale = (tok * groups) ** (-0.5)
    plan = Plan(peers, held, width, tok)

    def swap(array):
        return plan.arranged(
            lax.all_to_all(array, "feat", split_axis=0, concat_axis=0, tiled=True)
        )

    own = lax.axis_index("dp").reshape(1)
    home, back, back_t = routing(destinations, own, groups, tok, cap)
    slabs = exchange_rows(mix_and_sort(earlier, mix_weights, home, groups, width), groups)

    out_grads = swap(send_cotangent(plan, cotangent))
    down_spread_grad = swap(product(plan, out_grads, left_down, NN, "left_back_down"))
    hidden_grad = swap(product(plan, down_spread_grad, right_down, NN, "right_back_down"))

    packed, spreads = first_products(plan, slabs, back_t, right_gate, right_up)
    hidden, spread_grads, grad_left_gate, grad_left_up = middle(
        plan, swap(spreads), hidden_grad, left_gate, left_up, scale
    )
    slabs, grad_right_gate, grad_right_up = last_products(
        plan, swap(spread_grads), packed, back, right_gate, right_up, groups, scale
    )
    slabs = exchange_rows(slabs, groups)
    down_spread, grad_right_down = product_and_grad(
        plan, swap(hidden), down_spread_grad, right_down, scale, "right_down"
    )
    result, grad_left_down = product_and_grad(
        plan, swap(down_spread), out_grads, left_down, scale, "left_down"
    )
    result = lax.all_to_all(result, "feat", split_axis=0, concat_axis=0, tiled=True)
    output = result.reshape(peers, held, held, tok).transpose(1, 0, 2, 3).reshape(feats, tok)
    mixed_grad = unsort(slabs, home, width)

    def total(*grads):
        joined = jnp.concatenate(grads, axis=0)
        summed = lax.psum_scatter(joined, "dp", scatter_dimension=1, tiled=True).astype(F32)
        return jnp.split(summed, len(grads), axis=0)

    grad_left_gate, grad_left_up = total(grad_left_gate, grad_left_up)
    grad_right_gate, grad_right_up = total(grad_right_gate, grad_right_up)
    (grad_right_down,) = total(grad_right_down)
    (grad_left_down,) = total(grad_left_down)
    return (
        output,
        mixed_grad,
        grad_right_gate,
        grad_left_gate,
        grad_right_up,
        grad_left_up,
        grad_right_down,
        grad_left_down,
    )


def solution(mesh):
    return jax.shard_map(
        body,
        mesh=mesh,
        in_specs=(
            P(None, "feat", "dp"),
            P(),
            P(),
            P("feat", "dp"),
            P("feat", None, None),
            P("feat", None, None),
            P("feat", None, None),
            P("feat", None, None),
            P("feat", None, None),
            P("feat", None, None),
        ),
        out_specs=(
            P("feat", "dp"),
            P("feat", "dp"),
            P("feat", "dp", None),
            P("feat", "dp", None),
            P("feat", "dp", None),
            P("feat", "dp", None),
            P("feat", "dp", None),
            P("feat", "dp", None),
        ),
        check_vma=False,
    )
```

time: 603 us -> 482 us (0.80)
  the two profiles are of different devices: /device:TPU:0 before, /device:TPU:9 now
where the time goes in v1:
time: 482 us; the launch traced here: 481 us
  waiting for transfers between devices  222 us (46%)
  blocking collectives  91.9 us (19%)
  Pallas kernels  90.2 us (19%)
  starting transfers between devices  37.4 us (8%)
  local copies, waits for them, and re-layouts  18.8 us (4%)
  between operations  13.9 us (3%)
  other arithmetic  6.44 us (1%)
    ppermute x6, waiting for transfers between devices, exchange_rows(): received.append(lax.ppermute(slabs[k], 'dp', pairs))  125 us
    all_to_all x4, waiting for transfers between devices, swap(): lax.all_to_all(array, 'feat', split_axis=0, concat_axis=0, tiled=True)  96.2 us
    all_to_all x3, blocking collectives, swap(): lax.all_to_all(array, 'feat', split_axis=0, concat_axis=0, tiled=True)  91.9 us
    pallas_call x1, Pallas kernels, middle(): pl.pallas_call(functools.partial(middle_kernel, plan, scale), grid=(plan....  29.5 us
    all_to_all x4, starting transfers between devices, swap(): lax.all_to_all(array, 'feat', split_axis=0, concat_axis=0, tiled=True)  23.9 us
    pallas_call x2, Pallas kernels, product_and_grad(): pl.pallas_call(functools.partial(product_and_grad_kernel, plan, scale, Tr...  20 us
    unnamed x50, local copies, waits for them, and re-layouts  12 us
  transfers between devices with their start and end apart: 15, of which 9 were waited for; matrix products, arithmetic and copies ran while one was open for 2% of the time, Pallas kernels for 10%

profile of v1, /device:TPU:9, one launch (start us, length us, event | category | flops | bytes accessed | tf_op | source)
XLA Modules:
  0.0 480.8 jit_solution(3198502606528666269)
XLA Ops:
  7.2 1.6 copy-done.7
  8.8 2.8 send_cotangent.1
  11.6 29.6 %all_to_all.40.in_ref.other_ref = bf16[8,256,512]{2,1,0:T(8,128)(2,1)S(1)} all-to-all(bf16[8,256,512]{2,1,0:T(8,128)(2,1)S(1)} %send_cotangent.1), channel_id=1, replica_groups=mesh['dp'=4,'feat'=8] {'feat'}, dimensions={0} | all-to-all | bytes 4194304 | tf_op jit(solution)/shard_map/all_to_all | solution.py:500
  41.2 2.4 left_back_down.1
  43.6 1.3 copy-done.2
  44.9 5.0 %all-to-all-start.2 = ((bf16[8,256,512]{2,1,0:T(8,128)(2,1)}), bf16[8,256,512]{2,1,0:T(8,128)(2,1)S(1)}, u32[]{:S(2)}, u32[]{:S(2)}) async-start(bf16[8,256,512]{2,1,0:T(8,128)(2,1)} %copy-done.2), calls=%async_computation.2 | async-start | bytes 4194304 | tf_op jit(solution)/shard_map/all_to_all | solution.py:500
  49.9 1.8 routing.1
  51.7 0.9 copy-done.13
  52.6 8.1 %mix_and_sort.1 = (bf16[160,2048]{1,0:T(8,128)(2,1)S(1)}, bf16[160,2048]{1,0:T(8,128)(2,1)S(1)}, bf16[160,2048]{1,0:T(8,128)(2,1)S(1)}, bf16[160,2048]{1,0:T(8,128)(2,1)S(1)}) custom-call(f32[3]{0:T(128)S(1)} %copy-done.22, bf16[3,2048,640]{2,1,0:T(8,128)(2,1)} %earlier_ref.1, bf16[640,640]{1,0:T(8,128)(2,1)S(1)} %get-tuple-element.31.home_ref), custom_call_target="tpu_custom_call" | custom-call | tf_op jit(solution)/shard_map/mix_and_sort/pallas_call | solution.py:108
  60.9 2.3 collective-permute-start.1
  63.4 25.1 %collective-permute-done.refs_1_ = bf16[160,2048]{1,0:T(8,128)(2,1)S(1)} collective-permute-done((bf16[160,2048]{1,0:T(8,128)(2,1)S(1)}, bf16[160,2048]{1,0:T(8,128)(2,1)S(1)}, u32[]{:S(2)}, u32[]{:S(2)}) %collective-permute-start) | collective-permute-done | bytes 655392 | tf_op jit(solution)/shard_map/ppermute | solution.py:130
  88.5 16.4 %collective-permute-done.1.refs_2_ = bf16[160,2048]{1,0:T(8,128)(2,1)S(1)} collective-permute-done((bf16[160,2048]{1,0:T(8,128)(2,1)S(1)}, bf16[160,2048]{1,0:T(8,128)(2,1)S(1)}, u32[]{:S(2)}, u32[]{:S(2)}) %collective-permute-start.1) | collective-permute-done | bytes 655392 | tf_op jit(solution)/shard_map/ppermute | solution.py:130
  104.9 15.1 %collective-permute-done.2.refs_3_ = bf16[160,2048]{1,0:T(8,128)(2,1)S(1)} collective-permute-done((bf16[160,2048]{1,0:T(8,128)(2,1)S(1)}, bf16[160,2048]{1,0:T(8,128)(2,1)S(1)}, u32[]{:S(2)}, u32[]{:S(2)}) %collective-permute-start.2) | collective-permute-done | bytes 655392 | tf_op jit(solution)/shard_map/ppermute | solution.py:130
  120.0 9.0 %first_products.1 = (bf16[512,2048]{1,0:T(8,128)(2,1)}, bf16[8,512,512]{2,1,0:T(8,128)(2,1)}) custom-call(bf16[160,2048]{1,0:T(8,128)(2,1)S(1)} %get-tuple-element.32.refs_0_, bf16[160,2048]{1,0:T(8,128)(2,1)S(1)} %collective-permute-done.refs_1_, bf16[160,2048]{1,0:T(8,128)(2,1)S(1)} %collective-permute-done.1.refs_2_, ...), custom_call_target="tpu_custom_call" | custom-call | tf_op jit(solution)/shard_map/first_products/pallas_call | solution.py:321
  129.1 5.8 %all-to-all-start = ((bf16[8,512,512]{2,1,0:T(8,128)(2,1)}), bf16[8,512,512]{2,1,0:T(8,128)(2,1)}, u32[]{:S(2)}, u32[]{:S(2)}) async-start(bf16[8,512,512]{2,1,0:T(8,128)(2,1)} %get-tuple-element.37), calls=%async_computation | async-start | bytes 8388608 | tf_op jit(solution)/shard_map/all_to_all | solution.py:500
  134.9 2.4 right_back_down.1
  137.4 1.3 copy-done.3
  138.7 41.9 %all-to-all-done.spread_ref = bf16[8,512,512]{2,1,0:T(8,128)(2,1)} async-done(((bf16[8,512,512]{2,1,0:T(8,128)(2,1)}), bf16[8,512,512]{2,1,0:T(8,128)(2,1)}, u32[]{:S(2)}, u32[]{:S(2)}) %all-to-all-start) | async-done | bytes 4194336 | tf_op jit(solution)/shard_map/all_to_all | solution.py:500
  180.5 33.2 %all_to_all.41.hidden_grad_ref = bf16[8,256,512]{2,1,0:T(8,128)(2,1)} all-to-all(bf16[8,256,512]{2,1,0:T(8,128)(2,1)} %copy-done.3), channel_id=1, replica_groups=mesh['dp'=4,'feat'=8] {'feat'}, dimensions={0} | all-to-all | bytes 4194304 | tf_op jit(solution)/shard_map/all_to_all | solution.py:500
  213.8 29.5 %middle.1 = (bf16[8,256,512]{2,1,0:T(8,128)(2,1)S(1)}, bf16[8,512,512]{2,1,0:T(8,128)(2,1)}, bf16[16,128,128]{2,1,0:T(8,128)(2,1)S(1)}, bf16[16,128,128]{2,1,0:T(8,128)(2,1)S(1)}) custom-call(bf16[8,512,512]{2,1,0:T(8,128)(2,1)} %all-to-all-done.spread_ref, bf16[8,256,512]{2,1,0:T(8,128)(2,1)} %all_to_all.41.hidden_grad_ref, ...), custom_call_target="tpu_custom_call" | custom-call | tf_op jit(solution)/shard_map/middle/pallas_call | solution.py:390
  243.3 29.0 %all_to_all.42.in_ref = bf16[8,256,512]{2,1,0:T(8,128)(2,1)S(1)} all-to-all(bf16[8,256,512]{2,1,0:T(8,128)(2,1)S(1)} %get-tuple-element.38), channel_id=1, replica_groups=mesh['dp'=4,'feat'=8] {'feat'}, dimensions={0} | all-to-all | bytes 4194304 | tf_op jit(solution)/shard_map/all_to_all | solution.py:500
  272.3 9.6 %right_down.1 = (bf16[8,256,512]{2,1,0:T(8,128)(2,1)S(1)}, bf16[16,128,128]{2,1,0:T(8,128)(2,1)S(1)}) custom-call(bf16[8,256,512]{2,1,0:T(8,128)(2,1)S(1)} %all_to_all.42.in_ref, bf16[8,256,512]{2,1,0:T(8,128)(2,1)} %copy-done.1, bf16[16,128,128]{2,1,0:T(8,128)(2,1)S(1)} %copy-done.4), custom_call_target="tpu_custom_call" | custom-call | tf_op jit(solution)/shard_map/right_down/pallas_call | solution.py:281
  281.9 1.3 copy-done.8
  283.2 0.8 copy-done.17
  284.0 5.0 %all-to-all-start.5 = ((bf16[8,256,512]{2,1,0:T(8,128)(2,1)}), bf16[8,256,512]{2,1,0:T(8,128)(2,1)S(1)}, u32[]{:S(2)}, u32[]{:S(2)}) async-start(bf16[8,256,512]{2,1,0:T(8,128)(2,1)} %copy-done.8), calls=%async_computation.5 | async-start | bytes 4194304 | tf_op jit(solution)/shard_map/all_to_all | solution.py:500
  289.0 2.1 pad_maximum_fusion.1
  291.2 21.0 %all-to-all-done.5.in_ref = bf16[8,256,512]{2,1,0:T(8,128)(2,1)S(1)} async-done(((bf16[8,256,512]{2,1,0:T(8,128)(2,1)}), bf16[8,256,512]{2,1,0:T(8,128)(2,1)S(1)}, u32[]{:S(2)}, u32[]{:S(2)}) %all-to-all-start.5) | async-done | bytes 2097184 | tf_op jit(solution)/shard_map/all_to_all | solution.py:500
  312.2 8.1 %all-to-all-start.7 = ((bf16[8,512,512]{2,1,0:T(8,128)(2,1)}), bf16[8,512,512]{2,1,0:T(8,128)(2,1)}, u32[]{:S(2)}, u32[]{:S(2)}) async-start(bf16[8,512,512]{2,1,0:T(8,128)(2,1)} %get-tuple-element.41), calls=%async_computation.7 | async-start | bytes 8388608 | tf_op jit(solution)/shard_map/all_to_all | solution.py:500
  321.1 10.4 %left_down.1 = (bf16[8,256,512]{2,1,0:T(8,128)(2,1)}, bf16[16,128,128]{2,1,0:T(8,128)(2,1)S(1)}) custom-call(bf16[8,256,512]{2,1,0:T(8,128)(2,1)S(1)} %all-to-all-done.5.in_ref, bf16[8,256,512]{2,1,0:T(8,128)(2,1)} %copy-done, bf16[16,128,128]{2,1,0:T(8,128)(2,1)S(1)} %copy-done.6), custom_call_target="tpu_custom_call" | custom-call | tf_op jit(solution)/shard_map/left_down/pallas_call | solution.py:281
  331.5 0.8 copy-done.18
  332.6 33.3 %all-to-all-done.7 = bf16[8,512,512]{2,1,0:T(8,128)(2,1)} async-done(((bf16[8,512,512]{2,1,0:T(8,128)(2,1)}), bf16[8,512,512]{2,1,0:T(8,128)(2,1)}, u32[]{:S(2)}, u32[]{:S(2)}) %all-to-all-start.7) | async-done | bytes 4194336 | tf_op jit(solution)/shard_map/all_to_all | solution.py:500
  365.9 1.0 copy-done.10
  366.9 1.0 copy-done.12
  368.0 1.1 copy-done.14
  369.1 8.6 %last_products.1 = (bf16[160,2048]{1,0:T(8,128)(2,1)S(1)}, bf16[160,2048]{1,0:T(8,128)(2,1)}, bf16[160,2048]{1,0:T(8,128)(2,1)}, bf16[160,2048]{1,0:T(8,128)(2,1...) custom-call(bf16[8,2,256,512]{3,2,1,0:T(8,128)(2,1)} %bitcast.4.in_ref, ...), custom_call_target="tpu_custom_call" | custom-call | tf_op jit(solution)/shard_map/last_products/pallas_call | solution.py:458
  377.6 0.8 copy-done.23
  378.5 1.1 pad_maximum_fusion
  379.6 7.9 %all-to-all-start.6 = ((bf16[8,256,512]{2,1,0:T(8,128)(2,1)}), bf16[8,256,512]{2,1,0:T(8,128)(2,1)}, u32[]{:S(2)}, u32[]{:S(2)}) async-start(bf16[8,256,512]{2,1,0:T(8,128)(2,1)} %get-tuple-element.40), calls=%async_computation.6 | async-start | bytes 4194304 | tf_op jit(solution)/shard_map/all_to_all | solution.py:525
  387.5 2.5 collective-permute-start.4
  390.1 1.8 fusion
  391.9 1.6 convert_element_type.14
  393.6 38.7 %collective-permute-done.3.refs_1_ = bf16[160,2048]{1,0:T(8,128)(2,1)S(1)} collective-permute-done((bf16[160,2048]{1,0:T(8,128)(2,1)}, bf16[160,2048]{1,0:T(8,128)(2,1)S(1)}, u32[]{:S(2)}, u32[]{:S(2)}) %collective-permute-start.3) | collective-permute-done | bytes 655392 | tf_op jit(solution)/shard_map/ppermute | solution.py:130
  432.2 2.7 collective-permute-done.4.refs_2_
  434.9 27.2 %collective-permute-done.5.refs_3_ = bf16[160,2048]{1,0:T(8,128)(2,1)S(1)} collective-permute-done((bf16[160,2048]{1,0:T(8,128)(2,1)}, bf16[160,2048]{1,0:T(8,128)(2,1)S(1)}, u32[]{:S(2)}, u32[]{:S(2)}) %collective-permute-start.5) | collective-permute-done | bytes 655392 | tf_op jit(solution)/shard_map/ppermute | solution.py:130
  462.1 5.6 %unsort.1 = bf16[2048,640]{1,0:T(8,128)(2,1)} custom-call(bf16[640,640]{1,0:T(8,128)(2,1)S(1)} %get-tuple-element.31.home_ref, bf16[160,2048]{1,0:T(8,128)(2,1)S(1)} %get-tuple-element.44.refs_0_, bf16[160,2048]{1,0:T(8,128)(2,1)S(1)} %collective-permute-done.3.refs_1_, bf16[160,2048]{1,0:T(8,128)(2,1)S(1)} %collective-permute-done.4.refs_2_, ...), custom_call_target="tpu_custom_call" | custom-call | tf_op jit(solution)/shard_map/unsort/pallas_call | solution.py:144
  467.7 1.6 convert_element_type.15
  469.3 3.2 copy.18
  472.4 1.8 fusion.1
  (59 shorter events, 1.8 us)
Async XLA Ops:
  7.2 1.6 copy-start.7
  11.6 29.6 %copy-start.5 = (bf16[16,128,128]{2,1,0:T(8,128)(2,1)S(1)}, bf16[16,128,128]{2,1,0:T(8,128)(2,1)}, u32[]{:S(2)}) copy-start(bf16[16,128,128]{2,1,0:T(8,128)(2,1)} %factor_ref.7) | copy-start | bytes 1572868
  41.2 2.4 copy-start
  43.6 1.3 copy-start.2
  44.9 5.0 %copy-start.24 = (s32[2560]{0:T(1024)S(1)}, s32[2560]{0:T(1024)}, u32[]{:S(2)}) copy-start(s32[2560]{0:T(1024)} %param.12) | copy-start | bytes 30724
  44.9 7.6 %copy-start.22 = (f32[3]{0:T(128)S(1)}, f32[3]{0:T(128)}, u32[]{:S(2)}) copy-start(f32[3]{0:T(128)} %weights_ref.1) | copy-start | bytes 40
  44.9 84.1 %all-to-all-start.2 = ((bf16[8,256,512]{2,1,0:T(8,128)(2,1)}), bf16[8,256,512]{2,1,0:T(8,128)(2,1)S(1)}, u32[]{:S(2)}, u32[]{:S(2)}) async-start(bf16[8,256,512]{2,1,0:T(8,128)(2,1)} %copy-done.2), calls=%async_computation.2 | async-start | bytes 4194304 | tf_op jit(solution)/shard_map/all_to_all | solution.py:500
  51.7 0.9 copy-start.13
  52.6 67.4 %copy-start.9 = (bf16[16,128,128]{2,1,0:T(8,128)(2,1)S(1)}, bf16[16,128,128]{2,1,0:T(8,128)(2,1)}, u32[]{:S(2)}) copy-start(bf16[16,128,128]{2,1,0:T(8,128)(2,1)} %gate_ref.3) | copy-start | bytes 1572868
  52.6 67.4 %copy-start.11 = (bf16[16,128,128]{2,1,0:T(8,128)(2,1)S(1)}, bf16[16,128,128]{2,1,0:T(8,128)(2,1)}, u32[]{:S(2)}) copy-start(bf16[16,128,128]{2,1,0:T(8,128)(2,1)} %up_ref.3) | copy-start | bytes 1572868
  60.7 27.8 %collective-permute-start = (bf16[160,2048]{1,0:T(8,128)(2,1)S(1)}, bf16[160,2048]{1,0:T(8,128)(2,1)S(1)}, u32[]{:S(2)}, u32[]{:S(2)}) collective-permute-start(bf16[160,2048]{1,0:T(8,128)(2,1)S(1)} %get-tuple-element.33), channel_id=1, source_target_pairs={{0,8},{8,0},{16,24},{24,16},{1,9},{9,1},{17,25},{25,17},{2,10},{10... | collective-permute-start | bytes 1966088 | tf_op jit(solution)/shard_map/ppermute | solution.py:130
  60.9 44.0 %collective-permute-start.1 = (bf16[160,2048]{1,0:T(8,128)(2,1)S(1)}, bf16[160,2048]{1,0:T(8,128)(2,1)S(1)}, u32[]{:S(2)}, u32[]{:S(2)}) collective-permute-start(bf16[160,2048]{1,0:T(8,128)(2,1)S(1)} %get-tuple-element.34), channel_id=1, source_target_pairs={{0,16},{8,24},{16,0},{24,8},{1,17},{9,25},{17,1},{25,9},{2,18},{10... | collective-permute-start | bytes 1966088 | tf_op jit(solution)/shard_map/ppermute | solution.py:130
  63.2 56.8 %collective-permute-start.2 = (bf16[160,2048]{1,0:T(8,128)(2,1)S(1)}, bf16[160,2048]{1,0:T(8,128)(2,1)S(1)}, u32[]{:S(2)}, u32[]{:S(2)}) collective-permute-start(bf16[160,2048]{1,0:T(8,128)(2,1)S(1)} %get-tuple-element.35), channel_id=1, source_target_pairs={{0,24},{8,16},{16,8},{24,0},{1,25},{9,17},{17,9},{25,1},{2,26},{10... | collective-permute-start | bytes 1966088 | tf_op jit(solution)/shard_map/ppermute | solution.py:130
  129.1 5.9 %copy-start.1 = (bf16[8,256,512]{2,1,0:T(8,128)(2,1)}, bf16[8,256,512]{2,1,0:T(8,128)(2,1)S(1)}, u32[]{:S(2)}) copy-start(bf16[8,256,512]{2,1,0:T(8,128)(2,1)S(1)} %all-to-all-done.2.in_ref.other_ref) | copy-start | bytes 6291460
  129.1 5.9 %copy-start.4 = (bf16[16,128,128]{2,1,0:T(8,128)(2,1)S(1)}, bf16[16,128,128]{2,1,0:T(8,128)(2,1)}, u32[]{:S(2)}) copy-start(bf16[16,128,128]{2,1,0:T(8,128)(2,1)} %factor_ref.6) | copy-start | bytes 1572868
  129.1 51.5 %all-to-all-start = ((bf16[8,512,512]{2,1,0:T(8,128)(2,1)}), bf16[8,512,512]{2,1,0:T(8,128)(2,1)}, u32[]{:S(2)}, u32[]{:S(2)}) async-start(bf16[8,512,512]{2,1,0:T(8,128)(2,1)} %get-tuple-element.37), calls=%async_computation | async-start | bytes 8388608 | tf_op jit(solution)/shard_map/all_to_all | solution.py:500
  137.3 1.3 copy-start.3
  138.7 75.1 %copy-start.15 = (bf16[16,128,128]{2,1,0:T(8,128)(2,1)S(1)}, bf16[16,128,128]{2,1,0:T(8,128)(2,1)}, u32[]{:S(2)}) copy-start(bf16[16,128,128]{2,1,0:T(8,128)(2,1)} %gate_ref.2) | copy-start | bytes 1572868
  138.7 75.1 %copy-start.16 = (bf16[16,128,128]{2,1,0:T(8,128)(2,1)S(1)}, bf16[16,128,128]{2,1,0:T(8,128)(2,1)}, u32[]{:S(2)}) copy-start(bf16[16,128,128]{2,1,0:T(8,128)(2,1)} %up_ref.2) | copy-start | bytes 1572868
  243.3 29.0 %copy-start.19 = (bf16[16,128,128]{2,1,0:T(8,128)(2,1)}, bf16[16,128,128]{2,1,0:T(8,128)(2,1)S(1)}, u32[]{:S(2)}) copy-start(bf16[16,128,128]{2,1,0:T(8,128)(2,1)S(1)} %get-tuple-element.50) | copy-start | bytes 1572868
  243.3 29.0 %copy-start.21 = (bf16[16,128,128]{2,1,0:T(8,128)(2,1)}, bf16[16,128,128]{2,1,0:T(8,128)(2,1)S(1)}, u32[]{:S(2)}) copy-start(bf16[16,128,128]{2,1,0:T(8,128)(2,1)S(1)} %get-tuple-element.51) | copy-start | bytes 1572868
  281.9 1.3 copy-start.8
  283.2 0.8 copy-start.17
  284.0 5.0 %copy-start.20 = (bf16[16,128,128]{2,1,0:T(8,128)(2,1)S(1)}, bf16[16,128,128]{2,1,0:T(8,128)(2,1)}, u32[]{:S(2)}) copy-start(bf16[16,128,128]{2,1,0:T(8,128)(2,1)} %copy-done.19) | copy-start | bytes 1572868
  284.0 28.1 %all-to-all-start.5 = ((bf16[8,256,512]{2,1,0:T(8,128)(2,1)}), bf16[8,256,512]{2,1,0:T(8,128)(2,1)S(1)}, u32[]{:S(2)}, u32[]{:S(2)}) async-start(bf16[8,256,512]{2,1,0:T(8,128)(2,1)} %copy-done.8), calls=%async_computation.5 | async-start | bytes 4194304 | tf_op jit(solution)/shard_map/all_to_all | solution.py:500
  289.0 101.1 %reduce-scatter.7.cloned.1.call-start = ((), (), s32[]{:S(2)}) async-start(), calls=%async_computation.13 | async-start | bytes 1310720 | tf_op jit(solution)/shard_map/reduce_scatter | solution.py:531
  312.2 8.9 %copy-start.6 = (bf16[16,128,128]{2,1,0:T(8,128)(2,1)S(1)}, bf16[16,128,128]{2,1,0:T(8,128)(2,1)}, u32[]{:S(2)}) copy-start(bf16[16,128,128]{2,1,0:T(8,128)(2,1)} %factor_ref.7) | copy-start | bytes 1572868
  312.2 53.7 %all-to-all-start.7 = ((bf16[8,512,512]{2,1,0:T(8,128)(2,1)}), bf16[8,512,512]{2,1,0:T(8,128)(2,1)}, u32[]{:S(2)}, u32[]{:S(2)}) async-start(bf16[8,512,512]{2,1,0:T(8,128)(2,1)} %get-tuple-element.41), calls=%async_computation.7 | async-start | bytes 8388608 | tf_op jit(solution)/shard_map/all_to_all | solution.py:500
  320.3 71.7 %reduce-scatter.9.cloned.1.call-start = ((), (), s32[]{:S(2)}) async-start(), calls=%async_computation.14 | async-start | bytes 655360 | tf_op jit(solution)/shard_map/reduce_scatter | solution.py:531
  321.0 146.7 %reduce-scatter.11.cloned.1.call-start = ((), (), s32[]{:S(2)}) async-start(), calls=%async_computation.15 | async-start | bytes 655360 | tf_op jit(solution)/shard_map/reduce_scatter | solution.py:531
  331.5 0.8 copy-start.18
  332.3 140.2 %reduce-scatter.5.cloned.1.call-start = ((), (), s32[]{:S(2)}) async-start(), calls=%async_computation.12 | async-start | bytes 1310720 | tf_op jit(solution)/shard_map/reduce_scatter | solution.py:531
  365.9 1.0 copy-start.10
  366.9 1.0 copy-start.12
  368.0 1.1 copy-start.14
  377.6 0.8 copy-start.23
  379.6 89.7 %all-to-all-start.6 = ((bf16[8,256,512]{2,1,0:T(8,128)(2,1)}), bf16[8,256,512]{2,1,0:T(8,128)(2,1)}, u32[]{:S(2)}, u32[]{:S(2)}) async-start(bf16[8,256,512]{2,1,0:T(8,128)(2,1)} %get-tuple-element.40), calls=%async_computation.6 | async-start | bytes 4194304 | tf_op jit(solution)/shard_map/all_to_all | solution.py:525
  387.5 44.8 %collective-permute-start.3 = (bf16[160,2048]{1,0:T(8,128)(2,1)}, bf16[160,2048]{1,0:T(8,128)(2,1)S(1)}, u32[]{:S(2)}, u32[]{:S(2)}) collective-permute-start(bf16[160,2048]{1,0:T(8,128)(2,1)} %get-tuple-element.45), channel_id=1, source_target_pairs={{0,8},{8,0},{16,24},{24,16},{1,9},{9,1},{17,25},{25,17},{2,10},{10... | collective-permute-start | bytes 1966088 | tf_op jit(solution)/shard_map/ppermute | solution.py:130
  387.5 47.4 %collective-permute-start.4 = (bf16[160,2048]{1,0:T(8,128)(2,1)}, bf16[160,2048]{1,0:T(8,128)(2,1)S(1)}, u32[]{:S(2)}, u32[]{:S(2)}) collective-permute-start(bf16[160,2048]{1,0:T(8,128)(2,1)} %get-tuple-element.46), channel_id=1, source_target_pairs={{0,16},{8,24},{16,0},{24,8},{1,17},{9,25},{17,1},{25,9},{2,18},{10... | collective-permute-start | bytes 1966088 | tf_op jit(solution)/shard_map/ppermute | solution.py:130
  389.9 72.1 %collective-permute-start.5 = (bf16[160,2048]{1,0:T(8,128)(2,1)}, bf16[160,2048]{1,0:T(8,128)(2,1)S(1)}, u32[]{:S(2)}, u32[]{:S(2)}) collective-permute-start(bf16[160,2048]{1,0:T(8,128)(2,1)} %copy-done.23), channel_id=1, source_target_pairs={{0,24},{8,16},{16,8},{24,0},{1,25},{9,17},{17,9},{25,1},{2,26},{10... | collective-permute-start | bytes 1966088 | tf_op jit(solution)/shard_map/ppermute | solution.py:130
Sparse Core Ops, SparseCore 0:
  292.1 25.1 reduce-scatter.6
  323.5 17.7 reduce-scatter.8
  343.7 20.0 reduce-scatter.10
  379.7 72.3 reduce-scatter.4

commit v2 on v1

v2 whole, which is shorter than its diff:
```python
import functools
import math

import jax
import jax.numpy as jnp
from jax import lax
from jax.experimental import pallas as pl
from jax.experimental.pallas import tpu as pltpu
from jax.sharding import PartitionSpec as P

F32 = jnp.float32
BF16 = jnp.bfloat16
UNROLL = 16
VMEM_LIMIT = 48 * 1024 * 1024


def params(steps=1):
    return pltpu.CompilerParams(
        vmem_limit_bytes=VMEM_LIMIT, dimension_semantics=("arbitrary",) * steps
    )


def dot(a, b, over):
    return lax.dot_general(a, b, (over, ((), ())), preferred_element_type=F32)


def in_hbm(*arrays):
    return [pltpu.with_memory_space_constraint(array, pltpu.HBM) for array in arrays]


NN = ((1,), (0,))
NT = ((1,), (1,))
TN = ((0,), (0,))


def routing_kernel(sizes, own_ref, dest_ref, home_ref, back_ref, back_t_ref):
    groups, tok, cap, lanes = sizes
    rows, slots = dest_ref.shape
    own = own_ref[0]
    dest = dest_ref[...]
    group = lax.broadcasted_iota(jnp.int32, (rows, slots), 0)
    if groups & (groups - 1) == 0:
        relative = group ^ own
    else:
        relative = jnp.where(group >= own, group - own, group - own + groups)
    before = lax.broadcasted_iota(jnp.int32, (slots, slots), 0) < lax.broadcasted_iota(
        jnp.int32, (slots, slots), 1
    )
    before = jnp.where(before, 1.0, 0.0).astype(BF16)
    lane = lax.broadcasted_iota(jnp.int32, (lanes, slots), 0)

    def place(members):
        return dot(jnp.where(members, 1.0, 0.0).astype(BF16), before, NN).astype(jnp.int32)

    mine = jnp.sum(jnp.where(group == own, dest, 0), axis=0, keepdims=True)
    local = mine - group * tok
    leaving = (local >= 0) & (local < tok) & (group < groups) & (mine >= 0)
    index = jnp.where(leaving, relative * cap + place(leaving) + 1, 0)
    home = jnp.sum(index, axis=0, keepdims=True) - 1
    home_ref[...] = jnp.where(lane == home, 1.0, 0.0).astype(BF16)
    local = dest - own * tok
    arriving = (local >= 0) & (local < tok) & (dest >= 0)
    index = jnp.where(arriving, relative * cap + place(arriving), -1)
    total = jnp.zeros((lanes, slots), jnp.int32)
    for source in range(groups):
        total = total + jnp.where(
            lane == index[source : source + 1], local[source : source + 1] + 1, 0
        )
    row = jnp.sum(total.astype(F32), axis=1, keepdims=True).astype(jnp.int32) - 1
    taken = lax.broadcasted_iota(jnp.int32, (lanes, tok), 1) == row
    taken = jnp.where(taken, 1.0, 0.0)
    back_ref[...] = taken.astype(BF16)
    back_t_ref[...] = taken.T.astype(BF16)


def routing(destinations, own, groups, tok, cap):
    slots = destinations.shape[0] // groups
    lanes = groups * cap
    rows = -(-groups // 16) * 16
    table = destinations.reshape(groups, slots)
    table = jnp.pad(table, ((0, rows - groups), (0, 0)), constant_values=-1)
    return pl.pallas_call(
        functools.partial(routing_kernel, (groups, tok, cap, lanes)),
        grid=(1,),
        in_specs=[
            pl.BlockSpec(memory_space=pltpu.SMEM),
            pl.BlockSpec(table.shape, lambda i: (0, 0)),
        ],
        out_specs=[
            pl.BlockSpec((lanes, slots), lambda i: (0, 0)),
            pl.BlockSpec((lanes, tok), lambda i: (0, 0)),
            pl.BlockSpec((tok, lanes), lambda i: (0, 0)),
        ],
        out_shape=[
            pltpu.HBM((lanes, slots), BF16),
            pltpu.HBM((lanes, tok), BF16),
            pltpu.HBM((tok, lanes), BF16),
        ],
        compiler_params=params(),
        name="routing",
    )(own, table)


def mix_kernel(weights_ref, earlier_ref, home_ref, *out_refs):
    total = weights_ref[0] * earlier_ref[0].astype(F32)
    for k in range(1, earlier_ref.shape[0]):
        total = total + weights_ref[k] * earlier_ref[k].astype(F32)
    sent = dot(home_ref[...], total.astype(BF16), NT).astype(BF16)
    cap = out_refs[0].shape[0]
    for k, ref in enumerate(out_refs):
        ref[...] = sent[k * cap : (k + 1) * cap]


def pieces_of(*sizes):
    unit = math.gcd(*sizes)
    starts = [sum(sizes[:k]) for k in range(len(sizes))]
    return [(start // unit, size // unit) for start, size in zip(starts, sizes)], unit


def mix_and_sort(earlier, mix_weights, home, groups, piece, step):
    depth, _, slots = earlier.shape
    lanes = home.shape[0]
    cap = lanes // groups
    start, count = piece
    return pl.pallas_call(
        mix_kernel,
        grid=(count,),
        in_specs=[
            pl.BlockSpec(memory_space=pltpu.SMEM),
            pl.BlockSpec((depth, step, slots), lambda i: (0, start + i, 0)),
            pl.BlockSpec((lanes, slots), lambda i: (0, 0)),
        ],
        out_specs=[pl.BlockSpec((cap, step), lambda i: (0, i))] * groups,
        out_shape=[pltpu.HBM((cap, step * count), BF16)] * groups,
        compiler_params=params(),
        name=f"mix_and_sort_{start}",
    )(mix_weights, *in_hbm(earlier, home))


def exchange_rows(slabs, groups):
    received = [slabs[0]]
    for k in range(1, groups):
        if groups & (groups - 1) == 0:
            pairs = [(i, i ^ k) for i in range(groups)]
        else:
            pairs = [(i, (i + k) % groups) for i in range(groups)]
        received.append(lax.ppermute(slabs[k], "dp", pairs))
    return received


def unsort_kernel(groups, home_ref, *refs):
    in_refs, out_ref = refs[:groups], refs[-1]
    rows = jnp.concatenate([ref[...] for ref in in_refs], axis=0)
    out_ref[...] = dot(rows, home_ref[...], TN).astype(BF16)


def unsort(slabs, home, piece, step, feats, partial):
    lanes, slots = home.shape
    cap = slabs[0].shape[0]
    groups = len(slabs)
    start, count = piece
    more = [] if partial is None else [partial]
    return pl.pallas_call(
        functools.partial(unsort_kernel, groups),
        grid=(count,),
        in_specs=[pl.BlockSpec((lanes, slots), lambda i: (0, 0))]
        + [pl.BlockSpec((cap, step), lambda i: (0, i))] * groups
        + [pl.BlockSpec(memory_space=pl.ANY)] * len(more),
        out_specs=pl.BlockSpec((step, slots), lambda i: (start + i, 0)),
        out_shape=pltpu.HBM((feats, slots), BF16),
        input_output_aliases={1 + groups: 0} if more else {},
        compiler_params=params(),
        name=f"unsort_{start}",
    )(*in_hbm(home, *slabs, *more))


class Plan:
    def __init__(self, peers, held, width, tok):
        self.peers, self.held, self.width, self.tok = peers, held, width, tok
        self.piece = held * held
        self.direct = held % 16 == 0

    def sent_shape(self, parts):
        return pltpu.HBM((self.peers, parts * self.piece, self.tok), BF16)

    def sent_spec(self, parts, step, offset=0):
        return pl.BlockSpec((self.peers, parts * self.piece, step), lambda t: (0, 0, t + offset))

    def arranged(self, array):
        if self.direct:
            return array
        parts = array.shape[1] // self.piece
        array = array.reshape(self.peers, parts, self.held, self.held, self.tok)
        array = array.transpose(1, 2, 0, 3, 4)
        return array.reshape(parts * self.held, self.width, self.tok)

    def arrived_spec(self, parts, step, offset=0):
        if self.direct:
            return self.sent_spec(parts, step, offset)
        return pl.BlockSpec((parts * self.held, self.width, step), lambda t: (0, 0, t + offset))

    def each_block(self, unroll, step):
        def some(outer, carry):
            for inner in range(unroll):
                step(outer * unroll + inner)
            return carry

        unroll = min(unroll, self.held)
        lax.fori_loop(0, self.held // unroll, some, 0)

    def block(self, ref, part, b):
        if not self.direct:
            return ref[part * self.held + b]
        rows = pl.ds(pl.multiple_of(part * self.piece + b * self.held, self.held), self.held)
        return jnp.concatenate([ref[s, rows, :] for s in range(self.peers)], axis=0)

    def put(self, scratch, b, value):
        for at in range(scratch.shape[0]):
            scratch[at, pl.ds(b, self.width, stride=self.held), :] = value[
                :, at * 128 : (at + 1) * 128
            ]

    def store_range(self, out_ref, part, scratch, which):
        size = self.piece // 2
        rows = slice(part * size, (part + 1) * size)
        for at in range(scratch.shape[0]):
            for peer in range(self.peers):
                start = peer * self.piece + which * size
                out_ref[peer, rows, at * 128 : (at + 1) * 128] = scratch[
                    at, start : start + size
                ].astype(BF16)

    def store(self, out_ref, part, scratch):
        rows = slice(part * self.piece, (part + 1) * self.piece)
        for at in range(scratch.shape[0]):
            out_ref[:, rows, at * 128 : (at + 1) * 128] = (
                scratch[at].reshape(self.peers, self.piece, 128).astype(BF16)
            )


def step_of(tok):
    return 256 if tok % 256 == 0 else 128


def scratch_for(plan, step):
    return pltpu.VMEM((step // 128, plan.width * plan.held, 128), F32)


def whole(array):
    return pl.BlockSpec(array.shape, lambda t: (0,) * len(array.shape))


def clear_at_first(*refs):
    @pl.when(pl.program_id(0) == 0)
    def _():
        for ref in refs:
            ref[...] = jnp.zeros_like(ref)


def cotangent_kernel(plan, in_ref, out_ref, scratch):
    def one(b):
        rows = pl.ds(pl.multiple_of(b * plan.width, plan.width), plan.width)
        plan.put(scratch, b, in_ref[rows, :].astype(F32))

    plan.each_block(UNROLL, one)
    plan.store(out_ref, 0, scratch)


def send_cotangent(plan, cotangent):
    step = step_of(plan.tok)
    return pl.pallas_call(
        functools.partial(cotangent_kernel, plan),
        grid=(plan.tok // step,),
        in_specs=[pl.BlockSpec((plan.width * plan.held, step), lambda t: (0, t))],
        out_specs=plan.sent_spec(1, step),
        out_shape=plan.sent_shape(1),
        scratch_shapes=[scratch_for(plan, step)],
        compiler_params=params(),
        name="send_cotangent",
    )(*in_hbm(cotangent))


def product_kernel(plan, over, in_ref, factor_ref, out_ref, scratch):
    def one(b):
        plan.put(scratch, b, dot(factor_ref[b], plan.block(in_ref, 0, b), over))

    plan.each_block(UNROLL, one)
    plan.store(out_ref, 0, scratch)


def product(plan, arrived, factor, over, name):
    step = step_of(plan.tok)
    return pl.pallas_call(
        functools.partial(product_kernel, plan, over),
        grid=(plan.tok // step,),
        in_specs=[plan.arrived_spec(1, step), whole(factor)],
        out_specs=plan.sent_spec(1, step),
        out_shape=plan.sent_shape(1),
        scratch_shapes=[scratch_for(plan, step)],
        compiler_params=params(),
        name=name,
    )(arrived, *in_hbm(factor))


def cut_rows(own, array, out_refs):
    groups = len(out_refs)
    size = array.shape[1] // groups
    for k, ref in enumerate(out_refs):
        if groups & (groups - 1) == 0:
            target = own ^ k
        else:
            target = lax.rem(own + k, groups)
        ref[...] = array[:, pl.ds(pl.multiple_of(target * size, size), size), :].astype(BF16)


def sum_rows_kernel(*refs):
    total = refs[0][...].astype(F32)
    for ref in refs[1:-1]:
        total = total + ref[...].astype(F32)
    refs[-1][...] = total


def sum_rows(pieces):
    shape = pieces[0].shape
    return pl.pallas_call(
        sum_rows_kernel,
        grid=(1,),
        in_specs=[whole(piece) for piece in pieces],
        out_specs=whole(pieces[0]),
        out_shape=pltpu.HBM(shape, F32),
        compiler_params=params(),
        name="sum_rows",
    )(*in_hbm(*pieces))


def product_and_cut_kernel(plan, scale, own_ref, in_ref, other_ref, factor_ref, out_ref, *refs):
    out_refs, (sums, scratch) = refs[:-2], refs[-2:]

    def one(b):
        values = plan.block(in_ref, 0, b)
        others = plan.block(other_ref, 0, b)
        plan.put(scratch, b, dot(factor_ref[b], values, TN))
        sums[b] = dot(values, others, NT) * scale

    plan.each_block(UNROLL, one)
    plan.store(out_ref, 0, scratch)
    cut_rows(own_ref[0], sums, out_refs)


def product_and_cut(plan, arrived, other, factor, scale, own, groups, name):
    step = plan.tok
    held, width, columns = factor.shape
    cut = pltpu.HBM((held, width // groups, columns), BF16)
    outs = pl.pallas_call(
        functools.partial(product_and_cut_kernel, plan, scale),
        grid=(1,),
        in_specs=[
            pl.BlockSpec(memory_space=pltpu.SMEM),
            plan.arrived_spec(1, step),
            plan.arrived_spec(1, step),
            whole(factor),
        ],
        out_specs=[plan.sent_spec(1, step)] + [whole(cut)] * groups,
        out_shape=[plan.sent_shape(1)] + [cut] * groups,
        scratch_shapes=[pltpu.VMEM(factor.shape, F32), scratch_for(plan, step)],
        compiler_params=params(),
        name=name,
    )(own, arrived, other, *in_hbm(factor))
    return outs[0], outs[1:]


def product_and_grad_kernel(plan, scale, first, last, in_ref, other_ref, factor_ref, *refs):
    if not first:
        before_ref, refs = refs[0], refs[2:]
    out_ref, sums_ref, scratch = refs

    def one(b):
        values = plan.block(in_ref, 0, b)
        others = plan.block(other_ref, 0, b)
        plan.put(scratch, b, dot(factor_ref[b], values, TN))
        total = dot(values, others, NT)
        if not first:
            total = total + before_ref[b]
        sums_ref[b] = (total * scale).astype(BF16) if last else total

    plan.each_block(UNROLL, one)
    plan.store(out_ref, 0, scratch)


def product_and_grad(plan, full, arrived, other, factor, scale, half, halves, before, name):
    step = plan.tok
    first, last = half == 0, half == halves - 1
    sums = pltpu.HBM(factor.shape, BF16 if last else F32)
    return pl.pallas_call(
        functools.partial(product_and_grad_kernel, plan, scale, first, last),
        grid=(1,),
        in_specs=[
            plan.arrived_spec(1, step, half if arrived.shape[2] > step else 0),
            full.arrived_spec(1, step, half),
            whole(factor),
        ]
        + ([] if first else [whole(sums), pl.BlockSpec(memory_space=pl.ANY)]),
        out_specs=[full.sent_spec(1, step, half), whole(sums)],
        out_shape=[full.sent_shape(1), sums],
        input_output_aliases={} if first else {4: 0},
        scratch_shapes=[scratch_for(plan, step)],
        compiler_params=params(),
        name=f"{name}_{half}",
    )(arrived, other, *in_hbm(factor, *before))


def first_kernel(plan, groups, count, *refs):
    slab_refs, (back_t_ref, gate_ref, up_ref, packed_ref, out_ref, gates, ups) = (
        refs[: groups * count],
        refs[groups * count :],
    )
    b = 0
    for piece in range(count):
        here = slab_refs[piece * groups : (piece + 1) * groups]
        rows = jnp.concatenate([ref[...] for ref in here], axis=0)
        packed = dot(back_t_ref[...], rows, NN).astype(BF16)
        size = packed.shape[1]
        packed_ref[:, b * plan.width : b * plan.width + size] = packed
        for at in range(size // plan.width):
            values = packed[:, at * plan.width : (at + 1) * plan.width]
            plan.put(gates, b, dot(gate_ref[b], values, ((0,), (1,))))
            plan.put(ups, b, dot(up_ref[b], values, ((0,), (1,))))
            b += 1
    plan.store(out_ref, 0, gates)
    plan.store(out_ref, 1, ups)


def first_products(plan, pieces, back_t, right_gate, right_up, half):
    groups = len(pieces[0])
    feats = plan.held * plan.width
    slabs = [slab for piece in pieces for slab in piece]
    sent = plan.sent_shape(2)
    return pl.pallas_call(
        functools.partial(first_kernel, plan, groups, len(pieces)),
        grid=(1,),
        in_specs=[whole(slab) for slab in slabs]
        + [
            pl.BlockSpec((plan.tok, back_t.shape[1]), lambda i: (half, 0)),
            whole(right_gate),
            whole(right_up),
        ],
        out_specs=[
            pl.BlockSpec((plan.tok, feats), lambda i: (0, 0)),
            plan.sent_spec(2, plan.tok),
        ],
        out_shape=[pltpu.HBM((plan.tok, feats), BF16), sent],
        scratch_shapes=[scratch_for(plan, plan.tok)] * 2,
        compiler_params=params(),
        name=f"first_products_{half}",
    )(*in_hbm(*slabs, back_t, right_gate, right_up))


ROOT = 0.7978845608028654
CUBE = 0.044715


def gelu_and_slope(x):
    square = x * x
    wave = jnp.tanh(x * (ROOT + (ROOT * CUBE) * square))
    half = 0.5 + 0.5 * wave
    slope = half + x * (1.0 - wave * wave) * (0.5 * ROOT + (1.5 * ROOT * CUBE) * square)
    return x * half, slope


def middle_kernel(plan, scale, first, last, spread_ref, hidden_grad_ref, gate_ref, up_ref, *refs):
    if not first:
        before_ref, refs = refs[0], refs[3:]
    hidden_ref, low_ref, high_ref, sums_ref, hiddens, gates, ups = refs

    def add_sum(at, value):
        if not first:
            value = value + before_ref[at]
        sums_ref[at] = (value * scale).astype(BF16) if last else value

    def one(b):
        gate_in = plan.block(spread_ref, 0, b)
        up_in = plan.block(spread_ref, 1, b)
        gate_out = dot(gate_ref[b], gate_in, TN).astype(BF16).astype(F32)
        up_out = dot(up_ref[b], up_in, TN).astype(BF16).astype(F32)
        back = plan.block(hidden_grad_ref, 0, b).astype(F32)
        active, slope = gelu_and_slope(gate_out)
        plan.put(hiddens, b, active * up_out)
        gate_back = (back * up_out * slope).astype(BF16)
        up_back = (back * active).astype(BF16)
        plan.put(gates, b, dot(gate_ref[b], gate_back, NN))
        plan.put(ups, b, dot(up_ref[b], up_back, NN))
        add_sum(b, dot(gate_in, gate_back, NT))
        add_sum(plan.held + b, dot(up_in, up_back, NT))

    plan.each_block(UNROLL, one)
    plan.store(hidden_ref, 0, hiddens)
    for part, scratch in enumerate((gates, ups)):
        plan.store_range(low_ref, part, scratch, 0)
        plan.store_range(high_ref, part, scratch, 1)


def middle(plan, full, spreads, hidden_grad, left_gate, left_up, scale, half, halves, before):
    step = plan.tok
    first, last = half == 0, half == halves - 1
    sums = pltpu.HBM((2 * plan.held,) + left_gate.shape[1:], BF16 if last else F32)
    sums_spec = whole(sums)
    kept = pl.BlockSpec(memory_space=pl.ANY)
    return pl.pallas_call(
        functools.partial(middle_kernel, plan, scale, first, last),
        grid=(1,),
        in_specs=[
            plan.arrived_spec(2, step),
            full.arrived_spec(1, step, half),
            whole(left_gate),
            whole(left_up),
        ]
        + ([] if first else [sums_spec, kept, kept]),
        out_specs=[plan.sent_spec(1, step)] + [full.sent_spec(1, step, half)] * 2 + [sums_spec],
        out_shape=[plan.sent_shape(1), full.sent_shape(1), full.sent_shape(1), sums],
        input_output_aliases={} if first else {5: 1, 6: 2},
        scratch_shapes=[scratch_for(plan, step)] * 3,
        compiler_params=params(),
        name=f"middle_{half}",
    )(spreads, hidden_grad, *in_hbm(left_gate, left_up, *before))


def spread_blocks(plan, in_ref, at):
    if not plan.direct:
        return in_ref[0, at], in_ref[1, at]
    rows = slice(at * plan.held, (at + 1) * plan.held)
    return tuple(
        jnp.concatenate([in_ref[s, part, rows, :] for s in range(plan.peers)], axis=0)
        for part in range(2)
    )


def spread_form(plan, arrived, count, offset):
    size = plan.piece // 2
    if plan.direct:
        return arrived.reshape(plan.peers, 2, size, plan.tok), pl.BlockSpec(
            (plan.peers, 2, count * plan.held, plan.tok), lambda i: (0, 0, i + offset, 0)
        )
    array = arrived.reshape(plan.peers, 2, plan.held // 2, plan.held, plan.tok)
    array = array.transpose(1, 2, 0, 3, 4).reshape(2, plan.held // 2, plan.width, plan.tok)
    return array, pl.BlockSpec(
        (2, count, plan.width, plan.tok), lambda i: (0, i + offset, 0, 0)
    )


def last_kernel(plan, in_ref, back_ref, gate_ref, up_ref, *slab_refs):
    cap = slab_refs[0].shape[0]
    for at in range(gate_ref.shape[0]):
        gate_back, up_back = spread_blocks(plan, in_ref, at)
        back = dot(gate_ref[at], gate_back, NN) + dot(up_ref[at], up_back, NN)
        columns = slice(at * plan.width, (at + 1) * plan.width)
        sent = dot(back_ref[...], back.astype(BF16), NT).astype(BF16)
        for k, ref in enumerate(slab_refs):
            ref[:, columns] = sent[k * cap : (k + 1) * cap]


def last_products(plan, arrived, back, right_gate, right_up, groups, piece, unit):
    start, count = piece
    offset = start % (plan.held // 2 // unit)
    lanes = back.shape[0]
    cap = lanes // groups
    arrived, arrived_spec = spread_form(plan, arrived, unit, offset)
    factor_spec = pl.BlockSpec((unit,) + right_gate.shape[1:], lambda i: (start + i, 0, 0))
    size = unit * plan.width
    return pl.pallas_call(
        functools.partial(last_kernel, plan),
        grid=(count,),
        in_specs=[arrived_spec, whole(back), factor_spec, factor_spec],
        out_specs=[pl.BlockSpec((cap, size), lambda i: (0, i))] * groups,
        out_shape=[pltpu.HBM((cap, size * count), BF16)] * groups,
        compiler_params=params(),
        name=f"last_products_{start}",
    )(arrived, *in_hbm(back, right_gate, right_up))


def right_grads_kernel(plan, scale, halves, in_ref, *refs):
    packed_refs, grads_ref = refs[:halves], refs[-1]
    for at in range(grads_ref.shape[1]):
        columns = slice(at * plan.width, (at + 1) * plan.width)
        values = jnp.concatenate([ref[:, columns] for ref in packed_refs], axis=0)
        for part, spread in enumerate(spread_blocks(plan, in_ref, at)):
            grads_ref[part, at] = (dot(values, spread, ((0,), (1,))) * scale).astype(BF16)


def right_grads(plan, arrived, packed, factor, scale, unit, which, before):
    arrived, arrived_spec = spread_form(plan, arrived, unit, 0)
    block = factor.shape[1:]
    count = plan.held // 2 // unit
    start = which * count
    rows = packed[0].shape[0]
    return pl.pallas_call(
        functools.partial(right_grads_kernel, plan, scale, len(packed)),
        grid=(count,),
        in_specs=[arrived_spec]
        + [pl.BlockSpec((rows, unit * plan.width), lambda i: (0, start + i))] * len(packed)
        + [pl.BlockSpec(memory_space=pl.ANY)] * len(before),
        out_specs=pl.BlockSpec((2, unit) + block, lambda i: (0, start + i, 0, 0)),
        out_shape=pltpu.HBM((2,) + factor.shape, BF16),
        input_output_aliases={1 + len(packed): 0} if before else {},
        compiler_params=params(),
        name=f"right_grads_{which}",
    )(arrived, *in_hbm(*packed, *before))


def natural_kernel(in_ref, out_ref):
    held, _, held_there, tok = out_ref.shape
    out_ref[...] = in_ref[...].reshape(held, 1, held_there, tok)


def natural_order(plan, arrived):
    shape = (plan.held, plan.peers, plan.held, plan.tok)
    if not plan.direct:
        array = arrived.reshape(plan.peers, plan.held, plan.held, plan.tok)
        return array.transpose(1, 0, 2, 3).reshape(-1, plan.tok)
    array = pl.pallas_call(
        natural_kernel,
        grid=(plan.peers,),
        in_specs=[pl.BlockSpec((1, plan.piece, plan.tok), lambda s: (s, 0, 0))],
        out_specs=pl.BlockSpec((plan.held, 1, plan.held, plan.tok), lambda s: (0, s, 0, 0)),
        out_shape=pltpu.HBM(shape, BF16),
        compiler_params=params(),
        name="natural_order",
    )(arrived)
    return array.reshape(-1, plan.tok)


def body(
    earlier,
    mix_weights,
    destinations,
    cotangent,
    right_gate,
    left_gate,
    right_up,
    left_up,
    right_down,
    left_down,
):
    held, width = right_gate.shape[0], right_gate.shape[1]
    feats = earlier.shape[1]
    tok = cotangent.shape[1]
    groups = lax.axis_size("dp")
    peers = lax.axis_size("feat")
    cap = 5 * tok // (4 * groups)
    scale = (tok * groups) ** (-0.5)
    halves = 2 if tok % 256 == 0 else 1
    halves = 2 if tok % 256 == 0 else 1
    plan = Plan(peers, held, width, tok)
    part = Plan(peers, held, width, tok // halves)
    there, unit = pieces_of(
        held // 4, (held - held // 4) // 2, held - held // 4 - (held - held // 4) // 2
    )
    step = unit * width

    def move(array):
        return lax.all_to_all(array, "feat", split_axis=0, concat_axis=0, tiled=True)

    def swap(array):
        return plan.arranged(move(array))

    def after(array, *others):
        return lax.optimization_barrier((array, *others))[0]

    def total(grads):
        return lax.psum_scatter(grads, "dp", scatter_dimension=1, tiled=True)

    def exchanged_total(pieces):
        return sum_rows(exchange_rows(pieces, groups))

    own = lax.axis_index("dp").reshape(1)
    home, back, back_t = routing(destinations, own, groups, tok, cap)
    sent = [mix_and_sort(earlier, mix_weights, home, groups, p, step) for p in there]
    rows = [exchange_rows(slabs, groups) for slabs in sent]

    out_grads = swap(send_cotangent(plan, cotangent))
    out_grads = after(out_grads, rows[0], *sent[1:])
    down_spread_grad = swap(product(plan, out_grads, left_down, NN, "left_back_down"))
    down_spread_grad = after(down_spread_grad, rows[1])
    hidden_grad = product(plan, down_spread_grad, right_down, NN, "right_back_down")
    rows[2] = after(rows[2], hidden_grad)
    hidden_grad = swap(hidden_grad)

    packed, spreads = zip(
        *[first_products(part, rows, back_t, right_gate, right_up, h) for h in range(halves)]
    )
    arrived, moved = [], hidden_grad
    for h in range(halves):
        moved = move(after(spreads[h], moved))
        arrived.append(part.arranged(moved))
    if halves > 1:
        arrived[0] = after(arrived[0], spreads[1])
    hidden, before = [], ()
    for h in range(halves):
        if h:
            arrived[h] = after(arrived[h], hidden[0])
        sent_hidden, low, high, left_sums = middle(
            part, plan, arrived[h], hidden_grad, left_gate, left_up, scale, h, halves, before
        )
        hidden.append(sent_hidden)
        before = (left_sums, low, high)
    if halves > 1:
        hidden[0] = moved = move(after(hidden[0], moved))
    low = move(after(low, moved))
    left_sums = total(left_sums)
    high = move(after(high, low, left_sums))
    half = held // 2
    back_pieces, unit = pieces_of(
        half * 3 // 4, half - half * 3 // 4, half // 2, half - half // 2
    )
    step = unit * width
    factors = (back, right_gate, right_up, groups)
    sent = [last_products(plan, low, *factors, p, unit) for p in back_pieces[:2]]
    rows = [exchange_rows(slabs, groups) for slabs in sent]
    right_sums = right_grads(
        plan, after(low, sent), packed, right_gate, scale, unit, 0, ()
    )
    hidden[-1] = move(after(hidden[-1], high, rows[0], sent[1], right_sums))
    sent = [last_products(plan, high, *factors, p, unit) for p in back_pieces[2:]]
    rows += [exchange_rows(slabs, groups) for slabs in sent]
    right_sums = right_grads(
        plan, after(high, sent), packed, right_gate, scale, unit, 1, (right_sums,)
    )
    before = ()
    for h in range(halves):
        arrived = hidden[h]
        if h == halves - 1:
            arrived = after(arrived, rows[1], right_sums, *sent)
        down_spread, down_sums = product_and_grad(
            part, plan, part.arranged(arrived), down_spread_grad, right_down, scale, h, halves,
            before, "right_down",
        )
        before = (down_sums, down_spread)
    grad_right_down = down_sums
    down_spread = after(swap(down_spread), rows[2])
    result, grad_left_down = product_and_cut(
        plan, down_spread, out_grads, left_down, scale, own, groups, "left_down"
    )
    right_sums = right_sums.reshape((2 * held,) + right_gate.shape[1:])
    right_sums = total(jnp.concatenate((right_sums, grad_right_down))).astype(F32)
    grad_right_gate, grad_right_up, grad_right_down = jnp.split(right_sums, 3)
    grad_left_gate, grad_left_up = jnp.split(left_sums.astype(F32), 2)
    grad_left_down = exchanged_total(grad_left_down)
    mixed_grad = None
    for slabs, piece in zip(rows, back_pieces):
        mixed_grad = unsort(slabs, home, piece, step, feats, mixed_grad)
    output = natural_order(plan, move(result))

    return (
        output,
        mixed_grad,
        grad_right_gate,
        grad_left_gate,
        grad_right_up,
        grad_left_up,
        grad_right_down,
        grad_left_down,
    )


def solution(mesh):
    return jax.shard_map(
        body,
        mesh=mesh,
        in_specs=(
            P(None, "feat", "dp"),
            P(),
            P(),
            P("feat", "dp"),
            P("feat", None, None),
            P("feat", None, None),
            P("feat", None, None),
            P("feat", None, None),
            P("feat", None, None),
            P("feat", None, None),
        ),
        out_specs=(
            P("feat", "dp"),
            P("feat", "dp"),
            P("feat", "dp", None),
            P("feat", "dp", None),
            P("feat", "dp", None),
            P("feat", "dp", None),
            P("feat", "dp", None),
            P("feat", "dp", None),
        ),
        check_vma=False,
    )
```

time: 482 us -> 393 us (0.82)
  the two profiles are of different devices: /device:TPU:9 before, /device:TPU:0 now
where the time goes in v2:
time: 393 us; the launch traced here: 390 us
  waiting for transfers between devices  147 us (37%)
  Pallas kernels  119 us (30%)
  starting transfers between devices  95 us (24%)
  between operations  14.4 us (4%)
  local copies, waits for them, and re-layouts  12.5 us (3%)
    ppermute x24, waiting for transfers between devices, exchange_rows(): received.append(lax.ppermute(slabs[k], 'dp', pairs))  69.7 us
    all_to_all x11, waiting for transfers between devices, move(): lax.all_to_all(array, 'feat', split_axis=0, concat_axis=0, tiled=True)  53.1 us
    ppermute x24, starting transfers between devices, exchange_rows(): received.append(lax.ppermute(slabs[k], 'dp', pairs))  49.7 us
    all_to_all x11, starting transfers between devices, move(): lax.all_to_all(array, 'feat', split_axis=0, concat_axis=0, tiled=True)  44.8 us
    reduce_scatter x2, waiting for transfers between devices, total(): return lax.psum_scatter(grads, 'dp', scatter_dimension=1, tiled=True)  23.9 us
    pallas_call x2, Pallas kernels, middle(): pl.pallas_call(functools.partial(middle_kernel, plan, scale, first, last)...  22.8 us
    pallas_call x4, Pallas kernels, last_products(): pl.pallas_call(functools.partial(last_kernel, plan), grid=(count,), in_sp...  13.9 us
    pallas_call x2, Pallas kernels, first_products(): pl.pallas_call(functools.partial(first_kernel, plan, groups, len(pieces))...  13.5 us
  transfers between devices with their start and end apart: 37, of which 20 were waited for; matrix products, arithmetic and copies ran while one was open for 1% of the time, Pallas kernels for 25%

profile of v2, /device:TPU:0, one launch (start us, length us, event | category | flops | bytes accessed | tf_op | source)
XLA Modules:
  0.0 390.4 jit_solution(6116916167884699658)
XLA Ops:
  7.2 4.7 %send_cotangent.1 = bf16[8,256,512]{2,1,0:T(8,128)(2,1)} custom-call(bf16[2048,512]{1,0:T(8,128)(2,1)} %in_ref.1), custom_call_target="tpu_custom_call" | custom-call | tf_op jit(solution)/shard_map/send_cotangent/pallas_call | solution.py:271
  11.8 5.3 %all-to-all-start = ((bf16[8,256,512]{2,1,0:T(8,128)(2,1)}), bf16[8,256,512]{2,1,0:T(8,128)(2,1)S(1)}, u32[]{:S(2)}, u32[]{:S(2)}) async-start(bf16[8,256,512]{2,1,0:T(8,128)(2,1)} %send_cotangent.1), calls=%async_computation | async-start | bytes 4194304 | tf_op jit(solution)/shard_map/all_to_all | solution.py:660
  20.3 3.3 mix_and_sort_0.1
  27.9 4.5 %mix_and_sort_5.1 = (bf16[160,768]{1,0:T(8,128)(2,1)}, bf16[160,768]{1,0:T(8,128)(2,1)}, bf16[160,768]{1,0:T(8,128)(2,1)}, bf16[160,768]{1,0:T(8,128)(2,1)}) custom-call(f32[3]{0:T(128)S(1)} %copy-done.7, bf16[3,2048,640]{2,1,0:T(8,128)(2,1)} %earlier_ref.5, bf16[640,640]{1,0:T(8,128)(2,1)} %get-tuple-element.78.home_ref), custom_call_target="tpu_custom_call" | custom-call | tf_op jit(solution)/shard_map/mix_and_sort_5/pallas_call | solution.py:125
  32.4 4.5 %mix_and_sort_2.1 = (bf16[160,768]{1,0:T(8,128)(2,1)}, bf16[160,768]{1,0:T(8,128)(2,1)}, bf16[160,768]{1,0:T(8,128)(2,1)}, bf16[160,768]{1,0:T(8,128)(2,1)}) custom-call(f32[3]{0:T(128)S(1)} %copy-done.7, bf16[3,2048,640]{2,1,0:T(8,128)(2,1)} %earlier_ref.5, bf16[640,640]{1,0:T(8,128)(2,1)} %get-tuple-element.78.home_ref), custom_call_target="tpu_custom_call" | custom-call | tf_op jit(solution)/shard_map/mix_and_sort_2/pallas_call | solution.py:125
  36.8 3.5 collective-permute-done.1.refs_2_
  40.3 3.5 all-to-all-done.in_ref.other_ref
  43.8 4.6 %left_back_down.1 = bf16[8,256,512]{2,1,0:T(8,128)(2,1)} custom-call(bf16[8,256,512]{2,1,0:T(8,128)(2,1)S(1)} %all-to-all-done.in_ref.other_ref, bf16[16,128,128]{2,1,0:T(8,128)(2,1)} %factor_ref.9), custom_call_target="tpu_custom_call" | custom-call | tf_op jit(solution)/shard_map/left_back_down/pallas_call | solution.py:293
  48.4 3.7 all-to-all-start.1
  56.6 8.9 %collective-permute-done.3.refs_5_ = bf16[160,768]{1,0:T(8,128)(2,1)S(1)} collective-permute-done((bf16[160,768]{1,0:T(8,128)(2,1)}, bf16[160,768]{1,0:T(8,128)(2,1)S(1)}, u32[]{:S(2)}, u32[]{:S(2)}) %collective-permute-start.3) | collective-permute-done | bytes 245792 | tf_op jit(solution)/shard_map/ppermute | solution.py:147
  65.5 8.6 %collective-permute-done.4.refs_6_ = bf16[160,768]{1,0:T(8,128)(2,1)S(1)} collective-permute-done((bf16[160,768]{1,0:T(8,128)(2,1)S(1)}, bf16[160,768]{1,0:T(8,128)(2,1)S(1)}, u32[]{:S(2)}, u32[]{:S(2)}) %collective-permute-start.4) | collective-permute-done | bytes 245792 | tf_op jit(solution)/shard_map/ppermute | solution.py:147
  74.1 4.6 %all-to-all-done.1.in_ref.other_ref = bf16[8,256,512]{2,1,0:T(8,128)(2,1)S(1)} async-done(((bf16[8,256,512]{2,1,0:T(8,128)(2,1)}), bf16[8,256,512]{2,1,0:T(8,128)(2,1)S(1)}, u32[]{:S(2)}, u32[]{:S(2)}) %all-to-all-start.1) | async-done | bytes 2097184 | tf_op jit(solution)/shard_map/all_to_all | solution.py:660
  78.7 4.6 %right_back_down.1 = bf16[8,256,512]{2,1,0:T(8,128)(2,1)} custom-call(bf16[8,256,512]{2,1,0:T(8,128)(2,1)S(1)} %all-to-all-done.1.in_ref.other_ref, bf16[16,128,128]{2,1,0:T(8,128)(2,1)} %factor_ref.8), custom_call_target="tpu_custom_call" | custom-call | tf_op jit(solution)/shard_map/right_back_down/pallas_call | solution.py:293
  83.3 3.6 all-to-all-start.2
  91.4 8.8 %collective-permute-done.6.refs_9_ = bf16[160,768]{1,0:T(8,128)(2,1)S(1)} collective-permute-done((bf16[160,768]{1,0:T(8,128)(2,1)}, bf16[160,768]{1,0:T(8,128)(2,1)S(1)}, u32[]{:S(2)}, u32[]{:S(2)}) %collective-permute-start.6) | collective-permute-done | bytes 245792 | tf_op jit(solution)/shard_map/ppermute | solution.py:147
  100.2 8.9 %collective-permute-done.7.refs_10_ = bf16[160,768]{1,0:T(8,128)(2,1)S(1)} collective-permute-done((bf16[160,768]{1,0:T(8,128)(2,1)}, bf16[160,768]{1,0:T(8,128)(2,1)S(1)}, u32[]{:S(2)}, u32[]{:S(2)}) %collective-permute-start.7) | collective-permute-done | bytes 245792 | tf_op jit(solution)/shard_map/ppermute | solution.py:147
  109.9 6.7 %first_products_0.1 = (bf16[256,2048]{1,0:T(8,128)(2,1)}, bf16[8,512,256]{2,1,0:T(8,128)(2,1)}) custom-call(bf16[160,512]{1,0:T(8,128)(2,1)} %get-tuple-element.79.refs_0_, bf16[160,512]{1,0:T(8,128)(2,1)} %copy-done.16, bf16[160,512]{1,0:T(8,128)(2,1)} %copy-done.17, bf16[160,512]{1,0:T(8,128)(2,1)} %copy-done.18, ...), custom_call_target="tpu_custom_call" | custom-call | tf_op jit(solution)/shard_map/first_products_0/pallas_call | solution.py:438
  116.6 4.6 %all-to-all-start.3 = ((bf16[8,512,256]{2,1,0:T(8,128)(2,1)}), bf16[8,512,256]{2,1,0:T(8,128)(2,1)}, u32[]{:S(2)}, u32[]{:S(2)}) async-start(bf16[8,512,256]{2,1,0:T(8,128)(2,1)} %get-tuple-element.100), calls=%async_computation.3 | async-start | bytes 4194304 | tf_op jit(solution)/shard_map/all_to_all | solution.py:660
  121.1 6.7 %first_products_1.1 = (bf16[256,2048]{1,0:T(8,128)(2,1)}, bf16[8,512,256]{2,1,0:T(8,128)(2,1)}) custom-call(bf16[160,512]{1,0:T(8,128)(2,1)} %get-tuple-element.79.refs_0_, bf16[160,512]{1,0:T(8,128)(2,1)} %copy-done.16, bf16[160,512]{1,0:T(8,128)(2,1)} %copy-done.17, bf16[160,512]{1,0:T(8,128)(2,1)} %copy-done.18, ...), custom_call_target="tpu_custom_call" | custom-call | tf_op jit(solution)/shard_map/first_products_1/pallas_call | solution.py:438
  127.9 19.7 %all-to-all-done.3.spread_ref = bf16[8,512,256]{2,1,0:T(8,128)(2,1)} async-done(((bf16[8,512,256]{2,1,0:T(8,128)(2,1)}), bf16[8,512,256]{2,1,0:T(8,128)(2,1)}, u32[]{:S(2)}, u32[]{:S(2)}) %all-to-all-start.3) | async-done | bytes 2097184 | tf_op jit(solution)/shard_map/all_to_all | solution.py:660
  147.6 4.3 %all-to-all-start.4 = ((bf16[8,512,256]{2,1,0:T(8,128)(2,1)}), bf16[8,512,256]{2,1,0:T(8,128)(2,1)}, u32[]{:S(2)}, u32[]{:S(2)}) async-start(bf16[8,512,256]{2,1,0:T(8,128)(2,1)} %get-tuple-element.101), calls=%async_computation.4 | async-start | bytes 4194304 | tf_op jit(solution)/shard_map/all_to_all | solution.py:660
  152.0 11.2 %middle_0.1 = (bf16[8,256,256]{2,1,0:T(8,128)(2,1)}, bf16[8,256,512]{2,1,0:T(8,128)(2,1)}, bf16[8,256,512]{2,1,0:T(8,128)(2,1)}, f32[32,128,128]{2,1,0:T(8,128)}) custom-call(bf16[8,512,256]{2,1,0:T(8,128)(2,1)} %all-to-all-done.3.spread_ref, bf16[8,256,512]{2,1,0:T(8,128)(2,1)S(1)} %all-to-all-done.2.hidden_grad_ref, bf16[16,128,128]{2,1,0:T(8,128)(2,1)} %gate_ref.7, ...), custom_call_target="tpu_custom_call" | custom-call | tf_op jit(solution)/shard_map/middle_0/pallas_call | solution.py:508
  163.2 15.5 %all-to-all-done.4.spread_ref = bf16[8,512,256]{2,1,0:T(8,128)(2,1)} async-done(((bf16[8,512,256]{2,1,0:T(8,128)(2,1)}), bf16[8,512,256]{2,1,0:T(8,128)(2,1)}, u32[]{:S(2)}, u32[]{:S(2)}) %all-to-all-start.4) | async-done | bytes 2097184 | tf_op jit(solution)/shard_map/all_to_all | solution.py:660
  178.6 3.6 all-to-all-start.5
  182.5 11.6 %middle_1.1 = (bf16[8,256,256]{2,1,0:T(8,128)(2,1)}, bf16[8,256,512]{2,1,0:T(8,128)(2,1)}, bf16[8,256,512]{2,1,0:T(8,128)(2,1)}, bf16[32,128,128]{2,1,0:T(8,128)(2,1)}) custom-call(bf16[8,512,256]{2,1,0:T(8,128)(2,1)} %all-to-all-done.4.spread_ref, ...), custom_call_target="tpu_custom_call", output_to_operand_aliasing={{1}: (5, {}), {2}: (6, {})} | custom-call | tf_op jit(solution)/shard_map/middle_1/pallas_call | solution.py:508
  194.1 3.4 all-to-all-done.5.in_ref
  197.5 3.6 all-to-all-start.6
  201.1 23.9 %reduce-scatter.3.cloned.1.call-done = bf16[32,32,128]{2,1,0:T(8,128)(2,1)} async-done(((bf16[32,128,128]{2,1,0:T(8,128)(2,1)}), bf16[32,32,128]{2,1,0:T(8,128)(2,1)}) %reduce-scatter.3.cloned.1.call-update) | async-done | bytes 262160 | tf_op jit(solution)/shard_map/reduce_scatter | solution.py:669
  229.0 3.6 all-to-all-start.7
  234.2 4.4 %last_products_0.1 = (bf16[160,768]{1,0:T(8,128)(2,1)}, bf16[160,768]{1,0:T(8,128)(2,1)}, bf16[160,768]{1,0:T(8,128)(2,1)}, bf16[160,768]{1,0:T(8,128)(2,1)}) custom-call(bf16[8,2,128,512]{3,2,1,0:T(8,128)(2,1)S(1)} %bitcast.10, bf16[640,512]{1,0:T(8,128)(2,1)} %get-tuple-element.115.back_ref, bf16[16,128,128]{2,1,0:T(8,128)(2,1)} %gate_ref.11, ...), custom_call_target="tpu_custom_call" | custom-call | tf_op jit(solution)/shard_map/last_products_0/pallas_call | solution.py:569
  238.6 4.9 %collective-permute-start.9 = (bf16[160,768]{1,0:T(8,128)(2,1)}, bf16[160,768]{1,0:T(8,128)(2,1)S(1)}, u32[]{:S(2)}, u32[]{:S(2)}) collective-permute-start(bf16[160,768]{1,0:T(8,128)(2,1)} %get-tuple-element.117), channel_id=1, source_target_pairs={{0,8},{8,0},{16,24},{24,16},{1,9},{9,1},{17,25},{25,17},{2,10},{10... | collective-permute-start | bytes 737288 | tf_op jit(solution)/shard_map/ppermute | solution.py:147
  248.5 4.0 %right_grads_0.1.refs_2_ = bf16[2,16,128,128]{3,2,1,0:T(8,128)(2,1)} custom-call(bf16[8,2,128,512]{3,2,1,0:T(8,128)(2,1)S(1)} %bitcast.12, bf16[256,2048]{1,0:T(8,128)(2,1)} %get-tuple-element.125.refs_0_, bf16[256,2048]{1,0:T(8,128)(2,1)} %get-tuple-element.126.refs_1_), custom_call_target="tpu_custom_call" | custom-call | tf_op jit(solution)/shard_map/right_grads_0/pallas_call | solution.py:595
  255.0 8.9 %collective-permute-done.10.refs_2_ = bf16[160,768]{1,0:T(8,128)(2,1)S(1)} collective-permute-done((bf16[160,768]{1,0:T(8,128)(2,1)}, bf16[160,768]{1,0:T(8,128)(2,1)S(1)}, u32[]{:S(2)}, u32[]{:S(2)}) %collective-permute-start.10) | collective-permute-done | bytes 245792 | tf_op jit(solution)/shard_map/ppermute | solution.py:147
  264.7 4.2 %all-to-all-start.8 = ((bf16[8,256,256]{2,1,0:T(8,128)(2,1)}), bf16[8,256,256]{2,1,0:T(8,128)(2,1)}, u32[]{:S(2)}, u32[]{:S(2)}) async-start(bf16[8,256,256]{2,1,0:T(8,128)(2,1)} %get-tuple-element.127), calls=%async_computation.9 | async-start | bytes 2097152 | tf_op jit(solution)/shard_map/all_to_all | solution.py:660
  268.9 4.5 %collective-permute-start.12 = (bf16[160,256]{1,0:T(8,128)(2,1)}, bf16[160,256]{1,0:T(8,128)(2,1)S(1)}, u32[]{:S(2)}, u32[]{:S(2)}) collective-permute-start(bf16[160,256]{1,0:T(8,128)(2,1)} %get-tuple-element.121), channel_id=1, source_target_pairs={{0,8},{8,0},{16,24},{24,16},{1,9},{9,1},{17,25},{25,17},{2,10},{10... | collective-permute-start | bytes 245768 | tf_op jit(solution)/shard_map/ppermute | solution.py:147
  277.5 3.9 %right_down_0.1 = (bf16[8,256,512]{2,1,0:T(8,128)(2,1)}, f32[16,128,128]{2,1,0:T(8,128)}) custom-call(bf16[8,256,256]{2,1,0:T(8,128)(2,1)S(1)} %all-to-all-done.5.in_ref, bf16[8,256,512]{2,1,0:T(8,128)(2,1)S(1)} %copy-done.1, bf16[16,128,128]{2,1,0:T(8,128)(2,1)} %factor_ref.8), custom_call_target="tpu_custom_call" | custom-call | tf_op jit(solution)/shard_map/right_down_0/pallas_call | solution.py:394
  281.4 3.4 last_products_6.1
  284.9 3.5 last_products_4.1
  288.3 4.0 %right_grads_1.1 = bf16[2,16,128,128]{3,2,1,0:T(8,128)(2,1)} custom-call(bf16[8,2,128,512]{3,2,1,0:T(8,128)(2,1)S(1)} %bitcast.9, bf16[256,2048]{1,0:T(8,128)(2,1)} %get-tuple-element.125.refs_0_, bf16[256,2048]{1,0:T(8,128)(2,1)} %get-tuple-element.126.refs_1_, bf16[2,16,128,128]{3,2,1,0:T(8,128)(2,1)} %right_grads_0.1.refs_2_), custom_call_target="tpu_custom_call", output_to_operand_aliasing={{}: (3, {})} | custom-call | tf_op jit(solution)/shard_map/right_grads_1/pallas_call | solution.py:595
  294.0 4.4 %right_down_1.1 = (bf16[8,256,512]{2,1,0:T(8,128)(2,1)}, bf16[16,128,128]{2,1,0:T(8,128)(2,1)}) custom-call(bf16[8,256,256]{2,1,0:T(8,128)(2,1)} %all-to-all-done.8.in_ref, bf16[8,256,512]{2,1,0:T(8,128)(2,1)S(1)} %copy-done.2, bf16[16,128,128]{2,1,0:T(8,128)(2,1)} %factor_ref.8, ...), custom_call_target="tpu_custom_call", output_to_operand_aliasing={{0}: (4, {})} | custom-call | tf_op jit(solution)/shard_map/right_down_1/pallas_call | solution.py:394
  298.5 4.5 %all-to-all-start.9 = ((bf16[8,256,512]{2,1,0:T(8,128)(2,1)}), bf16[8,256,512]{2,1,0:T(8,128)(2,1)}, u32[]{:S(2)}, u32[]{:S(2)}) async-start(bf16[8,256,512]{2,1,0:T(8,128)(2,1)} %get-tuple-element.140), calls=%async_computation.10 | async-start | bytes 4194304 | tf_op jit(solution)/shard_map/all_to_all | solution.py:660
  310.3 5.9 %collective-permute-done.15.refs_1_ = bf16[160,512]{1,0:T(8,128)(2,1)S(1)} collective-permute-done((bf16[160,512]{1,0:T(8,128)(2,1)}, bf16[160,512]{1,0:T(8,128)(2,1)S(1)}, u32[]{:S(2)}, u32[]{:S(2)}) %collective-permute-start.15) | collective-permute-done | bytes 163872 | tf_op jit(solution)/shard_map/ppermute | solution.py:147
  316.3 8.3 %collective-permute-done.16.refs_2_ = bf16[160,512]{1,0:T(8,128)(2,1)S(1)} collective-permute-done((bf16[160,512]{1,0:T(8,128)(2,1)S(1)}, bf16[160,512]{1,0:T(8,128)(2,1)S(1)}, u32[]{:S(2)}, u32[]{:S(2)}) %collective-permute-start.16) | collective-permute-done | bytes 163872 | tf_op jit(solution)/shard_map/ppermute | solution.py:147
  326.0 3.7 all-to-all-done.9.in_ref
  329.6 6.0 %left_down.1 = (bf16[8,256,512]{2,1,0:T(8,128)(2,1)}, bf16[16,32,128]{2,1,0:T(8,128)(2,1)}, bf16[16,32,128]{2,1,0:T(8,128)(2,1)}, bf16[16,32,128]{2,1,0:T(8,128)(2,1)}, bf16[16,32,128]{2,1,0:T(8,128)(2,1)}) custom-call(s32[1]{0:T(128)} %bitcast.own_ref, bf16[8,256,512]{2,1,0:T(8,128)(2,1)} %all-to-all-done.9.in_ref, bf16[8,256,512]{2,1,0:T(8,128)(2,1)S(1)} %copy-done.6, ...), custom_call_target="tpu_custom_call" | custom-call | tf_op jit(solution)/shard_map/left_down/pallas_call | solution.py:354
  335.8 3.8 all-to-all-start.10
  339.5 9.6 %collective-permute-start.18 = (bf16[160,512]{1,0:T(8,128)(2,1)S(1)}, bf16[160,512]{1,0:T(8,128)(2,1)S(1)}, u32[]{:S(2)}, u32[]{:S(2)}) collective-permute-start(bf16[160,512]{1,0:T(8,128)(2,1)S(1)} %copy-done.37), channel_id=1, source_target_pairs={{0,8},{8,0},{16,24},{24,16},{1,9},{9,1},{17,25},{25,17},{2,10},{10... | collective-permute-start | bytes 491528 | tf_op jit(solution)/shard_map/ppermute | solution.py:147
  359.8 4.2 %unsort_0.1.refs_4_ = bf16[2048,640]{1,0:T(8,128)(2,1)} custom-call(bf16[640,640]{1,0:T(8,128)(2,1)} %get-tuple-element.78.home_ref, bf16[160,768]{1,0:T(8,128)(2,1)} %get-tuple-element.116.refs_0_, bf16[160,768]{1,0:T(8,128)(2,1)} %copy-done.19, bf16[160,768]{1,0:T(8,128)(2,1)} %copy-done.20, bf16[160,768]{1,0:T(8,128)(2,1)} %collective-permute-done.11.refs_3_), custom_call_target="tpu_custom_call" | custom-call | tf_op jit(solution)/shard_map/unsort_0/pallas_call | solution.py:163
  (145 shorter events, 75.9 us)
Async XLA Ops:
  11.8 31.9 %all-to-all-start = ((bf16[8,256,512]{2,1,0:T(8,128)(2,1)}), bf16[8,256,512]{2,1,0:T(8,128)(2,1)S(1)}, u32[]{:S(2)}, u32[]{:S(2)}) async-start(bf16[8,256,512]{2,1,0:T(8,128)(2,1)} %send_cotangent.1), calls=%async_computation | async-start | bytes 4194304 | tf_op jit(solution)/shard_map/all_to_all | solution.py:660
  23.5 13.3 %collective-permute-start = (bf16[160,512]{1,0:T(8,128)(2,1)}, bf16[160,512]{1,0:T(8,128)(2,1)S(1)}, u32[]{:S(2)}, u32[]{:S(2)}) collective-permute-start(bf16[160,512]{1,0:T(8,128)(2,1)} %get-tuple-element.80), channel_id=1, source_target_pairs={{0,8},{8,0},{16,24},{24,16},{1,9},{9,1},{17,25},{25,17},{2,10},{10... | collective-permute-start | bytes 491528 | tf_op jit(solution)/shard_map/ppermute | solution.py:147
  25.1 15.2 %collective-permute-start.1 = (bf16[160,512]{1,0:T(8,128)(2,1)}, bf16[160,512]{1,0:T(8,128)(2,1)S(1)}, u32[]{:S(2)}, u32[]{:S(2)}) collective-permute-start(bf16[160,512]{1,0:T(8,128)(2,1)} %get-tuple-element.81), channel_id=1, source_target_pairs={{0,16},{8,24},{16,0},{24,8},{1,17},{9,25},{17,1},{25,9},{2,18},{10... | collective-permute-start | bytes 491528 | tf_op jit(solution)/shard_map/ppermute | solution.py:147
  27.7 12.6 %collective-permute-start.2 = (bf16[160,512]{1,0:T(8,128)(2,1)}, bf16[160,512]{1,0:T(8,128)(2,1)S(1)}, u32[]{:S(2)}, u32[]{:S(2)}) collective-permute-start(bf16[160,512]{1,0:T(8,128)(2,1)} %get-tuple-element.82), channel_id=1, source_target_pairs={{0,24},{8,16},{16,8},{24,0},{1,25},{9,17},{17,9},{25,1},{2,26},{10... | collective-permute-start | bytes 491528 | tf_op jit(solution)/shard_map/ppermute | solution.py:147
  36.8 11.5 %copy-start.16 = (bf16[160,512]{1,0:T(8,128)(2,1)}, bf16[160,512]{1,0:T(8,128)(2,1)S(1)}, u32[]{:S(2)}) copy-start(bf16[160,512]{1,0:T(8,128)(2,1)S(1)} %collective-permute-done.refs_1_) | copy-start | bytes 491524
  48.4 30.3 %all-to-all-start.1 = ((bf16[8,256,512]{2,1,0:T(8,128)(2,1)}), bf16[8,256,512]{2,1,0:T(8,128)(2,1)S(1)}, u32[]{:S(2)}, u32[]{:S(2)}) async-start(bf16[8,256,512]{2,1,0:T(8,128)(2,1)} %left_back_down.1), calls=%async_computation.1 | async-start | bytes 4194304 | tf_op jit(solution)/shard_map/all_to_all | solution.py:660
  52.1 13.3 %collective-permute-start.3 = (bf16[160,768]{1,0:T(8,128)(2,1)}, bf16[160,768]{1,0:T(8,128)(2,1)S(1)}, u32[]{:S(2)}, u32[]{:S(2)}) collective-permute-start(bf16[160,768]{1,0:T(8,128)(2,1)} %get-tuple-element.84), channel_id=1, source_target_pairs={{0,8},{8,0},{16,24},{24,16},{1,9},{9,1},{17,25},{25,17},{2,10},{10... | collective-permute-start | bytes 737288 | tf_op jit(solution)/shard_map/ppermute | solution.py:147
  53.8 20.3 %collective-permute-start.4 = (bf16[160,768]{1,0:T(8,128)(2,1)S(1)}, bf16[160,768]{1,0:T(8,128)(2,1)S(1)}, u32[]{:S(2)}, u32[]{:S(2)}) collective-permute-start(bf16[160,768]{1,0:T(8,128)(2,1)S(1)} %copy-done.34), channel_id=1, source_target_pairs={{0,16},{8,24},{16,0},{24,8},{1,17},{9,25},{17,1},{25,9},{2,18},{10... | collective-permute-start | bytes 737288 | tf_op jit(solution)/shard_map/ppermute | solution.py:147
  56.4 17.7 %collective-permute-start.5 = (bf16[160,768]{1,0:T(8,128)(2,1)S(1)}, bf16[160,768]{1,0:T(8,128)(2,1)S(1)}, u32[]{:S(2)}, u32[]{:S(2)}) collective-permute-start(bf16[160,768]{1,0:T(8,128)(2,1)S(1)} %copy-done.33), channel_id=1, source_target_pairs={{0,24},{8,16},{16,8},{24,0},{1,25},{9,17},{17,9},{25,1},{2,26},{10... | collective-permute-start | bytes 737288 | tf_op jit(solution)/shard_map/ppermute | solution.py:147
  65.5 17.8 %copy-start.10 = (bf16[160,768]{1,0:T(8,128)(2,1)}, bf16[160,768]{1,0:T(8,128)(2,1)S(1)}, u32[]{:S(2)}) copy-start(bf16[160,768]{1,0:T(8,128)(2,1)S(1)} %collective-permute-done.3.refs_5_) | copy-start | bytes 737284
  83.3 33.3 %all-to-all-start.2 = ((bf16[8,256,512]{2,1,0:T(8,128)(2,1)}), bf16[8,256,512]{2,1,0:T(8,128)(2,1)S(1)}, u32[]{:S(2)}, u32[]{:S(2)}) async-start(bf16[8,256,512]{2,1,0:T(8,128)(2,1)} %right_back_down.1), calls=%async_computation.2 | async-start | bytes 4194304 | tf_op jit(solution)/shard_map/all_to_all | solution.py:660
  86.9 13.2 %collective-permute-start.6 = (bf16[160,768]{1,0:T(8,128)(2,1)}, bf16[160,768]{1,0:T(8,128)(2,1)S(1)}, u32[]{:S(2)}, u32[]{:S(2)}) collective-permute-start(bf16[160,768]{1,0:T(8,128)(2,1)} %get-tuple-element.88), channel_id=1, source_target_pairs={{0,8},{8,0},{16,24},{24,16},{1,9},{9,1},{17,25},{25,17},{2,10},{10... | collective-permute-start | bytes 737288 | tf_op jit(solution)/shard_map/ppermute | solution.py:147
  88.6 20.5 %collective-permute-start.7 = (bf16[160,768]{1,0:T(8,128)(2,1)}, bf16[160,768]{1,0:T(8,128)(2,1)S(1)}, u32[]{:S(2)}, u32[]{:S(2)}) collective-permute-start(bf16[160,768]{1,0:T(8,128)(2,1)} %get-tuple-element.89), channel_id=1, source_target_pairs={{0,16},{8,24},{16,0},{24,8},{1,17},{9,25},{17,1},{25,9},{2,18},{10... | collective-permute-start | bytes 737288 | tf_op jit(solution)/shard_map/ppermute | solution.py:147
  91.2 17.9 %collective-permute-start.8 = (bf16[160,768]{1,0:T(8,128)(2,1)}, bf16[160,768]{1,0:T(8,128)(2,1)S(1)}, u32[]{:S(2)}, u32[]{:S(2)}) collective-permute-start(bf16[160,768]{1,0:T(8,128)(2,1)} %get-tuple-element.90), channel_id=1, source_target_pairs={{0,24},{8,16},{16,8},{24,0},{1,25},{9,17},{17,9},{25,1},{2,26},{10... | collective-permute-start | bytes 737288 | tf_op jit(solution)/shard_map/ppermute | solution.py:147
  116.6 31.0 %all-to-all-start.3 = ((bf16[8,512,256]{2,1,0:T(8,128)(2,1)}), bf16[8,512,256]{2,1,0:T(8,128)(2,1)}, u32[]{:S(2)}, u32[]{:S(2)}) async-start(bf16[8,512,256]{2,1,0:T(8,128)(2,1)} %get-tuple-element.100), calls=%async_computation.3 | async-start | bytes 4194304 | tf_op jit(solution)/shard_map/all_to_all | solution.py:660
  147.6 31.0 %all-to-all-start.4 = ((bf16[8,512,256]{2,1,0:T(8,128)(2,1)}), bf16[8,512,256]{2,1,0:T(8,128)(2,1)}, u32[]{:S(2)}, u32[]{:S(2)}) async-start(bf16[8,512,256]{2,1,0:T(8,128)(2,1)} %get-tuple-element.101), calls=%async_computation.4 | async-start | bytes 4194304 | tf_op jit(solution)/shard_map/all_to_all | solution.py:660
  178.6 18.9 %all-to-all-start.5 = ((bf16[8,256,256]{2,1,0:T(8,128)(2,1)}), bf16[8,256,256]{2,1,0:T(8,128)(2,1)S(1)}, u32[]{:S(2)}, u32[]{:S(2)}) async-start(bf16[8,256,256]{2,1,0:T(8,128)(2,1)} %get-tuple-element.111), calls=%async_computation.5 | async-start | bytes 2097152 | tf_op jit(solution)/shard_map/all_to_all | solution.py:660
  182.2 42.9 %reduce-scatter.3.cloned.1.call-start = ((), (), s32[]{:S(2)}) async-start(), calls=%async_computation.13 | async-start | bytes 1310720 | tf_op jit(solution)/shard_map/reduce_scatter | solution.py:669
  197.5 30.2 %all-to-all-start.6 = ((bf16[8,256,512]{2,1,0:T(8,128)(2,1)}), bf16[8,256,512]{2,1,0:T(8,128)(2,1)S(1)}, u32[]{:S(2)}, u32[]{:S(2)}) async-start(bf16[8,256,512]{2,1,0:T(8,128)(2,1)} %get-tuple-element.112), calls=%async_computation.6 | async-start | bytes 4194304 | tf_op jit(solution)/shard_map/all_to_all | solution.py:660
  229.0 35.6 %all-to-all-start.7 = ((bf16[8,256,512]{2,1,0:T(8,128)(2,1)}), bf16[8,256,512]{2,1,0:T(8,128)(2,1)S(1)}, u32[]{:S(2)}, u32[]{:S(2)}) async-start(bf16[8,256,512]{2,1,0:T(8,128)(2,1)} %get-tuple-element.114), calls=%async_computation.8 | async-start | bytes 4194304 | tf_op jit(solution)/shard_map/all_to_all | solution.py:660
  238.6 16.4 %collective-permute-start.9 = (bf16[160,768]{1,0:T(8,128)(2,1)}, bf16[160,768]{1,0:T(8,128)(2,1)S(1)}, u32[]{:S(2)}, u32[]{:S(2)}) collective-permute-start(bf16[160,768]{1,0:T(8,128)(2,1)} %get-tuple-element.117), channel_id=1, source_target_pairs={{0,8},{8,0},{16,24},{24,16},{1,9},{9,1},{17,25},{25,17},{2,10},{10... | collective-permute-start | bytes 737288 | tf_op jit(solution)/shard_map/ppermute | solution.py:147
  243.5 20.5 %collective-permute-start.10 = (bf16[160,768]{1,0:T(8,128)(2,1)}, bf16[160,768]{1,0:T(8,128)(2,1)S(1)}, u32[]{:S(2)}, u32[]{:S(2)}) collective-permute-start(bf16[160,768]{1,0:T(8,128)(2,1)} %get-tuple-element.118), channel_id=1, source_target_pairs={{0,16},{8,24},{16,0},{24,8},{1,17},{9,25},{17,1},{25,9},{2,18},{10... | collective-permute-start | bytes 737288 | tf_op jit(solution)/shard_map/ppermute | solution.py:147
  244.6 20.1 %collective-permute-start.11 = (bf16[160,768]{1,0:T(8,128)(2,1)}, bf16[160,768]{1,0:T(8,128)(2,1)}, u32[]{:S(2)}, u32[]{:S(2)}) collective-permute-start(bf16[160,768]{1,0:T(8,128)(2,1)} %get-tuple-element.119), channel_id=1, source_target_pairs={{0,24},{8,16},{16,8},{24,0},{1,25},{9,17},{17,9},{25,1},{2,26},{10... | collective-permute-start | bytes 737288 | tf_op jit(solution)/shard_map/ppermute | solution.py:147
  255.0 26.4 %copy-start.19 = (bf16[160,768]{1,0:T(8,128)(2,1)}, bf16[160,768]{1,0:T(8,128)(2,1)S(1)}, u32[]{:S(2)}) copy-start(bf16[160,768]{1,0:T(8,128)(2,1)S(1)} %collective-permute-done.9.refs_1_) | copy-start | bytes 737284
  264.7 27.7 %all-to-all-start.8 = ((bf16[8,256,256]{2,1,0:T(8,128)(2,1)}), bf16[8,256,256]{2,1,0:T(8,128)(2,1)}, u32[]{:S(2)}, u32[]{:S(2)}) async-start(bf16[8,256,256]{2,1,0:T(8,128)(2,1)} %get-tuple-element.127), calls=%async_computation.9 | async-start | bytes 2097152 | tf_op jit(solution)/shard_map/all_to_all | solution.py:660
  268.9 23.5 %collective-permute-start.12 = (bf16[160,256]{1,0:T(8,128)(2,1)}, bf16[160,256]{1,0:T(8,128)(2,1)S(1)}, u32[]{:S(2)}, u32[]{:S(2)}) collective-permute-start(bf16[160,256]{1,0:T(8,128)(2,1)} %get-tuple-element.121), channel_id=1, source_target_pairs={{0,8},{8,0},{16,24},{24,16},{1,9},{9,1},{17,25},{25,17},{2,10},{10... | collective-permute-start | bytes 245768 | tf_op jit(solution)/shard_map/ppermute | solution.py:147
  273.4 18.9 %collective-permute-start.13 = (bf16[160,256]{1,0:T(8,128)(2,1)}, bf16[160,256]{1,0:T(8,128)(2,1)S(1)}, u32[]{:S(2)}, u32[]{:S(2)}) collective-permute-start(bf16[160,256]{1,0:T(8,128)(2,1)} %get-tuple-element.122), channel_id=1, source_target_pairs={{0,16},{8,24},{16,0},{24,8},{1,17},{9,25},{17,1},{25,9},{2,18},{10... | collective-permute-start | bytes 245768 | tf_op jit(solution)/shard_map/ppermute | solution.py:147
  274.5 17.9 %collective-permute-start.14 = (bf16[160,256]{1,0:T(8,128)(2,1)}, bf16[160,256]{1,0:T(8,128)(2,1)}, u32[]{:S(2)}, u32[]{:S(2)}) collective-permute-start(bf16[160,256]{1,0:T(8,128)(2,1)} %get-tuple-element.123), channel_id=1, source_target_pairs={{0,24},{8,16},{16,8},{24,0},{1,25},{9,17},{17,9},{25,1},{2,26},{10... | collective-permute-start | bytes 245768 | tf_op jit(solution)/shard_map/ppermute | solution.py:147
  298.5 31.2 %all-to-all-start.9 = ((bf16[8,256,512]{2,1,0:T(8,128)(2,1)}), bf16[8,256,512]{2,1,0:T(8,128)(2,1)}, u32[]{:S(2)}, u32[]{:S(2)}) async-start(bf16[8,256,512]{2,1,0:T(8,128)(2,1)} %get-tuple-element.140), calls=%async_computation.10 | async-start | bytes 4194304 | tf_op jit(solution)/shard_map/all_to_all | solution.py:660
  303.0 75.6 %reduce-scatter.5.cloned.1.call-start = ((), (), s32[]{:S(2)}) async-start(), calls=%async_computation.14 | async-start | bytes 1966080 | tf_op jit(solution)/shard_map/reduce_scatter | solution.py:669
  303.3 26.3 %copy-start.6 = (bf16[8,256,512]{2,1,0:T(8,128)(2,1)S(1)}, bf16[8,256,512]{2,1,0:T(8,128)(2,1)}, u32[]{:S(2)}) copy-start(bf16[8,256,512]{2,1,0:T(8,128)(2,1)} %copy-done.5) | copy-start | bytes 6291460
  305.9 10.4 %collective-permute-start.15 = (bf16[160,512]{1,0:T(8,128)(2,1)}, bf16[160,512]{1,0:T(8,128)(2,1)S(1)}, u32[]{:S(2)}, u32[]{:S(2)}) collective-permute-start(bf16[160,512]{1,0:T(8,128)(2,1)} %get-tuple-element.129), channel_id=1, source_target_pairs={{0,8},{8,0},{16,24},{24,16},{1,9},{9,1},{17,25},{25,17},{2,10},{10... | collective-permute-start | bytes 491528 | tf_op jit(solution)/shard_map/ppermute | solution.py:147
  306.9 17.6 %collective-permute-start.16 = (bf16[160,512]{1,0:T(8,128)(2,1)S(1)}, bf16[160,512]{1,0:T(8,128)(2,1)S(1)}, u32[]{:S(2)}, u32[]{:S(2)}) collective-permute-start(bf16[160,512]{1,0:T(8,128)(2,1)S(1)} %copy-done.39), channel_id=1, source_target_pairs={{0,16},{8,24},{16,0},{24,8},{1,17},{9,25},{17,1},{25,9},{2,18},{10... | collective-permute-start | bytes 491528 | tf_op jit(solution)/shard_map/ppermute | solution.py:147
  308.9 17.0 %collective-permute-start.17 = (bf16[160,512]{1,0:T(8,128)(2,1)S(1)}, bf16[160,512]{1,0:T(8,128)(2,1)S(1)}, u32[]{:S(2)}, u32[]{:S(2)}) collective-permute-start(bf16[160,512]{1,0:T(8,128)(2,1)S(1)} %copy-done.38), channel_id=1, source_target_pairs={{0,24},{8,16},{16,8},{24,0},{1,25},{9,17},{17,9},{25,1},{2,26},{10... | collective-permute-start | bytes 491528 | tf_op jit(solution)/shard_map/ppermute | solution.py:147
  316.3 19.4 %copy-start.21 = (bf16[160,512]{1,0:T(8,128)(2,1)}, bf16[160,512]{1,0:T(8,128)(2,1)S(1)}, u32[]{:S(2)}) copy-start(bf16[160,512]{1,0:T(8,128)(2,1)S(1)} %collective-permute-done.15.refs_1_) | copy-start | bytes 491524
  335.7 13.4 %copy-start.36 = (bf16[160,512]{1,0:T(8,128)(2,1)S(1)}, bf16[160,512]{1,0:T(8,128)(2,1)}, u32[]{:S(2)}) copy-start(bf16[160,512]{1,0:T(8,128)(2,1)} %get-tuple-element.134) | copy-start | bytes 491524
  335.7 15.7 %copy-start.35 = (bf16[160,512]{1,0:T(8,128)(2,1)S(1)}, bf16[160,512]{1,0:T(8,128)(2,1)}, u32[]{:S(2)}) copy-start(bf16[160,512]{1,0:T(8,128)(2,1)} %get-tuple-element.135) | copy-start | bytes 491524
  335.7 17.2 %copy-start.42 = (bf16[16,32,128]{2,1,0:T(8,128)(2,1)S(1)}, bf16[16,32,128]{2,1,0:T(8,128)(2,1)}, u32[]{:S(2)}) copy-start(bf16[16,32,128]{2,1,0:T(8,128)(2,1)} %get-tuple-element.145) | copy-start | bytes 393220
  335.7 17.7 %copy-start.41 = (bf16[16,32,128]{2,1,0:T(8,128)(2,1)S(1)}, bf16[16,32,128]{2,1,0:T(8,128)(2,1)}, u32[]{:S(2)}) copy-start(bf16[16,32,128]{2,1,0:T(8,128)(2,1)} %get-tuple-element.146) | copy-start | bytes 393220
  335.7 21.9 %copy-start.40 = (bf16[16,32,128]{2,1,0:T(8,128)(2,1)S(1)}, bf16[16,32,128]{2,1,0:T(8,128)(2,1)}, u32[]{:S(2)}) copy-start(bf16[16,32,128]{2,1,0:T(8,128)(2,1)} %get-tuple-element.147) | copy-start | bytes 393220
  335.8 23.2 %copy-start.9 = (bf16[32,32,128]{2,1,0:T(8,128)(2,1)S(1)}, bf16[32,32,128]{2,1,0:T(8,128)(2,1)}, u32[]{:S(2)}) copy-start(bf16[32,32,128]{2,1,0:T(8,128)(2,1)} %reduce-scatter.3.cloned.1.call-done) | copy-start | bytes 786436
  335.8 44.8 %all-to-all-start.10 = ((bf16[8,256,512]{2,1,0:T(8,128)(2,1)}), bf16[8,256,512]{2,1,0:T(8,128)(2,1)S(1)}, u32[]{:S(2)}, u32[]{:S(2)}) async-start(bf16[8,256,512]{2,1,0:T(8,128)(2,1)} %get-tuple-element.142), calls=%async_computation.11 | async-start | bytes 4194304 | tf_op jit(solution)/shard_map/all_to_all | solution.py:660
  339.5 18.1 %collective-permute-start.18 = (bf16[160,512]{1,0:T(8,128)(2,1)S(1)}, bf16[160,512]{1,0:T(8,128)(2,1)S(1)}, u32[]{:S(2)}, u32[]{:S(2)}) collective-permute-start(bf16[160,512]{1,0:T(8,128)(2,1)S(1)} %copy-done.37), channel_id=1, source_target_pairs={{0,8},{8,0},{16,24},{24,16},{1,9},{9,1},{17,25},{25,17},{2,10},{10... | collective-permute-start | bytes 491528 | tf_op jit(solution)/shard_map/ppermute | solution.py:147
  349.1 20.4 %collective-permute-start.19 = (bf16[160,512]{1,0:T(8,128)(2,1)S(1)}, bf16[160,512]{1,0:T(8,128)(2,1)S(1)}, u32[]{:S(2)}, u32[]{:S(2)}) collective-permute-start(bf16[160,512]{1,0:T(8,128)(2,1)S(1)} %copy-done.36), channel_id=1, source_target_pairs={{0,16},{8,24},{16,0},{24,8},{1,17},{9,25},{17,1},{25,9},{2,18},{10... | collective-permute-start | bytes 491528 | tf_op jit(solution)/shard_map/ppermute | solution.py:147
  351.4 18.1 %collective-permute-start.20 = (bf16[160,512]{1,0:T(8,128)(2,1)S(1)}, bf16[160,512]{1,0:T(8,128)(2,1)S(1)}, u32[]{:S(2)}, u32[]{:S(2)}) collective-permute-start(bf16[160,512]{1,0:T(8,128)(2,1)S(1)} %copy-done.35), channel_id=1, source_target_pairs={{0,24},{8,16},{16,8},{24,0},{1,25},{9,17},{17,9},{25,1},{2,26},{10... | collective-permute-start | bytes 491528 | tf_op jit(solution)/shard_map/ppermute | solution.py:147
  352.9 21.1 %collective-permute-start.21 = (bf16[16,32,128]{2,1,0:T(8,128)(2,1)S(1)}, bf16[16,32,128]{2,1,0:T(8,128)(2,1)S(1)}, u32[]{:S(2)}, u32[]{:S(2)}) collective-permute-start(bf16[16,32,128]{2,1,0:T(8,128)(2,1)S(1)} %copy-done.42), channel_id=1, source_target_pairs={{0,8},{8,0},{16,24},{24,16},{1,9},{9,1},{17,25},{25,17},{2,10},{10... | collective-permute-start | bytes 393224 | tf_op jit(solution)/shard_map/ppermute | solution.py:147
  353.5 22.6 %collective-permute-start.22 = (bf16[16,32,128]{2,1,0:T(8,128)(2,1)S(1)}, bf16[16,32,128]{2,1,0:T(8,128)(2,1)S(1)}, u32[]{:S(2)}, u32[]{:S(2)}) collective-permute-start(bf16[16,32,128]{2,1,0:T(8,128)(2,1)S(1)} %copy-done.41), channel_id=1, source_target_pairs={{0,16},{8,24},{16,0},{24,8},{1,17},{9,25},{17,1},{25,9},{2,18},{10... | collective-permute-start | bytes 393224 | tf_op jit(solution)/shard_map/ppermute | solution.py:147
  357.7 18.4 %collective-permute-start.23 = (bf16[16,32,128]{2,1,0:T(8,128)(2,1)S(1)}, bf16[16,32,128]{2,1,0:T(8,128)(2,1)S(1)}, u32[]{:S(2)}, u32[]{:S(2)}) collective-permute-start(bf16[16,32,128]{2,1,0:T(8,128)(2,1)S(1)} %copy-done.40), channel_id=1, source_target_pairs={{0,24},{8,16},{16,8},{24,0},{1,25},{9,17},{17,9},{25,1},{2,26},{10... | collective-permute-start | bytes 393224 | tf_op jit(solution)/shard_map/ppermute | solution.py:147
  (32 other events, 150.0 us)
Sparse Core Ops, SparseCore 0:
  194.2 30.7 reduce-scatter.2
  306.2 41.9 reduce-scatter.4

commit v3 on v2

--- a/solution.py
+++ b/solution.py
@@ -11,12 +11,12 @@
 F32 = jnp.float32
 BF16 = jnp.bfloat16
 UNROLL = 16
-VMEM_LIMIT = 48 * 1024 * 1024
-
-
-def params(steps=1):
+MIB = 1024 * 1024
+
+
+def params(limit=16):
     return pltpu.CompilerParams(
-        vmem_limit_bytes=VMEM_LIMIT, dimension_semantics=("arbitrary",) * steps
+        vmem_limit_bytes=limit * MIB, dimension_semantics=("arbitrary",)
     )
 
 
@@ -96,7 +96,7 @@
             pltpu.HBM((lanes, tok), BF16),
             pltpu.HBM((tok, lanes), BF16),
         ],
-        compiler_params=params(),
+        compiler_params=params(32),
         name="routing",
     )(own, table)
 
@@ -137,15 +137,23 @@
     )(mix_weights, *in_hbm(earlier, home))
 
 
+def partner(own, k, count):
+    return own ^ k if count & (count - 1) == 0 else lax.rem(own + k, count)
+
+
+def exchange(arrays, axis, count):
+    received = [arrays[0]]
+    for k in range(1, count):
+        if count & (count - 1) == 0:
+            pairs = [(i, i ^ k) for i in range(count)]
+        else:
+            pairs = [(i, (i + k) % count) for i in range(count)]
+        received.append(lax.ppermute(arrays[k], axis, pairs))
+    return received
+
+
 def exchange_rows(slabs, groups):
-    received = [slabs[0]]
-    for k in range(1, groups):
-        if groups & (groups - 1) == 0:
-            pairs = [(i, i ^ k) for i in range(groups)]
-        else:
-            pairs = [(i, (i + k) % groups) for i in range(groups)]
-        received.append(lax.ppermute(slabs[k], "dp", pairs))
-    return received
+    return exchange(slabs, "dp", groups)
 
 
 def unsort_kernel(groups, home_ref, *refs):
@@ -154,7 +162,7 @@
     out_ref[...] = dot(rows, home_ref[...], TN).astype(BF16)
 
 
-def unsort(slabs, home, piece, step, feats, partial):
+def unsort(slabs, piece, home, step, feats, partial):
     lanes, slots = home.shape
     cap = slabs[0].shape[0]
     groups = len(slabs)
@@ -299,114 +307,131 @@
         scratch_shapes=[scratch_for(plan, step)],
         compiler_params=params(),
         name=name,
-    )(arrived, *in_hbm(factor))
+    )(arrived, factor)
 
 
 def cut_rows(own, array, out_refs):
     groups = len(out_refs)
     size = array.shape[1] // groups
     for k, ref in enumerate(out_refs):
-        if groups & (groups - 1) == 0:
-            target = own ^ k
-        else:
-            target = lax.rem(own + k, groups)
+        target = partner(own, k, groups)
         ref[...] = array[:, pl.ds(pl.multiple_of(target * size, size), size), :].astype(BF16)
 
 
-def sum_rows_kernel(*refs):
-    total = refs[0][...].astype(F32)
-    for ref in refs[1:-1]:
-        total = total + ref[...].astype(F32)
-    refs[-1][...] = total
-
-
-def sum_rows(pieces):
-    shape = pieces[0].shape
-    return pl.pallas_call(
-        sum_rows_kernel,
+def split_rows(own, array, keep_ref, send_ref):
+    groups = 2 * keep_ref.shape[0]
+    size = array.shape[1] // groups
+    for k in range(groups):
+        start = pl.multiple_of((own ^ k) * size, size)
+        ref = send_ref if k % 2 else keep_ref
+        ref[k // 2] = array[:, pl.ds(start, size), :].astype(BF16)
+
+
+def split_shapes(blocks, factor, groups):
+    shape = (groups // 2, blocks, factor.shape[1] // groups, factor.shape[2])
+    return [pltpu.HBM(shape, BF16)] * 2
+
+
+def halve_kernel(count, *refs):
+    for at in range(count):
+        total = refs[2 * at][...].astype(F32) + refs[2 * at + 1][...].astype(F32)
+        outs = refs[2 * (count + at) : 2 * (count + at) + 2]
+        for k in range(total.shape[0]):
+            ref = outs[k % 2]
+            ref[k // 2] = total[k].astype(ref.dtype)
+
+
+def halve(pairs, name):
+    shapes = []
+    for keep, _ in pairs:
+        shape = (keep.shape[0] // 2,) + keep.shape[1:]
+        shapes += [pltpu.HBM(shape, F32), pltpu.HBM(shape, BF16)]
+    arrays = [array for pair in pairs for array in pair]
+    outs = pl.pallas_call(
+        functools.partial(halve_kernel, len(pairs)),
+        grid=(1,),
+        in_specs=[whole(array) for array in arrays],
+        out_specs=[whole(shape) for shape in shapes],
+        out_shape=shapes,
+        compiler_params=params(),
+        name=name,
+    )(*in_hbm(*arrays))
+    return [(outs[2 * at], outs[2 * at + 1]) for at in range(len(pairs))]
+
+
+def swap_rows(array, bit, groups):
+    return lax.ppermute(array, "dp", [(i, i ^ bit) for i in range(groups)])
+
+
+def finish(pairs, groups, name):
+    bit = 2
+    while bit < groups:
+        split = halve(pairs, f"{name}_{bit}")
+        pairs = [(keep, swap_rows(send, bit, groups)) for keep, send in split]
+        bit *= 2
+    return [[array[0] for array in pair] for pair in pairs]
+
+
+def sum_kernel(counts, *refs):
+    in_refs, out_refs = refs[: sum(counts)], refs[sum(counts) :]
+    at = 0
+    done = [0] * len(out_refs)
+    for count in counts:
+        total = in_refs[at][...].astype(F32)
+        for ref in in_refs[at + 1 : at + count]:
+            total = total + ref[...].astype(F32)
+        at += count
+        size = total.shape[0] // len(out_refs)
+        for part, ref in enumerate(out_refs):
+            ref[done[part] : done[part] + size] = total[part * size : (part + 1) * size]
+            done[part] += size
+
+
+def sums_of(sets, parts, name):
+    pieces = [piece for pieces in sets for piece in pieces]
+    size = sum(pieces[0].shape[0] for pieces in sets) // parts
+    out = pltpu.HBM((size,) + pieces[0].shape[1:], F32)
+    return pl.pallas_call(
+        functools.partial(sum_kernel, [len(pieces) for pieces in sets]),
         grid=(1,),
         in_specs=[whole(piece) for piece in pieces],
-        out_specs=whole(pieces[0]),
-        out_shape=pltpu.HBM(shape, F32),
+        out_specs=[whole(out)] * parts,
+        out_shape=[out] * parts,
         compiler_params=params(),
-        name="sum_rows",
+        name=name,
     )(*in_hbm(*pieces))
 
 
-def product_and_cut_kernel(plan, scale, own_ref, in_ref, other_ref, factor_ref, out_ref, *refs):
-    out_refs, (sums, scratch) = refs[:-2], refs[-2:]
+def grad_kernel(plan, scale, own_ref, in_ref, other_ref, *refs):
+    *out_refs, sums = refs
 
     def one(b):
-        values = plan.block(in_ref, 0, b)
-        others = plan.block(other_ref, 0, b)
-        plan.put(scratch, b, dot(factor_ref[b], values, TN))
-        sums[b] = dot(values, others, NT) * scale
+        sums[b] = dot(plan.block(in_ref, 0, b), plan.block(other_ref, 0, b), NT) * scale
 
     plan.each_block(UNROLL, one)
-    plan.store(out_ref, 0, scratch)
-    cut_rows(own_ref[0], sums, out_refs)
-
-
-def product_and_cut(plan, arrived, other, factor, scale, own, groups, name):
-    step = plan.tok
-    held, width, columns = factor.shape
-    cut = pltpu.HBM((held, width // groups, columns), BF16)
-    outs = pl.pallas_call(
-        functools.partial(product_and_cut_kernel, plan, scale),
+    split_rows(own_ref[0], sums, *out_refs)
+
+
+def cut_shape(blocks, factor, groups):
+    return pltpu.HBM((blocks, factor.shape[1] // groups, factor.shape[2]), BF16)
+
+
+def factor_grad(plan, own, arrived, other, factor, scale, groups, name):
+    outs = split_shapes(plan.held, factor, groups)
+    return pl.pallas_call(
+        functools.partial(grad_kernel, plan, scale),
         grid=(1,),
         in_specs=[
             pl.BlockSpec(memory_space=pltpu.SMEM),
-            plan.arrived_spec(1, step),
-            plan.arrived_spec(1, step),
-            whole(factor),
+            plan.arrived_spec(1, plan.tok),
+            plan.arrived_spec(1, plan.tok),
         ],
-        out_specs=[plan.sent_spec(1, step)] + [whole(cut)] * groups,
-        out_shape=[plan.sent_shape(1)] + [cut] * groups,
-        scratch_shapes=[pltpu.VMEM(factor.shape, F32), scratch_for(plan, step)],
+        out_specs=[whole(out) for out in outs],
+        out_shape=outs,
+        scratch_shapes=[pltpu.VMEM(factor.shape, F32)],
         compiler_params=params(),
         name=name,
-    )(own, arrived, other, *in_hbm(factor))
-    return outs[0], outs[1:]
-
-
-def product_and_grad_kernel(plan, scale, first, last, in_ref, other_ref, factor_ref, *refs):
-    if not first:
-        before_ref, refs = refs[0], refs[2:]
-    out_ref, sums_ref, scratch = refs
-
-    def one(b):
-        values = plan.block(in_ref, 0, b)
-        others = plan.block(other_ref, 0, b)
-        plan.put(scratch, b, dot(factor_ref[b], values, TN))
-        total = dot(values, others, NT)
-        if not first:
-            total = total + before_ref[b]
-        sums_ref[b] = (total * scale).astype(BF16) if last else total
-
-    plan.each_block(UNROLL, one)
-    plan.store(out_ref, 0, scratch)
-
-
-def product_and_grad(plan, full, arrived, other, factor, scale, half, halves, before, name):
-    step = plan.tok
-    first, last = half == 0, half == halves - 1
-    sums = pltpu.HBM(factor.shape, BF16 if last else F32)
-    return pl.pallas_call(
-        functools.partial(product_and_grad_kernel, plan, scale, first, last),
-        grid=(1,),
-        in_specs=[
-            plan.arrived_spec(1, step, half if arrived.shape[2] > step else 0),
-            full.arrived_spec(1, step, half),
-            whole(factor),
-        ]
-        + ([] if first else [whole(sums), pl.BlockSpec(memory_space=pl.ANY)]),
-        out_specs=[full.sent_spec(1, step, half), whole(sums)],
-        out_shape=[full.sent_shape(1), sums],
-        input_output_aliases={} if first else {4: 0},
-        scratch_shapes=[scratch_for(plan, step)],
-        compiler_params=params(),
-        name=f"{name}_{half}",
-    )(arrived, other, *in_hbm(factor, *before))
+    )(own, arrived, other)
 
 
 def first_kernel(plan, groups, count, *refs):
@@ -450,7 +475,7 @@
         ],
         out_shape=[pltpu.HBM((plan.tok, feats), BF16), sent],
         scratch_shapes=[scratch_for(plan, plan.tok)] * 2,
-        compiler_params=params(),
+        compiler_params=params(32),
         name=f"first_products_{half}",
     )(*in_hbm(*slabs, back_t, right_gate, right_up))
 
@@ -467,15 +492,13 @@
     return x * half, slope
 
 
-def middle_kernel(plan, scale, first, last, spread_ref, hidden_grad_ref, gate_ref, up_ref, *refs):
+def middle_kernel(
+    plan, scale, first, last, own_ref, spread_ref, hidden_grad_ref, gate_ref, up_ref, *refs
+):
     if not first:
-        before_ref, refs = refs[0], refs[3:]
-    hidden_ref, low_ref, high_ref, sums_ref, hiddens, gates, ups = refs
-
-    def add_sum(at, value):
-        if not first:
-            value = value + before_ref[at]
-        sums_ref[at] = (value * scale).astype(BF16) if last else value
+        before_ref, refs = refs[0], refs[4:]
+    hidden_ref, low_ref, high_ref = refs[:3]
+    out_refs, (sums, hiddens, gates, ups) = refs[3:-4], refs[-4:]
 
     def one(b):
         gate_in = plan.block(spread_ref, 0, b)
@@ -489,39 +512,55 @@
         up_back = (back * active).astype(BF16)
         plan.put(gates, b, dot(gate_ref[b], gate_back, NN))
         plan.put(ups, b, dot(up_ref[b], up_back, NN))
-        add_sum(b, dot(gate_in, gate_back, NT))
-        add_sum(plan.held + b, dot(up_in, up_back, NT))
+        for at, values, grads in (b, gate_in, gate_back), (plan.held + b, up_in, up_back):
+            total = dot(values, grads, NT)
+            if not first:
+                total = total + before_ref[at]
+            if last:
+                sums[at] = total * scale
+            else:
+                out_refs[0][at] = total
 
     plan.each_block(UNROLL, one)
     plan.store(hidden_ref, 0, hiddens)
     for part, scratch in enumerate((gates, ups)):
         plan.store_range(low_ref, part, scratch, 0)
         plan.store_range(high_ref, part, scratch, 1)
-
-
-def middle(plan, full, spreads, hidden_grad, left_gate, left_up, scale, half, halves, before):
+    if last:
+        cut_rows(own_ref[0], sums, out_refs)
+
+
+def middle(
+    plan, full, own, spreads, hidden_grad, left_gate, left_up, scale, groups, half, halves, before
+):
     step = plan.tok
     first, last = half == 0, half == halves - 1
-    sums = pltpu.HBM((2 * plan.held,) + left_gate.shape[1:], BF16 if last else F32)
-    sums_spec = whole(sums)
+    sums_shape = (2 * plan.held,) + left_gate.shape[1:]
+    if last:
+        sums = [cut_shape(2 * plan.held, left_gate, groups)] * groups
+    else:
+        sums = [pltpu.HBM(sums_shape, F32)]
     kept = pl.BlockSpec(memory_space=pl.ANY)
-    return pl.pallas_call(
+    here = full.sent_spec(1, step, half)
+    outs = pl.pallas_call(
         functools.partial(middle_kernel, plan, scale, first, last),
         grid=(1,),
         in_specs=[
+            pl.BlockSpec(memory_space=pltpu.SMEM),
             plan.arrived_spec(2, step),
             full.arrived_spec(1, step, half),
             whole(left_gate),
             whole(left_up),
         ]
-        + ([] if first else [sums_spec, kept, kept]),
-        out_specs=[plan.sent_spec(1, step)] + [full.sent_spec(1, step, half)] * 2 + [sums_spec],
-        out_shape=[plan.sent_shape(1), full.sent_shape(1), full.sent_shape(1), sums],
-        input_output_aliases={} if first else {5: 1, 6: 2},
-        scratch_shapes=[scratch_for(plan, step)] * 3,
-        compiler_params=params(),
+        + ([] if first else [pl.BlockSpec(sums_shape, lambda t: (0, 0, 0)), kept, kept, kept]),
+        out_specs=[here] * 3 + [whole(out) for out in sums],
+        out_shape=[full.sent_shape(1)] * 3 + sums,
+        input_output_aliases={} if first else {6: 0, 7: 1, 8: 2},
+        scratch_shapes=[pltpu.VMEM(sums_shape, F32)] + [scratch_for(plan, step)] * 3,
+        compiler_params=params(40),
         name=f"middle_{half}",
-    )(spreads, hidden_grad, *in_hbm(left_gate, left_up, *before))
+    )(own, spreads, hidden_grad, *in_hbm(left_gate, left_up, *before))
+    return outs[:3], outs[3:]
 
 
 def spread_blocks(plan, in_ref, at):
@@ -572,38 +611,38 @@
         in_specs=[arrived_spec, whole(back), factor_spec, factor_spec],
         out_specs=[pl.BlockSpec((cap, size), lambda i: (0, i))] * groups,
         out_shape=[pltpu.HBM((cap, size * count), BF16)] * groups,
-        compiler_params=params(),
+        compiler_params=params(32),
         name=f"last_products_{start}",
     )(arrived, *in_hbm(back, right_gate, right_up))
 
 
-def right_grads_kernel(plan, scale, halves, in_ref, *refs):
-    packed_refs, grads_ref = refs[:halves], refs[-1]
-    for at in range(grads_ref.shape[1]):
+def right_grads_kernel(plan, scale, halves, own_ref, in_ref, *refs):
+    packed_refs, out_refs, sums = refs[:halves], refs[halves:-1], refs[-1]
+    count = sums.shape[0] // 2
+    for at in range(count):
         columns = slice(at * plan.width, (at + 1) * plan.width)
         values = jnp.concatenate([ref[:, columns] for ref in packed_refs], axis=0)
         for part, spread in enumerate(spread_blocks(plan, in_ref, at)):
-            grads_ref[part, at] = (dot(values, spread, ((0,), (1,))) * scale).astype(BF16)
-
-
-def right_grads(plan, arrived, packed, factor, scale, unit, which, before):
-    arrived, arrived_spec = spread_form(plan, arrived, unit, 0)
-    block = factor.shape[1:]
-    count = plan.held // 2 // unit
-    start = which * count
+            sums[part * count + at] = dot(values, spread, ((0,), (1,))) * scale
+    split_rows(own_ref[0], sums, *out_refs)
+
+
+def right_grads(plan, own, arrived, packed, factor, scale, groups, which):
+    count = plan.held // 2
+    arrived, arrived_spec = spread_form(plan, arrived, count, 0)
     rows = packed[0].shape[0]
+    outs = split_shapes(2 * count, factor, groups)
     return pl.pallas_call(
         functools.partial(right_grads_kernel, plan, scale, len(packed)),
-        grid=(count,),
-        in_specs=[arrived_spec]
-        + [pl.BlockSpec((rows, unit * plan.width), lambda i: (0, start + i))] * len(packed)
-        + [pl.BlockSpec(memory_space=pl.ANY)] * len(before),
-        out_specs=pl.BlockSpec((2, unit) + block, lambda i: (0, start + i, 0, 0)),
-        out_shape=pltpu.HBM((2,) + factor.shape, BF16),
-        input_output_aliases={1 + len(packed): 0} if before else {},
-        compiler_params=params(),
+        grid=(1,),
+        in_specs=[pl.BlockSpec(memory_space=pltpu.SMEM), arrived_spec]
+        + [pl.BlockSpec((rows, count * plan.width), lambda i: (0, which))] * len(packed),
+        out_specs=[whole(out) for out in outs],
+        out_shape=outs,
+        scratch_shapes=[pltpu.VMEM((2 * count,) + factor.shape[1:], F32)],
+        compiler_params=params(32),
         name=f"right_grads_{which}",
-    )(arrived, *in_hbm(*packed, *before))
+    )(own, arrived, *in_hbm(*packed))
 
 
 def natural_kernel(in_ref, out_ref):
@@ -665,12 +704,6 @@
     def after(array, *others):
         return lax.optimization_barrier((array, *others))[0]
 
-    def total(grads):
-        return lax.psum_scatter(grads, "dp", scatter_dimension=1, tiled=True)
-
-    def exchanged_total(pieces):
-        return sum_rows(exchange_rows(pieces, groups))
-
     own = lax.axis_index("dp").reshape(1)
     home, back, back_t = routing(destinations, own, groups, tok, cap)
     sent = [mix_and_sort(earlier, mix_weights, home, groups, p, step) for p in there]
@@ -693,62 +726,65 @@
         arrived.append(part.arranged(moved))
     if halves > 1:
         arrived[0] = after(arrived[0], spreads[1])
-    hidden, before = [], ()
+    before = ()
     for h in range(halves):
         if h:
-            arrived[h] = after(arrived[h], hidden[0])
-        sent_hidden, low, high, left_sums = middle(
-            part, plan, arrived[h], hidden_grad, left_gate, left_up, scale, h, halves, before
+            arrived[h] = after(arrived[h], before[0])
+        (hidden, low, high), left_sums = middle(
+            part, plan, own, arrived[h], hidden_grad, left_gate, left_up, scale, groups, h, halves,
+            before,
         )
-        hidden.append(sent_hidden)
-        before = (left_sums, low, high)
-    if halves > 1:
-        hidden[0] = moved = move(after(hidden[0], moved))
-    low = move(after(low, moved))
-    left_sums = total(left_sums)
-    high = move(after(high, low, left_sums))
+        before = (left_sums[0], hidden, low, high)
+    low = move(low)
+    left_sums = exchange_rows(left_sums, groups)
+    high = move(after(high, low, *left_sums))
+    grad_left_gate, grad_left_up = sums_of([left_sums], 2, "sum_left")
     half = held // 2
-    back_pieces, unit = pieces_of(
-        half * 3 // 4, half - half * 3 // 4, half // 2, half - half // 2
-    )
+    most = max(half * 5 // 8, 1)
+    back_pieces, unit = pieces_of(most, half - most, half - most, most)
     step = unit * width
     factors = (back, right_gate, right_up, groups)
     sent = [last_products(plan, low, *factors, p, unit) for p in back_pieces[:2]]
     rows = [exchange_rows(slabs, groups) for slabs in sent]
-    right_sums = right_grads(
-        plan, after(low, sent), packed, right_gate, scale, unit, 0, ()
-    )
-    hidden[-1] = move(after(hidden[-1], high, rows[0], sent[1], right_sums))
+    right_low = right_grads(plan, own, after(low, sent), packed, right_gate, scale, groups, 0)
+    hidden = swap(after(hidden, high, rows[0], sent[1], right_low, grad_left_gate))
     sent = [last_products(plan, high, *factors, p, unit) for p in back_pieces[2:]]
     rows += [exchange_rows(slabs, groups) for slabs in sent]
-    right_sums = right_grads(
-        plan, after(high, sent), packed, right_gate, scale, unit, 1, (right_sums,)
-    )
-    before = ()
-    for h in range(halves):
-        arrived = hidden[h]
-        if h == halves - 1:
-            arrived = after(arrived, rows[1], right_sums, *sent)
-        down_spread, down_sums = product_and_grad(
-            part, plan, part.arranged(arrived), down_spread_grad, right_down, scale, h, halves,
-            before, "right_down",
-        )
-        before = (down_sums, down_spread)
-    grad_right_down = down_sums
-    down_spread = after(swap(down_spread), rows[2])
-    result, grad_left_down = product_and_cut(
-        plan, down_spread, out_grads, left_down, scale, own, groups, "left_down"
-    )
-    right_sums = right_sums.reshape((2 * held,) + right_gate.shape[1:])
-    right_sums = total(jnp.concatenate((right_sums, grad_right_down))).astype(F32)
-    grad_right_gate, grad_right_up, grad_right_down = jnp.split(right_sums, 3)
-    grad_left_gate, grad_left_up = jnp.split(left_sums.astype(F32), 2)
-    grad_left_down = exchanged_total(grad_left_down)
-    mixed_grad = None
-    for slabs, piece in zip(rows, back_pieces):
-        mixed_grad = unsort(slabs, home, piece, step, feats, mixed_grad)
+    right_high = right_grads(
+        plan, own, after(high, sent), packed, right_gate, scale, groups, 1
+    )
+    places = (home, step, feats)
+    mixed_grad = unsort(rows[0], back_pieces[0], *places, None)
+    right_low = [(right_low[0], swap_rows(right_low[1], 1, groups))]
+    hidden = after(hidden, rows[1], rows[2], sent[1], right_high, mixed_grad, right_low)
+    down_spread = product(plan, hidden, right_down, TN, "right_down")
+    down_grad = factor_grad(
+        plan, own, after(hidden, down_spread), down_spread_grad, right_down, scale, groups,
+        "right_down_grad",
+    )
+    down_spread = swap(down_spread)
+    mixed_grad = unsort(rows[1], back_pieces[1], *places, mixed_grad)
+    mixed_grad = unsort(rows[2], back_pieces[2], *places, mixed_grad)
+    right_low = finish(right_low, groups, "halve_right_low")
+    right_high = (right_high[0], swap_rows(right_high[1], 1, groups))
+    down_grad = (down_grad[0], swap_rows(down_grad[1], 1, groups))
+    down_spread = after(
+        down_spread, rows[3], right_low, right_high[1], down_grad[1], mixed_grad
+    )
+    result = product(plan, down_spread, left_down, TN, "left_down")
+    left_down_grad = factor_grad(
+        plan, own, after(down_spread, result), out_grads, left_down, scale, groups,
+        "left_down_grad",
+    )
     output = natural_order(plan, move(result))
-
+    mixed_grad = unsort(rows[3], back_pieces[3], *places, mixed_grad)
+    left_down_grad = [(left_down_grad[0], swap_rows(left_down_grad[1], 1, groups))]
+    right_high, down_grad = finish([right_high, down_grad], groups, "halve_right")
+    left_down_grad = finish(left_down_grad, groups, "halve_left_down")[0]
+    grad_right_gate, grad_right_up = sums_of([right_low[0], right_high], 2, "sum_right")
+    (grad_right_down,) = sums_of([down_grad], 1, "sum_right_down")
+    left_down_grad = after(left_down_grad, output, mixed_grad, grad_right_gate, grad_right_down)
+    (grad_left_down,) = sums_of([left_down_grad], 1, "sum_left_down")
     return (
         output,
         mixed_grad,

time: 393 us -> 378 us (0.962)
  Pallas kernels: 119 us -> 136 us
  between operations: 14.4 us -> 0.9 us
  waiting for transfers between devices: 147 us -> 136 us
    reduce_scatter x2 -> x0, waiting for transfers between devices: 23.9 us -> none  [total(): return lax.psum_scatter(grads, 'dp', scatter_dimension=1, tiled=True)]
    ppermute x24 -> x32, waiting for transfers between devices: 69.7 us -> 93.4 us  [the longest x24 82.2 us: exchange(): received.append(lax.ppermute(arrays[k], axis, pairs))]
    all_to_all x11 -> x10, waiting for transfers between devices: 53.1 us -> 42.4 us  [move(): lax.all_to_all(array, 'feat', split_axis=0, concat_axis=0, tiled=True)]
    pallas_call x2 -> x4, Pallas kernels: 9.12 us -> 15.3 us  [product(): pl.pallas_call(functools.partial(product_kernel, plan, over), grid=(plan....]
    pallas_call x4 -> x9, Pallas kernels: 16.2 us -> 19.4 us  [the longest x4 7.41 us: sums_of(): pl.pallas_call(functools.partial(sum_kernel, [len(pieces) for pieces in s...]
    all_to_all x11 -> x10, starting transfers between devices: 44.8 us -> 42.6 us  [move(): lax.all_to_all(array, 'feat', split_axis=0, concat_axis=0, tiled=True)]
    unnamed x86 -> x84, local copies, waits for them, and re-layouts: 9.72 us -> 10.5 us
    ppermute x24 -> x32, starting transfers between devices: 49.7 us -> 49.3 us  [the longest x24 38.5 us: exchange(): received.append(lax.ppermute(arrays[k], axis, pairs))]
  transfers between devices with their start and end apart: 37 -> 42, of which waited for: 20 -> 18; matrix products, arithmetic and copies ran while one was open for 1% -> 0% of each run, Pallas kernels for 25% -> 27%
where the time goes in v3:
time: 378 us; the launch traced here: 375 us
  Pallas kernels  136 us (36%)
  waiting for transfers between devices  136 us (36%)
  starting transfers between devices  92 us (24%)
  local copies, waits for them, and re-layouts  10.5 us (3%)
    ppermute x24, waiting for transfers between devices, exchange(): received.append(lax.ppermute(arrays[k], axis, pairs))  82.2 us
    all_to_all x10, starting transfers between devices, move(): lax.all_to_all(array, 'feat', split_axis=0, concat_axis=0, tiled=True)  42.6 us
    all_to_all x10, waiting for transfers between devices, move(): lax.all_to_all(array, 'feat', split_axis=0, concat_axis=0, tiled=True)  42.4 us
    ppermute x24, starting transfers between devices, exchange(): received.append(lax.ppermute(arrays[k], axis, pairs))  38.5 us
    pallas_call x2, Pallas kernels, middle(): pl.pallas_call(functools.partial(middle_kernel, plan, scale, first, last)...  22.9 us
    pallas_call x4, Pallas kernels, last_products(): pl.pallas_call(functools.partial(last_kernel, plan), grid=(count,), in_sp...  17.4 us
    pallas_call x4, Pallas kernels, unsort(): pl.pallas_call(functools.partial(unsort_kernel, groups), grid=(count,), i...  16.7 us
    pallas_call x4, Pallas kernels, product(): pl.pallas_call(functools.partial(product_kernel, plan, over), grid=(plan....  15.3 us
  transfers between devices with their start and end apart: 42, of which 18 were waited for; matrix products, arithmetic and copies ran while one was open for 0% of the time, Pallas kernels for 27%

profile of v3, /device:TPU:0, one launch (start us, length us, event | category | flops | bytes accessed | tf_op | source)
XLA Modules:
  0.0 375.5 jit_solution(3390031656409245095)
XLA Ops:
  0.6 4.7 %send_cotangent.1 = bf16[8,256,512]{2,1,0:T(8,128)(2,1)} custom-call(bf16[2048,512]{1,0:T(8,128)(2,1)} %in_ref.1), custom_call_target="tpu_custom_call" | custom-call | tf_op jit(solution)/shard_map/send_cotangent/pallas_call | solution.py:279
  5.3 5.3 %all-to-all-start = ((bf16[8,256,512]{2,1,0:T(8,128)(2,1)}), bf16[8,256,512]{2,1,0:T(8,128)(2,1)S(1)}, u32[]{:S(2)}, u32[]{:S(2)}) async-start(bf16[8,256,512]{2,1,0:T(8,128)(2,1)} %send_cotangent.1), calls=%async_computation | async-start | bytes 4194304 | tf_op jit(solution)/shard_map/all_to_all | solution.py:699
  21.4 4.4 %mix_and_sort_5.1 = (bf16[160,768]{1,0:T(8,128)(2,1)}, bf16[160,768]{1,0:T(8,128)(2,1)}, bf16[160,768]{1,0:T(8,128)(2,1)}, bf16[160,768]{1,0:T(8,128)(2,1)}) custom-call(f32[3]{0:T(128)S(1)} %copy-done.9, bf16[3,2048,640]{2,1,0:T(8,128)(2,1)} %earlier_ref.5, bf16[640,640]{1,0:T(8,128)(2,1)} %get-tuple-element.94.home_ref), custom_call_target="tpu_custom_call" | custom-call | tf_op jit(solution)/shard_map/mix_and_sort_5/pallas_call | solution.py:125
  25.8 4.5 %mix_and_sort_2.1 = (bf16[160,768]{1,0:T(8,128)(2,1)}, bf16[160,768]{1,0:T(8,128)(2,1)}, bf16[160,768]{1,0:T(8,128)(2,1)}, bf16[160,768]{1,0:T(8,128)(2,1)}) custom-call(f32[3]{0:T(128)S(1)} %copy-done.9, bf16[3,2048,640]{2,1,0:T(8,128)(2,1)} %earlier_ref.5, bf16[640,640]{1,0:T(8,128)(2,1)} %get-tuple-element.94.home_ref), custom_call_target="tpu_custom_call" | custom-call | tf_op jit(solution)/shard_map/mix_and_sort_2/pallas_call | solution.py:125
  30.3 3.4 collective-permute-done.1.refs_2_
  33.8 3.5 all-to-all-done.in_ref.other_ref
  40.5 3.7 all-to-all-start.1
  48.7 8.8 %collective-permute-done.3.refs_5_ = bf16[160,768]{1,0:T(8,128)(2,1)S(1)} collective-permute-done((bf16[160,768]{1,0:T(8,128)(2,1)}, bf16[160,768]{1,0:T(8,128)(2,1)S(1)}, u32[]{:S(2)}, u32[]{:S(2)}) %collective-permute-start.3) | collective-permute-done | bytes 245792 | tf_op jit(solution)/shard_map/ppermute | solution.py:151
  57.5 8.9 %collective-permute-done.4.refs_6_ = bf16[160,768]{1,0:T(8,128)(2,1)S(1)} collective-permute-done((bf16[160,768]{1,0:T(8,128)(2,1)}, bf16[160,768]{1,0:T(8,128)(2,1)S(1)}, u32[]{:S(2)}, u32[]{:S(2)}) %collective-permute-start.4) | collective-permute-done | bytes 245792 | tf_op jit(solution)/shard_map/ppermute | solution.py:151
  67.1 3.7 all-to-all-done.1.in_ref.other_ref
  74.0 3.6 all-to-all-start.2
  82.1 8.8 %collective-permute-done.6.refs_9_ = bf16[160,768]{1,0:T(8,128)(2,1)S(1)} collective-permute-done((bf16[160,768]{1,0:T(8,128)(2,1)}, bf16[160,768]{1,0:T(8,128)(2,1)S(1)}, u32[]{:S(2)}, u32[]{:S(2)}) %collective-permute-start.6) | collective-permute-done | bytes 245792 | tf_op jit(solution)/shard_map/ppermute | solution.py:151
  90.9 8.9 %collective-permute-done.7.refs_10_ = bf16[160,768]{1,0:T(8,128)(2,1)S(1)} collective-permute-done((bf16[160,768]{1,0:T(8,128)(2,1)}, bf16[160,768]{1,0:T(8,128)(2,1)S(1)}, u32[]{:S(2)}, u32[]{:S(2)}) %collective-permute-start.7) | collective-permute-done | bytes 245792 | tf_op jit(solution)/shard_map/ppermute | solution.py:151
  100.6 6.7 %first_products_0.1 = (bf16[256,2048]{1,0:T(8,128)(2,1)}, bf16[8,512,256]{2,1,0:T(8,128)(2,1)}) custom-call(bf16[160,512]{1,0:T(8,128)(2,1)} %get-tuple-element.95.refs_0_, bf16[160,512]{1,0:T(8,128)(2,1)} %copy-done.15, bf16[160,512]{1,0:T(8,128)(2,1)} %copy-done.16, bf16[160,512]{1,0:T(8,128)(2,1)} %copy-done.17, ...), custom_call_target="tpu_custom_call" | custom-call | tf_op jit(solution)/shard_map/first_products_0/pallas_call | solution.py:463
  107.3 4.6 %all-to-all-start.3 = ((bf16[8,512,256]{2,1,0:T(8,128)(2,1)}), bf16[8,512,256]{2,1,0:T(8,128)(2,1)}, u32[]{:S(2)}, u32[]{:S(2)}) async-start(bf16[8,512,256]{2,1,0:T(8,128)(2,1)} %get-tuple-element.116), calls=%async_computation.3 | async-start | bytes 4194304 | tf_op jit(solution)/shard_map/all_to_all | solution.py:699
  111.9 6.7 %first_products_1.1 = (bf16[256,2048]{1,0:T(8,128)(2,1)}, bf16[8,512,256]{2,1,0:T(8,128)(2,1)}) custom-call(bf16[160,512]{1,0:T(8,128)(2,1)} %get-tuple-element.95.refs_0_, bf16[160,512]{1,0:T(8,128)(2,1)} %copy-done.15, bf16[160,512]{1,0:T(8,128)(2,1)} %copy-done.16, bf16[160,512]{1,0:T(8,128)(2,1)} %copy-done.17, ...), custom_call_target="tpu_custom_call" | custom-call | tf_op jit(solution)/shard_map/first_products_1/pallas_call | solution.py:463
  118.6 19.7 %all-to-all-done.3.spread_ref = bf16[8,512,256]{2,1,0:T(8,128)(2,1)} async-done(((bf16[8,512,256]{2,1,0:T(8,128)(2,1)}), bf16[8,512,256]{2,1,0:T(8,128)(2,1)}, u32[]{:S(2)}, u32[]{:S(2)}) %all-to-all-start.3) | async-done | bytes 2097184 | tf_op jit(solution)/shard_map/all_to_all | solution.py:699
  138.4 4.4 %all-to-all-start.4 = ((bf16[8,512,256]{2,1,0:T(8,128)(2,1)}), bf16[8,512,256]{2,1,0:T(8,128)(2,1)}, u32[]{:S(2)}, u32[]{:S(2)}) async-start(bf16[8,512,256]{2,1,0:T(8,128)(2,1)} %get-tuple-element.117), calls=%async_computation.4 | async-start | bytes 4194304 | tf_op jit(solution)/shard_map/all_to_all | solution.py:699
  142.8 11.2 %middle_0.1 = (bf16[8,256,512]{2,1,0:T(8,128)(2,1)}, bf16[8,256,512]{2,1,0:T(8,128)(2,1)}, bf16[8,256,512]{2,1,0:T(8,128)(2,1)}, f32[32,128,128]{2,1,0:T(8,128)}) custom-call(s32[1]{0:T(128)} %bitcast.own_ref, bf16[8,512,256]{2,1,0:T(8,128)(2,1)} %all-to-all-done.3.spread_ref, bf16[8,256,512]{2,1,0:T(8,128)(2,1)S(1)} %all-to-all-done.2.hidden_grad_ref, ...), custom_call_target="tpu_custom_call" | custom-call | tf_op jit(solution)/shard_map/middle_0/pallas_call | solution.py:545
  154.0 15.4 %all-to-all-done.4.spread_ref = bf16[8,512,256]{2,1,0:T(8,128)(2,1)} async-done(((bf16[8,512,256]{2,1,0:T(8,128)(2,1)}), bf16[8,512,256]{2,1,0:T(8,128)(2,1)}, u32[]{:S(2)}, u32[]{:S(2)}) %all-to-all-start.4) | async-done | bytes 2097184 | tf_op jit(solution)/shard_map/all_to_all | solution.py:699
  169.4 11.6 %middle_1.1 = (bf16[8,256,512]{2,1,0:T(8,128)(2,1)}, bf16[8,256,512]{2,1,0:T(8,128)(2,1)}, bf16[8,256,512]{2,1,0:T(8,128)(2,1)}, bf16[32,32,128]{2,1,0:T(8,128)(...) custom-call(s32[1]{0:T(128)} %bitcast.own_ref, ...), custom_call_target="tpu_custom_call", output_to_operand_aliasing={{0}: (6, {}), {1}: (7, {}), {2}: (8, {})} | custom-call | tf_op jit(solution)/shard_map/middle_1/pallas_call | solution.py:545
  181.0 3.6 all-to-all-start.5
  184.7 4.9 %collective-permute-start.9 = (bf16[32,32,128]{2,1,0:T(8,128)(2,1)}, bf16[32,32,128]{2,1,0:T(8,128)(2,1)S(1)}, u32[]{:S(2)}, u32[]{:S(2)}) collective-permute-start(bf16[32,32,128]{2,1,0:T(8,128)(2,1)} %get-tuple-element.128), channel_id=1, source_target_pairs={{0,8},{8,0},{16,24},{24,16},{1,9},{9,1},{17,25},{25,17},{2,10},{10... | collective-permute-start | bytes 786440 | tf_op jit(solution)/shard_map/ppermute | solution.py:151
  192.0 9.7 %collective-permute-done.9.refs_1_ = bf16[32,32,128]{2,1,0:T(8,128)(2,1)S(1)} collective-permute-done((bf16[32,32,128]{2,1,0:T(8,128)(2,1)}, bf16[32,32,128]{2,1,0:T(8,128)(2,1)S(1)}, u32[]{:S(2)}, u32[]{:S(2)}) %collective-permute-start.9) | collective-permute-done | bytes 262176 | tf_op jit(solution)/shard_map/ppermute | solution.py:151
  201.7 9.4 %collective-permute-done.10.refs_2_ = bf16[32,32,128]{2,1,0:T(8,128)(2,1)S(1)} collective-permute-done((bf16[32,32,128]{2,1,0:T(8,128)(2,1)}, bf16[32,32,128]{2,1,0:T(8,128)(2,1)S(1)}, u32[]{:S(2)}, u32[]{:S(2)}) %collective-permute-start.10) | collective-permute-done | bytes 262176 | tf_op jit(solution)/shard_map/ppermute | solution.py:151
  213.2 4.0 %all-to-all-start.6 = ((bf16[8,256,512]{2,1,0:T(8,128)(2,1)}), bf16[8,256,512]{2,1,0:T(8,128)(2,1)S(1)}, u32[]{:S(2)}, u32[]{:S(2)}) async-start(bf16[8,256,512]{2,1,0:T(8,128)(2,1)} %get-tuple-element.131), calls=%async_computation.6 | async-start | bytes 4194304 | tf_op jit(solution)/shard_map/all_to_all | solution.py:699
  218.8 4.9 %last_products_0.1 = (bf16[160,640]{1,0:T(8,128)(2,1)}, bf16[160,640]{1,0:T(8,128)(2,1)}, bf16[160,640]{1,0:T(8,128)(2,1)}, bf16[160,640]{1,0:T(8,128)(2,1)}) custom-call(bf16[8,2,128,512]{3,2,1,0:T(8,128)(2,1)S(1)} %bitcast.17, bf16[640,512]{1,0:T(8,128)(2,1)} %get-tuple-element.132.back_ref, bf16[16,128,128]{2,1,0:T(8,128)(2,1)} %gate_ref.11, ...), custom_call_target="tpu_custom_call" | custom-call | tf_op jit(solution)/shard_map/last_products_0/pallas_call | solution.py:608
  223.7 4.5 %collective-permute-start.12 = (bf16[160,640]{1,0:T(8,128)(2,1)}, bf16[160,640]{1,0:T(8,128)(2,1)S(1)}, u32[]{:S(2)}, u32[]{:S(2)}) collective-permute-start(bf16[160,640]{1,0:T(8,128)(2,1)} %get-tuple-element.134), channel_id=1, source_target_pairs={{0,8},{8,0},{16,24},{24,16},{1,9},{9,1},{17,25},{25,17},{2,10},{10... | collective-permute-start | bytes 614408 | tf_op jit(solution)/shard_map/ppermute | solution.py:151
  232.8 3.8 %last_products_5.1 = (bf16[160,384]{1,0:T(8,128)(2,1)}, bf16[160,384]{1,0:T(8,128)(2,1)}, bf16[160,384]{1,0:T(8,128)(2,1)}, bf16[160,384]{1,0:T(8,128)(2,1)}) custom-call(bf16[8,2,128,512]{3,2,1,0:T(8,128)(2,1)S(1)} %bitcast.18, bf16[640,512]{1,0:T(8,128)(2,1)} %get-tuple-element.132.back_ref, bf16[16,128,128]{2,1,0:T(8,128)(2,1)} %gate_ref.11, ...), custom_call_target="tpu_custom_call" | custom-call | tf_op jit(solution)/shard_map/last_products_5/pallas_call | solution.py:608
  239.3 6.8 %collective-permute-done.13.refs_2_ = bf16[160,640]{1,0:T(8,128)(2,1)S(1)} collective-permute-done((bf16[160,640]{1,0:T(8,128)(2,1)}, bf16[160,640]{1,0:T(8,128)(2,1)S(1)}, u32[]{:S(2)}, u32[]{:S(2)}) %collective-permute-start.13) | collective-permute-done | bytes 204832 | tf_op jit(solution)/shard_map/ppermute | solution.py:151
  246.8 4.4 %all-to-all-start.7 = ((bf16[8,256,512]{2,1,0:T(8,128)(2,1)}), bf16[8,256,512]{2,1,0:T(8,128)(2,1)}, u32[]{:S(2)}, u32[]{:S(2)}) async-start(bf16[8,256,512]{2,1,0:T(8,128)(2,1)} %get-tuple-element.147), calls=%async_computation.7 | async-start | bytes 4194304 | tf_op jit(solution)/shard_map/all_to_all | solution.py:699
  251.2 3.7 collective-permute-start.21
  259.3 3.6 last_products_8.1
  262.9 4.5 %collective-permute-done.15.refs_1_ = bf16[160,384]{1,0:T(8,128)(2,1)S(1)} collective-permute-done((bf16[160,384]{1,0:T(8,128)(2,1)}, bf16[160,384]{1,0:T(8,128)(2,1)S(1)}, u32[]{:S(2)}, u32[]{:S(2)}) %collective-permute-start.15) | collective-permute-done | bytes 122912 | tf_op jit(solution)/shard_map/ppermute | solution.py:151
  270.0 4.8 %unsort_0.1.refs_4_ = bf16[2048,640]{1,0:T(8,128)(2,1)} custom-call(bf16[640,640]{1,0:T(8,128)(2,1)} %get-tuple-element.94.home_ref, bf16[160,640]{1,0:T(8,128)(2,1)} %get-tuple-element.133.refs_0_, bf16[160,640]{1,0:T(8,128)(2,1)} %copy-done.24, bf16[160,640]{1,0:T(8,128)(2,1)} %copy-done.25, bf16[160,640]{1,0:T(8,128)(2,1)} %collective-permute-done.14.refs_3_), custom_call_target="tpu_custom_call" | custom-call | tf_op jit(solution)/shard_map/unsort_0/pallas_call | solution.py:171
  274.8 5.0 %last_products_11.1 = (bf16[160,640]{1,0:T(8,128)(2,1)}, bf16[160,640]{1,0:T(8,128)(2,1)}, bf16[160,640]{1,0:T(8,128)(2,1)}, bf16[160,640]{1,0:T(8,128)(2,1)}) custom-call(bf16[8,2,128,512]{3,2,1,0:T(8,128)(2,1)S(1)} %bitcast.15, bf16[640,512]{1,0:T(8,128)(2,1)} %get-tuple-element.132.back_ref, bf16[16,128,128]{2,1,0:T(8,128)(2,1)} %gate_ref.11, ...), custom_call_target="tpu_custom_call" | custom-call | tf_op jit(solution)/shard_map/last_products_11/pallas_call | solution.py:608
  284.6 4.3 %right_down.1 = bf16[8,256,512]{2,1,0:T(8,128)(2,1)} custom-call(bf16[8,256,512]{2,1,0:T(8,128)(2,1)} %all-to-all-done.7.in_ref, bf16[16,128,128]{2,1,0:T(8,128)(2,1)S(1)} %copy-done.7), custom_call_target="tpu_custom_call" | custom-call | tf_op jit(solution)/shard_map/right_down/pallas_call | solution.py:301
  289.0 4.5 %all-to-all-start.8 = ((bf16[8,256,512]{2,1,0:T(8,128)(2,1)}), bf16[8,256,512]{2,1,0:T(8,128)(2,1)}, u32[]{:S(2)}, u32[]{:S(2)}) async-start(bf16[8,256,512]{2,1,0:T(8,128)(2,1)} %right_down.1), calls=%async_computation.8 | async-start | bytes 4194304 | tf_op jit(solution)/shard_map/all_to_all | solution.py:699
  307.1 3.5 unsort_5.1.refs_4_
  310.6 3.5 unsort_8.1.refs_4_
  314.1 8.8 %collective-permute-done.22.refs_1_ = bf16[160,640]{1,0:T(8,128)(2,1)S(1)} collective-permute-done((bf16[160,640]{1,0:T(8,128)(2,1)S(1)}, bf16[160,640]{1,0:T(8,128)(2,1)S(1)}, u32[]{:S(2)}, u32[]{:S(2)}) %collective-permute-start.22) | collective-permute-done | bytes 204832 | tf_op jit(solution)/shard_map/ppermute | solution.py:151
  323.0 4.1 %collective-permute-done.24.refs_3_ = bf16[160,640]{1,0:T(8,128)(2,1)S(1)} collective-permute-done((bf16[160,640]{1,0:T(8,128)(2,1)S(1)}, bf16[160,640]{1,0:T(8,128)(2,1)S(1)}, u32[]{:S(2)}, u32[]{:S(2)}) %collective-permute-start.24) | collective-permute-done | bytes 204832 | tf_op jit(solution)/shard_map/ppermute | solution.py:151
  327.1 4.6 %left_down.1 = bf16[8,256,512]{2,1,0:T(8,128)(2,1)} custom-call(bf16[8,256,512]{2,1,0:T(8,128)(2,1)} %all-to-all-done.8.in_ref, bf16[16,128,128]{2,1,0:T(8,128)(2,1)S(1)} %copy-done.8), custom_call_target="tpu_custom_call" | custom-call | tf_op jit(solution)/shard_map/left_down/pallas_call | solution.py:301
  331.8 4.5 %all-to-all-start.9 = ((bf16[8,256,512]{2,1,0:T(8,128)(2,1)}), bf16[8,256,512]{2,1,0:T(8,128)(2,1)}, u32[]{:S(2)}, u32[]{:S(2)}) async-start(bf16[8,256,512]{2,1,0:T(8,128)(2,1)} %left_down.1), calls=%async_computation.9 | async-start | bytes 4194304 | tf_op jit(solution)/shard_map/all_to_all | solution.py:699
  344.6 6.8 %collective-permute-done.30.refs_1_ = bf16[2,16,32,128]{3,2,1,0:T(8,128)(2,1)S(1)} collective-permute-done((bf16[2,16,32,128]{3,2,1,0:T(8,128)(2,1)}, bf16[2,16,32,128]{3,2,1,0:T(8,128)(2,1)S(1)}, u32[]{:S(2)}, u32[]{:S(2)}) %collective-permute-start.30) | collective-permute-done | bytes 262176 | tf_op jit(solution)/shard_map/ppermute | solution.py:363
  356.6 3.7 collective-permute-done.29
  362.6 4.8 %unsort_11.1 = bf16[2048,640]{1,0:T(8,128)(2,1)} custom-call(bf16[640,640]{1,0:T(8,128)(2,1)} %get-tuple-element.94.home_ref, bf16[160,640]{1,0:T(8,128)(2,1)} %get-tuple-element.152.refs_0_, bf16[160,640]{1,0:T(8,128)(2,1)} %copy-done.26, bf16[160,640]{1,0:T(8,128)(2,1)} %copy-done.27, bf16[160,640]{1,0:T(8,128)(2,1)} %copy-done.28, ...), custom_call_target="tpu_custom_call", output_to_operand_aliasing={{}: (5, {})} | custom-call | tf_op jit(solution)/shard_map/unsort_11/pallas_call | solution.py:171
  367.4 5.6 %natural_order.1 = bf16[16,8,16,512]{3,2,1,0:T(8,128)(2,1)} custom-call(bf16[8,256,512]{2,1,0:T(8,128)(2,1)} %all-to-all-done.9.in_ref), custom_call_target="tpu_custom_call" | custom-call | tf_op jit(solution)/shard_map/natural_order/pallas_call | solution.py:658
  (155 shorter events, 85.3 us)
Async XLA Ops:
  5.3 31.9 %all-to-all-start = ((bf16[8,256,512]{2,1,0:T(8,128)(2,1)}), bf16[8,256,512]{2,1,0:T(8,128)(2,1)S(1)}, u32[]{:S(2)}, u32[]{:S(2)}) async-start(bf16[8,256,512]{2,1,0:T(8,128)(2,1)} %send_cotangent.1), calls=%async_computation | async-start | bytes 4194304 | tf_op jit(solution)/shard_map/all_to_all | solution.py:699
  17.0 13.4 %collective-permute-start = (bf16[160,512]{1,0:T(8,128)(2,1)}, bf16[160,512]{1,0:T(8,128)(2,1)S(1)}, u32[]{:S(2)}, u32[]{:S(2)}) collective-permute-start(bf16[160,512]{1,0:T(8,128)(2,1)} %get-tuple-element.96), channel_id=1, source_target_pairs={{0,8},{8,0},{16,24},{24,16},{1,9},{9,1},{17,25},{25,17},{2,10},{10... | collective-permute-start | bytes 491528 | tf_op jit(solution)/shard_map/ppermute | solution.py:151
  18.6 15.2 %collective-permute-start.1 = (bf16[160,512]{1,0:T(8,128)(2,1)}, bf16[160,512]{1,0:T(8,128)(2,1)S(1)}, u32[]{:S(2)}, u32[]{:S(2)}) collective-permute-start(bf16[160,512]{1,0:T(8,128)(2,1)} %get-tuple-element.97), channel_id=1, source_target_pairs={{0,16},{8,24},{16,0},{24,8},{1,17},{9,25},{17,1},{25,9},{2,18},{10... | collective-permute-start | bytes 491528 | tf_op jit(solution)/shard_map/ppermute | solution.py:151
  21.2 12.6 %collective-permute-start.2 = (bf16[160,512]{1,0:T(8,128)(2,1)}, bf16[160,512]{1,0:T(8,128)(2,1)S(1)}, u32[]{:S(2)}, u32[]{:S(2)}) collective-permute-start(bf16[160,512]{1,0:T(8,128)(2,1)} %get-tuple-element.98), channel_id=1, source_target_pairs={{0,24},{8,16},{16,8},{24,0},{1,25},{9,17},{17,9},{25,1},{2,26},{10... | collective-permute-start | bytes 491528 | tf_op jit(solution)/shard_map/ppermute | solution.py:151
  25.8 11.4 %copy-start.8 = (bf16[16,128,128]{2,1,0:T(8,128)(2,1)S(1)}, bf16[16,128,128]{2,1,0:T(8,128)(2,1)}, u32[]{:S(2)}) copy-start(bf16[16,128,128]{2,1,0:T(8,128)(2,1)} %factor_ref.7) | copy-start | bytes 1572868
  30.3 10.1 %copy-start.15 = (bf16[160,512]{1,0:T(8,128)(2,1)}, bf16[160,512]{1,0:T(8,128)(2,1)S(1)}, u32[]{:S(2)}) copy-start(bf16[160,512]{1,0:T(8,128)(2,1)S(1)} %collective-permute-done.refs_1_) | copy-start | bytes 491524
  40.5 30.3 %copy-start.7 = (bf16[16,128,128]{2,1,0:T(8,128)(2,1)S(1)}, bf16[16,128,128]{2,1,0:T(8,128)(2,1)}, u32[]{:S(2)}) copy-start(bf16[16,128,128]{2,1,0:T(8,128)(2,1)} %factor_ref.6) | copy-start | bytes 1572868
  40.5 30.3 %all-to-all-start.1 = ((bf16[8,256,512]{2,1,0:T(8,128)(2,1)}), bf16[8,256,512]{2,1,0:T(8,128)(2,1)S(1)}, u32[]{:S(2)}, u32[]{:S(2)}) async-start(bf16[8,256,512]{2,1,0:T(8,128)(2,1)} %left_back_down.1), calls=%async_computation.1 | async-start | bytes 4194304 | tf_op jit(solution)/shard_map/all_to_all | solution.py:699
  44.3 13.2 %collective-permute-start.3 = (bf16[160,768]{1,0:T(8,128)(2,1)}, bf16[160,768]{1,0:T(8,128)(2,1)S(1)}, u32[]{:S(2)}, u32[]{:S(2)}) collective-permute-start(bf16[160,768]{1,0:T(8,128)(2,1)} %get-tuple-element.100), channel_id=1, source_target_pairs={{0,8},{8,0},{16,24},{24,16},{1,9},{9,1},{17,25},{25,17},{2,10},{10... | collective-permute-start | bytes 737288 | tf_op jit(solution)/shard_map/ppermute | solution.py:151
  45.9 20.5 %collective-permute-start.4 = (bf16[160,768]{1,0:T(8,128)(2,1)}, bf16[160,768]{1,0:T(8,128)(2,1)S(1)}, u32[]{:S(2)}, u32[]{:S(2)}) collective-permute-start(bf16[160,768]{1,0:T(8,128)(2,1)} %get-tuple-element.101), channel_id=1, source_target_pairs={{0,16},{8,24},{16,0},{24,8},{1,17},{9,25},{17,1},{25,9},{2,18},{10... | collective-permute-start | bytes 737288 | tf_op jit(solution)/shard_map/ppermute | solution.py:151
  48.5 18.6 %collective-permute-start.5 = (bf16[160,768]{1,0:T(8,128)(2,1)}, bf16[160,768]{1,0:T(8,128)(2,1)}, u32[]{:S(2)}, u32[]{:S(2)}) collective-permute-start(bf16[160,768]{1,0:T(8,128)(2,1)} %get-tuple-element.102), channel_id=1, source_target_pairs={{0,24},{8,16},{16,8},{24,0},{1,25},{9,17},{17,9},{25,1},{2,26},{10... | collective-permute-start | bytes 737288 | tf_op jit(solution)/shard_map/ppermute | solution.py:151
  57.5 16.6 %copy-start.10 = (bf16[160,768]{1,0:T(8,128)(2,1)}, bf16[160,768]{1,0:T(8,128)(2,1)S(1)}, u32[]{:S(2)}) copy-start(bf16[160,768]{1,0:T(8,128)(2,1)S(1)} %collective-permute-done.3.refs_5_) | copy-start | bytes 737284
  74.0 33.3 %all-to-all-start.2 = ((bf16[8,256,512]{2,1,0:T(8,128)(2,1)}), bf16[8,256,512]{2,1,0:T(8,128)(2,1)S(1)}, u32[]{:S(2)}, u32[]{:S(2)}) async-start(bf16[8,256,512]{2,1,0:T(8,128)(2,1)} %right_back_down.1), calls=%async_computation.2 | async-start | bytes 4194304 | tf_op jit(solution)/shard_map/all_to_all | solution.py:699
  77.7 13.2 %collective-permute-start.6 = (bf16[160,768]{1,0:T(8,128)(2,1)}, bf16[160,768]{1,0:T(8,128)(2,1)S(1)}, u32[]{:S(2)}, u32[]{:S(2)}) collective-permute-start(bf16[160,768]{1,0:T(8,128)(2,1)} %get-tuple-element.104), channel_id=1, source_target_pairs={{0,8},{8,0},{16,24},{24,16},{1,9},{9,1},{17,25},{25,17},{2,10},{10... | collective-permute-start | bytes 737288 | tf_op jit(solution)/shard_map/ppermute | solution.py:151
  79.3 20.5 %collective-permute-start.7 = (bf16[160,768]{1,0:T(8,128)(2,1)}, bf16[160,768]{1,0:T(8,128)(2,1)S(1)}, u32[]{:S(2)}, u32[]{:S(2)}) collective-permute-start(bf16[160,768]{1,0:T(8,128)(2,1)} %get-tuple-element.105), channel_id=1, source_target_pairs={{0,16},{8,24},{16,0},{24,8},{1,17},{9,25},{17,1},{25,9},{2,18},{10... | collective-permute-start | bytes 737288 | tf_op jit(solution)/shard_map/ppermute | solution.py:151
  81.9 17.9 %collective-permute-start.8 = (bf16[160,768]{1,0:T(8,128)(2,1)}, bf16[160,768]{1,0:T(8,128)(2,1)S(1)}, u32[]{:S(2)}, u32[]{:S(2)}) collective-permute-start(bf16[160,768]{1,0:T(8,128)(2,1)} %get-tuple-element.106), channel_id=1, source_target_pairs={{0,24},{8,16},{16,8},{24,0},{1,25},{9,17},{17,9},{25,1},{2,26},{10... | collective-permute-start | bytes 737288 | tf_op jit(solution)/shard_map/ppermute | solution.py:151
  107.3 31.0 %all-to-all-start.3 = ((bf16[8,512,256]{2,1,0:T(8,128)(2,1)}), bf16[8,512,256]{2,1,0:T(8,128)(2,1)}, u32[]{:S(2)}, u32[]{:S(2)}) async-start(bf16[8,512,256]{2,1,0:T(8,128)(2,1)} %get-tuple-element.116), calls=%async_computation.3 | async-start | bytes 4194304 | tf_op jit(solution)/shard_map/all_to_all | solution.py:699
  138.4 31.0 %all-to-all-start.4 = ((bf16[8,512,256]{2,1,0:T(8,128)(2,1)}), bf16[8,512,256]{2,1,0:T(8,128)(2,1)}, u32[]{:S(2)}, u32[]{:S(2)}) async-start(bf16[8,512,256]{2,1,0:T(8,128)(2,1)} %get-tuple-element.117), calls=%async_computation.4 | async-start | bytes 4194304 | tf_op jit(solution)/shard_map/all_to_all | solution.py:699
  181.0 30.8 %all-to-all-start.5 = ((bf16[8,256,512]{2,1,0:T(8,128)(2,1)}), bf16[8,256,512]{2,1,0:T(8,128)(2,1)S(1)}, u32[]{:S(2)}, u32[]{:S(2)}) async-start(bf16[8,256,512]{2,1,0:T(8,128)(2,1)} %get-tuple-element.126), calls=%async_computation.5 | async-start | bytes 4194304 | tf_op jit(solution)/shard_map/all_to_all | solution.py:699
  184.7 17.0 %collective-permute-start.9 = (bf16[32,32,128]{2,1,0:T(8,128)(2,1)}, bf16[32,32,128]{2,1,0:T(8,128)(2,1)S(1)}, u32[]{:S(2)}, u32[]{:S(2)}) collective-permute-start(bf16[32,32,128]{2,1,0:T(8,128)(2,1)} %get-tuple-element.128), channel_id=1, source_target_pairs={{0,8},{8,0},{16,24},{24,16},{1,9},{9,1},{17,25},{25,17},{2,10},{10... | collective-permute-start | bytes 786440 | tf_op jit(solution)/shard_map/ppermute | solution.py:151
  189.6 21.6 %collective-permute-start.10 = (bf16[32,32,128]{2,1,0:T(8,128)(2,1)}, bf16[32,32,128]{2,1,0:T(8,128)(2,1)S(1)}, u32[]{:S(2)}, u32[]{:S(2)}) collective-permute-start(bf16[32,32,128]{2,1,0:T(8,128)(2,1)} %get-tuple-element.129), channel_id=1, source_target_pairs={{0,16},{8,24},{16,0},{24,8},{1,17},{9,25},{17,1},{25,9},{2,18},{10... | collective-permute-start | bytes 786440 | tf_op jit(solution)/shard_map/ppermute | solution.py:151
  190.7 21.2 %collective-permute-start.11 = (bf16[32,32,128]{2,1,0:T(8,128)(2,1)}, bf16[32,32,128]{2,1,0:T(8,128)(2,1)}, u32[]{:S(2)}, u32[]{:S(2)}) collective-permute-start(bf16[32,32,128]{2,1,0:T(8,128)(2,1)} %get-tuple-element.130), channel_id=1, source_target_pairs={{0,24},{8,16},{16,8},{24,0},{1,25},{9,17},{17,9},{25,1},{2,26},{10... | collective-permute-start | bytes 786440 | tf_op jit(solution)/shard_map/ppermute | solution.py:151
  201.7 29.0 %copy-start.22 = (bf16[32,32,128]{2,1,0:T(8,128)(2,1)}, bf16[32,32,128]{2,1,0:T(8,128)(2,1)S(1)}, u32[]{:S(2)}) copy-start(bf16[32,32,128]{2,1,0:T(8,128)(2,1)S(1)} %collective-permute-done.9.refs_1_) | copy-start | bytes 786436
  213.2 33.6 %all-to-all-start.6 = ((bf16[8,256,512]{2,1,0:T(8,128)(2,1)}), bf16[8,256,512]{2,1,0:T(8,128)(2,1)S(1)}, u32[]{:S(2)}, u32[]{:S(2)}) async-start(bf16[8,256,512]{2,1,0:T(8,128)(2,1)} %get-tuple-element.131), calls=%async_computation.6 | async-start | bytes 4194304 | tf_op jit(solution)/shard_map/all_to_all | solution.py:699
  223.7 15.6 %collective-permute-start.12 = (bf16[160,640]{1,0:T(8,128)(2,1)}, bf16[160,640]{1,0:T(8,128)(2,1)S(1)}, u32[]{:S(2)}, u32[]{:S(2)}) collective-permute-start(bf16[160,640]{1,0:T(8,128)(2,1)} %get-tuple-element.134), channel_id=1, source_target_pairs={{0,8},{8,0},{16,24},{24,16},{1,9},{9,1},{17,25},{25,17},{2,10},{10... | collective-permute-start | bytes 614408 | tf_op jit(solution)/shard_map/ppermute | solution.py:151
  228.2 17.8 %collective-permute-start.13 = (bf16[160,640]{1,0:T(8,128)(2,1)}, bf16[160,640]{1,0:T(8,128)(2,1)S(1)}, u32[]{:S(2)}, u32[]{:S(2)}) collective-permute-start(bf16[160,640]{1,0:T(8,128)(2,1)} %get-tuple-element.135), channel_id=1, source_target_pairs={{0,16},{8,24},{16,0},{24,8},{1,17},{9,25},{17,1},{25,9},{2,18},{10... | collective-permute-start | bytes 614408 | tf_op jit(solution)/shard_map/ppermute | solution.py:151
  229.3 17.5 %collective-permute-start.14 = (bf16[160,640]{1,0:T(8,128)(2,1)}, bf16[160,640]{1,0:T(8,128)(2,1)}, u32[]{:S(2)}, u32[]{:S(2)}) collective-permute-start(bf16[160,640]{1,0:T(8,128)(2,1)} %get-tuple-element.136), channel_id=1, source_target_pairs={{0,24},{8,16},{16,8},{24,0},{1,25},{9,17},{17,9},{25,1},{2,26},{10... | collective-permute-start | bytes 614408 | tf_op jit(solution)/shard_map/ppermute | solution.py:151
  246.8 37.8 %all-to-all-start.7 = ((bf16[8,256,512]{2,1,0:T(8,128)(2,1)}), bf16[8,256,512]{2,1,0:T(8,128)(2,1)}, u32[]{:S(2)}, u32[]{:S(2)}) async-start(bf16[8,256,512]{2,1,0:T(8,128)(2,1)} %get-tuple-element.147), calls=%async_computation.7 | async-start | bytes 4194304 | tf_op jit(solution)/shard_map/all_to_all | solution.py:699
  251.2 31.5 %collective-permute-start.21 = (bf16[2,16,32,128]{3,2,1,0:T(8,128)(2,1)}, bf16[2,16,32,128]{3,2,1,0:T(8,128)(2,1)S(1)}, u32[]{:S(2)}, u32[]{:S(2)}) collective-permute-start(bf16[2,16,32,128]{3,2,1,0:T(8,128)(2,1)} %get-tuple-element.145), channel_id=1, source_target_pairs={{0,8},{8,0},{16,24},{24,16},{1,9},{9,1},{17,25},{25,17},{2,10},{10... | collective-permute-start | bytes 786440 | tf_op jit(solution)/shard_map/ppermute | solution.py:363
  254.9 12.5 %collective-permute-start.15 = (bf16[160,384]{1,0:T(8,128)(2,1)}, bf16[160,384]{1,0:T(8,128)(2,1)S(1)}, u32[]{:S(2)}, u32[]{:S(2)}) collective-permute-start(bf16[160,384]{1,0:T(8,128)(2,1)} %get-tuple-element.138), channel_id=1, source_target_pairs={{0,8},{8,0},{16,24},{24,16},{1,9},{9,1},{17,25},{25,17},{2,10},{10... | collective-permute-start | bytes 368648 | tf_op jit(solution)/shard_map/ppermute | solution.py:151
  255.0 13.1 %collective-permute-start.16 = (bf16[160,384]{1,0:T(8,128)(2,1)}, bf16[160,384]{1,0:T(8,128)(2,1)S(1)}, u32[]{:S(2)}, u32[]{:S(2)}) collective-permute-start(bf16[160,384]{1,0:T(8,128)(2,1)} %get-tuple-element.139), channel_id=1, source_target_pairs={{0,16},{8,24},{16,0},{24,8},{1,17},{9,25},{17,1},{25,9},{2,18},{10... | collective-permute-start | bytes 368648 | tf_op jit(solution)/shard_map/ppermute | solution.py:151
  257.9 24.7 %collective-permute-start.17 = (bf16[160,384]{1,0:T(8,128)(2,1)}, bf16[160,384]{1,0:T(8,128)(2,1)S(1)}, u32[]{:S(2)}, u32[]{:S(2)}) collective-permute-start(bf16[160,384]{1,0:T(8,128)(2,1)} %get-tuple-element.140), channel_id=1, source_target_pairs={{0,24},{8,16},{16,8},{24,0},{1,25},{9,17},{17,9},{25,1},{2,26},{10... | collective-permute-start | bytes 368648 | tf_op jit(solution)/shard_map/ppermute | solution.py:151
  262.9 20.4 %collective-permute-start.18 = (bf16[160,384]{1,0:T(8,128)(2,1)}, bf16[160,384]{1,0:T(8,128)(2,1)S(1)}, u32[]{:S(2)}, u32[]{:S(2)}) collective-permute-start(bf16[160,384]{1,0:T(8,128)(2,1)} %get-tuple-element.149), channel_id=1, source_target_pairs={{0,8},{8,0},{16,24},{24,16},{1,9},{9,1},{17,25},{25,17},{2,10},{10... | collective-permute-start | bytes 368648 | tf_op jit(solution)/shard_map/ppermute | solution.py:151
  267.4 16.5 %collective-permute-start.19 = (bf16[160,384]{1,0:T(8,128)(2,1)}, bf16[160,384]{1,0:T(8,128)(2,1)S(1)}, u32[]{:S(2)}, u32[]{:S(2)}) collective-permute-start(bf16[160,384]{1,0:T(8,128)(2,1)} %get-tuple-element.150), channel_id=1, source_target_pairs={{0,16},{8,24},{16,0},{24,8},{1,17},{9,25},{17,1},{25,9},{2,18},{10... | collective-permute-start | bytes 368648 | tf_op jit(solution)/shard_map/ppermute | solution.py:151
  268.1 16.5 %collective-permute-start.20 = (bf16[160,384]{1,0:T(8,128)(2,1)}, bf16[160,384]{1,0:T(8,128)(2,1)}, u32[]{:S(2)}, u32[]{:S(2)}) collective-permute-start(bf16[160,384]{1,0:T(8,128)(2,1)} %get-tuple-element.151), channel_id=1, source_target_pairs={{0,24},{8,16},{16,8},{24,0},{1,25},{9,17},{17,9},{25,1},{2,26},{10... | collective-permute-start | bytes 368648 | tf_op jit(solution)/shard_map/ppermute | solution.py:151
  289.0 38.2 %all-to-all-start.8 = ((bf16[8,256,512]{2,1,0:T(8,128)(2,1)}), bf16[8,256,512]{2,1,0:T(8,128)(2,1)}, u32[]{:S(2)}, u32[]{:S(2)}) async-start(bf16[8,256,512]{2,1,0:T(8,128)(2,1)} %right_down.1), calls=%async_computation.8 | async-start | bytes 4194304 | tf_op jit(solution)/shard_map/all_to_all | solution.py:699
  295.3 9.9 %copy-start.39 = (bf16[160,640]{1,0:T(8,128)(2,1)S(1)}, bf16[160,640]{1,0:T(8,128)(2,1)}, u32[]{:S(2)}) copy-start(bf16[160,640]{1,0:T(8,128)(2,1)} %get-tuple-element.155) | copy-start | bytes 614404
  295.3 9.9 %collective-permute-start.25 = (bf16[1,16,32,128]{3,2,1,0:T(8,128)(2,1)}, bf16[1,16,32,128]{3,2,1,0:T(8,128)(2,1)S(1)}, u32[]{:S(2)}, u32[]{:S(2)}) collective-permute-start(bf16[1,16,32,128]{3,2,1,0:T(8,128)(2,1)} %get-tuple-element.161), channel_id=1, source_target_pairs={{0,16},{8,24},{16,0},{24,8},{1,17},{9,25},{17,1},{25,9},{2,18},{10... | collective-permute-start | bytes 393224 | tf_op jit(solution)/shard_map/ppermute | solution.py:363
  297.4 29.7 %collective-permute-start.26 = (bf16[2,16,32,128]{3,2,1,0:T(8,128)(2,1)}, bf16[2,16,32,128]{3,2,1,0:T(8,128)(2,1)S(1)}, u32[]{:S(2)}, u32[]{:S(2)}) collective-permute-start(bf16[2,16,32,128]{3,2,1,0:T(8,128)(2,1)} %get-tuple-element.158), channel_id=1, source_target_pairs={{0,8},{8,0},{16,24},{24,16},{1,9},{9,1},{17,25},{25,17},{2,10},{10... | collective-permute-start | bytes 786440 | tf_op jit(solution)/shard_map/ppermute | solution.py:363
  301.0 26.1 %collective-permute-start.27 = (bf16[2,16,32,128]{3,2,1,0:T(8,128)(2,1)}, bf16[2,16,32,128]{3,2,1,0:T(8,128)(2,1)S(1)}, u32[]{:S(2)}, u32[]{:S(2)}) collective-permute-start(bf16[2,16,32,128]{3,2,1,0:T(8,128)(2,1)} %get-tuple-element.163), channel_id=1, source_target_pairs={{0,8},{8,0},{16,24},{24,16},{1,9},{9,1},{17,25},{25,17},{2,10},{10... | collective-permute-start | bytes 786440 | tf_op jit(solution)/shard_map/ppermute | solution.py:363
  302.5 20.5 %collective-permute-start.22 = (bf16[160,640]{1,0:T(8,128)(2,1)S(1)}, bf16[160,640]{1,0:T(8,128)(2,1)S(1)}, u32[]{:S(2)}, u32[]{:S(2)}) collective-permute-start(bf16[160,640]{1,0:T(8,128)(2,1)S(1)} %copy-done.41), channel_id=1, source_target_pairs={{0,8},{8,0},{16,24},{24,16},{1,9},{9,1},{17,25},{25,17},{2,10},{10... | collective-permute-start | bytes 614408 | tf_op jit(solution)/shard_map/ppermute | solution.py:151
  303.0 19.9 %collective-permute-start.23 = (bf16[160,640]{1,0:T(8,128)(2,1)S(1)}, bf16[160,640]{1,0:T(8,128)(2,1)S(1)}, u32[]{:S(2)}, u32[]{:S(2)}) collective-permute-start(bf16[160,640]{1,0:T(8,128)(2,1)S(1)} %copy-done.40), channel_id=1, source_target_pairs={{0,16},{8,24},{16,0},{24,8},{1,17},{9,25},{17,1},{25,9},{2,18},{10... | collective-permute-start | bytes 614408 | tf_op jit(solution)/shard_map/ppermute | solution.py:151
  305.2 21.9 %collective-permute-start.24 = (bf16[160,640]{1,0:T(8,128)(2,1)S(1)}, bf16[160,640]{1,0:T(8,128)(2,1)S(1)}, u32[]{:S(2)}, u32[]{:S(2)}) collective-permute-start(bf16[160,640]{1,0:T(8,128)(2,1)S(1)} %copy-done.39), channel_id=1, source_target_pairs={{0,24},{8,16},{16,8},{24,0},{1,25},{9,17},{17,9},{25,1},{2,26},{10... | collective-permute-start | bytes 614408 | tf_op jit(solution)/shard_map/ppermute | solution.py:151
  331.8 35.7 %all-to-all-start.9 = ((bf16[8,256,512]{2,1,0:T(8,128)(2,1)}), bf16[8,256,512]{2,1,0:T(8,128)(2,1)}, u32[]{:S(2)}, u32[]{:S(2)}) async-start(bf16[8,256,512]{2,1,0:T(8,128)(2,1)} %left_down.1), calls=%async_computation.9 | async-start | bytes 4194304 | tf_op jit(solution)/shard_map/all_to_all | solution.py:699
  339.4 12.0 %collective-permute-start.30 = (bf16[2,16,32,128]{3,2,1,0:T(8,128)(2,1)}, bf16[2,16,32,128]{3,2,1,0:T(8,128)(2,1)S(1)}, u32[]{:S(2)}, u32[]{:S(2)}) collective-permute-start(bf16[2,16,32,128]{3,2,1,0:T(8,128)(2,1)} %get-tuple-element.175), channel_id=1, source_target_pairs={{0,8},{8,0},{16,24},{24,16},{1,9},{9,1},{17,25},{25,17},{2,10},{10... | collective-permute-start | bytes 786440 | tf_op jit(solution)/shard_map/ppermute | solution.py:363
  341.6 12.4 %collective-permute-start.28 = (bf16[1,16,32,128]{3,2,1,0:T(8,128)(2,1)}, bf16[1,16,32,128]{3,2,1,0:T(8,128)(2,1)S(1)}, u32[]{:S(2)}, u32[]{:S(2)}) collective-permute-start(bf16[1,16,32,128]{3,2,1,0:T(8,128)(2,1)} %get-tuple-element.167), channel_id=1, source_target_pairs={{0,16},{8,24},{16,0},{24,8},{1,17},{9,25},{17,1},{25,9},{2,18},{10... | collective-permute-start | bytes 393224 | tf_op jit(solution)/shard_map/ppermute | solution.py:363
  344.6 15.6 %collective-permute-start.29 = (bf16[1,16,32,128]{3,2,1,0:T(8,128)(2,1)}, bf16[1,16,32,128]{3,2,1,0:T(8,128)(2,1)S(1)}, u32[]{:S(2)}, u32[]{:S(2)}) collective-permute-start(bf16[1,16,32,128]{3,2,1,0:T(8,128)(2,1)} %get-tuple-element.172), channel_id=1, source_target_pairs={{0,16},{8,24},{16,0},{24,8},{1,17},{9,25},{17,1},{25,9},{2,18},{10... | collective-permute-start | bytes 393224 | tf_op jit(solution)/shard_map/ppermute | solution.py:363
  354.0 19.1 %collective-permute-start.31 = (bf16[1,16,32,128]{3,2,1,0:T(8,128)(2,1)}, bf16[1,16,32,128]{3,2,1,0:T(8,128)(2,1)S(1)}, u32[]{:S(2)}, u32[]{:S(2)}) collective-permute-start(bf16[1,16,32,128]{3,2,1,0:T(8,128)(2,1)} %get-tuple-element.177), channel_id=1, source_target_pairs={{0,16},{8,24},{16,0},{24,8},{1,17},{9,25},{17,1},{25,9},{2,18},{10... | collective-permute-start | bytes 393224 | tf_op jit(solution)/shard_map/ppermute | solution.py:363
  (36 other events, 146.0 us)

commit v4 on v3

--- a/solution.py
+++ b/solution.py
@@ -613,7 +613,7 @@
         out_shape=[pltpu.HBM((cap, size * count), BF16)] * groups,
         compiler_params=params(32),
         name=f"last_products_{start}",
-    )(arrived, *in_hbm(back, right_gate, right_up))
+    )(*in_hbm(arrived, back, right_gate, right_up))
 
 
 def right_grads_kernel(plan, scale, halves, own_ref, in_ref, *refs):
@@ -642,12 +642,13 @@
         scratch_shapes=[pltpu.VMEM((2 * count,) + factor.shape[1:], F32)],
         compiler_params=params(32),
         name=f"right_grads_{which}",
-    )(own, arrived, *in_hbm(*packed))
+    )(own, *in_hbm(arrived, *packed))
 
 
 def natural_kernel(in_ref, out_ref):
     held, _, held_there, tok = out_ref.shape
-    out_ref[...] = in_ref[...].reshape(held, 1, held_there, tok)
+    for peer in range(in_ref.shape[0]):
+        out_ref[:, peer] = in_ref[peer].reshape(held, held_there, tok)
 
 
 def natural_order(plan, arrived):
@@ -655,11 +656,12 @@
     if not plan.direct:
         array = arrived.reshape(plan.peers, plan.held, plan.held, plan.tok)
         return array.transpose(1, 0, 2, 3).reshape(-1, plan.tok)
+    step = plan.peers // 2
     array = pl.pallas_call(
         natural_kernel,
-        grid=(plan.peers,),
-        in_specs=[pl.BlockSpec((1, plan.piece, plan.tok), lambda s: (s, 0, 0))],
-        out_specs=pl.BlockSpec((plan.held, 1, plan.held, plan.tok), lambda s: (0, s, 0, 0)),
+        grid=(plan.peers // step,),
+        in_specs=[pl.BlockSpec((step, plan.piece, plan.tok), lambda s: (s, 0, 0))],
+        out_specs=pl.BlockSpec((plan.held, step, plan.held, plan.tok), lambda s: (0, s, 0, 0)),
         out_shape=pltpu.HBM(shape, BF16),
         compiler_params=params(),
         name="natural_order",
@@ -750,40 +752,41 @@
     hidden = swap(after(hidden, high, rows[0], sent[1], right_low, grad_left_gate))
     sent = [last_products(plan, high, *factors, p, unit) for p in back_pieces[2:]]
     rows += [exchange_rows(slabs, groups) for slabs in sent]
-    right_high = right_grads(
-        plan, own, after(high, sent), packed, right_gate, scale, groups, 1
-    )
     places = (home, step, feats)
-    mixed_grad = unsort(rows[0], back_pieces[0], *places, None)
-    right_low = [(right_low[0], swap_rows(right_low[1], 1, groups))]
-    hidden = after(hidden, rows[1], rows[2], sent[1], right_high, mixed_grad, right_low)
+    right_low = (right_low[0], swap_rows(right_low[1], 1, groups))
+    hidden = after(hidden, rows[1], rows[2], sent[1])
     down_spread = product(plan, hidden, right_down, TN, "right_down")
     down_grad = factor_grad(
         plan, own, after(hidden, down_spread), down_spread_grad, right_down, scale, groups,
         "right_down_grad",
     )
+    mixed_grad = unsort(rows[0], back_pieces[0], *places, None)
+    mixed_grad = unsort(rows[1], back_pieces[1], *places, mixed_grad)
+    right_high = right_grads(
+        plan, own, after(high, rows[3], mixed_grad, down_grad), packed, right_gate, scale, groups, 1
+    )
     down_spread = swap(down_spread)
-    mixed_grad = unsort(rows[1], back_pieces[1], *places, mixed_grad)
-    mixed_grad = unsort(rows[2], back_pieces[2], *places, mixed_grad)
-    right_low = finish(right_low, groups, "halve_right_low")
     right_high = (right_high[0], swap_rows(right_high[1], 1, groups))
     down_grad = (down_grad[0], swap_rows(down_grad[1], 1, groups))
-    down_spread = after(
-        down_spread, rows[3], right_low, right_high[1], down_grad[1], mixed_grad
-    )
+    down_spread = after(down_spread, right_low[1], right_high[1], down_grad[1])
     result = product(plan, down_spread, left_down, TN, "left_down")
     left_down_grad = factor_grad(
         plan, own, after(down_spread, result), out_grads, left_down, scale, groups,
         "left_down_grad",
     )
     output = natural_order(plan, move(result))
+    left_down_grad = [(left_down_grad[0], swap_rows(left_down_grad[1], 1, groups))]
+    mixed_grad = unsort(rows[2], back_pieces[2], *places, mixed_grad)
     mixed_grad = unsort(rows[3], back_pieces[3], *places, mixed_grad)
-    left_down_grad = [(left_down_grad[0], swap_rows(left_down_grad[1], 1, groups))]
-    right_high, down_grad = finish([right_high, down_grad], groups, "halve_right")
+    left_down_grad = after(left_down_grad, mixed_grad)
+    right_low, right_high, down_grad = finish(
+        [right_low, right_high, down_grad], groups, "halve_right"
+    )
     left_down_grad = finish(left_down_grad, groups, "halve_left_down")[0]
-    grad_right_gate, grad_right_up = sums_of([right_low[0], right_high], 2, "sum_right")
     (grad_right_down,) = sums_of([down_grad], 1, "sum_right_down")
-    left_down_grad = after(left_down_grad, output, mixed_grad, grad_right_gate, grad_right_down)
+    right_low = after(right_low, output, grad_right_down)
+    grad_right_gate, grad_right_up = sums_of([right_low, right_high], 2, "sum_right")
+    left_down_grad = after(left_down_grad, grad_right_gate)
     (grad_left_down,) = sums_of([left_down_grad], 1, "sum_left_down")
     return (
         output,

time: 378 us -> 371 us (0.981)
  waiting for transfers between devices: 136 us -> 123 us
  starting transfers between devices: 92 us -> 103 us
  local copies, waits for them, and re-layouts: 10.5 us -> 4.82 us
    ppermute x24, waiting for transfers between devices: 82.2 us -> 72 us  [exchange(): received.append(lax.ppermute(arrays[k], axis, pairs))]
    ppermute x24, starting transfers between devices: 38.5 us -> 44.4 us  [exchange(): received.append(lax.ppermute(arrays[k], axis, pairs))]
    unnamed x84 -> x58, local copies, waits for them, and re-layouts: 10.5 us -> 4.8 us
  transfers between devices with their start and end apart: 42 -> 42, of which waited for: 18 -> 19; matrix products, arithmetic and copies ran while one was open for 0% -> 0% of each run, Pallas kernels for 27% -> 28%
where the time goes in v4:
time: 371 us; the launch traced here: 368 us
  Pallas kernels  136 us (37%)
  waiting for transfers between devices  123 us (33%)
  starting transfers between devices  103 us (28%)
  local copies, waits for them, and re-layouts  4.82 us (1%)
    ppermute x24, waiting for transfers between devices, exchange(): received.append(lax.ppermute(arrays[k], axis, pairs))  72 us
    all_to_all x10, starting transfers between devices, move(): lax.all_to_all(array, 'feat', split_axis=0, concat_axis=0, tiled=True)  45 us
    ppermute x24, starting transfers between devices, exchange(): received.append(lax.ppermute(arrays[k], axis, pairs))  44.4 us
    all_to_all x10, waiting for transfers between devices, move(): lax.all_to_all(array, 'feat', split_axis=0, concat_axis=0, tiled=True)  43 us
    pallas_call x2, Pallas kernels, middle(): pl.pallas_call(functools.partial(middle_kernel, plan, scale, first, last)...  23.3 us
    pallas_call x4, Pallas kernels, last_products(): pl.pallas_call(functools.partial(last_kernel, plan), grid=(count,), in_sp...  18.4 us
    pallas_call x4, Pallas kernels, unsort(): pl.pallas_call(functools.partial(unsort_kernel, groups), grid=(count,), i...  16.7 us
    pallas_call x4, Pallas kernels, product(): pl.pallas_call(functools.partial(product_kernel, plan, over), grid=(plan....  16.3 us
  transfers between devices with their start and end apart: 42, of which 19 were waited for; matrix products, arithmetic and copies ran while one was open for 0% of the time, Pallas kernels for 28%

profile of v4, /device:TPU:0, one launch (start us, length us, event | category | flops | bytes accessed | tf_op | source)
XLA Modules:
  0.0 368.3 jit_solution(1289564981053515578)
XLA Ops:
  0.6 4.7 %send_cotangent.1 = bf16[8,256,512]{2,1,0:T(8,128)(2,1)} custom-call(bf16[2048,512]{1,0:T(8,128)(2,1)} %in_ref.1), custom_call_target="tpu_custom_call" | custom-call | tf_op jit(solution)/shard_map/send_cotangent/pallas_call | solution.py:279
  5.3 5.3 %all-to-all-start = ((bf16[8,256,512]{2,1,0:T(8,128)(2,1)}), bf16[8,256,512]{2,1,0:T(8,128)(2,1)S(1)}, u32[]{:S(2)}, u32[]{:S(2)}) async-start(bf16[8,256,512]{2,1,0:T(8,128)(2,1)} %send_cotangent.1), calls=%async_computation | async-start | bytes 4194304 | tf_op jit(solution)/shard_map/all_to_all | solution.py:701
  21.4 4.4 %mix_and_sort_5.1 = (bf16[160,768]{1,0:T(8,128)(2,1)}, bf16[160,768]{1,0:T(8,128)(2,1)}, bf16[160,768]{1,0:T(8,128)(2,1)}, bf16[160,768]{1,0:T(8,128)(2,1)}) custom-call(f32[3]{0:T(128)S(1)} %copy-done.2, bf16[3,2048,640]{2,1,0:T(8,128)(2,1)} %earlier_ref.5, bf16[640,640]{1,0:T(8,128)(2,1)} %get-tuple-element.98.home_ref), custom_call_target="tpu_custom_call" | custom-call | tf_op jit(solution)/shard_map/mix_and_sort_5/pallas_call | solution.py:125
  25.9 4.5 %mix_and_sort_2.1 = (bf16[160,768]{1,0:T(8,128)(2,1)}, bf16[160,768]{1,0:T(8,128)(2,1)}, bf16[160,768]{1,0:T(8,128)(2,1)}, bf16[160,768]{1,0:T(8,128)(2,1)}) custom-call(f32[3]{0:T(128)S(1)} %copy-done.2, bf16[3,2048,640]{2,1,0:T(8,128)(2,1)} %earlier_ref.5, bf16[640,640]{1,0:T(8,128)(2,1)} %get-tuple-element.98.home_ref), custom_call_target="tpu_custom_call" | custom-call | tf_op jit(solution)/shard_map/mix_and_sort_2/pallas_call | solution.py:125
  30.4 3.4 collective-permute-done.1.refs_2_
  33.8 3.4 all-to-all-done.in_ref.other_ref
  40.5 4.5 %all-to-all-start.1 = ((bf16[8,256,512]{2,1,0:T(8,128)(2,1)}), bf16[8,256,512]{2,1,0:T(8,128)(2,1)}, u32[]{:S(2)}, u32[]{:S(2)}) async-start(bf16[8,256,512]{2,1,0:T(8,128)(2,1)} %left_back_down.1), calls=%async_computation.1 | async-start | bytes 4194304 | tf_op jit(solution)/shard_map/all_to_all | solution.py:701
  49.4 8.7 %collective-permute-done.3.refs_5_ = bf16[160,768]{1,0:T(8,128)(2,1)S(1)} collective-permute-done((bf16[160,768]{1,0:T(8,128)(2,1)}, bf16[160,768]{1,0:T(8,128)(2,1)S(1)}, u32[]{:S(2)}, u32[]{:S(2)}) %collective-permute-start.3) | collective-permute-done | bytes 245792 | tf_op jit(solution)/shard_map/ppermute | solution.py:151
  58.2 9.1 %collective-permute-done.4.refs_6_ = bf16[160,768]{1,0:T(8,128)(2,1)} collective-permute-done((bf16[160,768]{1,0:T(8,128)(2,1)}, bf16[160,768]{1,0:T(8,128)(2,1)}, u32[]{:S(2)}, u32[]{:S(2)}) %collective-permute-start.4) | collective-permute-done | bytes 245792 | tf_op jit(solution)/shard_map/ppermute | solution.py:151
  67.2 4.4 %all-to-all-done.1.in_ref.other_ref = bf16[8,256,512]{2,1,0:T(8,128)(2,1)} async-done(((bf16[8,256,512]{2,1,0:T(8,128)(2,1)}), bf16[8,256,512]{2,1,0:T(8,128)(2,1)}, u32[]{:S(2)}, u32[]{:S(2)}) %all-to-all-start.1) | async-done | bytes 2097184 | tf_op jit(solution)/shard_map/all_to_all | solution.py:701
  71.6 4.3 %right_back_down.1 = bf16[8,256,512]{2,1,0:T(8,128)(2,1)} custom-call(bf16[8,256,512]{2,1,0:T(8,128)(2,1)} %all-to-all-done.1.in_ref.other_ref, bf16[16,128,128]{2,1,0:T(8,128)(2,1)S(1)} %copy-done), custom_call_target="tpu_custom_call" | custom-call | tf_op jit(solution)/shard_map/right_back_down/pallas_call | solution.py:301
  75.9 4.3 %all-to-all-start.2 = ((bf16[8,256,512]{2,1,0:T(8,128)(2,1)}), bf16[8,256,512]{2,1,0:T(8,128)(2,1)}, u32[]{:S(2)}, u32[]{:S(2)}) async-start(bf16[8,256,512]{2,1,0:T(8,128)(2,1)} %right_back_down.1), calls=%async_computation.2 | async-start | bytes 4194304 | tf_op jit(solution)/shard_map/all_to_all | solution.py:701
  84.7 8.7 %collective-permute-done.6.refs_9_ = bf16[160,768]{1,0:T(8,128)(2,1)S(1)} collective-permute-done((bf16[160,768]{1,0:T(8,128)(2,1)}, bf16[160,768]{1,0:T(8,128)(2,1)S(1)}, u32[]{:S(2)}, u32[]{:S(2)}) %collective-permute-start.6) | collective-permute-done | bytes 245792 | tf_op jit(solution)/shard_map/ppermute | solution.py:151
  93.5 8.9 %collective-permute-done.7.refs_10_ = bf16[160,768]{1,0:T(8,128)(2,1)S(1)} collective-permute-done((bf16[160,768]{1,0:T(8,128)(2,1)}, bf16[160,768]{1,0:T(8,128)(2,1)S(1)}, u32[]{:S(2)}, u32[]{:S(2)}) %collective-permute-start.7) | collective-permute-done | bytes 245792 | tf_op jit(solution)/shard_map/ppermute | solution.py:151
  103.2 6.7 %first_products_0.1 = (bf16[256,2048]{1,0:T(8,128)(2,1)}, bf16[8,512,256]{2,1,0:T(8,128)(2,1)}) custom-call(bf16[160,512]{1,0:T(8,128)(2,1)} %get-tuple-element.99.refs_0_, bf16[160,512]{1,0:T(8,128)(2,1)} %copy-done.7, bf16[160,512]{1,0:T(8,128)(2,1)} %copy-done.8, bf16[160,512]{1,0:T(8,128)(2,1)} %copy-done.9, ...), custom_call_target="tpu_custom_call" | custom-call | tf_op jit(solution)/shard_map/first_products_0/pallas_call | solution.py:463
  109.9 4.5 %all-to-all-start.3 = ((bf16[8,512,256]{2,1,0:T(8,128)(2,1)}), bf16[8,512,256]{2,1,0:T(8,128)(2,1)}, u32[]{:S(2)}, u32[]{:S(2)}) async-start(bf16[8,512,256]{2,1,0:T(8,128)(2,1)} %get-tuple-element.120), calls=%async_computation.3 | async-start | bytes 4194304 | tf_op jit(solution)/shard_map/all_to_all | solution.py:701
  114.5 6.7 %first_products_1.1 = (bf16[256,2048]{1,0:T(8,128)(2,1)}, bf16[8,512,256]{2,1,0:T(8,128)(2,1)}) custom-call(bf16[160,512]{1,0:T(8,128)(2,1)} %get-tuple-element.99.refs_0_, bf16[160,512]{1,0:T(8,128)(2,1)} %copy-done.7, bf16[160,512]{1,0:T(8,128)(2,1)} %copy-done.8, bf16[160,512]{1,0:T(8,128)(2,1)} %copy-done.9, ...), custom_call_target="tpu_custom_call" | custom-call | tf_op jit(solution)/shard_map/first_products_1/pallas_call | solution.py:463
  121.2 19.7 %all-to-all-done.3.spread_ref = bf16[8,512,256]{2,1,0:T(8,128)(2,1)} async-done(((bf16[8,512,256]{2,1,0:T(8,128)(2,1)}), bf16[8,512,256]{2,1,0:T(8,128)(2,1)}, u32[]{:S(2)}, u32[]{:S(2)}) %all-to-all-start.3) | async-done | bytes 2097184 | tf_op jit(solution)/shard_map/all_to_all | solution.py:701
  140.9 4.4 %all-to-all-start.4 = ((bf16[8,512,256]{2,1,0:T(8,128)(2,1)}), bf16[8,512,256]{2,1,0:T(8,128)(2,1)}, u32[]{:S(2)}, u32[]{:S(2)}) async-start(bf16[8,512,256]{2,1,0:T(8,128)(2,1)} %get-tuple-element.121), calls=%async_computation.4 | async-start | bytes 4194304 | tf_op jit(solution)/shard_map/all_to_all | solution.py:701
  145.3 11.5 %middle_0.1 = (bf16[8,256,512]{2,1,0:T(8,128)(2,1)}, bf16[8,256,512]{2,1,0:T(8,128)(2,1)}, bf16[8,256,512]{2,1,0:T(8,128)(2,1)}, f32[32,128,128]{2,1,0:T(8,128)}) custom-call(s32[1]{0:T(128)} %bitcast.own_ref, bf16[8,512,256]{2,1,0:T(8,128)(2,1)} %all-to-all-done.3.spread_ref, bf16[8,256,512]{2,1,0:T(8,128)(2,1)} %all-to-all-done.2.hidden_grad_ref, ...), custom_call_target="tpu_custom_call" | custom-call | tf_op jit(solution)/shard_map/middle_0/pallas_call | solution.py:545
  156.8 15.2 %all-to-all-done.4.spread_ref = bf16[8,512,256]{2,1,0:T(8,128)(2,1)} async-done(((bf16[8,512,256]{2,1,0:T(8,128)(2,1)}), bf16[8,512,256]{2,1,0:T(8,128)(2,1)}, u32[]{:S(2)}, u32[]{:S(2)}) %all-to-all-start.4) | async-done | bytes 2097184 | tf_op jit(solution)/shard_map/all_to_all | solution.py:701
  171.9 11.8 %middle_1.1 = (bf16[8,256,512]{2,1,0:T(8,128)(2,1)}, bf16[8,256,512]{2,1,0:T(8,128)(2,1)}, bf16[8,256,512]{2,1,0:T(8,128)(2,1)}, bf16[32,32,128]{2,1,0:T(8,128)(...) custom-call(s32[1]{0:T(128)} %bitcast.own_ref, ...), custom_call_target="tpu_custom_call", output_to_operand_aliasing={{0}: (6, {}), {1}: (7, {}), {2}: (8, {})} | custom-call | tf_op jit(solution)/shard_map/middle_1/pallas_call | solution.py:545
  183.8 4.3 %all-to-all-start.5 = ((bf16[8,256,512]{2,1,0:T(8,128)(2,1)}), bf16[8,256,512]{2,1,0:T(8,128)(2,1)}, u32[]{:S(2)}, u32[]{:S(2)}) async-start(bf16[8,256,512]{2,1,0:T(8,128)(2,1)} %get-tuple-element.130), calls=%async_computation.5 | async-start | bytes 4194304 | tf_op jit(solution)/shard_map/all_to_all | solution.py:701
  188.1 4.9 %collective-permute-start.9 = (bf16[32,32,128]{2,1,0:T(8,128)(2,1)}, bf16[32,32,128]{2,1,0:T(8,128)(2,1)S(1)}, u32[]{:S(2)}, u32[]{:S(2)}) collective-permute-start(bf16[32,32,128]{2,1,0:T(8,128)(2,1)} %get-tuple-element.132), channel_id=1, source_target_pairs={{0,8},{8,0},{16,24},{24,16},{1,9},{9,1},{17,25},{25,17},{2,10},{10... | collective-permute-start | bytes 786440 | tf_op jit(solution)/shard_map/ppermute | solution.py:151
  195.5 9.6 %collective-permute-done.9.refs_1_ = bf16[32,32,128]{2,1,0:T(8,128)(2,1)S(1)} collective-permute-done((bf16[32,32,128]{2,1,0:T(8,128)(2,1)}, bf16[32,32,128]{2,1,0:T(8,128)(2,1)S(1)}, u32[]{:S(2)}, u32[]{:S(2)}) %collective-permute-start.9) | collective-permute-done | bytes 262176 | tf_op jit(solution)/shard_map/ppermute | solution.py:151
  205.1 9.6 %collective-permute-done.10.refs_2_ = bf16[32,32,128]{2,1,0:T(8,128)(2,1)} collective-permute-done((bf16[32,32,128]{2,1,0:T(8,128)(2,1)}, bf16[32,32,128]{2,1,0:T(8,128)(2,1)}, u32[]{:S(2)}, u32[]{:S(2)}) %collective-permute-start.10) | collective-permute-done | bytes 262176 | tf_op jit(solution)/shard_map/ppermute | solution.py:151
  214.8 4.6 %all-to-all-start.6 = ((bf16[8,256,512]{2,1,0:T(8,128)(2,1)}), bf16[8,256,512]{2,1,0:T(8,128)(2,1)}, u32[]{:S(2)}, u32[]{:S(2)}) async-start(bf16[8,256,512]{2,1,0:T(8,128)(2,1)} %get-tuple-element.135), calls=%async_computation.6 | async-start | bytes 4194304 | tf_op jit(solution)/shard_map/all_to_all | solution.py:701
  219.4 5.4 %last_products_0.1 = (bf16[160,640]{1,0:T(8,128)(2,1)}, bf16[160,640]{1,0:T(8,128)(2,1)}, bf16[160,640]{1,0:T(8,128)(2,1)}, bf16[160,640]{1,0:T(8,128)(2,1)}) custom-call(bf16[8,2,128,512]{3,2,1,0:T(8,128)(2,1)} %bitcast.1.in_ref, bf16[640,512]{1,0:T(8,128)(2,1)} %get-tuple-element.136.back_ref, bf16[16,128,128]{2,1,0:T(8,128)(2,1)} %gate_ref.11, ...), custom_call_target="tpu_custom_call" | custom-call | tf_op jit(solution)/shard_map/last_products_0/pallas_call | solution.py:608
  224.8 5.2 %collective-permute-start.12 = (bf16[160,640]{1,0:T(8,128)(2,1)}, bf16[160,640]{1,0:T(8,128)(2,1)S(1)}, u32[]{:S(2)}, u32[]{:S(2)}) collective-permute-start(bf16[160,640]{1,0:T(8,128)(2,1)} %get-tuple-element.138), channel_id=1, source_target_pairs={{0,8},{8,0},{16,24},{24,16},{1,9},{9,1},{17,25},{25,17},{2,10},{10... | collective-permute-start | bytes 614408 | tf_op jit(solution)/shard_map/ppermute | solution.py:151
  234.4 3.9 %last_products_5.1 = (bf16[160,384]{1,0:T(8,128)(2,1)}, bf16[160,384]{1,0:T(8,128)(2,1)}, bf16[160,384]{1,0:T(8,128)(2,1)}, bf16[160,384]{1,0:T(8,128)(2,1)}) custom-call(bf16[8,2,128,512]{3,2,1,0:T(8,128)(2,1)} %bitcast.1.in_ref, bf16[640,512]{1,0:T(8,128)(2,1)} %get-tuple-element.136.back_ref, bf16[16,128,128]{2,1,0:T(8,128)(2,1)} %gate_ref.11, ...), custom_call_target="tpu_custom_call" | custom-call | tf_op jit(solution)/shard_map/last_products_5/pallas_call | solution.py:608
  241.7 6.1 %collective-permute-done.13.refs_2_ = bf16[160,640]{1,0:T(8,128)(2,1)S(1)} collective-permute-done((bf16[160,640]{1,0:T(8,128)(2,1)}, bf16[160,640]{1,0:T(8,128)(2,1)S(1)}, u32[]{:S(2)}, u32[]{:S(2)}) %collective-permute-start.13) | collective-permute-done | bytes 204832 | tf_op jit(solution)/shard_map/ppermute | solution.py:151
  248.4 4.4 %all-to-all-start.7 = ((bf16[8,256,512]{2,1,0:T(8,128)(2,1)}), bf16[8,256,512]{2,1,0:T(8,128)(2,1)}, u32[]{:S(2)}, u32[]{:S(2)}) async-start(bf16[8,256,512]{2,1,0:T(8,128)(2,1)} %get-tuple-element.151), calls=%async_computation.7 | async-start | bytes 4194304 | tf_op jit(solution)/shard_map/all_to_all | solution.py:701
  252.8 3.4 collective-permute-start.15
  258.7 3.8 %last_products_8.1 = (bf16[160,384]{1,0:T(8,128)(2,1)}, bf16[160,384]{1,0:T(8,128)(2,1)}, bf16[160,384]{1,0:T(8,128)(2,1)}, bf16[160,384]{1,0:T(8,128)(2,1)}) custom-call(bf16[8,2,128,512]{3,2,1,0:T(8,128)(2,1)} %bitcast.3.in_ref, bf16[640,512]{1,0:T(8,128)(2,1)} %get-tuple-element.136.back_ref, bf16[16,128,128]{2,1,0:T(8,128)(2,1)} %gate_ref.11, ...), custom_call_target="tpu_custom_call" | custom-call | tf_op jit(solution)/shard_map/last_products_8/pallas_call | solution.py:608
  267.6 5.4 %last_products_11.1 = (bf16[160,640]{1,0:T(8,128)(2,1)}, bf16[160,640]{1,0:T(8,128)(2,1)}, bf16[160,640]{1,0:T(8,128)(2,1)}, bf16[160,640]{1,0:T(8,128)(2,1)}) custom-call(bf16[8,2,128,512]{3,2,1,0:T(8,128)(2,1)} %bitcast.3.in_ref, bf16[640,512]{1,0:T(8,128)(2,1)} %get-tuple-element.136.back_ref, bf16[16,128,128]{2,1,0:T(8,128)(2,1)} %gate_ref.11, ...), custom_call_target="tpu_custom_call" | custom-call | tf_op jit(solution)/shard_map/last_products_11/pallas_call | solution.py:608
  273.0 6.4 %collective-permute-done.19.refs_2_ = bf16[160,384]{1,0:T(8,128)(2,1)S(1)} collective-permute-done((bf16[160,384]{1,0:T(8,128)(2,1)}, bf16[160,384]{1,0:T(8,128)(2,1)S(1)}, u32[]{:S(2)}, u32[]{:S(2)}) %collective-permute-start.19) | collective-permute-done | bytes 122912 | tf_op jit(solution)/shard_map/ppermute | solution.py:151
  279.4 4.4 %right_down.1 = bf16[8,256,512]{2,1,0:T(8,128)(2,1)} custom-call(bf16[8,256,512]{2,1,0:T(8,128)(2,1)} %all-to-all-done.7.in_ref, bf16[16,128,128]{2,1,0:T(8,128)(2,1)S(1)} %copy-done), custom_call_target="tpu_custom_call" | custom-call | tf_op jit(solution)/shard_map/right_down/pallas_call | solution.py:301
  283.8 4.4 %all-to-all-start.8 = ((bf16[8,256,512]{2,1,0:T(8,128)(2,1)}), bf16[8,256,512]{2,1,0:T(8,128)(2,1)}, u32[]{:S(2)}, u32[]{:S(2)}) async-start(bf16[8,256,512]{2,1,0:T(8,128)(2,1)} %right_down.1), calls=%async_computation.8 | async-start | bytes 4194304 | tf_op jit(solution)/shard_map/all_to_all | solution.py:701
  295.1 4.8 %unsort_0.1.refs_4_ = bf16[2048,640]{1,0:T(8,128)(2,1)} custom-call(bf16[640,640]{1,0:T(8,128)(2,1)} %get-tuple-element.98.home_ref, bf16[160,640]{1,0:T(8,128)(2,1)} %get-tuple-element.137.refs_0_, bf16[160,640]{1,0:T(8,128)(2,1)} %copy-done.15, bf16[160,640]{1,0:T(8,128)(2,1)} %copy-done.16, bf16[160,640]{1,0:T(8,128)(2,1)} %collective-permute-done.14.refs_3_), custom_call_target="tpu_custom_call" | custom-call | tf_op jit(solution)/shard_map/unsort_0/pallas_call | solution.py:171
  299.9 3.5 unsort_5.1.refs_4_
  303.4 3.7 %right_down_grad.1 = (bf16[2,16,32,128]{3,2,1,0:T(8,128)(2,1)}, bf16[2,16,32,128]{3,2,1,0:T(8,128)(2,1)}) custom-call(s32[1]{0:T(128)} %bitcast.own_ref, bf16[8,256,512]{2,1,0:T(8,128)(2,1)} %all-to-all-done.7.in_ref, bf16[8,256,512]{2,1,0:T(8,128)(2,1)} %all-to-all-done.1.in_ref.other_ref), custom_call_target="tpu_custom_call" | custom-call | tf_op jit(solution)/shard_map/right_down_grad/pallas_call | solution.py:421
  309.6 3.4 right_grads_1.1
  313.0 4.0 %collective-permute-start.25 = (bf16[2,16,32,128]{3,2,1,0:T(8,128)(2,1)}, bf16[2,16,32,128]{3,2,1,0:T(8,128)(2,1)S(1)}, u32[]{:S(2)}, u32[]{:S(2)}) collective-permute-start(bf16[2,16,32,128]{3,2,1,0:T(8,128)(2,1)} %get-tuple-element.165), channel_id=1, source_target_pairs={{0,8},{8,0},{16,24},{24,16},{1,9},{9,1},{17,25},{25,17},{2,10},{10... | collective-permute-start | bytes 786440 | tf_op jit(solution)/shard_map/ppermute | solution.py:363
  317.4 5.6 %collective-permute-done.25.refs_3_ = bf16[2,16,32,128]{3,2,1,0:T(8,128)(2,1)S(1)} collective-permute-done((bf16[2,16,32,128]{3,2,1,0:T(8,128)(2,1)}, bf16[2,16,32,128]{3,2,1,0:T(8,128)(2,1)S(1)}, u32[]{:S(2)}, u32[]{:S(2)}) %collective-permute-start.25) | collective-permute-done | bytes 262176 | tf_op jit(solution)/shard_map/ppermute | solution.py:363
  323.0 4.4 %left_down.1 = bf16[8,256,512]{2,1,0:T(8,128)(2,1)} custom-call(bf16[8,256,512]{2,1,0:T(8,128)(2,1)} %all-to-all-done.8.in_ref, bf16[16,128,128]{2,1,0:T(8,128)(2,1)S(1)} %copy-done.1), custom_call_target="tpu_custom_call" | custom-call | tf_op jit(solution)/shard_map/left_down/pallas_call | solution.py:301
  327.4 4.4 %all-to-all-start.9 = ((bf16[8,256,512]{2,1,0:T(8,128)(2,1)}), bf16[8,256,512]{2,1,0:T(8,128)(2,1)}, u32[]{:S(2)}, u32[]{:S(2)}) async-start(bf16[8,256,512]{2,1,0:T(8,128)(2,1)} %left_down.1), calls=%async_computation.9 | async-start | bytes 4194304 | tf_op jit(solution)/shard_map/all_to_all | solution.py:701
  342.1 3.5 unsort_8.1.refs_4_
  345.6 4.9 %unsort_11.1 = bf16[2048,640]{1,0:T(8,128)(2,1)} custom-call(bf16[640,640]{1,0:T(8,128)(2,1)} %get-tuple-element.98.home_ref, bf16[160,640]{1,0:T(8,128)(2,1)} %get-tuple-element.156.refs_0_, bf16[160,640]{1,0:T(8,128)(2,1)} %collective-permute-done.22.refs_1_, bf16[160,640]{1,0:T(8,128)(2,1)} %collective-permute-done.23.refs_2_, ...), custom_call_target="tpu_custom_call", output_to_operand_aliasing={{}: (5, {})} | custom-call | tf_op jit(solution)/shard_map/unsort_11/pallas_call | solution.py:171
  (128 shorter events, 80.3 us)
Async XLA Ops:
  5.3 31.9 %all-to-all-start = ((bf16[8,256,512]{2,1,0:T(8,128)(2,1)}), bf16[8,256,512]{2,1,0:T(8,128)(2,1)S(1)}, u32[]{:S(2)}, u32[]{:S(2)}) async-start(bf16[8,256,512]{2,1,0:T(8,128)(2,1)} %send_cotangent.1), calls=%async_computation | async-start | bytes 4194304 | tf_op jit(solution)/shard_map/all_to_all | solution.py:701
  17.0 13.3 %collective-permute-start = (bf16[160,512]{1,0:T(8,128)(2,1)}, bf16[160,512]{1,0:T(8,128)(2,1)S(1)}, u32[]{:S(2)}, u32[]{:S(2)}) collective-permute-start(bf16[160,512]{1,0:T(8,128)(2,1)} %get-tuple-element.100), channel_id=1, source_target_pairs={{0,8},{8,0},{16,24},{24,16},{1,9},{9,1},{17,25},{25,17},{2,10},{10... | collective-permute-start | bytes 491528 | tf_op jit(solution)/shard_map/ppermute | solution.py:151
  18.6 15.2 %collective-permute-start.1 = (bf16[160,512]{1,0:T(8,128)(2,1)}, bf16[160,512]{1,0:T(8,128)(2,1)S(1)}, u32[]{:S(2)}, u32[]{:S(2)}) collective-permute-start(bf16[160,512]{1,0:T(8,128)(2,1)} %get-tuple-element.101), channel_id=1, source_target_pairs={{0,16},{8,24},{16,0},{24,8},{1,17},{9,25},{17,1},{25,9},{2,18},{10... | collective-permute-start | bytes 491528 | tf_op jit(solution)/shard_map/ppermute | solution.py:151
  21.2 12.6 %collective-permute-start.2 = (bf16[160,512]{1,0:T(8,128)(2,1)}, bf16[160,512]{1,0:T(8,128)(2,1)S(1)}, u32[]{:S(2)}, u32[]{:S(2)}) collective-permute-start(bf16[160,512]{1,0:T(8,128)(2,1)} %get-tuple-element.102), channel_id=1, source_target_pairs={{0,24},{8,16},{16,8},{24,0},{1,25},{9,17},{17,9},{25,1},{2,26},{10... | collective-permute-start | bytes 491528 | tf_op jit(solution)/shard_map/ppermute | solution.py:151
  25.9 11.4 %copy-start.1 = (bf16[16,128,128]{2,1,0:T(8,128)(2,1)S(1)}, bf16[16,128,128]{2,1,0:T(8,128)(2,1)}, u32[]{:S(2)}) copy-start(bf16[16,128,128]{2,1,0:T(8,128)(2,1)} %factor_ref.7) | copy-start | bytes 1572868
  30.4 10.1 %copy-start.7 = (bf16[160,512]{1,0:T(8,128)(2,1)}, bf16[160,512]{1,0:T(8,128)(2,1)S(1)}, u32[]{:S(2)}) copy-start(bf16[160,512]{1,0:T(8,128)(2,1)S(1)} %collective-permute-done.refs_1_) | copy-start | bytes 491524
  40.5 31.1 %copy-start = (bf16[16,128,128]{2,1,0:T(8,128)(2,1)S(1)}, bf16[16,128,128]{2,1,0:T(8,128)(2,1)}, u32[]{:S(2)}) copy-start(bf16[16,128,128]{2,1,0:T(8,128)(2,1)} %factor_ref.6) | copy-start | bytes 1572868
  40.5 31.1 %all-to-all-start.1 = ((bf16[8,256,512]{2,1,0:T(8,128)(2,1)}), bf16[8,256,512]{2,1,0:T(8,128)(2,1)}, u32[]{:S(2)}, u32[]{:S(2)}) async-start(bf16[8,256,512]{2,1,0:T(8,128)(2,1)} %left_back_down.1), calls=%async_computation.1 | async-start | bytes 4194304 | tf_op jit(solution)/shard_map/all_to_all | solution.py:701
  45.0 13.2 %collective-permute-start.3 = (bf16[160,768]{1,0:T(8,128)(2,1)}, bf16[160,768]{1,0:T(8,128)(2,1)S(1)}, u32[]{:S(2)}, u32[]{:S(2)}) collective-permute-start(bf16[160,768]{1,0:T(8,128)(2,1)} %get-tuple-element.104), channel_id=1, source_target_pairs={{0,8},{8,0},{16,24},{24,16},{1,9},{9,1},{17,25},{25,17},{2,10},{10... | collective-permute-start | bytes 737288 | tf_op jit(solution)/shard_map/ppermute | solution.py:151
  46.6 20.6 %collective-permute-start.4 = (bf16[160,768]{1,0:T(8,128)(2,1)}, bf16[160,768]{1,0:T(8,128)(2,1)}, u32[]{:S(2)}, u32[]{:S(2)}) collective-permute-start(bf16[160,768]{1,0:T(8,128)(2,1)} %get-tuple-element.105), channel_id=1, source_target_pairs={{0,16},{8,24},{16,0},{24,8},{1,17},{9,25},{17,1},{25,9},{2,18},{10... | collective-permute-start | bytes 737288 | tf_op jit(solution)/shard_map/ppermute | solution.py:151
  49.2 18.0 %collective-permute-start.5 = (bf16[160,768]{1,0:T(8,128)(2,1)}, bf16[160,768]{1,0:T(8,128)(2,1)}, u32[]{:S(2)}, u32[]{:S(2)}) collective-permute-start(bf16[160,768]{1,0:T(8,128)(2,1)} %get-tuple-element.106), channel_id=1, source_target_pairs={{0,24},{8,16},{16,8},{24,0},{1,25},{9,17},{17,9},{25,1},{2,26},{10... | collective-permute-start | bytes 737288 | tf_op jit(solution)/shard_map/ppermute | solution.py:151
  58.2 17.7 %copy-start.3 = (bf16[160,768]{1,0:T(8,128)(2,1)}, bf16[160,768]{1,0:T(8,128)(2,1)S(1)}, u32[]{:S(2)}) copy-start(bf16[160,768]{1,0:T(8,128)(2,1)S(1)} %collective-permute-done.3.refs_5_) | copy-start | bytes 737284
  75.9 34.0 %all-to-all-start.2 = ((bf16[8,256,512]{2,1,0:T(8,128)(2,1)}), bf16[8,256,512]{2,1,0:T(8,128)(2,1)}, u32[]{:S(2)}, u32[]{:S(2)}) async-start(bf16[8,256,512]{2,1,0:T(8,128)(2,1)} %right_back_down.1), calls=%async_computation.2 | async-start | bytes 4194304 | tf_op jit(solution)/shard_map/all_to_all | solution.py:701
  80.3 13.2 %collective-permute-start.6 = (bf16[160,768]{1,0:T(8,128)(2,1)}, bf16[160,768]{1,0:T(8,128)(2,1)S(1)}, u32[]{:S(2)}, u32[]{:S(2)}) collective-permute-start(bf16[160,768]{1,0:T(8,128)(2,1)} %get-tuple-element.108), channel_id=1, source_target_pairs={{0,8},{8,0},{16,24},{24,16},{1,9},{9,1},{17,25},{25,17},{2,10},{10... | collective-permute-start | bytes 737288 | tf_op jit(solution)/shard_map/ppermute | solution.py:151
  81.9 20.5 %collective-permute-start.7 = (bf16[160,768]{1,0:T(8,128)(2,1)}, bf16[160,768]{1,0:T(8,128)(2,1)S(1)}, u32[]{:S(2)}, u32[]{:S(2)}) collective-permute-start(bf16[160,768]{1,0:T(8,128)(2,1)} %get-tuple-element.109), channel_id=1, source_target_pairs={{0,16},{8,24},{16,0},{24,8},{1,17},{9,25},{17,1},{25,9},{2,18},{10... | collective-permute-start | bytes 737288 | tf_op jit(solution)/shard_map/ppermute | solution.py:151
  84.5 17.9 %collective-permute-start.8 = (bf16[160,768]{1,0:T(8,128)(2,1)}, bf16[160,768]{1,0:T(8,128)(2,1)S(1)}, u32[]{:S(2)}, u32[]{:S(2)}) collective-permute-start(bf16[160,768]{1,0:T(8,128)(2,1)} %get-tuple-element.110), channel_id=1, source_target_pairs={{0,24},{8,16},{16,8},{24,0},{1,25},{9,17},{17,9},{25,1},{2,26},{10... | collective-permute-start | bytes 737288 | tf_op jit(solution)/shard_map/ppermute | solution.py:151
  109.9 31.0 %all-to-all-start.3 = ((bf16[8,512,256]{2,1,0:T(8,128)(2,1)}), bf16[8,512,256]{2,1,0:T(8,128)(2,1)}, u32[]{:S(2)}, u32[]{:S(2)}) async-start(bf16[8,512,256]{2,1,0:T(8,128)(2,1)} %get-tuple-element.120), calls=%async_computation.3 | async-start | bytes 4194304 | tf_op jit(solution)/shard_map/all_to_all | solution.py:701
  140.9 31.0 %all-to-all-start.4 = ((bf16[8,512,256]{2,1,0:T(8,128)(2,1)}), bf16[8,512,256]{2,1,0:T(8,128)(2,1)}, u32[]{:S(2)}, u32[]{:S(2)}) async-start(bf16[8,512,256]{2,1,0:T(8,128)(2,1)} %get-tuple-element.121), calls=%async_computation.4 | async-start | bytes 4194304 | tf_op jit(solution)/shard_map/all_to_all | solution.py:701
  183.8 31.0 %all-to-all-start.5 = ((bf16[8,256,512]{2,1,0:T(8,128)(2,1)}), bf16[8,256,512]{2,1,0:T(8,128)(2,1)}, u32[]{:S(2)}, u32[]{:S(2)}) async-start(bf16[8,256,512]{2,1,0:T(8,128)(2,1)} %get-tuple-element.130), calls=%async_computation.5 | async-start | bytes 4194304 | tf_op jit(solution)/shard_map/all_to_all | solution.py:701
  188.1 17.0 %collective-permute-start.9 = (bf16[32,32,128]{2,1,0:T(8,128)(2,1)}, bf16[32,32,128]{2,1,0:T(8,128)(2,1)S(1)}, u32[]{:S(2)}, u32[]{:S(2)}) collective-permute-start(bf16[32,32,128]{2,1,0:T(8,128)(2,1)} %get-tuple-element.132), channel_id=1, source_target_pairs={{0,8},{8,0},{16,24},{24,16},{1,9},{9,1},{17,25},{25,17},{2,10},{10... | collective-permute-start | bytes 786440 | tf_op jit(solution)/shard_map/ppermute | solution.py:151
  193.0 21.7 %collective-permute-start.10 = (bf16[32,32,128]{2,1,0:T(8,128)(2,1)}, bf16[32,32,128]{2,1,0:T(8,128)(2,1)}, u32[]{:S(2)}, u32[]{:S(2)}) collective-permute-start(bf16[32,32,128]{2,1,0:T(8,128)(2,1)} %get-tuple-element.133), channel_id=1, source_target_pairs={{0,16},{8,24},{16,0},{24,8},{1,17},{9,25},{17,1},{25,9},{2,18},{10... | collective-permute-start | bytes 786440 | tf_op jit(solution)/shard_map/ppermute | solution.py:151
  194.1 20.6 %collective-permute-start.11 = (bf16[32,32,128]{2,1,0:T(8,128)(2,1)}, bf16[32,32,128]{2,1,0:T(8,128)(2,1)}, u32[]{:S(2)}, u32[]{:S(2)}) collective-permute-start(bf16[32,32,128]{2,1,0:T(8,128)(2,1)} %get-tuple-element.134), channel_id=1, source_target_pairs={{0,24},{8,16},{16,8},{24,0},{1,25},{9,17},{17,9},{25,1},{2,26},{10... | collective-permute-start | bytes 786440 | tf_op jit(solution)/shard_map/ppermute | solution.py:151
  214.8 33.0 %all-to-all-start.6 = ((bf16[8,256,512]{2,1,0:T(8,128)(2,1)}), bf16[8,256,512]{2,1,0:T(8,128)(2,1)}, u32[]{:S(2)}, u32[]{:S(2)}) async-start(bf16[8,256,512]{2,1,0:T(8,128)(2,1)} %get-tuple-element.135), calls=%async_computation.6 | async-start | bytes 4194304 | tf_op jit(solution)/shard_map/all_to_all | solution.py:701
  224.8 16.9 %collective-permute-start.12 = (bf16[160,640]{1,0:T(8,128)(2,1)}, bf16[160,640]{1,0:T(8,128)(2,1)S(1)}, u32[]{:S(2)}, u32[]{:S(2)}) collective-permute-start(bf16[160,640]{1,0:T(8,128)(2,1)} %get-tuple-element.138), channel_id=1, source_target_pairs={{0,8},{8,0},{16,24},{24,16},{1,9},{9,1},{17,25},{25,17},{2,10},{10... | collective-permute-start | bytes 614408 | tf_op jit(solution)/shard_map/ppermute | solution.py:151
  229.9 17.8 %collective-permute-start.13 = (bf16[160,640]{1,0:T(8,128)(2,1)}, bf16[160,640]{1,0:T(8,128)(2,1)S(1)}, u32[]{:S(2)}, u32[]{:S(2)}) collective-permute-start(bf16[160,640]{1,0:T(8,128)(2,1)} %get-tuple-element.139), channel_id=1, source_target_pairs={{0,16},{8,24},{16,0},{24,8},{1,17},{9,25},{17,1},{25,9},{2,18},{10... | collective-permute-start | bytes 614408 | tf_op jit(solution)/shard_map/ppermute | solution.py:151
  231.0 16.8 %collective-permute-start.14 = (bf16[160,640]{1,0:T(8,128)(2,1)}, bf16[160,640]{1,0:T(8,128)(2,1)}, u32[]{:S(2)}, u32[]{:S(2)}) collective-permute-start(bf16[160,640]{1,0:T(8,128)(2,1)} %get-tuple-element.140), channel_id=1, source_target_pairs={{0,24},{8,16},{16,8},{24,0},{1,25},{9,17},{17,9},{25,1},{2,26},{10... | collective-permute-start | bytes 614408 | tf_op jit(solution)/shard_map/ppermute | solution.py:151
  248.4 31.0 %all-to-all-start.7 = ((bf16[8,256,512]{2,1,0:T(8,128)(2,1)}), bf16[8,256,512]{2,1,0:T(8,128)(2,1)}, u32[]{:S(2)}, u32[]{:S(2)}) async-start(bf16[8,256,512]{2,1,0:T(8,128)(2,1)} %get-tuple-element.151), calls=%async_computation.7 | async-start | bytes 4194304 | tf_op jit(solution)/shard_map/all_to_all | solution.py:701
  252.8 12.7 %collective-permute-start.15 = (bf16[160,384]{1,0:T(8,128)(2,1)}, bf16[160,384]{1,0:T(8,128)(2,1)S(1)}, u32[]{:S(2)}, u32[]{:S(2)}) collective-permute-start(bf16[160,384]{1,0:T(8,128)(2,1)} %get-tuple-element.142), channel_id=1, source_target_pairs={{0,8},{8,0},{16,24},{24,16},{1,9},{9,1},{17,25},{25,17},{2,10},{10... | collective-permute-start | bytes 368648 | tf_op jit(solution)/shard_map/ppermute | solution.py:151
  256.2 16.7 %collective-permute-start.16 = (bf16[160,384]{1,0:T(8,128)(2,1)}, bf16[160,384]{1,0:T(8,128)(2,1)S(1)}, u32[]{:S(2)}, u32[]{:S(2)}) collective-permute-start(bf16[160,384]{1,0:T(8,128)(2,1)} %get-tuple-element.143), channel_id=1, source_target_pairs={{0,16},{8,24},{16,0},{24,8},{1,17},{9,25},{17,1},{25,9},{2,18},{10... | collective-permute-start | bytes 368648 | tf_op jit(solution)/shard_map/ppermute | solution.py:151
  257.3 15.7 %collective-permute-start.17 = (bf16[160,384]{1,0:T(8,128)(2,1)}, bf16[160,384]{1,0:T(8,128)(2,1)S(1)}, u32[]{:S(2)}, u32[]{:S(2)}) collective-permute-start(bf16[160,384]{1,0:T(8,128)(2,1)} %get-tuple-element.144), channel_id=1, source_target_pairs={{0,24},{8,16},{16,8},{24,0},{1,25},{9,17},{17,9},{25,1},{2,26},{10... | collective-permute-start | bytes 368648 | tf_op jit(solution)/shard_map/ppermute | solution.py:151
  262.5 10.5 %collective-permute-start.18 = (bf16[160,384]{1,0:T(8,128)(2,1)}, bf16[160,384]{1,0:T(8,128)(2,1)S(1)}, u32[]{:S(2)}, u32[]{:S(2)}) collective-permute-start(bf16[160,384]{1,0:T(8,128)(2,1)} %get-tuple-element.153), channel_id=1, source_target_pairs={{0,8},{8,0},{16,24},{24,16},{1,9},{9,1},{17,25},{25,17},{2,10},{10... | collective-permute-start | bytes 368648 | tf_op jit(solution)/shard_map/ppermute | solution.py:151
  263.5 15.8 %collective-permute-start.19 = (bf16[160,384]{1,0:T(8,128)(2,1)}, bf16[160,384]{1,0:T(8,128)(2,1)S(1)}, u32[]{:S(2)}, u32[]{:S(2)}) collective-permute-start(bf16[160,384]{1,0:T(8,128)(2,1)} %get-tuple-element.154), channel_id=1, source_target_pairs={{0,16},{8,24},{16,0},{24,8},{1,17},{9,25},{17,1},{25,9},{2,18},{10... | collective-permute-start | bytes 368648 | tf_op jit(solution)/shard_map/ppermute | solution.py:151
  266.2 13.2 %collective-permute-start.20 = (bf16[160,384]{1,0:T(8,128)(2,1)}, bf16[160,384]{1,0:T(8,128)(2,1)S(1)}, u32[]{:S(2)}, u32[]{:S(2)}) collective-permute-start(bf16[160,384]{1,0:T(8,128)(2,1)} %get-tuple-element.155), channel_id=1, source_target_pairs={{0,24},{8,16},{16,8},{24,0},{1,25},{9,17},{17,9},{25,1},{2,26},{10... | collective-permute-start | bytes 368648 | tf_op jit(solution)/shard_map/ppermute | solution.py:151
  273.0 10.8 %copy-start.21 = (bf16[160,384]{1,0:T(8,128)(2,1)}, bf16[160,384]{1,0:T(8,128)(2,1)S(1)}, u32[]{:S(2)}) copy-start(bf16[160,384]{1,0:T(8,128)(2,1)S(1)} %collective-permute-done.18.refs_1_) | copy-start | bytes 368644
  283.8 39.1 %all-to-all-start.8 = ((bf16[8,256,512]{2,1,0:T(8,128)(2,1)}), bf16[8,256,512]{2,1,0:T(8,128)(2,1)}, u32[]{:S(2)}, u32[]{:S(2)}) async-start(bf16[8,256,512]{2,1,0:T(8,128)(2,1)} %right_down.1), calls=%async_computation.8 | async-start | bytes 4194304 | tf_op jit(solution)/shard_map/all_to_all | solution.py:701
  288.2 20.0 %collective-permute-start.22 = (bf16[160,640]{1,0:T(8,128)(2,1)}, bf16[160,640]{1,0:T(8,128)(2,1)}, u32[]{:S(2)}, u32[]{:S(2)}) collective-permute-start(bf16[160,640]{1,0:T(8,128)(2,1)} %get-tuple-element.157), channel_id=1, source_target_pairs={{0,8},{8,0},{16,24},{24,16},{1,9},{9,1},{17,25},{25,17},{2,10},{10... | collective-permute-start | bytes 614408 | tf_op jit(solution)/shard_map/ppermute | solution.py:151
  291.6 18.0 %collective-permute-start.23 = (bf16[160,640]{1,0:T(8,128)(2,1)}, bf16[160,640]{1,0:T(8,128)(2,1)}, u32[]{:S(2)}, u32[]{:S(2)}) collective-permute-start(bf16[160,640]{1,0:T(8,128)(2,1)} %get-tuple-element.158), channel_id=1, source_target_pairs={{0,16},{8,24},{16,0},{24,8},{1,17},{9,25},{17,1},{25,9},{2,18},{10... | collective-permute-start | bytes 614408 | tf_op jit(solution)/shard_map/ppermute | solution.py:151
  292.7 16.9 %collective-permute-start.24 = (bf16[160,640]{1,0:T(8,128)(2,1)}, bf16[160,640]{1,0:T(8,128)(2,1)}, u32[]{:S(2)}, u32[]{:S(2)}) collective-permute-start(bf16[160,640]{1,0:T(8,128)(2,1)} %get-tuple-element.159), channel_id=1, source_target_pairs={{0,24},{8,16},{16,8},{24,0},{1,25},{9,17},{17,9},{25,1},{2,26},{10... | collective-permute-start | bytes 614408 | tf_op jit(solution)/shard_map/ppermute | solution.py:151
  294.1 23.0 %collective-permute-start.21 = (bf16[2,16,32,128]{3,2,1,0:T(8,128)(2,1)}, bf16[2,16,32,128]{3,2,1,0:T(8,128)(2,1)S(1)}, u32[]{:S(2)}, u32[]{:S(2)}) collective-permute-start(bf16[2,16,32,128]{3,2,1,0:T(8,128)(2,1)} %get-tuple-element.149), channel_id=1, source_target_pairs={{0,8},{8,0},{16,24},{24,16},{1,9},{9,1},{17,25},{25,17},{2,10},{10... | collective-permute-start | bytes 786440 | tf_op jit(solution)/shard_map/ppermute | solution.py:363
  307.2 10.2 %collective-permute-start.26 = (bf16[2,16,32,128]{3,2,1,0:T(8,128)(2,1)}, bf16[2,16,32,128]{3,2,1,0:T(8,128)(2,1)S(1)}, u32[]{:S(2)}, u32[]{:S(2)}) collective-permute-start(bf16[2,16,32,128]{3,2,1,0:T(8,128)(2,1)} %get-tuple-element.163), channel_id=1, source_target_pairs={{0,8},{8,0},{16,24},{24,16},{1,9},{9,1},{17,25},{25,17},{2,10},{10... | collective-permute-start | bytes 786440 | tf_op jit(solution)/shard_map/ppermute | solution.py:363
  313.0 10.0 %collective-permute-start.25 = (bf16[2,16,32,128]{3,2,1,0:T(8,128)(2,1)}, bf16[2,16,32,128]{3,2,1,0:T(8,128)(2,1)S(1)}, u32[]{:S(2)}, u32[]{:S(2)}) collective-permute-start(bf16[2,16,32,128]{3,2,1,0:T(8,128)(2,1)} %get-tuple-element.165), channel_id=1, source_target_pairs={{0,8},{8,0},{16,24},{24,16},{1,9},{9,1},{17,25},{25,17},{2,10},{10... | collective-permute-start | bytes 786440 | tf_op jit(solution)/shard_map/ppermute | solution.py:363
  317.0 10.4 %copy-start.11 = (bf16[2,16,32,128]{3,2,1,0:T(8,128)(2,1)}, bf16[2,16,32,128]{3,2,1,0:T(8,128)(2,1)S(1)}, u32[]{:S(2)}) copy-start(bf16[2,16,32,128]{3,2,1,0:T(8,128)(2,1)S(1)} %collective-permute-done.21.refs_1_) | copy-start | bytes 786436
  327.4 31.0 %all-to-all-start.9 = ((bf16[8,256,512]{2,1,0:T(8,128)(2,1)}), bf16[8,256,512]{2,1,0:T(8,128)(2,1)}, u32[]{:S(2)}, u32[]{:S(2)}) async-start(bf16[8,256,512]{2,1,0:T(8,128)(2,1)} %left_down.1), calls=%async_computation.9 | async-start | bytes 4194304 | tf_op jit(solution)/shard_map/all_to_all | solution.py:701
  334.9 16.8 %collective-permute-start.30 = (bf16[2,16,32,128]{3,2,1,0:T(8,128)(2,1)}, bf16[2,16,32,128]{3,2,1,0:T(8,128)(2,1)S(1)}, u32[]{:S(2)}, u32[]{:S(2)}) collective-permute-start(bf16[2,16,32,128]{3,2,1,0:T(8,128)(2,1)} %get-tuple-element.181), channel_id=1, source_target_pairs={{0,8},{8,0},{16,24},{24,16},{1,9},{9,1},{17,25},{25,17},{2,10},{10... | collective-permute-start | bytes 786440 | tf_op jit(solution)/shard_map/ppermute | solution.py:363
  339.2 16.8 %collective-permute-start.28 = (bf16[1,16,32,128]{3,2,1,0:T(8,128)(2,1)}, bf16[1,16,32,128]{3,2,1,0:T(8,128)(2,1)S(1)}, u32[]{:S(2)}, u32[]{:S(2)}) collective-permute-start(bf16[1,16,32,128]{3,2,1,0:T(8,128)(2,1)} %get-tuple-element.171), channel_id=1, source_target_pairs={{0,16},{8,24},{16,0},{24,8},{1,17},{9,25},{17,1},{25,9},{2,18},{10... | collective-permute-start | bytes 393224 | tf_op jit(solution)/shard_map/ppermute | solution.py:363
  340.4 20.7 %collective-permute-start.27 = (bf16[1,16,32,128]{3,2,1,0:T(8,128)(2,1)}, bf16[1,16,32,128]{3,2,1,0:T(8,128)(2,1)S(1)}, u32[]{:S(2)}, u32[]{:S(2)}) collective-permute-start(bf16[1,16,32,128]{3,2,1,0:T(8,128)(2,1)} %get-tuple-element.169), channel_id=1, source_target_pairs={{0,16},{8,24},{16,0},{24,8},{1,17},{9,25},{17,1},{25,9},{2,18},{10... | collective-permute-start | bytes 393224 | tf_op jit(solution)/shard_map/ppermute | solution.py:363
  350.5 12.9 %collective-permute-start.29 = (bf16[1,16,32,128]{3,2,1,0:T(8,128)(2,1)S(1)}, bf16[1,16,32,128]{3,2,1,0:T(8,128)(2,1)S(1)}, u32[]{:S(2)}, u32[]{:S(2)}) collective-permute-start(bf16[1,16,32,128]{3,2,1,0:T(8,128)(2,1)S(1)} %copy-done.28), channel_id=1, source_target_pairs={{0,16},{8,24},{16,0},{24,8},{1,17},{9,25},{17,1},{25,9},{2,18},{10... | collective-permute-start | bytes 393224 | tf_op jit(solution)/shard_map/ppermute | solution.py:363
  354.2 11.7 %collective-permute-start.31 = (bf16[1,16,32,128]{3,2,1,0:T(8,128)(2,1)}, bf16[1,16,32,128]{3,2,1,0:T(8,128)(2,1)S(1)}, u32[]{:S(2)}, u32[]{:S(2)}) collective-permute-start(bf16[1,16,32,128]{3,2,1,0:T(8,128)(2,1)} %get-tuple-element.185), channel_id=1, source_target_pairs={{0,16},{8,24},{16,0},{24,8},{1,17},{9,25},{17,1},{25,9},{2,18},{10... | collective-permute-start | bytes 393224 | tf_op jit(solution)/shard_map/ppermute | solution.py:363
  (23 other events, 94.2 us)

commit v5 on v4

--- a/solution.py
+++ b/solution.py
@@ -275,7 +275,7 @@
 
 
 def send_cotangent(plan, cotangent):
-    step = step_of(plan.tok)
+    step = 128
     return pl.pallas_call(
         functools.partial(cotangent_kernel, plan),
         grid=(plan.tok // step,),
@@ -455,7 +455,7 @@
     plan.store(out_ref, 1, ups)
 
 
-def first_products(plan, pieces, back_t, right_gate, right_up, half):
+def first_products(plan, pieces, back_t, right_gate, right_up, half, offset):
     groups = len(pieces[0])
     feats = plan.held * plan.width
     slabs = [slab for piece in pieces for slab in piece]
@@ -465,7 +465,7 @@
         grid=(1,),
         in_specs=[whole(slab) for slab in slabs]
         + [
-            pl.BlockSpec((plan.tok, back_t.shape[1]), lambda i: (half, 0)),
+            pl.BlockSpec((plan.tok, back_t.shape[1]), lambda i: (offset, 0)),
             whole(right_gate),
             whole(right_up),
         ],
@@ -531,24 +531,25 @@
 
 
 def middle(
-    plan, full, own, spreads, hidden_grad, left_gate, left_up, scale, groups, half, halves, before
+    plan, full, own, spreads, hidden_grad, left_gate, left_up, scale, groups, half, offset, last,
+    before,
 ):
     step = plan.tok
-    first, last = half == 0, half == halves - 1
+    first = half == 0
     sums_shape = (2 * plan.held,) + left_gate.shape[1:]
     if last:
         sums = [cut_shape(2 * plan.held, left_gate, groups)] * groups
     else:
         sums = [pltpu.HBM(sums_shape, F32)]
     kept = pl.BlockSpec(memory_space=pl.ANY)
-    here = full.sent_spec(1, step, half)
+    here = full.sent_spec(1, step, offset)
     outs = pl.pallas_call(
         functools.partial(middle_kernel, plan, scale, first, last),
         grid=(1,),
         in_specs=[
             pl.BlockSpec(memory_space=pltpu.SMEM),
             plan.arrived_spec(2, step),
-            full.arrived_spec(1, step, half),
+            full.arrived_spec(1, step, offset),
             whole(left_gate),
             whole(left_up),
         ]
@@ -557,7 +558,7 @@
         out_shape=[full.sent_shape(1)] * 3 + sums,
         input_output_aliases={} if first else {6: 0, 7: 1, 8: 2},
         scratch_shapes=[pltpu.VMEM(sums_shape, F32)] + [scratch_for(plan, step)] * 3,
-        compiler_params=params(40),
+        compiler_params=params(48),
         name=f"middle_{half}",
     )(own, spreads, hidden_grad, *in_hbm(left_gate, left_up, *before))
     return outs[:3], outs[3:]
@@ -573,17 +574,21 @@
     )
 
 
-def spread_form(plan, arrived, count, offset):
+def spread_form(plan, arrived):
     size = plan.piece // 2
     if plan.direct:
-        return arrived.reshape(plan.peers, 2, size, plan.tok), pl.BlockSpec(
+        return in_hbm(arrived.reshape(plan.peers, 2, size, plan.tok))[0]
+    array = arrived.reshape(plan.peers, 2, plan.held // 2, plan.held, plan.tok)
+    array = array.transpose(1, 2, 0, 3, 4).reshape(2, plan.held // 2, plan.width, plan.tok)
+    return in_hbm(array)[0]
+
+
+def spread_spec(plan, count, offset):
+    if plan.direct:
+        return pl.BlockSpec(
             (plan.peers, 2, count * plan.held, plan.tok), lambda i: (0, 0, i + offset, 0)
         )
-    array = arrived.reshape(plan.peers, 2, plan.held // 2, plan.held, plan.tok)
-    array = array.transpose(1, 2, 0, 3, 4).reshape(2, plan.held // 2, plan.width, plan.tok)
-    return array, pl.BlockSpec(
-        (2, count, plan.width, plan.tok), lambda i: (0, i + offset, 0, 0)
-    )
+    return pl.BlockSpec((2, count, plan.width, plan.tok), lambda i: (0, i + offset, 0, 0))
 
 
 def last_kernel(plan, in_ref, back_ref, gate_ref, up_ref, *slab_refs):
@@ -602,7 +607,7 @@
     offset = start % (plan.held // 2 // unit)
     lanes = back.shape[0]
     cap = lanes // groups
-    arrived, arrived_spec = spread_form(plan, arrived, unit, offset)
+    arrived_spec = spread_spec(plan, unit, offset)
     factor_spec = pl.BlockSpec((unit,) + right_gate.shape[1:], lambda i: (start + i, 0, 0))
     size = unit * plan.width
     return pl.pallas_call(
@@ -629,14 +634,16 @@
 
 def right_grads(plan, own, arrived, packed, factor, scale, groups, which):
     count = plan.held // 2
-    arrived, arrived_spec = spread_form(plan, arrived, count, 0)
-    rows = packed[0].shape[0]
+    arrived_spec = spread_spec(plan, count, 0)
     outs = split_shapes(2 * count, factor, groups)
     return pl.pallas_call(
         functools.partial(right_grads_kernel, plan, scale, len(packed)),
         grid=(1,),
         in_specs=[pl.BlockSpec(memory_space=pltpu.SMEM), arrived_spec]
-        + [pl.BlockSpec((rows, count * plan.width), lambda i: (0, which))] * len(packed),
+        + [
+            pl.BlockSpec((array.shape[0], count * plan.width), lambda i: (0, which))
+            for array in packed
+        ],
         out_specs=[whole(out) for out in outs],
         out_shape=outs,
         scratch_shapes=[pltpu.VMEM((2 * count,) + factor.shape[1:], F32)],
@@ -688,10 +695,11 @@
     peers = lax.axis_size("feat")
     cap = 5 * tok // (4 * groups)
     scale = (tok * groups) ** (-0.5)
-    halves = 2 if tok % 256 == 0 else 1
-    halves = 2 if tok % 256 == 0 else 1
+    sizes = [3 * tok // 4, tok // 4] if tok % 512 == 0 else [tok]
+    offsets = [0, 3][: len(sizes)]
+    halves = len(sizes)
     plan = Plan(peers, held, width, tok)
-    part = Plan(peers, held, width, tok // halves)
+    parts = [Plan(peers, held, width, size) for size in sizes]
     there, unit = pieces_of(
         held // 4, (held - held // 4) // 2, held - held // 4 - (held - held // 4) // 2
     )
@@ -720,12 +728,15 @@
     hidden_grad = swap(hidden_grad)
 
     packed, spreads = zip(
-        *[first_products(part, rows, back_t, right_gate, right_up, h) for h in range(halves)]
+        *[
+            first_products(parts[h], rows, back_t, right_gate, right_up, h, offsets[h])
+            for h in range(halves)
+        ]
     )
     arrived, moved = [], hidden_grad
     for h in range(halves):
         moved = move(after(spreads[h], moved))
-        arrived.append(part.arranged(moved))
+        arrived.append(parts[h].arranged(moved))
     if halves > 1:
         arrived[0] = after(arrived[0], spreads[1])
     before = ()
@@ -733,13 +744,13 @@
         if h:
             arrived[h] = after(arrived[h], before[0])
         (hidden, low, high), left_sums = middle(
-            part, plan, own, arrived[h], hidden_grad, left_gate, left_up, scale, groups, h, halves,
-            before,
+            parts[h], plan, own, arrived[h], hidden_grad, left_gate, left_up, scale, groups, h,
+            offsets[h], h == halves - 1, before,
         )
         before = (left_sums[0], hidden, low, high)
-    low = move(low)
+    low = spread_form(plan, move(low))
     left_sums = exchange_rows(left_sums, groups)
-    high = move(after(high, low, *left_sums))
+    high = spread_form(plan, move(after(high, low, *left_sums)))
     grad_left_gate, grad_left_up = sums_of([left_sums], 2, "sum_left")
     half = held // 2
     most = max(half * 5 // 8, 1)
@@ -768,7 +779,7 @@
     down_spread = swap(down_spread)
     right_high = (right_high[0], swap_rows(right_high[1], 1, groups))
     down_grad = (down_grad[0], swap_rows(down_grad[1], 1, groups))
-    down_spread = after(down_spread, right_low[1], right_high[1], down_grad[1])
+    down_spread = after(down_spread, right_low[1], right_high[0], down_grad[1])
     result = product(plan, down_spread, left_down, TN, "left_down")
     left_down_grad = factor_grad(
         plan, own, after(down_spread, result), out_grads, left_down, scale, groups,

time: 371 us -> 371 us (level)
  starting transfers between devices: 103 us -> 96.6 us
  waiting for transfers between devices: 123 us -> 129 us
  local copies, waits for them, and re-layouts: 4.82 us -> 9.87 us
  Pallas kernels: 136 us -> 132 us
    ppermute x24, waiting for transfers between devices: 72 us -> 82.4 us  [exchange(): received.append(lax.ppermute(arrays[k], axis, pairs))]
    unnamed x58 -> x104, local copies, waits for them, and re-layouts: 4.8 us -> 9.86 us
where the time goes in v5:
time: 371 us; the launch traced here: 368 us
  Pallas kernels  132 us (36%)
  waiting for transfers between devices  129 us (35%)
  starting transfers between devices  96.6 us (26%)
  local copies, waits for them, and re-layouts  9.87 us (3%)
    ppermute x24, waiting for transfers between devices, exchange(): received.append(lax.ppermute(arrays[k], axis, pairs))  82.4 us
    ppermute x24, starting transfers between devices, exchange(): received.append(lax.ppermute(arrays[k], axis, pairs))  43.5 us
    all_to_all x10, starting transfers between devices, move(): lax.all_to_all(array, 'feat', split_axis=0, concat_axis=0, tiled=True)  41.7 us
    all_to_all x10, waiting for transfers between devices, move(): lax.all_to_all(array, 'feat', split_axis=0, concat_axis=0, tiled=True)  41.4 us
    pallas_call x2, Pallas kernels, middle(): pl.pallas_call(functools.partial(middle_kernel, plan, scale, first, last)...  22.8 us
    pallas_call x4, Pallas kernels, last_products(): pl.pallas_call(functools.partial(last_kernel, plan), grid=(count,), in_sp...  18.5 us
    pallas_call x4, Pallas kernels, unsort(): pl.pallas_call(functools.partial(unsort_kernel, groups), grid=(count,), i...  16.7 us
    pallas_call x4, Pallas kernels, product(): pl.pallas_call(functools.partial(product_kernel, plan, over), grid=(plan....  14.2 us
  transfers between devices with their start and end apart: 42, of which 19 were waited for; matrix products, arithmetic and copies ran while one was open for 0% of the time, Pallas kernels for 28%

profile of v5, /device:TPU:0, one launch (start us, length us, event | category | flops | bytes accessed | tf_op | source)
XLA Modules:
  0.0 368.3 jit_solution(17602689147536172739)
XLA Ops:
  0.6 4.9 %send_cotangent.1 = bf16[8,256,512]{2,1,0:T(8,128)(2,1)} custom-call(bf16[2048,512]{1,0:T(8,128)(2,1)} %in_ref.1), custom_call_target="tpu_custom_call" | custom-call | tf_op jit(solution)/shard_map/send_cotangent/pallas_call | solution.py:279
  5.5 5.3 %all-to-all-start = ((bf16[8,256,512]{2,1,0:T(8,128)(2,1)}), bf16[8,256,512]{2,1,0:T(8,128)(2,1)S(1)}, u32[]{:S(2)}, u32[]{:S(2)}) async-start(bf16[8,256,512]{2,1,0:T(8,128)(2,1)} %send_cotangent.1), calls=%async_computation | async-start | bytes 4194304 | tf_op jit(solution)/shard_map/all_to_all | solution.py:709
  13.9 3.3 mix_and_sort_0.1
  21.6 4.5 %mix_and_sort_5.1 = (bf16[160,768]{1,0:T(8,128)(2,1)}, bf16[160,768]{1,0:T(8,128)(2,1)}, bf16[160,768]{1,0:T(8,128)(2,1)}, bf16[160,768]{1,0:T(8,128)(2,1)}) custom-call(f32[3]{0:T(128)S(1)} %copy-done.10, bf16[3,2048,640]{2,1,0:T(8,128)(2,1)} %earlier_ref.5, bf16[640,640]{1,0:T(8,128)(2,1)} %get-tuple-element.98.home_ref), custom_call_target="tpu_custom_call" | custom-call | tf_op jit(solution)/shard_map/mix_and_sort_5/pallas_call | solution.py:125
  26.0 4.5 %mix_and_sort_2.1 = (bf16[160,768]{1,0:T(8,128)(2,1)}, bf16[160,768]{1,0:T(8,128)(2,1)}, bf16[160,768]{1,0:T(8,128)(2,1)}, bf16[160,768]{1,0:T(8,128)(2,1)}) custom-call(f32[3]{0:T(128)S(1)} %copy-done.10, bf16[3,2048,640]{2,1,0:T(8,128)(2,1)} %earlier_ref.5, bf16[640,640]{1,0:T(8,128)(2,1)} %get-tuple-element.98.home_ref), custom_call_target="tpu_custom_call" | custom-call | tf_op jit(solution)/shard_map/mix_and_sort_2/pallas_call | solution.py:125
  30.6 3.4 collective-permute-done.1.refs_2_
  34.0 3.5 all-to-all-done.in_ref.other_ref
  40.7 3.7 %all-to-all-start.1 = ((bf16[8,256,512]{2,1,0:T(8,128)(2,1)}), bf16[8,256,512]{2,1,0:T(8,128)(2,1)S(1)}, u32[]{:S(2)}, u32[]{:S(2)}) async-start(bf16[8,256,512]{2,1,0:T(8,128)(2,1)} %left_back_down.1), calls=%async_computation.1 | async-start | bytes 4194304 | tf_op jit(solution)/shard_map/all_to_all | solution.py:709
  48.9 8.8 %collective-permute-done.3.refs_5_ = bf16[160,768]{1,0:T(8,128)(2,1)S(1)} collective-permute-done((bf16[160,768]{1,0:T(8,128)(2,1)}, bf16[160,768]{1,0:T(8,128)(2,1)S(1)}, u32[]{:S(2)}, u32[]{:S(2)}) %collective-permute-start.3) | collective-permute-done | bytes 245792 | tf_op jit(solution)/shard_map/ppermute | solution.py:151
  57.7 8.9 %collective-permute-done.4.refs_6_ = bf16[160,768]{1,0:T(8,128)(2,1)S(1)} collective-permute-done((bf16[160,768]{1,0:T(8,128)(2,1)}, bf16[160,768]{1,0:T(8,128)(2,1)S(1)}, u32[]{:S(2)}, u32[]{:S(2)}) %collective-permute-start.4) | collective-permute-done | bytes 245792 | tf_op jit(solution)/shard_map/ppermute | solution.py:151
  66.6 4.4 %all-to-all-done.1.in_ref.other_ref = bf16[8,256,512]{2,1,0:T(8,128)(2,1)S(1)} async-done(((bf16[8,256,512]{2,1,0:T(8,128)(2,1)}), bf16[8,256,512]{2,1,0:T(8,128)(2,1)S(1)}, u32[]{:S(2)}, u32[]{:S(2)}) %all-to-all-start.1) | async-done | bytes 2097184 | tf_op jit(solution)/shard_map/all_to_all | solution.py:709
  74.3 3.6 all-to-all-start.2
  82.4 8.8 %collective-permute-done.6.refs_9_ = bf16[160,768]{1,0:T(8,128)(2,1)S(1)} collective-permute-done((bf16[160,768]{1,0:T(8,128)(2,1)}, bf16[160,768]{1,0:T(8,128)(2,1)S(1)}, u32[]{:S(2)}, u32[]{:S(2)}) %collective-permute-start.6) | collective-permute-done | bytes 245792 | tf_op jit(solution)/shard_map/ppermute | solution.py:151
  91.2 8.9 %collective-permute-done.7.refs_10_ = bf16[160,768]{1,0:T(8,128)(2,1)S(1)} collective-permute-done((bf16[160,768]{1,0:T(8,128)(2,1)}, bf16[160,768]{1,0:T(8,128)(2,1)S(1)}, u32[]{:S(2)}, u32[]{:S(2)}) %collective-permute-start.7) | collective-permute-done | bytes 245792 | tf_op jit(solution)/shard_map/ppermute | solution.py:151
  100.8 8.8 %first_products_0.1 = (bf16[384,2048]{1,0:T(8,128)(2,1)}, bf16[8,512,384]{2,1,0:T(8,128)(2,1)}) custom-call(bf16[160,512]{1,0:T(8,128)(2,1)} %get-tuple-element.99.refs_0_, bf16[160,512]{1,0:T(8,128)(2,1)} %copy-done.19, bf16[160,512]{1,0:T(8,128)(2,1)} %copy-done.20, bf16[160,512]{1,0:T(8,128)(2,1)} %copy-done.21, ...), custom_call_target="tpu_custom_call" | custom-call | tf_op jit(solution)/shard_map/first_products_0/pallas_call | solution.py:463
  109.6 4.5 %all-to-all-start.3 = ((bf16[8,512,384]{2,1,0:T(8,128)(2,1)}), bf16[8,512,384]{2,1,0:T(8,128)(2,1)}, u32[]{:S(2)}, u32[]{:S(2)}) async-start(bf16[8,512,384]{2,1,0:T(8,128)(2,1)} %get-tuple-element.120), calls=%async_computation.3 | async-start | bytes 6291456 | tf_op jit(solution)/shard_map/all_to_all | solution.py:709
  114.1 5.1 %first_products_1.1 = (bf16[128,2048]{1,0:T(8,128)(2,1)}, bf16[8,512,128]{2,1,0:T(8,128)(2,1)}) custom-call(bf16[160,512]{1,0:T(8,128)(2,1)} %get-tuple-element.99.refs_0_, bf16[160,512]{1,0:T(8,128)(2,1)} %copy-done.19, bf16[160,512]{1,0:T(8,128)(2,1)} %copy-done.20, bf16[160,512]{1,0:T(8,128)(2,1)} %copy-done.21, ...), custom_call_target="tpu_custom_call" | custom-call | tf_op jit(solution)/shard_map/first_products_1/pallas_call | solution.py:463
  119.3 32.8 %all-to-all-done.3.spread_ref = bf16[8,512,384]{2,1,0:T(8,128)(2,1)} async-done(((bf16[8,512,384]{2,1,0:T(8,128)(2,1)}), bf16[8,512,384]{2,1,0:T(8,128)(2,1)}, u32[]{:S(2)}, u32[]{:S(2)}) %all-to-all-start.3) | async-done | bytes 3145760 | tf_op jit(solution)/shard_map/all_to_all | solution.py:709
  152.0 3.7 %all-to-all-start.4 = ((bf16[8,512,128]{2,1,0:T(8,128)(2,1)}), bf16[8,512,128]{2,1,0:T(8,128)(2,1)S(1)}, u32[]{:S(2)}, u32[]{:S(2)}) async-start(bf16[8,512,128]{2,1,0:T(8,128)(2,1)} %get-tuple-element.121), calls=%async_computation.4 | async-start | bytes 2097152 | tf_op jit(solution)/shard_map/all_to_all | solution.py:709
  155.8 14.9 %middle_0.1 = (bf16[8,256,512]{2,1,0:T(8,128)(2,1)}, bf16[8,256,512]{2,1,0:T(8,128)(2,1)}, bf16[8,256,512]{2,1,0:T(8,128)(2,1)}, f32[32,128,128]{2,1,0:T(8,128)}) custom-call(s32[1]{0:T(128)} %bitcast.own_ref, bf16[8,512,384]{2,1,0:T(8,128)(2,1)} %all-to-all-done.3.spread_ref, bf16[8,256,512]{2,1,0:T(8,128)(2,1)S(1)} %all-to-all-done.2.hidden_grad_ref, ...), custom_call_target="tpu_custom_call" | custom-call | tf_op jit(solution)/shard_map/middle_0/pallas_call | solution.py:546
  170.9 7.9 %middle_1.1 = (bf16[8,256,512]{2,1,0:T(8,128)(2,1)}, bf16[8,256,512]{2,1,0:T(8,128)(2,1)}, bf16[8,256,512]{2,1,0:T(8,128)(2,1)}, bf16[32,32,128]{2,1,0:T(8,128)(...) custom-call(s32[1]{0:T(128)} %bitcast.own_ref, ...), custom_call_target="tpu_custom_call", output_to_operand_aliasing={{0}: (6, {}), {1}: (7, {}), {2}: (8, {})} | custom-call | tf_op jit(solution)/shard_map/middle_1/pallas_call | solution.py:546
  178.8 3.8 %all-to-all-start.5 = ((bf16[8,256,512]{2,1,0:T(8,128)(2,1)}), bf16[8,256,512]{2,1,0:T(8,128)(2,1)S(1)}, u32[]{:S(2)}, u32[]{:S(2)}) async-start(bf16[8,256,512]{2,1,0:T(8,128)(2,1)} %get-tuple-element.130), calls=%async_computation.5 | async-start | bytes 4194304 | tf_op jit(solution)/shard_map/all_to_all | solution.py:709
  182.7 4.9 %collective-permute-start.9 = (bf16[32,32,128]{2,1,0:T(8,128)(2,1)}, bf16[32,32,128]{2,1,0:T(8,128)(2,1)S(1)}, u32[]{:S(2)}, u32[]{:S(2)}) collective-permute-start(bf16[32,32,128]{2,1,0:T(8,128)(2,1)} %get-tuple-element.132), channel_id=1, source_target_pairs={{0,8},{8,0},{16,24},{24,16},{1,9},{9,1},{17,25},{25,17},{2,10},{10... | collective-permute-start | bytes 786440 | tf_op jit(solution)/shard_map/ppermute | solution.py:151
  190.1 9.9 %collective-permute-done.9.refs_1_ = bf16[32,32,128]{2,1,0:T(8,128)(2,1)S(1)} collective-permute-done((bf16[32,32,128]{2,1,0:T(8,128)(2,1)}, bf16[32,32,128]{2,1,0:T(8,128)(2,1)S(1)}, u32[]{:S(2)}, u32[]{:S(2)}) %collective-permute-start.9) | collective-permute-done | bytes 262176 | tf_op jit(solution)/shard_map/ppermute | solution.py:151
  200.0 8.9 %collective-permute-done.10.refs_2_ = bf16[32,32,128]{2,1,0:T(8,128)(2,1)S(1)} collective-permute-done((bf16[32,32,128]{2,1,0:T(8,128)(2,1)S(1)}, bf16[32,32,128]{2,1,0:T(8,128)(2,1)S(1)}, u32[]{:S(2)}, u32[]{:S(2)}) %collective-permute-start.10) | collective-permute-done | bytes 262176 | tf_op jit(solution)/shard_map/ppermute | solution.py:151
  210.6 3.8 %all-to-all-start.6 = ((bf16[8,256,512]{2,1,0:T(8,128)(2,1)}), bf16[8,256,512]{2,1,0:T(8,128)(2,1)S(1)}, u32[]{:S(2)}, u32[]{:S(2)}) async-start(bf16[8,256,512]{2,1,0:T(8,128)(2,1)} %get-tuple-element.135), calls=%async_computation.6 | async-start | bytes 4194304 | tf_op jit(solution)/shard_map/all_to_all | solution.py:709
  214.5 5.4 %last_products_0.1 = (bf16[160,640]{1,0:T(8,128)(2,1)}, bf16[160,640]{1,0:T(8,128)(2,1)}, bf16[160,640]{1,0:T(8,128)(2,1)}, bf16[160,640]{1,0:T(8,128)(2,1)}) custom-call(bf16[8,2,128,512]{3,2,1,0:T(8,128)(2,1)} %bitcast.15, bf16[640,512]{1,0:T(8,128)(2,1)} %get-tuple-element.136.back_ref, bf16[16,128,128]{2,1,0:T(8,128)(2,1)} %gate_ref.11, ...), custom_call_target="tpu_custom_call" | custom-call | tf_op jit(solution)/shard_map/last_products_0/pallas_call | solution.py:613
  219.8 5.0 %collective-permute-start.12 = (bf16[160,640]{1,0:T(8,128)(2,1)}, bf16[160,640]{1,0:T(8,128)(2,1)S(1)}, u32[]{:S(2)}, u32[]{:S(2)}) collective-permute-start(bf16[160,640]{1,0:T(8,128)(2,1)} %get-tuple-element.138), channel_id=1, source_target_pairs={{0,8},{8,0},{16,24},{24,16},{1,9},{9,1},{17,25},{25,17},{2,10},{10... | collective-permute-start | bytes 614408 | tf_op jit(solution)/shard_map/ppermute | solution.py:151
  229.4 3.9 %last_products_5.1 = (bf16[160,384]{1,0:T(8,128)(2,1)}, bf16[160,384]{1,0:T(8,128)(2,1)}, bf16[160,384]{1,0:T(8,128)(2,1)}, bf16[160,384]{1,0:T(8,128)(2,1)}) custom-call(bf16[8,2,128,512]{3,2,1,0:T(8,128)(2,1)} %bitcast.16, bf16[640,512]{1,0:T(8,128)(2,1)} %get-tuple-element.136.back_ref, bf16[16,128,128]{2,1,0:T(8,128)(2,1)} %gate_ref.11, ...), custom_call_target="tpu_custom_call" | custom-call | tf_op jit(solution)/shard_map/last_products_5/pallas_call | solution.py:613
  233.3 3.4 right_grads_0.1
  236.7 6.0 %collective-permute-done.13.refs_2_ = bf16[160,640]{1,0:T(8,128)(2,1)S(1)} collective-permute-done((bf16[160,640]{1,0:T(8,128)(2,1)}, bf16[160,640]{1,0:T(8,128)(2,1)S(1)}, u32[]{:S(2)}, u32[]{:S(2)}) %collective-permute-start.13) | collective-permute-done | bytes 204832 | tf_op jit(solution)/shard_map/ppermute | solution.py:151
  244.0 4.2 %all-to-all-start.7 = ((bf16[8,256,512]{2,1,0:T(8,128)(2,1)}), bf16[8,256,512]{2,1,0:T(8,128)(2,1)S(1)}, u32[]{:S(2)}, u32[]{:S(2)}) async-start(bf16[8,256,512]{2,1,0:T(8,128)(2,1)} %get-tuple-element.151), calls=%async_computation.7 | async-start | bytes 4194304 | tf_op jit(solution)/shard_map/all_to_all | solution.py:709
  248.2 3.9 %collective-permute-start.15 = (bf16[160,384]{1,0:T(8,128)(2,1)}, bf16[160,384]{1,0:T(8,128)(2,1)S(1)}, u32[]{:S(2)}, u32[]{:S(2)}) collective-permute-start(bf16[160,384]{1,0:T(8,128)(2,1)} %get-tuple-element.142), channel_id=1, source_target_pairs={{0,8},{8,0},{16,24},{24,16},{1,9},{9,1},{17,25},{25,17},{2,10},{10... | collective-permute-start | bytes 368648 | tf_op jit(solution)/shard_map/ppermute | solution.py:151
  254.6 3.9 %last_products_8.1 = (bf16[160,384]{1,0:T(8,128)(2,1)}, bf16[160,384]{1,0:T(8,128)(2,1)}, bf16[160,384]{1,0:T(8,128)(2,1)}, bf16[160,384]{1,0:T(8,128)(2,1)}) custom-call(bf16[8,2,128,512]{3,2,1,0:T(8,128)(2,1)} %bitcast.12, bf16[640,512]{1,0:T(8,128)(2,1)} %get-tuple-element.136.back_ref, bf16[16,128,128]{2,1,0:T(8,128)(2,1)} %gate_ref.11, ...), custom_call_target="tpu_custom_call" | custom-call | tf_op jit(solution)/shard_map/last_products_8/pallas_call | solution.py:613
  262.9 5.4 %last_products_11.1 = (bf16[160,640]{1,0:T(8,128)(2,1)}, bf16[160,640]{1,0:T(8,128)(2,1)}, bf16[160,640]{1,0:T(8,128)(2,1)}, bf16[160,640]{1,0:T(8,128)(2,1)}) custom-call(bf16[8,2,128,512]{3,2,1,0:T(8,128)(2,1)} %bitcast.13, bf16[640,512]{1,0:T(8,128)(2,1)} %get-tuple-element.136.back_ref, bf16[16,128,128]{2,1,0:T(8,128)(2,1)} %gate_ref.11, ...), custom_call_target="tpu_custom_call" | custom-call | tf_op jit(solution)/shard_map/last_products_11/pallas_call | solution.py:613
  268.3 7.0 %collective-permute-done.19.refs_2_ = bf16[160,384]{1,0:T(8,128)(2,1)S(1)} collective-permute-done((bf16[160,384]{1,0:T(8,128)(2,1)}, bf16[160,384]{1,0:T(8,128)(2,1)S(1)}, u32[]{:S(2)}, u32[]{:S(2)}) %collective-permute-start.19) | collective-permute-done | bytes 122912 | tf_op jit(solution)/shard_map/ppermute | solution.py:151
  280.0 4.5 %all-to-all-start.8 = ((bf16[8,256,512]{2,1,0:T(8,128)(2,1)}), bf16[8,256,512]{2,1,0:T(8,128)(2,1)}, u32[]{:S(2)}, u32[]{:S(2)}) async-start(bf16[8,256,512]{2,1,0:T(8,128)(2,1)} %right_down.1), calls=%async_computation.8 | async-start | bytes 4194304 | tf_op jit(solution)/shard_map/all_to_all | solution.py:709
  284.4 3.5 collective-permute-start.21
  295.7 4.8 %unsort_0.1.refs_4_ = bf16[2048,640]{1,0:T(8,128)(2,1)} custom-call(bf16[640,640]{1,0:T(8,128)(2,1)} %get-tuple-element.98.home_ref, bf16[160,640]{1,0:T(8,128)(2,1)} %get-tuple-element.137.refs_0_, bf16[160,640]{1,0:T(8,128)(2,1)} %copy-done.29, bf16[160,640]{1,0:T(8,128)(2,1)} %copy-done.30, bf16[160,640]{1,0:T(8,128)(2,1)} %copy-done.31), custom_call_target="tpu_custom_call" | custom-call | tf_op jit(solution)/shard_map/unsort_0/pallas_call | solution.py:171
  300.5 3.5 unsort_5.1.refs_4_
  304.0 5.3 %collective-permute-done.22.refs_1_ = bf16[160,640]{1,0:T(8,128)(2,1)S(1)} collective-permute-done((bf16[160,640]{1,0:T(8,128)(2,1)S(1)}, bf16[160,640]{1,0:T(8,128)(2,1)S(1)}, u32[]{:S(2)}, u32[]{:S(2)}) %collective-permute-start.22) | collective-permute-done | bytes 204832 | tf_op jit(solution)/shard_map/ppermute | solution.py:151
  309.3 6.6 %collective-permute-done.24.refs_3_ = bf16[160,640]{1,0:T(8,128)(2,1)S(1)} collective-permute-done((bf16[160,640]{1,0:T(8,128)(2,1)S(1)}, bf16[160,640]{1,0:T(8,128)(2,1)S(1)}, u32[]{:S(2)}, u32[]{:S(2)}) %collective-permute-start.24) | collective-permute-done | bytes 204832 | tf_op jit(solution)/shard_map/ppermute | solution.py:151
  315.9 3.5 right_grads_1.1
  319.4 4.5 %left_down.1 = bf16[8,256,512]{2,1,0:T(8,128)(2,1)} custom-call(bf16[8,256,512]{2,1,0:T(8,128)(2,1)} %all-to-all-done.8.in_ref, bf16[16,128,128]{2,1,0:T(8,128)(2,1)S(1)} %copy-done.9), custom_call_target="tpu_custom_call" | custom-call | tf_op jit(solution)/shard_map/left_down/pallas_call | solution.py:301
  324.0 4.5 %all-to-all-start.9 = ((bf16[8,256,512]{2,1,0:T(8,128)(2,1)}), bf16[8,256,512]{2,1,0:T(8,128)(2,1)}, u32[]{:S(2)}, u32[]{:S(2)}) async-start(bf16[8,256,512]{2,1,0:T(8,128)(2,1)} %left_down.1), calls=%async_computation.9 | async-start | bytes 4194304 | tf_op jit(solution)/shard_map/all_to_all | solution.py:709
  333.7 4.0 %collective-permute-done.26.refs_3_ = bf16[2,16,32,128]{3,2,1,0:T(8,128)(2,1)S(1)} collective-permute-done((bf16[2,16,32,128]{3,2,1,0:T(8,128)(2,1)S(1)}, bf16[2,16,32,128]{3,2,1,0:T(8,128)(2,1)S(1)}, u32[]{:S(2)}, u32[]{:S(2)}) %collective-permute-start.26) | collective-permute-done | bytes 262176 | tf_op jit(solution)/shard_map/ppermute | solution.py:363
  343.7 3.5 unsort_8.1.refs_4_
  347.2 4.9 %unsort_11.1 = bf16[2048,640]{1,0:T(8,128)(2,1)} custom-call(bf16[640,640]{1,0:T(8,128)(2,1)} %get-tuple-element.98.home_ref, bf16[160,640]{1,0:T(8,128)(2,1)} %get-tuple-element.156.refs_0_, bf16[160,640]{1,0:T(8,128)(2,1)} %copy-done.32, bf16[160,640]{1,0:T(8,128)(2,1)} %copy-done.33, bf16[160,640]{1,0:T(8,128)(2,1)} %copy-done.34, ...), custom_call_target="tpu_custom_call", output_to_operand_aliasing={{}: (5, {})} | custom-call | tf_op jit(solution)/shard_map/unsort_11/pallas_call | solution.py:171
  (174 shorter events, 80.8 us)
Async XLA Ops:
  5.5 31.9 %all-to-all-start = ((bf16[8,256,512]{2,1,0:T(8,128)(2,1)}), bf16[8,256,512]{2,1,0:T(8,128)(2,1)S(1)}, u32[]{:S(2)}, u32[]{:S(2)}) async-start(bf16[8,256,512]{2,1,0:T(8,128)(2,1)} %send_cotangent.1), calls=%async_computation | async-start | bytes 4194304 | tf_op jit(solution)/shard_map/all_to_all | solution.py:709
  17.2 13.4 %collective-permute-start = (bf16[160,512]{1,0:T(8,128)(2,1)}, bf16[160,512]{1,0:T(8,128)(2,1)S(1)}, u32[]{:S(2)}, u32[]{:S(2)}) collective-permute-start(bf16[160,512]{1,0:T(8,128)(2,1)} %get-tuple-element.100), channel_id=1, source_target_pairs={{0,8},{8,0},{16,24},{24,16},{1,9},{9,1},{17,25},{25,17},{2,10},{10... | collective-permute-start | bytes 491528 | tf_op jit(solution)/shard_map/ppermute | solution.py:151
  18.8 15.2 %collective-permute-start.1 = (bf16[160,512]{1,0:T(8,128)(2,1)}, bf16[160,512]{1,0:T(8,128)(2,1)S(1)}, u32[]{:S(2)}, u32[]{:S(2)}) collective-permute-start(bf16[160,512]{1,0:T(8,128)(2,1)} %get-tuple-element.101), channel_id=1, source_target_pairs={{0,16},{8,24},{16,0},{24,8},{1,17},{9,25},{17,1},{25,9},{2,18},{10... | collective-permute-start | bytes 491528 | tf_op jit(solution)/shard_map/ppermute | solution.py:151
  21.4 12.6 %collective-permute-start.2 = (bf16[160,512]{1,0:T(8,128)(2,1)}, bf16[160,512]{1,0:T(8,128)(2,1)S(1)}, u32[]{:S(2)}, u32[]{:S(2)}) collective-permute-start(bf16[160,512]{1,0:T(8,128)(2,1)} %get-tuple-element.102), channel_id=1, source_target_pairs={{0,24},{8,16},{16,8},{24,0},{1,25},{9,17},{17,9},{25,1},{2,26},{10... | collective-permute-start | bytes 491528 | tf_op jit(solution)/shard_map/ppermute | solution.py:151
  40.7 30.3 %copy-start.6 = (bf16[16,128,128]{2,1,0:T(8,128)(2,1)S(1)}, bf16[16,128,128]{2,1,0:T(8,128)(2,1)}, u32[]{:S(2)}) copy-start(bf16[16,128,128]{2,1,0:T(8,128)(2,1)} %factor_ref.6) | copy-start | bytes 1572868
  40.7 30.3 %all-to-all-start.1 = ((bf16[8,256,512]{2,1,0:T(8,128)(2,1)}), bf16[8,256,512]{2,1,0:T(8,128)(2,1)S(1)}, u32[]{:S(2)}, u32[]{:S(2)}) async-start(bf16[8,256,512]{2,1,0:T(8,128)(2,1)} %left_back_down.1), calls=%async_computation.1 | async-start | bytes 4194304 | tf_op jit(solution)/shard_map/all_to_all | solution.py:709
  44.5 13.2 %collective-permute-start.3 = (bf16[160,768]{1,0:T(8,128)(2,1)}, bf16[160,768]{1,0:T(8,128)(2,1)S(1)}, u32[]{:S(2)}, u32[]{:S(2)}) collective-permute-start(bf16[160,768]{1,0:T(8,128)(2,1)} %get-tuple-element.104), channel_id=1, source_target_pairs={{0,8},{8,0},{16,24},{24,16},{1,9},{9,1},{17,25},{25,17},{2,10},{10... | collective-permute-start | bytes 737288 | tf_op jit(solution)/shard_map/ppermute | solution.py:151
  46.1 20.5 %collective-permute-start.4 = (bf16[160,768]{1,0:T(8,128)(2,1)}, bf16[160,768]{1,0:T(8,128)(2,1)S(1)}, u32[]{:S(2)}, u32[]{:S(2)}) collective-permute-start(bf16[160,768]{1,0:T(8,128)(2,1)} %get-tuple-element.105), channel_id=1, source_target_pairs={{0,16},{8,24},{16,0},{24,8},{1,17},{9,25},{17,1},{25,9},{2,18},{10... | collective-permute-start | bytes 737288 | tf_op jit(solution)/shard_map/ppermute | solution.py:151
  48.7 17.9 %collective-permute-start.5 = (bf16[160,768]{1,0:T(8,128)(2,1)}, bf16[160,768]{1,0:T(8,128)(2,1)S(1)}, u32[]{:S(2)}, u32[]{:S(2)}) collective-permute-start(bf16[160,768]{1,0:T(8,128)(2,1)} %get-tuple-element.106), channel_id=1, source_target_pairs={{0,24},{8,16},{16,8},{24,0},{1,25},{9,17},{17,9},{25,1},{2,26},{10... | collective-permute-start | bytes 737288 | tf_op jit(solution)/shard_map/ppermute | solution.py:151
  74.3 35.3 %all-to-all-start.2 = ((bf16[8,256,512]{2,1,0:T(8,128)(2,1)}), bf16[8,256,512]{2,1,0:T(8,128)(2,1)S(1)}, u32[]{:S(2)}, u32[]{:S(2)}) async-start(bf16[8,256,512]{2,1,0:T(8,128)(2,1)} %right_back_down.1), calls=%async_computation.2 | async-start | bytes 4194304 | tf_op jit(solution)/shard_map/all_to_all | solution.py:709
  77.9 13.2 %collective-permute-start.6 = (bf16[160,768]{1,0:T(8,128)(2,1)}, bf16[160,768]{1,0:T(8,128)(2,1)S(1)}, u32[]{:S(2)}, u32[]{:S(2)}) collective-permute-start(bf16[160,768]{1,0:T(8,128)(2,1)} %get-tuple-element.108), channel_id=1, source_target_pairs={{0,8},{8,0},{16,24},{24,16},{1,9},{9,1},{17,25},{25,17},{2,10},{10... | collective-permute-start | bytes 737288 | tf_op jit(solution)/shard_map/ppermute | solution.py:151
  79.5 20.5 %collective-permute-start.7 = (bf16[160,768]{1,0:T(8,128)(2,1)}, bf16[160,768]{1,0:T(8,128)(2,1)S(1)}, u32[]{:S(2)}, u32[]{:S(2)}) collective-permute-start(bf16[160,768]{1,0:T(8,128)(2,1)} %get-tuple-element.109), channel_id=1, source_target_pairs={{0,16},{8,24},{16,0},{24,8},{1,17},{9,25},{17,1},{25,9},{2,18},{10... | collective-permute-start | bytes 737288 | tf_op jit(solution)/shard_map/ppermute | solution.py:151
  82.1 17.9 %collective-permute-start.8 = (bf16[160,768]{1,0:T(8,128)(2,1)}, bf16[160,768]{1,0:T(8,128)(2,1)S(1)}, u32[]{:S(2)}, u32[]{:S(2)}) collective-permute-start(bf16[160,768]{1,0:T(8,128)(2,1)} %get-tuple-element.110), channel_id=1, source_target_pairs={{0,24},{8,16},{16,8},{24,0},{1,25},{9,17},{17,9},{25,1},{2,26},{10... | collective-permute-start | bytes 737288 | tf_op jit(solution)/shard_map/ppermute | solution.py:151
  109.6 42.4 %all-to-all-start.3 = ((bf16[8,512,384]{2,1,0:T(8,128)(2,1)}), bf16[8,512,384]{2,1,0:T(8,128)(2,1)}, u32[]{:S(2)}, u32[]{:S(2)}) async-start(bf16[8,512,384]{2,1,0:T(8,128)(2,1)} %get-tuple-element.120), calls=%async_computation.3 | async-start | bytes 6291456 | tf_op jit(solution)/shard_map/all_to_all | solution.py:709
  152.0 18.9 %all-to-all-start.4 = ((bf16[8,512,128]{2,1,0:T(8,128)(2,1)}), bf16[8,512,128]{2,1,0:T(8,128)(2,1)S(1)}, u32[]{:S(2)}, u32[]{:S(2)}) async-start(bf16[8,512,128]{2,1,0:T(8,128)(2,1)} %get-tuple-element.121), calls=%async_computation.4 | async-start | bytes 2097152 | tf_op jit(solution)/shard_map/all_to_all | solution.py:709
  178.8 30.5 %all-to-all-start.5 = ((bf16[8,256,512]{2,1,0:T(8,128)(2,1)}), bf16[8,256,512]{2,1,0:T(8,128)(2,1)S(1)}, u32[]{:S(2)}, u32[]{:S(2)}) async-start(bf16[8,256,512]{2,1,0:T(8,128)(2,1)} %get-tuple-element.130), calls=%async_computation.5 | async-start | bytes 4194304 | tf_op jit(solution)/shard_map/all_to_all | solution.py:709
  182.7 17.3 %collective-permute-start.9 = (bf16[32,32,128]{2,1,0:T(8,128)(2,1)}, bf16[32,32,128]{2,1,0:T(8,128)(2,1)S(1)}, u32[]{:S(2)}, u32[]{:S(2)}) collective-permute-start(bf16[32,32,128]{2,1,0:T(8,128)(2,1)} %get-tuple-element.132), channel_id=1, source_target_pairs={{0,8},{8,0},{16,24},{24,16},{1,9},{9,1},{17,25},{25,17},{2,10},{10... | collective-permute-start | bytes 786440 | tf_op jit(solution)/shard_map/ppermute | solution.py:151
  187.5 21.3 %collective-permute-start.10 = (bf16[32,32,128]{2,1,0:T(8,128)(2,1)S(1)}, bf16[32,32,128]{2,1,0:T(8,128)(2,1)S(1)}, u32[]{:S(2)}, u32[]{:S(2)}) collective-permute-start(bf16[32,32,128]{2,1,0:T(8,128)(2,1)S(1)} %copy-done.47), channel_id=1, source_target_pairs={{0,16},{8,24},{16,0},{24,8},{1,17},{9,25},{17,1},{25,9},{2,18},{10... | collective-permute-start | bytes 786440 | tf_op jit(solution)/shard_map/ppermute | solution.py:151
  188.6 20.2 %collective-permute-start.11 = (bf16[32,32,128]{2,1,0:T(8,128)(2,1)S(1)}, bf16[32,32,128]{2,1,0:T(8,128)(2,1)S(1)}, u32[]{:S(2)}, u32[]{:S(2)}) collective-permute-start(bf16[32,32,128]{2,1,0:T(8,128)(2,1)S(1)} %copy-done.46), channel_id=1, source_target_pairs={{0,24},{8,16},{16,8},{24,0},{1,25},{9,17},{17,9},{25,1},{2,26},{10... | collective-permute-start | bytes 786440 | tf_op jit(solution)/shard_map/ppermute | solution.py:151
  200.0 27.4 %copy-start.25 = (bf16[32,32,128]{2,1,0:T(8,128)(2,1)}, bf16[32,32,128]{2,1,0:T(8,128)(2,1)S(1)}, u32[]{:S(2)}) copy-start(bf16[32,32,128]{2,1,0:T(8,128)(2,1)S(1)} %collective-permute-done.9.refs_1_) | copy-start | bytes 786436
  208.8 18.5 %copy-start.26 = (bf16[32,32,128]{2,1,0:T(8,128)(2,1)}, bf16[32,32,128]{2,1,0:T(8,128)(2,1)S(1)}, u32[]{:S(2)}) copy-start(bf16[32,32,128]{2,1,0:T(8,128)(2,1)S(1)} %collective-permute-done.10.refs_2_) | copy-start | bytes 786436
  210.6 32.1 %all-to-all-start.6 = ((bf16[8,256,512]{2,1,0:T(8,128)(2,1)}), bf16[8,256,512]{2,1,0:T(8,128)(2,1)S(1)}, u32[]{:S(2)}, u32[]{:S(2)}) async-start(bf16[8,256,512]{2,1,0:T(8,128)(2,1)} %get-tuple-element.135), calls=%async_computation.6 | async-start | bytes 4194304 | tf_op jit(solution)/shard_map/all_to_all | solution.py:709
  219.8 16.8 %collective-permute-start.12 = (bf16[160,640]{1,0:T(8,128)(2,1)}, bf16[160,640]{1,0:T(8,128)(2,1)S(1)}, u32[]{:S(2)}, u32[]{:S(2)}) collective-permute-start(bf16[160,640]{1,0:T(8,128)(2,1)} %get-tuple-element.138), channel_id=1, source_target_pairs={{0,8},{8,0},{16,24},{24,16},{1,9},{9,1},{17,25},{25,17},{2,10},{10... | collective-permute-start | bytes 614408 | tf_op jit(solution)/shard_map/ppermute | solution.py:151
  224.9 17.8 %collective-permute-start.13 = (bf16[160,640]{1,0:T(8,128)(2,1)}, bf16[160,640]{1,0:T(8,128)(2,1)S(1)}, u32[]{:S(2)}, u32[]{:S(2)}) collective-permute-start(bf16[160,640]{1,0:T(8,128)(2,1)} %get-tuple-element.139), channel_id=1, source_target_pairs={{0,16},{8,24},{16,0},{24,8},{1,17},{9,25},{17,1},{25,9},{2,18},{10... | collective-permute-start | bytes 614408 | tf_op jit(solution)/shard_map/ppermute | solution.py:151
  225.9 16.8 %collective-permute-start.14 = (bf16[160,640]{1,0:T(8,128)(2,1)}, bf16[160,640]{1,0:T(8,128)(2,1)S(1)}, u32[]{:S(2)}, u32[]{:S(2)}) collective-permute-start(bf16[160,640]{1,0:T(8,128)(2,1)} %get-tuple-element.140), channel_id=1, source_target_pairs={{0,24},{8,16},{16,8},{24,0},{1,25},{9,17},{17,9},{25,1},{2,26},{10... | collective-permute-start | bytes 614408 | tf_op jit(solution)/shard_map/ppermute | solution.py:151
  236.7 41.9 %copy-start.29 = (bf16[160,640]{1,0:T(8,128)(2,1)}, bf16[160,640]{1,0:T(8,128)(2,1)S(1)}, u32[]{:S(2)}) copy-start(bf16[160,640]{1,0:T(8,128)(2,1)S(1)} %collective-permute-done.12.refs_1_) | copy-start | bytes 614404
  242.7 35.9 %copy-start.30 = (bf16[160,640]{1,0:T(8,128)(2,1)}, bf16[160,640]{1,0:T(8,128)(2,1)S(1)}, u32[]{:S(2)}) copy-start(bf16[160,640]{1,0:T(8,128)(2,1)S(1)} %collective-permute-done.13.refs_2_) | copy-start | bytes 614404
  242.7 35.9 %copy-start.31 = (bf16[160,640]{1,0:T(8,128)(2,1)}, bf16[160,640]{1,0:T(8,128)(2,1)S(1)}, u32[]{:S(2)}) copy-start(bf16[160,640]{1,0:T(8,128)(2,1)S(1)} %collective-permute-done.14.refs_3_) | copy-start | bytes 614404
  244.0 31.3 %all-to-all-start.7 = ((bf16[8,256,512]{2,1,0:T(8,128)(2,1)}), bf16[8,256,512]{2,1,0:T(8,128)(2,1)S(1)}, u32[]{:S(2)}, u32[]{:S(2)}) async-start(bf16[8,256,512]{2,1,0:T(8,128)(2,1)} %get-tuple-element.151), calls=%async_computation.7 | async-start | bytes 4194304 | tf_op jit(solution)/shard_map/all_to_all | solution.py:709
  248.2 13.2 %collective-permute-start.15 = (bf16[160,384]{1,0:T(8,128)(2,1)}, bf16[160,384]{1,0:T(8,128)(2,1)S(1)}, u32[]{:S(2)}, u32[]{:S(2)}) collective-permute-start(bf16[160,384]{1,0:T(8,128)(2,1)} %get-tuple-element.142), channel_id=1, source_target_pairs={{0,8},{8,0},{16,24},{24,16},{1,9},{9,1},{17,25},{25,17},{2,10},{10... | collective-permute-start | bytes 368648 | tf_op jit(solution)/shard_map/ppermute | solution.py:151
  252.1 16.1 %collective-permute-start.16 = (bf16[160,384]{1,0:T(8,128)(2,1)}, bf16[160,384]{1,0:T(8,128)(2,1)S(1)}, u32[]{:S(2)}, u32[]{:S(2)}) collective-permute-start(bf16[160,384]{1,0:T(8,128)(2,1)} %get-tuple-element.143), channel_id=1, source_target_pairs={{0,16},{8,24},{16,0},{24,8},{1,17},{9,25},{17,1},{25,9},{2,18},{10... | collective-permute-start | bytes 368648 | tf_op jit(solution)/shard_map/ppermute | solution.py:151
  253.2 15.1 %collective-permute-start.17 = (bf16[160,384]{1,0:T(8,128)(2,1)}, bf16[160,384]{1,0:T(8,128)(2,1)S(1)}, u32[]{:S(2)}, u32[]{:S(2)}) collective-permute-start(bf16[160,384]{1,0:T(8,128)(2,1)} %get-tuple-element.144), channel_id=1, source_target_pairs={{0,24},{8,16},{16,8},{24,0},{1,25},{9,17},{17,9},{25,1},{2,26},{10... | collective-permute-start | bytes 368648 | tf_op jit(solution)/shard_map/ppermute | solution.py:151
  258.4 9.8 %collective-permute-start.18 = (bf16[160,384]{1,0:T(8,128)(2,1)}, bf16[160,384]{1,0:T(8,128)(2,1)S(1)}, u32[]{:S(2)}, u32[]{:S(2)}) collective-permute-start(bf16[160,384]{1,0:T(8,128)(2,1)} %get-tuple-element.153), channel_id=1, source_target_pairs={{0,8},{8,0},{16,24},{24,16},{1,9},{9,1},{17,25},{25,17},{2,10},{10... | collective-permute-start | bytes 368648 | tf_op jit(solution)/shard_map/ppermute | solution.py:151
  259.5 15.8 %collective-permute-start.19 = (bf16[160,384]{1,0:T(8,128)(2,1)}, bf16[160,384]{1,0:T(8,128)(2,1)S(1)}, u32[]{:S(2)}, u32[]{:S(2)}) collective-permute-start(bf16[160,384]{1,0:T(8,128)(2,1)} %get-tuple-element.154), channel_id=1, source_target_pairs={{0,16},{8,24},{16,0},{24,8},{1,17},{9,25},{17,1},{25,9},{2,18},{10... | collective-permute-start | bytes 368648 | tf_op jit(solution)/shard_map/ppermute | solution.py:151
  261.5 13.8 %collective-permute-start.20 = (bf16[160,384]{1,0:T(8,128)(2,1)}, bf16[160,384]{1,0:T(8,128)(2,1)}, u32[]{:S(2)}, u32[]{:S(2)}) collective-permute-start(bf16[160,384]{1,0:T(8,128)(2,1)} %get-tuple-element.155), channel_id=1, source_target_pairs={{0,24},{8,16},{16,8},{24,0},{1,25},{9,17},{17,9},{25,1},{2,26},{10... | collective-permute-start | bytes 368648 | tf_op jit(solution)/shard_map/ppermute | solution.py:151
  280.0 39.5 %all-to-all-start.8 = ((bf16[8,256,512]{2,1,0:T(8,128)(2,1)}), bf16[8,256,512]{2,1,0:T(8,128)(2,1)}, u32[]{:S(2)}, u32[]{:S(2)}) async-start(bf16[8,256,512]{2,1,0:T(8,128)(2,1)} %right_down.1), calls=%async_computation.8 | async-start | bytes 4194304 | tf_op jit(solution)/shard_map/all_to_all | solution.py:709
  284.4 35.0 %collective-permute-start.21 = (bf16[2,16,32,128]{3,2,1,0:T(8,128)(2,1)}, bf16[2,16,32,128]{3,2,1,0:T(8,128)(2,1)S(1)}, u32[]{:S(2)}, u32[]{:S(2)}) collective-permute-start(bf16[2,16,32,128]{3,2,1,0:T(8,128)(2,1)} %get-tuple-element.149), channel_id=1, source_target_pairs={{0,8},{8,0},{16,24},{24,16},{1,9},{9,1},{17,25},{25,17},{2,10},{10... | collective-permute-start | bytes 786440 | tf_op jit(solution)/shard_map/ppermute | solution.py:363
  291.1 28.3 %collective-permute-start.25 = (bf16[2,16,32,128]{3,2,1,0:T(8,128)(2,1)}, bf16[2,16,32,128]{3,2,1,0:T(8,128)(2,1)S(1)}, u32[]{:S(2)}, u32[]{:S(2)}) collective-permute-start(bf16[2,16,32,128]{3,2,1,0:T(8,128)(2,1)} %get-tuple-element.163), channel_id=1, source_target_pairs={{0,8},{8,0},{16,24},{24,16},{1,9},{9,1},{17,25},{25,17},{2,10},{10... | collective-permute-start | bytes 786440 | tf_op jit(solution)/shard_map/ppermute | solution.py:363
  291.1 18.2 %collective-permute-start.22 = (bf16[160,640]{1,0:T(8,128)(2,1)S(1)}, bf16[160,640]{1,0:T(8,128)(2,1)S(1)}, u32[]{:S(2)}, u32[]{:S(2)}) collective-permute-start(bf16[160,640]{1,0:T(8,128)(2,1)S(1)} %copy-done.50), channel_id=1, source_target_pairs={{0,8},{8,0},{16,24},{24,16},{1,9},{9,1},{17,25},{25,17},{2,10},{10... | collective-permute-start | bytes 614408 | tf_op jit(solution)/shard_map/ppermute | solution.py:151
  293.1 16.2 %collective-permute-start.23 = (bf16[160,640]{1,0:T(8,128)(2,1)S(1)}, bf16[160,640]{1,0:T(8,128)(2,1)S(1)}, u32[]{:S(2)}, u32[]{:S(2)}) collective-permute-start(bf16[160,640]{1,0:T(8,128)(2,1)S(1)} %copy-done.49), channel_id=1, source_target_pairs={{0,16},{8,24},{16,0},{24,8},{1,17},{9,25},{17,1},{25,9},{2,18},{10... | collective-permute-start | bytes 614408 | tf_op jit(solution)/shard_map/ppermute | solution.py:151
  294.2 21.7 %collective-permute-start.24 = (bf16[160,640]{1,0:T(8,128)(2,1)S(1)}, bf16[160,640]{1,0:T(8,128)(2,1)S(1)}, u32[]{:S(2)}, u32[]{:S(2)}) collective-permute-start(bf16[160,640]{1,0:T(8,128)(2,1)S(1)} %copy-done.48), channel_id=1, source_target_pairs={{0,24},{8,16},{16,8},{24,0},{1,25},{9,17},{17,9},{25,1},{2,26},{10... | collective-permute-start | bytes 614408 | tf_op jit(solution)/shard_map/ppermute | solution.py:151
  324.0 35.9 %all-to-all-start.9 = ((bf16[8,256,512]{2,1,0:T(8,128)(2,1)}), bf16[8,256,512]{2,1,0:T(8,128)(2,1)}, u32[]{:S(2)}, u32[]{:S(2)}) async-start(bf16[8,256,512]{2,1,0:T(8,128)(2,1)} %left_down.1), calls=%async_computation.9 | async-start | bytes 4194304 | tf_op jit(solution)/shard_map/all_to_all | solution.py:709
  328.5 9.2 %collective-permute-start.26 = (bf16[2,16,32,128]{3,2,1,0:T(8,128)(2,1)S(1)}, bf16[2,16,32,128]{3,2,1,0:T(8,128)(2,1)S(1)}, u32[]{:S(2)}, u32[]{:S(2)}) collective-permute-start(bf16[2,16,32,128]{3,2,1,0:T(8,128)(2,1)S(1)} %copy-done.45), channel_id=1, source_target_pairs={{0,8},{8,0},{16,24},{24,16},{1,9},{9,1},{17,25},{25,17},{2,10},{10... | collective-permute-start | bytes 786440 | tf_op jit(solution)/shard_map/ppermute | solution.py:363
  331.7 20.4 %collective-permute-start.30 = (bf16[2,16,32,128]{3,2,1,0:T(8,128)(2,1)}, bf16[2,16,32,128]{3,2,1,0:T(8,128)(2,1)S(1)}, u32[]{:S(2)}, u32[]{:S(2)}) collective-permute-start(bf16[2,16,32,128]{3,2,1,0:T(8,128)(2,1)} %get-tuple-element.181), channel_id=1, source_target_pairs={{0,8},{8,0},{16,24},{24,16},{1,9},{9,1},{17,25},{25,17},{2,10},{10... | collective-permute-start | bytes 786440 | tf_op jit(solution)/shard_map/ppermute | solution.py:363
  340.8 16.8 %collective-permute-start.28 = (bf16[1,16,32,128]{3,2,1,0:T(8,128)(2,1)}, bf16[1,16,32,128]{3,2,1,0:T(8,128)(2,1)S(1)}, u32[]{:S(2)}, u32[]{:S(2)}) collective-permute-start(bf16[1,16,32,128]{3,2,1,0:T(8,128)(2,1)} %get-tuple-element.171), channel_id=1, source_target_pairs={{0,16},{8,24},{16,0},{24,8},{1,17},{9,25},{17,1},{25,9},{2,18},{10... | collective-permute-start | bytes 393224 | tf_op jit(solution)/shard_map/ppermute | solution.py:363
  340.8 21.7 %collective-permute-start.27 = (bf16[1,16,32,128]{3,2,1,0:T(8,128)(2,1)}, bf16[1,16,32,128]{3,2,1,0:T(8,128)(2,1)S(1)}, u32[]{:S(2)}, u32[]{:S(2)}) collective-permute-start(bf16[1,16,32,128]{3,2,1,0:T(8,128)(2,1)} %get-tuple-element.169), channel_id=1, source_target_pairs={{0,16},{8,24},{16,0},{24,8},{1,17},{9,25},{17,1},{25,9},{2,18},{10... | collective-permute-start | bytes 393224 | tf_op jit(solution)/shard_map/ppermute | solution.py:363
  352.1 11.2 %collective-permute-start.29 = (bf16[1,16,32,128]{3,2,1,0:T(8,128)(2,1)S(1)}, bf16[1,16,32,128]{3,2,1,0:T(8,128)(2,1)S(1)}, u32[]{:S(2)}, u32[]{:S(2)}) collective-permute-start(bf16[1,16,32,128]{3,2,1,0:T(8,128)(2,1)S(1)} %copy-done.51), channel_id=1, source_target_pairs={{0,16},{8,24},{16,0},{24,8},{1,17},{9,25},{17,1},{25,9},{2,18},{10... | collective-permute-start | bytes 393224 | tf_op jit(solution)/shard_map/ppermute | solution.py:363
  354.6 11.3 %collective-permute-start.31 = (bf16[1,16,32,128]{3,2,1,0:T(8,128)(2,1)}, bf16[1,16,32,128]{3,2,1,0:T(8,128)(2,1)S(1)}, u32[]{:S(2)}, u32[]{:S(2)}) collective-permute-start(bf16[1,16,32,128]{3,2,1,0:T(8,128)(2,1)} %get-tuple-element.185), channel_id=1, source_target_pairs={{0,16},{8,24},{16,0},{24,8},{1,17},{9,25},{17,1},{25,9},{2,18},{10... | collective-permute-start | bytes 393224 | tf_op jit(solution)/shard_map/ppermute | solution.py:363
  (46 other events, 270.5 us)

commit v6 on v5

--- a/solution.py
+++ b/solution.py
@@ -779,7 +779,7 @@
     down_spread = swap(down_spread)
     right_high = (right_high[0], swap_rows(right_high[1], 1, groups))
     down_grad = (down_grad[0], swap_rows(down_grad[1], 1, groups))
-    down_spread = after(down_spread, right_low[1], right_high[0], down_grad[1])
+    down_spread = after(down_spread, right_low[1], right_high[1], down_grad[1])
     result = product(plan, down_spread, left_down, TN, "left_down")
     left_down_grad = factor_grad(
         plan, own, after(down_spread, result), out_grads, left_down, scale, groups,

time: 371 us -> 366 us (0.987)
  waiting for transfers between devices: 129 us -> 124 us
    ppermute x24, waiting for transfers between devices: 82.4 us -> 74 us  [exchange(): received.append(lax.ppermute(arrays[k], axis, pairs))]
    unnamed x104 -> x92, local copies, waits for them, and re-layouts: 9.86 us -> 6.21 us
  transfers between devices with their start and end apart: 42 -> 42, of which waited for: 19 -> 19; matrix products, arithmetic and copies ran while one was open for 0% -> 0% of each run, Pallas kernels for 28% -> 29%
where the time goes in v6:
time: 366 us; the launch traced here: 363 us
  Pallas kernels  132 us (36%)
  waiting for transfers between devices  124 us (34%)
  starting transfers between devices  100 us (27%)
  local copies, waits for them, and re-layouts  6.23 us (2%)
    ppermute x24, waiting for transfers between devices, exchange(): received.append(lax.ppermute(arrays[k], axis, pairs))  74 us
    ppermute x24, starting transfers between devices, exchange(): received.append(lax.ppermute(arrays[k], axis, pairs))  44.9 us
    all_to_all x10, waiting for transfers between devices, move(): lax.all_to_all(array, 'feat', split_axis=0, concat_axis=0, tiled=True)  41.6 us
    all_to_all x10, starting transfers between devices, move(): lax.all_to_all(array, 'feat', split_axis=0, concat_axis=0, tiled=True)  41.6 us
    pallas_call x2, Pallas kernels, middle(): pl.pallas_call(functools.partial(middle_kernel, plan, scale, first, last)...  22.8 us
    pallas_call x4, Pallas kernels, last_products(): pl.pallas_call(functools.partial(last_kernel, plan), grid=(count,), in_sp...  18.5 us
    pallas_call x4, Pallas kernels, unsort(): pl.pallas_call(functools.partial(unsort_kernel, groups), grid=(count,), i...  16.9 us
    pallas_call x4, Pallas kernels, product(): pl.pallas_call(functools.partial(product_kernel, plan, over), grid=(plan....  14.2 us
  transfers between devices with their start and end apart: 42, of which 19 were waited for; matrix products, arithmetic and copies ran while one was open for 0% of the time, Pallas kernels for 29%

profile of v6, /device:TPU:0, one launch (start us, length us, event | category | flops | bytes accessed | tf_op | source)
XLA Modules:
  0.0 363.4 jit_solution(11879967422906462817)
XLA Ops:
  0.6 4.9 %send_cotangent.1 = bf16[8,256,512]{2,1,0:T(8,128)(2,1)} custom-call(bf16[2048,512]{1,0:T(8,128)(2,1)} %in_ref.1), custom_call_target="tpu_custom_call" | custom-call | tf_op jit(solution)/shard_map/send_cotangent/pallas_call | solution.py:279
  5.5 5.3 %all-to-all-start = ((bf16[8,256,512]{2,1,0:T(8,128)(2,1)}), bf16[8,256,512]{2,1,0:T(8,128)(2,1)S(1)}, u32[]{:S(2)}, u32[]{:S(2)}) async-start(bf16[8,256,512]{2,1,0:T(8,128)(2,1)} %send_cotangent.1), calls=%async_computation | async-start | bytes 4194304 | tf_op jit(solution)/shard_map/all_to_all | solution.py:709
  13.9 3.3 mix_and_sort_0.1
  21.6 4.5 %mix_and_sort_5.1 = (bf16[160,768]{1,0:T(8,128)(2,1)}, bf16[160,768]{1,0:T(8,128)(2,1)}, bf16[160,768]{1,0:T(8,128)(2,1)}, bf16[160,768]{1,0:T(8,128)(2,1)}) custom-call(f32[3]{0:T(128)S(1)} %copy-done.8, bf16[3,2048,640]{2,1,0:T(8,128)(2,1)} %earlier_ref.5, bf16[640,640]{1,0:T(8,128)(2,1)} %get-tuple-element.98.home_ref), custom_call_target="tpu_custom_call" | custom-call | tf_op jit(solution)/shard_map/mix_and_sort_5/pallas_call | solution.py:125
  26.0 4.5 %mix_and_sort_2.1 = (bf16[160,768]{1,0:T(8,128)(2,1)}, bf16[160,768]{1,0:T(8,128)(2,1)}, bf16[160,768]{1,0:T(8,128)(2,1)}, bf16[160,768]{1,0:T(8,128)(2,1)}) custom-call(f32[3]{0:T(128)S(1)} %copy-done.8, bf16[3,2048,640]{2,1,0:T(8,128)(2,1)} %earlier_ref.5, bf16[640,640]{1,0:T(8,128)(2,1)} %get-tuple-element.98.home_ref), custom_call_target="tpu_custom_call" | custom-call | tf_op jit(solution)/shard_map/mix_and_sort_2/pallas_call | solution.py:125
  30.5 3.4 collective-permute-done.1.refs_2_
  34.0 3.5 all-to-all-done.in_ref.other_ref
  40.7 3.7 %all-to-all-start.1 = ((bf16[8,256,512]{2,1,0:T(8,128)(2,1)}), bf16[8,256,512]{2,1,0:T(8,128)(2,1)S(1)}, u32[]{:S(2)}, u32[]{:S(2)}) async-start(bf16[8,256,512]{2,1,0:T(8,128)(2,1)} %left_back_down.1), calls=%async_computation.1 | async-start | bytes 4194304 | tf_op jit(solution)/shard_map/all_to_all | solution.py:709
  48.9 8.8 %collective-permute-done.3.refs_5_ = bf16[160,768]{1,0:T(8,128)(2,1)S(1)} collective-permute-done((bf16[160,768]{1,0:T(8,128)(2,1)}, bf16[160,768]{1,0:T(8,128)(2,1)S(1)}, u32[]{:S(2)}, u32[]{:S(2)}) %collective-permute-start.3) | collective-permute-done | bytes 245792 | tf_op jit(solution)/shard_map/ppermute | solution.py:151
  57.7 8.9 %collective-permute-done.4.refs_6_ = bf16[160,768]{1,0:T(8,128)(2,1)S(1)} collective-permute-done((bf16[160,768]{1,0:T(8,128)(2,1)}, bf16[160,768]{1,0:T(8,128)(2,1)S(1)}, u32[]{:S(2)}, u32[]{:S(2)}) %collective-permute-start.4) | collective-permute-done | bytes 245792 | tf_op jit(solution)/shard_map/ppermute | solution.py:151
  66.6 4.4 %all-to-all-done.1.in_ref.other_ref = bf16[8,256,512]{2,1,0:T(8,128)(2,1)S(1)} async-done(((bf16[8,256,512]{2,1,0:T(8,128)(2,1)}), bf16[8,256,512]{2,1,0:T(8,128)(2,1)S(1)}, u32[]{:S(2)}, u32[]{:S(2)}) %all-to-all-start.1) | async-done | bytes 2097184 | tf_op jit(solution)/shard_map/all_to_all | solution.py:709
  74.3 3.6 all-to-all-start.2
  82.4 8.8 %collective-permute-done.6.refs_9_ = bf16[160,768]{1,0:T(8,128)(2,1)S(1)} collective-permute-done((bf16[160,768]{1,0:T(8,128)(2,1)}, bf16[160,768]{1,0:T(8,128)(2,1)S(1)}, u32[]{:S(2)}, u32[]{:S(2)}) %collective-permute-start.6) | collective-permute-done | bytes 245792 | tf_op jit(solution)/shard_map/ppermute | solution.py:151
  91.2 8.9 %collective-permute-done.7.refs_10_ = bf16[160,768]{1,0:T(8,128)(2,1)S(1)} collective-permute-done((bf16[160,768]{1,0:T(8,128)(2,1)}, bf16[160,768]{1,0:T(8,128)(2,1)S(1)}, u32[]{:S(2)}, u32[]{:S(2)}) %collective-permute-start.7) | collective-permute-done | bytes 245792 | tf_op jit(solution)/shard_map/ppermute | solution.py:151
  100.8 8.8 %first_products_0.1 = (bf16[384,2048]{1,0:T(8,128)(2,1)}, bf16[8,512,384]{2,1,0:T(8,128)(2,1)}) custom-call(bf16[160,512]{1,0:T(8,128)(2,1)} %get-tuple-element.99.refs_0_, bf16[160,512]{1,0:T(8,128)(2,1)} %copy-done.17, bf16[160,512]{1,0:T(8,128)(2,1)} %copy-done.18, bf16[160,512]{1,0:T(8,128)(2,1)} %copy-done.19, ...), custom_call_target="tpu_custom_call" | custom-call | tf_op jit(solution)/shard_map/first_products_0/pallas_call | solution.py:463
  109.6 4.5 %all-to-all-start.3 = ((bf16[8,512,384]{2,1,0:T(8,128)(2,1)}), bf16[8,512,384]{2,1,0:T(8,128)(2,1)}, u32[]{:S(2)}, u32[]{:S(2)}) async-start(bf16[8,512,384]{2,1,0:T(8,128)(2,1)} %get-tuple-element.120), calls=%async_computation.3 | async-start | bytes 6291456 | tf_op jit(solution)/shard_map/all_to_all | solution.py:709
  114.1 5.1 %first_products_1.1 = (bf16[128,2048]{1,0:T(8,128)(2,1)}, bf16[8,512,128]{2,1,0:T(8,128)(2,1)}) custom-call(bf16[160,512]{1,0:T(8,128)(2,1)} %get-tuple-element.99.refs_0_, bf16[160,512]{1,0:T(8,128)(2,1)} %copy-done.17, bf16[160,512]{1,0:T(8,128)(2,1)} %copy-done.18, bf16[160,512]{1,0:T(8,128)(2,1)} %copy-done.19, ...), custom_call_target="tpu_custom_call" | custom-call | tf_op jit(solution)/shard_map/first_products_1/pallas_call | solution.py:463
  119.2 32.8 %all-to-all-done.3.spread_ref = bf16[8,512,384]{2,1,0:T(8,128)(2,1)} async-done(((bf16[8,512,384]{2,1,0:T(8,128)(2,1)}), bf16[8,512,384]{2,1,0:T(8,128)(2,1)}, u32[]{:S(2)}, u32[]{:S(2)}) %all-to-all-start.3) | async-done | bytes 3145760 | tf_op jit(solution)/shard_map/all_to_all | solution.py:709
  152.0 3.7 %all-to-all-start.4 = ((bf16[8,512,128]{2,1,0:T(8,128)(2,1)}), bf16[8,512,128]{2,1,0:T(8,128)(2,1)S(1)}, u32[]{:S(2)}, u32[]{:S(2)}) async-start(bf16[8,512,128]{2,1,0:T(8,128)(2,1)} %get-tuple-element.121), calls=%async_computation.4 | async-start | bytes 2097152 | tf_op jit(solution)/shard_map/all_to_all | solution.py:709
  155.7 14.9 %middle_0.1 = (bf16[8,256,512]{2,1,0:T(8,128)(2,1)}, bf16[8,256,512]{2,1,0:T(8,128)(2,1)}, bf16[8,256,512]{2,1,0:T(8,128)(2,1)}, f32[32,128,128]{2,1,0:T(8,128)}) custom-call(s32[1]{0:T(128)} %bitcast.own_ref, bf16[8,512,384]{2,1,0:T(8,128)(2,1)} %all-to-all-done.3.spread_ref, bf16[8,256,512]{2,1,0:T(8,128)(2,1)S(1)} %all-to-all-done.2.hidden_grad_ref, ...), custom_call_target="tpu_custom_call" | custom-call | tf_op jit(solution)/shard_map/middle_0/pallas_call | solution.py:546
  170.9 7.9 %middle_1.1 = (bf16[8,256,512]{2,1,0:T(8,128)(2,1)}, bf16[8,256,512]{2,1,0:T(8,128)(2,1)}, bf16[8,256,512]{2,1,0:T(8,128)(2,1)}, bf16[32,32,128]{2,1,0:T(8,128)(...) custom-call(s32[1]{0:T(128)} %bitcast.own_ref, ...), custom_call_target="tpu_custom_call", output_to_operand_aliasing={{0}: (6, {}), {1}: (7, {}), {2}: (8, {})} | custom-call | tf_op jit(solution)/shard_map/middle_1/pallas_call | solution.py:546
  178.8 3.8 %all-to-all-start.5 = ((bf16[8,256,512]{2,1,0:T(8,128)(2,1)}), bf16[8,256,512]{2,1,0:T(8,128)(2,1)S(1)}, u32[]{:S(2)}, u32[]{:S(2)}) async-start(bf16[8,256,512]{2,1,0:T(8,128)(2,1)} %get-tuple-element.130), calls=%async_computation.5 | async-start | bytes 4194304 | tf_op jit(solution)/shard_map/all_to_all | solution.py:709
  182.6 4.9 %collective-permute-start.9 = (bf16[32,32,128]{2,1,0:T(8,128)(2,1)}, bf16[32,32,128]{2,1,0:T(8,128)(2,1)S(1)}, u32[]{:S(2)}, u32[]{:S(2)}) collective-permute-start(bf16[32,32,128]{2,1,0:T(8,128)(2,1)} %get-tuple-element.132), channel_id=1, source_target_pairs={{0,8},{8,0},{16,24},{24,16},{1,9},{9,1},{17,25},{25,17},{2,10},{10... | collective-permute-start | bytes 786440 | tf_op jit(solution)/shard_map/ppermute | solution.py:151
  190.0 9.9 %collective-permute-done.9.refs_1_ = bf16[32,32,128]{2,1,0:T(8,128)(2,1)S(1)} collective-permute-done((bf16[32,32,128]{2,1,0:T(8,128)(2,1)}, bf16[32,32,128]{2,1,0:T(8,128)(2,1)S(1)}, u32[]{:S(2)}, u32[]{:S(2)}) %collective-permute-start.9) | collective-permute-done | bytes 262176 | tf_op jit(solution)/shard_map/ppermute | solution.py:151
  199.9 8.9 %collective-permute-done.10.refs_2_ = bf16[32,32,128]{2,1,0:T(8,128)(2,1)S(1)} collective-permute-done((bf16[32,32,128]{2,1,0:T(8,128)(2,1)S(1)}, bf16[32,32,128]{2,1,0:T(8,128)(2,1)S(1)}, u32[]{:S(2)}, u32[]{:S(2)}) %collective-permute-start.10) | collective-permute-done | bytes 262176 | tf_op jit(solution)/shard_map/ppermute | solution.py:151
  210.6 3.8 %all-to-all-start.6 = ((bf16[8,256,512]{2,1,0:T(8,128)(2,1)}), bf16[8,256,512]{2,1,0:T(8,128)(2,1)S(1)}, u32[]{:S(2)}, u32[]{:S(2)}) async-start(bf16[8,256,512]{2,1,0:T(8,128)(2,1)} %get-tuple-element.135), calls=%async_computation.6 | async-start | bytes 4194304 | tf_op jit(solution)/shard_map/all_to_all | solution.py:709
  214.4 5.4 %last_products_0.1 = (bf16[160,640]{1,0:T(8,128)(2,1)}, bf16[160,640]{1,0:T(8,128)(2,1)}, bf16[160,640]{1,0:T(8,128)(2,1)}, bf16[160,640]{1,0:T(8,128)(2,1)}) custom-call(bf16[8,2,128,512]{3,2,1,0:T(8,128)(2,1)} %bitcast.15, bf16[640,512]{1,0:T(8,128)(2,1)} %get-tuple-element.136.back_ref, bf16[16,128,128]{2,1,0:T(8,128)(2,1)} %gate_ref.11, ...), custom_call_target="tpu_custom_call" | custom-call | tf_op jit(solution)/shard_map/last_products_0/pallas_call | solution.py:613
  219.8 5.0 %collective-permute-start.12 = (bf16[160,640]{1,0:T(8,128)(2,1)}, bf16[160,640]{1,0:T(8,128)(2,1)S(1)}, u32[]{:S(2)}, u32[]{:S(2)}) collective-permute-start(bf16[160,640]{1,0:T(8,128)(2,1)} %get-tuple-element.138), channel_id=1, source_target_pairs={{0,8},{8,0},{16,24},{24,16},{1,9},{9,1},{17,25},{25,17},{2,10},{10... | collective-permute-start | bytes 614408 | tf_op jit(solution)/shard_map/ppermute | solution.py:151
  229.3 3.9 %last_products_5.1 = (bf16[160,384]{1,0:T(8,128)(2,1)}, bf16[160,384]{1,0:T(8,128)(2,1)}, bf16[160,384]{1,0:T(8,128)(2,1)}, bf16[160,384]{1,0:T(8,128)(2,1)}) custom-call(bf16[8,2,128,512]{3,2,1,0:T(8,128)(2,1)} %bitcast.16, bf16[640,512]{1,0:T(8,128)(2,1)} %get-tuple-element.136.back_ref, bf16[16,128,128]{2,1,0:T(8,128)(2,1)} %gate_ref.11, ...), custom_call_target="tpu_custom_call" | custom-call | tf_op jit(solution)/shard_map/last_products_5/pallas_call | solution.py:613
  233.2 3.4 right_grads_0.1
  236.6 6.0 %collective-permute-done.13.refs_2_ = bf16[160,640]{1,0:T(8,128)(2,1)S(1)} collective-permute-done((bf16[160,640]{1,0:T(8,128)(2,1)}, bf16[160,640]{1,0:T(8,128)(2,1)S(1)}, u32[]{:S(2)}, u32[]{:S(2)}) %collective-permute-start.13) | collective-permute-done | bytes 204832 | tf_op jit(solution)/shard_map/ppermute | solution.py:151
  244.0 4.2 %all-to-all-start.7 = ((bf16[8,256,512]{2,1,0:T(8,128)(2,1)}), bf16[8,256,512]{2,1,0:T(8,128)(2,1)S(1)}, u32[]{:S(2)}, u32[]{:S(2)}) async-start(bf16[8,256,512]{2,1,0:T(8,128)(2,1)} %get-tuple-element.151), calls=%async_computation.7 | async-start | bytes 4194304 | tf_op jit(solution)/shard_map/all_to_all | solution.py:709
  248.2 3.9 %collective-permute-start.15 = (bf16[160,384]{1,0:T(8,128)(2,1)}, bf16[160,384]{1,0:T(8,128)(2,1)S(1)}, u32[]{:S(2)}, u32[]{:S(2)}) collective-permute-start(bf16[160,384]{1,0:T(8,128)(2,1)} %get-tuple-element.142), channel_id=1, source_target_pairs={{0,8},{8,0},{16,24},{24,16},{1,9},{9,1},{17,25},{25,17},{2,10},{10... | collective-permute-start | bytes 368648 | tf_op jit(solution)/shard_map/ppermute | solution.py:151
  254.5 3.8 %last_products_8.1 = (bf16[160,384]{1,0:T(8,128)(2,1)}, bf16[160,384]{1,0:T(8,128)(2,1)}, bf16[160,384]{1,0:T(8,128)(2,1)}, bf16[160,384]{1,0:T(8,128)(2,1)}) custom-call(bf16[8,2,128,512]{3,2,1,0:T(8,128)(2,1)} %bitcast.12, bf16[640,512]{1,0:T(8,128)(2,1)} %get-tuple-element.136.back_ref, bf16[16,128,128]{2,1,0:T(8,128)(2,1)} %gate_ref.11, ...), custom_call_target="tpu_custom_call" | custom-call | tf_op jit(solution)/shard_map/last_products_8/pallas_call | solution.py:613
  262.8 5.4 %last_products_11.1 = (bf16[160,640]{1,0:T(8,128)(2,1)}, bf16[160,640]{1,0:T(8,128)(2,1)}, bf16[160,640]{1,0:T(8,128)(2,1)}, bf16[160,640]{1,0:T(8,128)(2,1)}) custom-call(bf16[8,2,128,512]{3,2,1,0:T(8,128)(2,1)} %bitcast.13, bf16[640,512]{1,0:T(8,128)(2,1)} %get-tuple-element.136.back_ref, bf16[16,128,128]{2,1,0:T(8,128)(2,1)} %gate_ref.11, ...), custom_call_target="tpu_custom_call" | custom-call | tf_op jit(solution)/shard_map/last_products_11/pallas_call | solution.py:613
  268.3 7.0 %collective-permute-done.19.refs_2_ = bf16[160,384]{1,0:T(8,128)(2,1)S(1)} collective-permute-done((bf16[160,384]{1,0:T(8,128)(2,1)}, bf16[160,384]{1,0:T(8,128)(2,1)S(1)}, u32[]{:S(2)}, u32[]{:S(2)}) %collective-permute-start.19) | collective-permute-done | bytes 122912 | tf_op jit(solution)/shard_map/ppermute | solution.py:151
  278.6 4.4 %all-to-all-start.8 = ((bf16[8,256,512]{2,1,0:T(8,128)(2,1)}), bf16[8,256,512]{2,1,0:T(8,128)(2,1)}, u32[]{:S(2)}, u32[]{:S(2)}) async-start(bf16[8,256,512]{2,1,0:T(8,128)(2,1)} %right_down.1), calls=%async_computation.8 | async-start | bytes 4194304 | tf_op jit(solution)/shard_map/all_to_all | solution.py:709
  282.9 3.5 collective-permute-start.22
  289.9 4.8 %unsort_0.1.refs_4_ = bf16[2048,640]{1,0:T(8,128)(2,1)} custom-call(bf16[640,640]{1,0:T(8,128)(2,1)} %get-tuple-element.98.home_ref, bf16[160,640]{1,0:T(8,128)(2,1)} %get-tuple-element.137.refs_0_, bf16[160,640]{1,0:T(8,128)(2,1)} %copy-done.27, bf16[160,640]{1,0:T(8,128)(2,1)} %copy-done.28, bf16[160,640]{1,0:T(8,128)(2,1)} %copy-done.29), custom_call_target="tpu_custom_call" | custom-call | tf_op jit(solution)/shard_map/unsort_0/pallas_call | solution.py:171
  294.8 3.7 %unsort_5.1.refs_4_ = bf16[2048,640]{1,0:T(8,128)(2,1)} custom-call(bf16[640,640]{1,0:T(8,128)(2,1)} %get-tuple-element.98.home_ref, bf16[160,384]{1,0:T(8,128)(2,1)} %get-tuple-element.141.refs_0_, bf16[160,384]{1,0:T(8,128)(2,1)} %copy-done.39, bf16[160,384]{1,0:T(8,128)(2,1)} %copy-done.40, ...), custom_call_target="tpu_custom_call", output_to_operand_aliasing={{}: (5, {})} | custom-call | tf_op jit(solution)/shard_map/unsort_5/pallas_call | solution.py:171
  301.0 3.4 collective-permute-done.23.refs_2_
  304.4 3.5 right_grads_1.1
  307.9 4.0 %collective-permute-start.25 = (bf16[2,16,32,128]{3,2,1,0:T(8,128)(2,1)}, bf16[2,16,32,128]{3,2,1,0:T(8,128)(2,1)S(1)}, u32[]{:S(2)}, u32[]{:S(2)}) collective-permute-start(bf16[2,16,32,128]{3,2,1,0:T(8,128)(2,1)} %get-tuple-element.165), channel_id=1, source_target_pairs={{0,8},{8,0},{16,24},{24,16},{1,9},{9,1},{17,25},{25,17},{2,10},{10... | collective-permute-start | bytes 786440 | tf_op jit(solution)/shard_map/ppermute | solution.py:363
  312.2 5.7 %collective-permute-done.25.refs_3_ = bf16[2,16,32,128]{3,2,1,0:T(8,128)(2,1)S(1)} collective-permute-done((bf16[2,16,32,128]{3,2,1,0:T(8,128)(2,1)}, bf16[2,16,32,128]{3,2,1,0:T(8,128)(2,1)S(1)}, u32[]{:S(2)}, u32[]{:S(2)}) %collective-permute-start.25) | collective-permute-done | bytes 262176 | tf_op jit(solution)/shard_map/ppermute | solution.py:363
  317.9 4.4 %left_down.1 = bf16[8,256,512]{2,1,0:T(8,128)(2,1)} custom-call(bf16[8,256,512]{2,1,0:T(8,128)(2,1)} %all-to-all-done.8.in_ref, bf16[16,128,128]{2,1,0:T(8,128)(2,1)S(1)} %copy-done.7), custom_call_target="tpu_custom_call" | custom-call | tf_op jit(solution)/shard_map/left_down/pallas_call | solution.py:301
  322.4 4.5 %all-to-all-start.9 = ((bf16[8,256,512]{2,1,0:T(8,128)(2,1)}), bf16[8,256,512]{2,1,0:T(8,128)(2,1)}, u32[]{:S(2)}, u32[]{:S(2)}) async-start(bf16[8,256,512]{2,1,0:T(8,128)(2,1)} %left_down.1), calls=%async_computation.9 | async-start | bytes 4194304 | tf_op jit(solution)/shard_map/all_to_all | solution.py:709
  337.1 3.5 unsort_8.1.refs_4_
  340.7 4.9 %unsort_11.1 = bf16[2048,640]{1,0:T(8,128)(2,1)} custom-call(bf16[640,640]{1,0:T(8,128)(2,1)} %get-tuple-element.98.home_ref, bf16[160,640]{1,0:T(8,128)(2,1)} %get-tuple-element.156.refs_0_, bf16[160,640]{1,0:T(8,128)(2,1)} %copy-done.30, bf16[160,640]{1,0:T(8,128)(2,1)} %copy-done.31, bf16[160,640]{1,0:T(8,128)(2,1)} %copy-done.32, ...), custom_call_target="tpu_custom_call", output_to_operand_aliasing={{}: (5, {})} | custom-call | tf_op jit(solution)/shard_map/unsort_11/pallas_call | solution.py:171
  (162 shorter events, 78.7 us)
Async XLA Ops:
  5.5 31.9 %all-to-all-start = ((bf16[8,256,512]{2,1,0:T(8,128)(2,1)}), bf16[8,256,512]{2,1,0:T(8,128)(2,1)S(1)}, u32[]{:S(2)}, u32[]{:S(2)}) async-start(bf16[8,256,512]{2,1,0:T(8,128)(2,1)} %send_cotangent.1), calls=%async_computation | async-start | bytes 4194304 | tf_op jit(solution)/shard_map/all_to_all | solution.py:709
  17.2 13.4 %collective-permute-start = (bf16[160,512]{1,0:T(8,128)(2,1)}, bf16[160,512]{1,0:T(8,128)(2,1)S(1)}, u32[]{:S(2)}, u32[]{:S(2)}) collective-permute-start(bf16[160,512]{1,0:T(8,128)(2,1)} %get-tuple-element.100), channel_id=1, source_target_pairs={{0,8},{8,0},{16,24},{24,16},{1,9},{9,1},{17,25},{25,17},{2,10},{10... | collective-permute-start | bytes 491528 | tf_op jit(solution)/shard_map/ppermute | solution.py:151
  18.8 15.2 %collective-permute-start.1 = (bf16[160,512]{1,0:T(8,128)(2,1)}, bf16[160,512]{1,0:T(8,128)(2,1)S(1)}, u32[]{:S(2)}, u32[]{:S(2)}) collective-permute-start(bf16[160,512]{1,0:T(8,128)(2,1)} %get-tuple-element.101), channel_id=1, source_target_pairs={{0,16},{8,24},{16,0},{24,8},{1,17},{9,25},{17,1},{25,9},{2,18},{10... | collective-permute-start | bytes 491528 | tf_op jit(solution)/shard_map/ppermute | solution.py:151
  21.3 12.6 %collective-permute-start.2 = (bf16[160,512]{1,0:T(8,128)(2,1)}, bf16[160,512]{1,0:T(8,128)(2,1)S(1)}, u32[]{:S(2)}, u32[]{:S(2)}) collective-permute-start(bf16[160,512]{1,0:T(8,128)(2,1)} %get-tuple-element.102), channel_id=1, source_target_pairs={{0,24},{8,16},{16,8},{24,0},{1,25},{9,17},{17,9},{25,1},{2,26},{10... | collective-permute-start | bytes 491528 | tf_op jit(solution)/shard_map/ppermute | solution.py:151
  40.7 30.3 %copy-start.4 = (bf16[16,128,128]{2,1,0:T(8,128)(2,1)S(1)}, bf16[16,128,128]{2,1,0:T(8,128)(2,1)}, u32[]{:S(2)}) copy-start(bf16[16,128,128]{2,1,0:T(8,128)(2,1)} %factor_ref.6) | copy-start | bytes 1572868
  40.7 30.3 %all-to-all-start.1 = ((bf16[8,256,512]{2,1,0:T(8,128)(2,1)}), bf16[8,256,512]{2,1,0:T(8,128)(2,1)S(1)}, u32[]{:S(2)}, u32[]{:S(2)}) async-start(bf16[8,256,512]{2,1,0:T(8,128)(2,1)} %left_back_down.1), calls=%async_computation.1 | async-start | bytes 4194304 | tf_op jit(solution)/shard_map/all_to_all | solution.py:709
  44.5 13.2 %collective-permute-start.3 = (bf16[160,768]{1,0:T(8,128)(2,1)}, bf16[160,768]{1,0:T(8,128)(2,1)S(1)}, u32[]{:S(2)}, u32[]{:S(2)}) collective-permute-start(bf16[160,768]{1,0:T(8,128)(2,1)} %get-tuple-element.104), channel_id=1, source_target_pairs={{0,8},{8,0},{16,24},{24,16},{1,9},{9,1},{17,25},{25,17},{2,10},{10... | collective-permute-start | bytes 737288 | tf_op jit(solution)/shard_map/ppermute | solution.py:151
  46.1 20.5 %collective-permute-start.4 = (bf16[160,768]{1,0:T(8,128)(2,1)}, bf16[160,768]{1,0:T(8,128)(2,1)S(1)}, u32[]{:S(2)}, u32[]{:S(2)}) collective-permute-start(bf16[160,768]{1,0:T(8,128)(2,1)} %get-tuple-element.105), channel_id=1, source_target_pairs={{0,16},{8,24},{16,0},{24,8},{1,17},{9,25},{17,1},{25,9},{2,18},{10... | collective-permute-start | bytes 737288 | tf_op jit(solution)/shard_map/ppermute | solution.py:151
  48.7 17.9 %collective-permute-start.5 = (bf16[160,768]{1,0:T(8,128)(2,1)}, bf16[160,768]{1,0:T(8,128)(2,1)S(1)}, u32[]{:S(2)}, u32[]{:S(2)}) collective-permute-start(bf16[160,768]{1,0:T(8,128)(2,1)} %get-tuple-element.106), channel_id=1, source_target_pairs={{0,24},{8,16},{16,8},{24,0},{1,25},{9,17},{17,9},{25,1},{2,26},{10... | collective-permute-start | bytes 737288 | tf_op jit(solution)/shard_map/ppermute | solution.py:151
  74.3 35.3 %all-to-all-start.2 = ((bf16[8,256,512]{2,1,0:T(8,128)(2,1)}), bf16[8,256,512]{2,1,0:T(8,128)(2,1)S(1)}, u32[]{:S(2)}, u32[]{:S(2)}) async-start(bf16[8,256,512]{2,1,0:T(8,128)(2,1)} %right_back_down.1), calls=%async_computation.2 | async-start | bytes 4194304 | tf_op jit(solution)/shard_map/all_to_all | solution.py:709
  77.9 13.2 %collective-permute-start.6 = (bf16[160,768]{1,0:T(8,128)(2,1)}, bf16[160,768]{1,0:T(8,128)(2,1)S(1)}, u32[]{:S(2)}, u32[]{:S(2)}) collective-permute-start(bf16[160,768]{1,0:T(8,128)(2,1)} %get-tuple-element.108), channel_id=1, source_target_pairs={{0,8},{8,0},{16,24},{24,16},{1,9},{9,1},{17,25},{25,17},{2,10},{10... | collective-permute-start | bytes 737288 | tf_op jit(solution)/shard_map/ppermute | solution.py:151
  79.5 20.5 %collective-permute-start.7 = (bf16[160,768]{1,0:T(8,128)(2,1)}, bf16[160,768]{1,0:T(8,128)(2,1)S(1)}, u32[]{:S(2)}, u32[]{:S(2)}) collective-permute-start(bf16[160,768]{1,0:T(8,128)(2,1)} %get-tuple-element.109), channel_id=1, source_target_pairs={{0,16},{8,24},{16,0},{24,8},{1,17},{9,25},{17,1},{25,9},{2,18},{10... | collective-permute-start | bytes 737288 | tf_op jit(solution)/shard_map/ppermute | solution.py:151
  82.1 17.9 %collective-permute-start.8 = (bf16[160,768]{1,0:T(8,128)(2,1)}, bf16[160,768]{1,0:T(8,128)(2,1)S(1)}, u32[]{:S(2)}, u32[]{:S(2)}) collective-permute-start(bf16[160,768]{1,0:T(8,128)(2,1)} %get-tuple-element.110), channel_id=1, source_target_pairs={{0,24},{8,16},{16,8},{24,0},{1,25},{9,17},{17,9},{25,1},{2,26},{10... | collective-permute-start | bytes 737288 | tf_op jit(solution)/shard_map/ppermute | solution.py:151
  109.6 42.4 %all-to-all-start.3 = ((bf16[8,512,384]{2,1,0:T(8,128)(2,1)}), bf16[8,512,384]{2,1,0:T(8,128)(2,1)}, u32[]{:S(2)}, u32[]{:S(2)}) async-start(bf16[8,512,384]{2,1,0:T(8,128)(2,1)} %get-tuple-element.120), calls=%async_computation.3 | async-start | bytes 6291456 | tf_op jit(solution)/shard_map/all_to_all | solution.py:709
  152.0 18.9 %all-to-all-start.4 = ((bf16[8,512,128]{2,1,0:T(8,128)(2,1)}), bf16[8,512,128]{2,1,0:T(8,128)(2,1)S(1)}, u32[]{:S(2)}, u32[]{:S(2)}) async-start(bf16[8,512,128]{2,1,0:T(8,128)(2,1)} %get-tuple-element.121), calls=%async_computation.4 | async-start | bytes 2097152 | tf_op jit(solution)/shard_map/all_to_all | solution.py:709
  178.8 30.5 %all-to-all-start.5 = ((bf16[8,256,512]{2,1,0:T(8,128)(2,1)}), bf16[8,256,512]{2,1,0:T(8,128)(2,1)S(1)}, u32[]{:S(2)}, u32[]{:S(2)}) async-start(bf16[8,256,512]{2,1,0:T(8,128)(2,1)} %get-tuple-element.130), calls=%async_computation.5 | async-start | bytes 4194304 | tf_op jit(solution)/shard_map/all_to_all | solution.py:709
  182.6 17.3 %collective-permute-start.9 = (bf16[32,32,128]{2,1,0:T(8,128)(2,1)}, bf16[32,32,128]{2,1,0:T(8,128)(2,1)S(1)}, u32[]{:S(2)}, u32[]{:S(2)}) collective-permute-start(bf16[32,32,128]{2,1,0:T(8,128)(2,1)} %get-tuple-element.132), channel_id=1, source_target_pairs={{0,8},{8,0},{16,24},{24,16},{1,9},{9,1},{17,25},{25,17},{2,10},{10... | collective-permute-start | bytes 786440 | tf_op jit(solution)/shard_map/ppermute | solution.py:151
  187.5 21.3 %collective-permute-start.10 = (bf16[32,32,128]{2,1,0:T(8,128)(2,1)S(1)}, bf16[32,32,128]{2,1,0:T(8,128)(2,1)S(1)}, u32[]{:S(2)}, u32[]{:S(2)}) collective-permute-start(bf16[32,32,128]{2,1,0:T(8,128)(2,1)S(1)} %copy-done.44), channel_id=1, source_target_pairs={{0,16},{8,24},{16,0},{24,8},{1,17},{9,25},{17,1},{25,9},{2,18},{10... | collective-permute-start | bytes 786440 | tf_op jit(solution)/shard_map/ppermute | solution.py:151
  188.6 20.2 %collective-permute-start.11 = (bf16[32,32,128]{2,1,0:T(8,128)(2,1)S(1)}, bf16[32,32,128]{2,1,0:T(8,128)(2,1)S(1)}, u32[]{:S(2)}, u32[]{:S(2)}) collective-permute-start(bf16[32,32,128]{2,1,0:T(8,128)(2,1)S(1)} %copy-done.43), channel_id=1, source_target_pairs={{0,24},{8,16},{16,8},{24,0},{1,25},{9,17},{17,9},{25,1},{2,26},{10... | collective-permute-start | bytes 786440 | tf_op jit(solution)/shard_map/ppermute | solution.py:151
  199.9 27.3 %copy-start.23 = (bf16[32,32,128]{2,1,0:T(8,128)(2,1)}, bf16[32,32,128]{2,1,0:T(8,128)(2,1)S(1)}, u32[]{:S(2)}) copy-start(bf16[32,32,128]{2,1,0:T(8,128)(2,1)S(1)} %collective-permute-done.9.refs_1_) | copy-start | bytes 786436
  208.8 18.5 %copy-start.24 = (bf16[32,32,128]{2,1,0:T(8,128)(2,1)}, bf16[32,32,128]{2,1,0:T(8,128)(2,1)S(1)}, u32[]{:S(2)}) copy-start(bf16[32,32,128]{2,1,0:T(8,128)(2,1)S(1)} %collective-permute-done.10.refs_2_) | copy-start | bytes 786436
  210.6 32.1 %all-to-all-start.6 = ((bf16[8,256,512]{2,1,0:T(8,128)(2,1)}), bf16[8,256,512]{2,1,0:T(8,128)(2,1)S(1)}, u32[]{:S(2)}, u32[]{:S(2)}) async-start(bf16[8,256,512]{2,1,0:T(8,128)(2,1)} %get-tuple-element.135), calls=%async_computation.6 | async-start | bytes 4194304 | tf_op jit(solution)/shard_map/all_to_all | solution.py:709
  219.8 16.8 %collective-permute-start.12 = (bf16[160,640]{1,0:T(8,128)(2,1)}, bf16[160,640]{1,0:T(8,128)(2,1)S(1)}, u32[]{:S(2)}, u32[]{:S(2)}) collective-permute-start(bf16[160,640]{1,0:T(8,128)(2,1)} %get-tuple-element.138), channel_id=1, source_target_pairs={{0,8},{8,0},{16,24},{24,16},{1,9},{9,1},{17,25},{25,17},{2,10},{10... | collective-permute-start | bytes 614408 | tf_op jit(solution)/shard_map/ppermute | solution.py:151
  224.8 17.8 %collective-permute-start.13 = (bf16[160,640]{1,0:T(8,128)(2,1)}, bf16[160,640]{1,0:T(8,128)(2,1)S(1)}, u32[]{:S(2)}, u32[]{:S(2)}) collective-permute-start(bf16[160,640]{1,0:T(8,128)(2,1)} %get-tuple-element.139), channel_id=1, source_target_pairs={{0,16},{8,24},{16,0},{24,8},{1,17},{9,25},{17,1},{25,9},{2,18},{10... | collective-permute-start | bytes 614408 | tf_op jit(solution)/shard_map/ppermute | solution.py:151
  225.9 16.8 %collective-permute-start.14 = (bf16[160,640]{1,0:T(8,128)(2,1)}, bf16[160,640]{1,0:T(8,128)(2,1)S(1)}, u32[]{:S(2)}, u32[]{:S(2)}) collective-permute-start(bf16[160,640]{1,0:T(8,128)(2,1)} %get-tuple-element.140), channel_id=1, source_target_pairs={{0,24},{8,16},{16,8},{24,0},{1,25},{9,17},{17,9},{25,1},{2,26},{10... | collective-permute-start | bytes 614408 | tf_op jit(solution)/shard_map/ppermute | solution.py:151
  236.6 41.9 %copy-start.27 = (bf16[160,640]{1,0:T(8,128)(2,1)}, bf16[160,640]{1,0:T(8,128)(2,1)S(1)}, u32[]{:S(2)}) copy-start(bf16[160,640]{1,0:T(8,128)(2,1)S(1)} %collective-permute-done.12.refs_1_) | copy-start | bytes 614404
  242.7 35.9 %copy-start.28 = (bf16[160,640]{1,0:T(8,128)(2,1)}, bf16[160,640]{1,0:T(8,128)(2,1)S(1)}, u32[]{:S(2)}) copy-start(bf16[160,640]{1,0:T(8,128)(2,1)S(1)} %collective-permute-done.13.refs_2_) | copy-start | bytes 614404
  242.7 35.9 %copy-start.29 = (bf16[160,640]{1,0:T(8,128)(2,1)}, bf16[160,640]{1,0:T(8,128)(2,1)S(1)}, u32[]{:S(2)}) copy-start(bf16[160,640]{1,0:T(8,128)(2,1)S(1)} %collective-permute-done.14.refs_3_) | copy-start | bytes 614404
  244.0 31.3 %all-to-all-start.7 = ((bf16[8,256,512]{2,1,0:T(8,128)(2,1)}), bf16[8,256,512]{2,1,0:T(8,128)(2,1)S(1)}, u32[]{:S(2)}, u32[]{:S(2)}) async-start(bf16[8,256,512]{2,1,0:T(8,128)(2,1)} %get-tuple-element.151), calls=%async_computation.7 | async-start | bytes 4194304 | tf_op jit(solution)/shard_map/all_to_all | solution.py:709
  248.2 13.2 %collective-permute-start.15 = (bf16[160,384]{1,0:T(8,128)(2,1)}, bf16[160,384]{1,0:T(8,128)(2,1)S(1)}, u32[]{:S(2)}, u32[]{:S(2)}) collective-permute-start(bf16[160,384]{1,0:T(8,128)(2,1)} %get-tuple-element.142), channel_id=1, source_target_pairs={{0,8},{8,0},{16,24},{24,16},{1,9},{9,1},{17,25},{25,17},{2,10},{10... | collective-permute-start | bytes 368648 | tf_op jit(solution)/shard_map/ppermute | solution.py:151
  252.1 16.1 %collective-permute-start.16 = (bf16[160,384]{1,0:T(8,128)(2,1)}, bf16[160,384]{1,0:T(8,128)(2,1)S(1)}, u32[]{:S(2)}, u32[]{:S(2)}) collective-permute-start(bf16[160,384]{1,0:T(8,128)(2,1)} %get-tuple-element.143), channel_id=1, source_target_pairs={{0,16},{8,24},{16,0},{24,8},{1,17},{9,25},{17,1},{25,9},{2,18},{10... | collective-permute-start | bytes 368648 | tf_op jit(solution)/shard_map/ppermute | solution.py:151
  253.1 15.1 %collective-permute-start.17 = (bf16[160,384]{1,0:T(8,128)(2,1)}, bf16[160,384]{1,0:T(8,128)(2,1)S(1)}, u32[]{:S(2)}, u32[]{:S(2)}) collective-permute-start(bf16[160,384]{1,0:T(8,128)(2,1)} %get-tuple-element.144), channel_id=1, source_target_pairs={{0,24},{8,16},{16,8},{24,0},{1,25},{9,17},{17,9},{25,1},{2,26},{10... | collective-permute-start | bytes 368648 | tf_op jit(solution)/shard_map/ppermute | solution.py:151
  258.4 9.9 %collective-permute-start.18 = (bf16[160,384]{1,0:T(8,128)(2,1)}, bf16[160,384]{1,0:T(8,128)(2,1)S(1)}, u32[]{:S(2)}, u32[]{:S(2)}) collective-permute-start(bf16[160,384]{1,0:T(8,128)(2,1)} %get-tuple-element.153), channel_id=1, source_target_pairs={{0,8},{8,0},{16,24},{24,16},{1,9},{9,1},{17,25},{25,17},{2,10},{10... | collective-permute-start | bytes 368648 | tf_op jit(solution)/shard_map/ppermute | solution.py:151
  259.5 15.8 %collective-permute-start.19 = (bf16[160,384]{1,0:T(8,128)(2,1)}, bf16[160,384]{1,0:T(8,128)(2,1)S(1)}, u32[]{:S(2)}, u32[]{:S(2)}) collective-permute-start(bf16[160,384]{1,0:T(8,128)(2,1)} %get-tuple-element.154), channel_id=1, source_target_pairs={{0,16},{8,24},{16,0},{24,8},{1,17},{9,25},{17,1},{25,9},{2,18},{10... | collective-permute-start | bytes 368648 | tf_op jit(solution)/shard_map/ppermute | solution.py:151
  261.4 13.8 %collective-permute-start.20 = (bf16[160,384]{1,0:T(8,128)(2,1)}, bf16[160,384]{1,0:T(8,128)(2,1)}, u32[]{:S(2)}, u32[]{:S(2)}) collective-permute-start(bf16[160,384]{1,0:T(8,128)(2,1)} %get-tuple-element.155), channel_id=1, source_target_pairs={{0,24},{8,16},{16,8},{24,0},{1,25},{9,17},{17,9},{25,1},{2,26},{10... | collective-permute-start | bytes 368648 | tf_op jit(solution)/shard_map/ppermute | solution.py:151
  278.6 39.3 %all-to-all-start.8 = ((bf16[8,256,512]{2,1,0:T(8,128)(2,1)}), bf16[8,256,512]{2,1,0:T(8,128)(2,1)}, u32[]{:S(2)}, u32[]{:S(2)}) async-start(bf16[8,256,512]{2,1,0:T(8,128)(2,1)} %right_down.1), calls=%async_computation.8 | async-start | bytes 4194304 | tf_op jit(solution)/shard_map/all_to_all | solution.py:709
  282.9 18.0 %collective-permute-start.22 = (bf16[160,640]{1,0:T(8,128)(2,1)}, bf16[160,640]{1,0:T(8,128)(2,1)S(1)}, u32[]{:S(2)}, u32[]{:S(2)}) collective-permute-start(bf16[160,640]{1,0:T(8,128)(2,1)} %get-tuple-element.157), channel_id=1, source_target_pairs={{0,8},{8,0},{16,24},{24,16},{1,9},{9,1},{17,25},{25,17},{2,10},{10... | collective-permute-start | bytes 614408 | tf_op jit(solution)/shard_map/ppermute | solution.py:151
  286.4 17.9 %collective-permute-start.23 = (bf16[160,640]{1,0:T(8,128)(2,1)}, bf16[160,640]{1,0:T(8,128)(2,1)S(1)}, u32[]{:S(2)}, u32[]{:S(2)}) collective-permute-start(bf16[160,640]{1,0:T(8,128)(2,1)} %get-tuple-element.158), channel_id=1, source_target_pairs={{0,16},{8,24},{16,0},{24,8},{1,17},{9,25},{17,1},{25,9},{2,18},{10... | collective-permute-start | bytes 614408 | tf_op jit(solution)/shard_map/ppermute | solution.py:151
  287.5 16.8 %collective-permute-start.24 = (bf16[160,640]{1,0:T(8,128)(2,1)}, bf16[160,640]{1,0:T(8,128)(2,1)S(1)}, u32[]{:S(2)}, u32[]{:S(2)}) collective-permute-start(bf16[160,640]{1,0:T(8,128)(2,1)} %get-tuple-element.159), channel_id=1, source_target_pairs={{0,24},{8,16},{16,8},{24,0},{1,25},{9,17},{17,9},{25,1},{2,26},{10... | collective-permute-start | bytes 614408 | tf_op jit(solution)/shard_map/ppermute | solution.py:151
  288.9 23.0 %collective-permute-start.21 = (bf16[2,16,32,128]{3,2,1,0:T(8,128)(2,1)}, bf16[2,16,32,128]{3,2,1,0:T(8,128)(2,1)S(1)}, u32[]{:S(2)}, u32[]{:S(2)}) collective-permute-start(bf16[2,16,32,128]{3,2,1,0:T(8,128)(2,1)} %get-tuple-element.149), channel_id=1, source_target_pairs={{0,8},{8,0},{16,24},{24,16},{1,9},{9,1},{17,25},{25,17},{2,10},{10... | collective-permute-start | bytes 786440 | tf_op jit(solution)/shard_map/ppermute | solution.py:363
  300.0 12.2 %collective-permute-start.26 = (bf16[2,16,32,128]{3,2,1,0:T(8,128)(2,1)}, bf16[2,16,32,128]{3,2,1,0:T(8,128)(2,1)S(1)}, u32[]{:S(2)}, u32[]{:S(2)}) collective-permute-start(bf16[2,16,32,128]{3,2,1,0:T(8,128)(2,1)} %get-tuple-element.163), channel_id=1, source_target_pairs={{0,8},{8,0},{16,24},{24,16},{1,9},{9,1},{17,25},{25,17},{2,10},{10... | collective-permute-start | bytes 786440 | tf_op jit(solution)/shard_map/ppermute | solution.py:363
  307.9 10.0 %collective-permute-start.25 = (bf16[2,16,32,128]{3,2,1,0:T(8,128)(2,1)}, bf16[2,16,32,128]{3,2,1,0:T(8,128)(2,1)S(1)}, u32[]{:S(2)}, u32[]{:S(2)}) collective-permute-start(bf16[2,16,32,128]{3,2,1,0:T(8,128)(2,1)} %get-tuple-element.165), channel_id=1, source_target_pairs={{0,8},{8,0},{16,24},{24,16},{1,9},{9,1},{17,25},{25,17},{2,10},{10... | collective-permute-start | bytes 786440 | tf_op jit(solution)/shard_map/ppermute | solution.py:363
  322.4 31.1 %all-to-all-start.9 = ((bf16[8,256,512]{2,1,0:T(8,128)(2,1)}), bf16[8,256,512]{2,1,0:T(8,128)(2,1)}, u32[]{:S(2)}, u32[]{:S(2)}) async-start(bf16[8,256,512]{2,1,0:T(8,128)(2,1)} %left_down.1), calls=%async_computation.9 | async-start | bytes 4194304 | tf_op jit(solution)/shard_map/all_to_all | solution.py:709
  330.0 16.8 %collective-permute-start.30 = (bf16[2,16,32,128]{3,2,1,0:T(8,128)(2,1)}, bf16[2,16,32,128]{3,2,1,0:T(8,128)(2,1)S(1)}, u32[]{:S(2)}, u32[]{:S(2)}) collective-permute-start(bf16[2,16,32,128]{3,2,1,0:T(8,128)(2,1)} %get-tuple-element.181), channel_id=1, source_target_pairs={{0,8},{8,0},{16,24},{24,16},{1,9},{9,1},{17,25},{25,17},{2,10},{10... | collective-permute-start | bytes 786440 | tf_op jit(solution)/shard_map/ppermute | solution.py:363
  334.2 16.8 %collective-permute-start.28 = (bf16[1,16,32,128]{3,2,1,0:T(8,128)(2,1)}, bf16[1,16,32,128]{3,2,1,0:T(8,128)(2,1)S(1)}, u32[]{:S(2)}, u32[]{:S(2)}) collective-permute-start(bf16[1,16,32,128]{3,2,1,0:T(8,128)(2,1)} %get-tuple-element.171), channel_id=1, source_target_pairs={{0,16},{8,24},{16,0},{24,8},{1,17},{9,25},{17,1},{25,9},{2,18},{10... | collective-permute-start | bytes 393224 | tf_op jit(solution)/shard_map/ppermute | solution.py:363
  335.5 20.7 %collective-permute-start.27 = (bf16[1,16,32,128]{3,2,1,0:T(8,128)(2,1)}, bf16[1,16,32,128]{3,2,1,0:T(8,128)(2,1)S(1)}, u32[]{:S(2)}, u32[]{:S(2)}) collective-permute-start(bf16[1,16,32,128]{3,2,1,0:T(8,128)(2,1)} %get-tuple-element.169), channel_id=1, source_target_pairs={{0,16},{8,24},{16,0},{24,8},{1,17},{9,25},{17,1},{25,9},{2,18},{10... | collective-permute-start | bytes 393224 | tf_op jit(solution)/shard_map/ppermute | solution.py:363
  345.5 12.9 %collective-permute-start.29 = (bf16[1,16,32,128]{3,2,1,0:T(8,128)(2,1)S(1)}, bf16[1,16,32,128]{3,2,1,0:T(8,128)(2,1)S(1)}, u32[]{:S(2)}, u32[]{:S(2)}) collective-permute-start(bf16[1,16,32,128]{3,2,1,0:T(8,128)(2,1)S(1)} %copy-done.45), channel_id=1, source_target_pairs={{0,16},{8,24},{16,0},{24,8},{1,17},{9,25},{17,1},{25,9},{2,18},{10... | collective-permute-start | bytes 393224 | tf_op jit(solution)/shard_map/ppermute | solution.py:363
  349.3 11.7 %collective-permute-start.31 = (bf16[1,16,32,128]{3,2,1,0:T(8,128)(2,1)}, bf16[1,16,32,128]{3,2,1,0:T(8,128)(2,1)S(1)}, u32[]{:S(2)}, u32[]{:S(2)}) collective-permute-start(bf16[1,16,32,128]{3,2,1,0:T(8,128)(2,1)} %get-tuple-element.185), channel_id=1, source_target_pairs={{0,16},{8,24},{16,0},{24,8},{1,17},{9,25},{17,1},{25,9},{2,18},{10... | collective-permute-start | bytes 393224 | tf_op jit(solution)/shard_map/ppermute | solution.py:363
  (40 other events, 266.0 us)

commit v7 on v6

--- a/solution.py
+++ b/solution.py
@@ -275,7 +275,7 @@
 
 
 def send_cotangent(plan, cotangent):
-    step = 128
+    step = step_of(plan.tok)
     return pl.pallas_call(
         functools.partial(cotangent_kernel, plan),
         grid=(plan.tok // step,),
@@ -779,7 +779,8 @@
     down_spread = swap(down_spread)
     right_high = (right_high[0], swap_rows(right_high[1], 1, groups))
     down_grad = (down_grad[0], swap_rows(down_grad[1], 1, groups))
-    down_spread = after(down_spread, right_low[1], right_high[1], down_grad[1])
+    mixed_grad = unsort(rows[2], back_pieces[2], *places, mixed_grad)
+    down_spread = after(down_spread, right_low[1], right_high[1], down_grad[1], mixed_grad)
     result = product(plan, down_spread, left_down, TN, "left_down")
     left_down_grad = factor_grad(
         plan, own, after(down_spread, result), out_grads, left_down, scale, groups,
@@ -787,7 +788,6 @@
     )
     output = natural_order(plan, move(result))
     left_down_grad = [(left_down_grad[0], swap_rows(left_down_grad[1], 1, groups))]
-    mixed_grad = unsort(rows[2], back_pieces[2], *places, mixed_grad)
     mixed_grad = unsort(rows[3], back_pieces[3], *places, mixed_grad)
     left_down_grad = after(left_down_grad, mixed_grad)
     right_low, right_high, down_grad = finish(

time: 366 us -> 366 us (level)
  transfers between devices with their start and end apart: 42 -> 42, of which waited for: 19 -> 18; matrix products, arithmetic and copies ran while one was open for 0% -> 0% of each run, Pallas kernels for 29% -> 28%
where the time goes in v7:
time: 366 us; the launch traced here: 363 us
  Pallas kernels  132 us (36%)
  waiting for transfers between devices  124 us (34%)
  starting transfers between devices  100 us (27%)
  local copies, waits for them, and re-layouts  6.25 us (2%)
    ppermute x24, waiting for transfers between devices, exchange(): received.append(lax.ppermute(arrays[k], axis, pairs))  73.9 us
    ppermute x24, starting transfers between devices, exchange(): received.append(lax.ppermute(arrays[k], axis, pairs))  45 us
    all_to_all x10, starting transfers between devices, move(): lax.all_to_all(array, 'feat', split_axis=0, concat_axis=0, tiled=True)  41.6 us
    all_to_all x10, waiting for transfers between devices, move(): lax.all_to_all(array, 'feat', split_axis=0, concat_axis=0, tiled=True)  41.4 us
    pallas_call x2, Pallas kernels, middle(): pl.pallas_call(functools.partial(middle_kernel, plan, scale, first, last)...  22.8 us
    pallas_call x4, Pallas kernels, last_products(): pl.pallas_call(functools.partial(last_kernel, plan), grid=(count,), in_sp...  18.4 us
    pallas_call x4, Pallas kernels, unsort(): pl.pallas_call(functools.partial(unsort_kernel, groups), grid=(count,), i...  16.8 us
    pallas_call x4, Pallas kernels, product(): pl.pallas_call(functools.partial(product_kernel, plan, over), grid=(plan....  14.1 us
  transfers between devices with their start and end apart: 42, of which 18 were waited for; matrix products, arithmetic and copies ran while one was open for 0% of the time, Pallas kernels for 28%

profile of v7, /device:TPU:0, one launch (start us, length us, event | category | flops | bytes accessed | tf_op | source)
XLA Modules:
  0.0 363.4 jit_solution(17511371593366208196)
XLA Ops:
  0.6 4.7 %send_cotangent.1 = bf16[8,256,512]{2,1,0:T(8,128)(2,1)} custom-call(bf16[2048,512]{1,0:T(8,128)(2,1)} %in_ref.1), custom_call_target="tpu_custom_call" | custom-call | tf_op jit(solution)/shard_map/send_cotangent/pallas_call | solution.py:279
  5.3 5.3 %all-to-all-start = ((bf16[8,256,512]{2,1,0:T(8,128)(2,1)}), bf16[8,256,512]{2,1,0:T(8,128)(2,1)S(1)}, u32[]{:S(2)}, u32[]{:S(2)}) async-start(bf16[8,256,512]{2,1,0:T(8,128)(2,1)} %send_cotangent.1), calls=%async_computation | async-start | bytes 4194304 | tf_op jit(solution)/shard_map/all_to_all | solution.py:709
  13.7 3.3 mix_and_sort_0.1
  21.4 4.5 %mix_and_sort_5.1 = (bf16[160,768]{1,0:T(8,128)(2,1)}, bf16[160,768]{1,0:T(8,128)(2,1)}, bf16[160,768]{1,0:T(8,128)(2,1)}, bf16[160,768]{1,0:T(8,128)(2,1)}) custom-call(f32[3]{0:T(128)S(1)} %copy-done.8, bf16[3,2048,640]{2,1,0:T(8,128)(2,1)} %earlier_ref.5, bf16[640,640]{1,0:T(8,128)(2,1)} %get-tuple-element.98.home_ref), custom_call_target="tpu_custom_call" | custom-call | tf_op jit(solution)/shard_map/mix_and_sort_5/pallas_call | solution.py:125
  25.8 4.5 %mix_and_sort_2.1 = (bf16[160,768]{1,0:T(8,128)(2,1)}, bf16[160,768]{1,0:T(8,128)(2,1)}, bf16[160,768]{1,0:T(8,128)(2,1)}, bf16[160,768]{1,0:T(8,128)(2,1)}) custom-call(f32[3]{0:T(128)S(1)} %copy-done.8, bf16[3,2048,640]{2,1,0:T(8,128)(2,1)} %earlier_ref.5, bf16[640,640]{1,0:T(8,128)(2,1)} %get-tuple-element.98.home_ref), custom_call_target="tpu_custom_call" | custom-call | tf_op jit(solution)/shard_map/mix_and_sort_2/pallas_call | solution.py:125
  30.3 3.4 collective-permute-done.1.refs_2_
  33.8 3.5 all-to-all-done.in_ref.other_ref
  40.5 3.7 %all-to-all-start.1 = ((bf16[8,256,512]{2,1,0:T(8,128)(2,1)}), bf16[8,256,512]{2,1,0:T(8,128)(2,1)S(1)}, u32[]{:S(2)}, u32[]{:S(2)}) async-start(bf16[8,256,512]{2,1,0:T(8,128)(2,1)} %left_back_down.1), calls=%async_computation.1 | async-start | bytes 4194304 | tf_op jit(solution)/shard_map/all_to_all | solution.py:709
  48.7 8.8 %collective-permute-done.3.refs_5_ = bf16[160,768]{1,0:T(8,128)(2,1)S(1)} collective-permute-done((bf16[160,768]{1,0:T(8,128)(2,1)}, bf16[160,768]{1,0:T(8,128)(2,1)S(1)}, u32[]{:S(2)}, u32[]{:S(2)}) %collective-permute-start.3) | collective-permute-done | bytes 245792 | tf_op jit(solution)/shard_map/ppermute | solution.py:151
  57.5 8.9 %collective-permute-done.4.refs_6_ = bf16[160,768]{1,0:T(8,128)(2,1)S(1)} collective-permute-done((bf16[160,768]{1,0:T(8,128)(2,1)}, bf16[160,768]{1,0:T(8,128)(2,1)S(1)}, u32[]{:S(2)}, u32[]{:S(2)}) %collective-permute-start.4) | collective-permute-done | bytes 245792 | tf_op jit(solution)/shard_map/ppermute | solution.py:151
  66.4 4.4 %all-to-all-done.1.in_ref.other_ref = bf16[8,256,512]{2,1,0:T(8,128)(2,1)S(1)} async-done(((bf16[8,256,512]{2,1,0:T(8,128)(2,1)}), bf16[8,256,512]{2,1,0:T(8,128)(2,1)S(1)}, u32[]{:S(2)}, u32[]{:S(2)}) %all-to-all-start.1) | async-done | bytes 2097184 | tf_op jit(solution)/shard_map/all_to_all | solution.py:709
  74.1 3.6 all-to-all-start.2
  82.1 8.8 %collective-permute-done.6.refs_9_ = bf16[160,768]{1,0:T(8,128)(2,1)S(1)} collective-permute-done((bf16[160,768]{1,0:T(8,128)(2,1)}, bf16[160,768]{1,0:T(8,128)(2,1)S(1)}, u32[]{:S(2)}, u32[]{:S(2)}) %collective-permute-start.6) | collective-permute-done | bytes 245792 | tf_op jit(solution)/shard_map/ppermute | solution.py:151
  90.9 8.9 %collective-permute-done.7.refs_10_ = bf16[160,768]{1,0:T(8,128)(2,1)S(1)} collective-permute-done((bf16[160,768]{1,0:T(8,128)(2,1)}, bf16[160,768]{1,0:T(8,128)(2,1)S(1)}, u32[]{:S(2)}, u32[]{:S(2)}) %collective-permute-start.7) | collective-permute-done | bytes 245792 | tf_op jit(solution)/shard_map/ppermute | solution.py:151
  100.6 8.8 %first_products_0.1 = (bf16[384,2048]{1,0:T(8,128)(2,1)}, bf16[8,512,384]{2,1,0:T(8,128)(2,1)}) custom-call(bf16[160,512]{1,0:T(8,128)(2,1)} %get-tuple-element.99.refs_0_, bf16[160,512]{1,0:T(8,128)(2,1)} %copy-done.17, bf16[160,512]{1,0:T(8,128)(2,1)} %copy-done.18, bf16[160,512]{1,0:T(8,128)(2,1)} %copy-done.19, ...), custom_call_target="tpu_custom_call" | custom-call | tf_op jit(solution)/shard_map/first_products_0/pallas_call | solution.py:463
  109.4 4.5 %all-to-all-start.3 = ((bf16[8,512,384]{2,1,0:T(8,128)(2,1)}), bf16[8,512,384]{2,1,0:T(8,128)(2,1)}, u32[]{:S(2)}, u32[]{:S(2)}) async-start(bf16[8,512,384]{2,1,0:T(8,128)(2,1)} %get-tuple-element.120), calls=%async_computation.3 | async-start | bytes 6291456 | tf_op jit(solution)/shard_map/all_to_all | solution.py:709
  113.9 5.1 %first_products_1.1 = (bf16[128,2048]{1,0:T(8,128)(2,1)}, bf16[8,512,128]{2,1,0:T(8,128)(2,1)}) custom-call(bf16[160,512]{1,0:T(8,128)(2,1)} %get-tuple-element.99.refs_0_, bf16[160,512]{1,0:T(8,128)(2,1)} %copy-done.17, bf16[160,512]{1,0:T(8,128)(2,1)} %copy-done.18, bf16[160,512]{1,0:T(8,128)(2,1)} %copy-done.19, ...), custom_call_target="tpu_custom_call" | custom-call | tf_op jit(solution)/shard_map/first_products_1/pallas_call | solution.py:463
  119.0 32.8 %all-to-all-done.3.spread_ref = bf16[8,512,384]{2,1,0:T(8,128)(2,1)} async-done(((bf16[8,512,384]{2,1,0:T(8,128)(2,1)}), bf16[8,512,384]{2,1,0:T(8,128)(2,1)}, u32[]{:S(2)}, u32[]{:S(2)}) %all-to-all-start.3) | async-done | bytes 3145760 | tf_op jit(solution)/shard_map/all_to_all | solution.py:709
  151.8 3.7 %all-to-all-start.4 = ((bf16[8,512,128]{2,1,0:T(8,128)(2,1)}), bf16[8,512,128]{2,1,0:T(8,128)(2,1)S(1)}, u32[]{:S(2)}, u32[]{:S(2)}) async-start(bf16[8,512,128]{2,1,0:T(8,128)(2,1)} %get-tuple-element.121), calls=%async_computation.4 | async-start | bytes 2097152 | tf_op jit(solution)/shard_map/all_to_all | solution.py:709
  155.5 14.9 %middle_0.1 = (bf16[8,256,512]{2,1,0:T(8,128)(2,1)}, bf16[8,256,512]{2,1,0:T(8,128)(2,1)}, bf16[8,256,512]{2,1,0:T(8,128)(2,1)}, f32[32,128,128]{2,1,0:T(8,128)}) custom-call(s32[1]{0:T(128)} %bitcast.own_ref, bf16[8,512,384]{2,1,0:T(8,128)(2,1)} %all-to-all-done.3.spread_ref, bf16[8,256,512]{2,1,0:T(8,128)(2,1)S(1)} %all-to-all-done.2.hidden_grad_ref, ...), custom_call_target="tpu_custom_call" | custom-call | tf_op jit(solution)/shard_map/middle_0/pallas_call | solution.py:546
  170.7 7.9 %middle_1.1 = (bf16[8,256,512]{2,1,0:T(8,128)(2,1)}, bf16[8,256,512]{2,1,0:T(8,128)(2,1)}, bf16[8,256,512]{2,1,0:T(8,128)(2,1)}, bf16[32,32,128]{2,1,0:T(8,128)(...) custom-call(s32[1]{0:T(128)} %bitcast.own_ref, ...), custom_call_target="tpu_custom_call", output_to_operand_aliasing={{0}: (6, {}), {1}: (7, {}), {2}: (8, {})} | custom-call | tf_op jit(solution)/shard_map/middle_1/pallas_call | solution.py:546
  178.6 3.8 %all-to-all-start.5 = ((bf16[8,256,512]{2,1,0:T(8,128)(2,1)}), bf16[8,256,512]{2,1,0:T(8,128)(2,1)S(1)}, u32[]{:S(2)}, u32[]{:S(2)}) async-start(bf16[8,256,512]{2,1,0:T(8,128)(2,1)} %get-tuple-element.130), calls=%async_computation.5 | async-start | bytes 4194304 | tf_op jit(solution)/shard_map/all_to_all | solution.py:709
  182.4 4.9 %collective-permute-start.9 = (bf16[32,32,128]{2,1,0:T(8,128)(2,1)}, bf16[32,32,128]{2,1,0:T(8,128)(2,1)S(1)}, u32[]{:S(2)}, u32[]{:S(2)}) collective-permute-start(bf16[32,32,128]{2,1,0:T(8,128)(2,1)} %get-tuple-element.132), channel_id=1, source_target_pairs={{0,8},{8,0},{16,24},{24,16},{1,9},{9,1},{17,25},{25,17},{2,10},{10... | collective-permute-start | bytes 786440 | tf_op jit(solution)/shard_map/ppermute | solution.py:151
  189.8 9.9 %collective-permute-done.9.refs_1_ = bf16[32,32,128]{2,1,0:T(8,128)(2,1)S(1)} collective-permute-done((bf16[32,32,128]{2,1,0:T(8,128)(2,1)}, bf16[32,32,128]{2,1,0:T(8,128)(2,1)S(1)}, u32[]{:S(2)}, u32[]{:S(2)}) %collective-permute-start.9) | collective-permute-done | bytes 262176 | tf_op jit(solution)/shard_map/ppermute | solution.py:151
  199.7 8.8 %collective-permute-done.10.refs_2_ = bf16[32,32,128]{2,1,0:T(8,128)(2,1)S(1)} collective-permute-done((bf16[32,32,128]{2,1,0:T(8,128)(2,1)S(1)}, bf16[32,32,128]{2,1,0:T(8,128)(2,1)S(1)}, u32[]{:S(2)}, u32[]{:S(2)}) %collective-permute-start.10) | collective-permute-done | bytes 262176 | tf_op jit(solution)/shard_map/ppermute | solution.py:151
  210.4 3.8 %all-to-all-start.6 = ((bf16[8,256,512]{2,1,0:T(8,128)(2,1)}), bf16[8,256,512]{2,1,0:T(8,128)(2,1)S(1)}, u32[]{:S(2)}, u32[]{:S(2)}) async-start(bf16[8,256,512]{2,1,0:T(8,128)(2,1)} %get-tuple-element.135), calls=%async_computation.6 | async-start | bytes 4194304 | tf_op jit(solution)/shard_map/all_to_all | solution.py:709
  214.2 5.4 %last_products_0.1 = (bf16[160,640]{1,0:T(8,128)(2,1)}, bf16[160,640]{1,0:T(8,128)(2,1)}, bf16[160,640]{1,0:T(8,128)(2,1)}, bf16[160,640]{1,0:T(8,128)(2,1)}) custom-call(bf16[8,2,128,512]{3,2,1,0:T(8,128)(2,1)} %bitcast.15, bf16[640,512]{1,0:T(8,128)(2,1)} %get-tuple-element.136.back_ref, bf16[16,128,128]{2,1,0:T(8,128)(2,1)} %gate_ref.11, ...), custom_call_target="tpu_custom_call" | custom-call | tf_op jit(solution)/shard_map/last_products_0/pallas_call | solution.py:613
  219.6 5.0 %collective-permute-start.12 = (bf16[160,640]{1,0:T(8,128)(2,1)}, bf16[160,640]{1,0:T(8,128)(2,1)S(1)}, u32[]{:S(2)}, u32[]{:S(2)}) collective-permute-start(bf16[160,640]{1,0:T(8,128)(2,1)} %get-tuple-element.138), channel_id=1, source_target_pairs={{0,8},{8,0},{16,24},{24,16},{1,9},{9,1},{17,25},{25,17},{2,10},{10... | collective-permute-start | bytes 614408 | tf_op jit(solution)/shard_map/ppermute | solution.py:151
  229.2 3.9 %last_products_5.1 = (bf16[160,384]{1,0:T(8,128)(2,1)}, bf16[160,384]{1,0:T(8,128)(2,1)}, bf16[160,384]{1,0:T(8,128)(2,1)}, bf16[160,384]{1,0:T(8,128)(2,1)}) custom-call(bf16[8,2,128,512]{3,2,1,0:T(8,128)(2,1)} %bitcast.16, bf16[640,512]{1,0:T(8,128)(2,1)} %get-tuple-element.136.back_ref, bf16[16,128,128]{2,1,0:T(8,128)(2,1)} %gate_ref.11, ...), custom_call_target="tpu_custom_call" | custom-call | tf_op jit(solution)/shard_map/last_products_5/pallas_call | solution.py:613
  233.0 3.4 right_grads_0.1
  236.5 6.0 %collective-permute-done.13.refs_2_ = bf16[160,640]{1,0:T(8,128)(2,1)S(1)} collective-permute-done((bf16[160,640]{1,0:T(8,128)(2,1)}, bf16[160,640]{1,0:T(8,128)(2,1)S(1)}, u32[]{:S(2)}, u32[]{:S(2)}) %collective-permute-start.13) | collective-permute-done | bytes 204832 | tf_op jit(solution)/shard_map/ppermute | solution.py:151
  243.8 4.2 %all-to-all-start.7 = ((bf16[8,256,512]{2,1,0:T(8,128)(2,1)}), bf16[8,256,512]{2,1,0:T(8,128)(2,1)S(1)}, u32[]{:S(2)}, u32[]{:S(2)}) async-start(bf16[8,256,512]{2,1,0:T(8,128)(2,1)} %get-tuple-element.151), calls=%async_computation.7 | async-start | bytes 4194304 | tf_op jit(solution)/shard_map/all_to_all | solution.py:709
  248.0 3.9 %collective-permute-start.15 = (bf16[160,384]{1,0:T(8,128)(2,1)}, bf16[160,384]{1,0:T(8,128)(2,1)S(1)}, u32[]{:S(2)}, u32[]{:S(2)}) collective-permute-start(bf16[160,384]{1,0:T(8,128)(2,1)} %get-tuple-element.142), channel_id=1, source_target_pairs={{0,8},{8,0},{16,24},{24,16},{1,9},{9,1},{17,25},{25,17},{2,10},{10... | collective-permute-start | bytes 368648 | tf_op jit(solution)/shard_map/ppermute | solution.py:151
  254.4 3.8 %last_products_8.1 = (bf16[160,384]{1,0:T(8,128)(2,1)}, bf16[160,384]{1,0:T(8,128)(2,1)}, bf16[160,384]{1,0:T(8,128)(2,1)}, bf16[160,384]{1,0:T(8,128)(2,1)}) custom-call(bf16[8,2,128,512]{3,2,1,0:T(8,128)(2,1)} %bitcast.12, bf16[640,512]{1,0:T(8,128)(2,1)} %get-tuple-element.136.back_ref, bf16[16,128,128]{2,1,0:T(8,128)(2,1)} %gate_ref.11, ...), custom_call_target="tpu_custom_call" | custom-call | tf_op jit(solution)/shard_map/last_products_8/pallas_call | solution.py:613
  262.6 5.4 %last_products_11.1 = (bf16[160,640]{1,0:T(8,128)(2,1)}, bf16[160,640]{1,0:T(8,128)(2,1)}, bf16[160,640]{1,0:T(8,128)(2,1)}, bf16[160,640]{1,0:T(8,128)(2,1)}) custom-call(bf16[8,2,128,512]{3,2,1,0:T(8,128)(2,1)} %bitcast.13, bf16[640,512]{1,0:T(8,128)(2,1)} %get-tuple-element.136.back_ref, bf16[16,128,128]{2,1,0:T(8,128)(2,1)} %gate_ref.11, ...), custom_call_target="tpu_custom_call" | custom-call | tf_op jit(solution)/shard_map/last_products_11/pallas_call | solution.py:613
  268.1 7.0 %collective-permute-done.19.refs_2_ = bf16[160,384]{1,0:T(8,128)(2,1)S(1)} collective-permute-done((bf16[160,384]{1,0:T(8,128)(2,1)}, bf16[160,384]{1,0:T(8,128)(2,1)S(1)}, u32[]{:S(2)}, u32[]{:S(2)}) %collective-permute-start.19) | collective-permute-done | bytes 122912 | tf_op jit(solution)/shard_map/ppermute | solution.py:151
  278.4 4.4 %all-to-all-start.8 = ((bf16[8,256,512]{2,1,0:T(8,128)(2,1)}), bf16[8,256,512]{2,1,0:T(8,128)(2,1)}, u32[]{:S(2)}, u32[]{:S(2)}) async-start(bf16[8,256,512]{2,1,0:T(8,128)(2,1)} %right_down.1), calls=%async_computation.8 | async-start | bytes 4194304 | tf_op jit(solution)/shard_map/all_to_all | solution.py:709
  282.8 3.5 collective-permute-start.22
  289.7 4.8 %unsort_0.1.refs_4_ = bf16[2048,640]{1,0:T(8,128)(2,1)} custom-call(bf16[640,640]{1,0:T(8,128)(2,1)} %get-tuple-element.98.home_ref, bf16[160,640]{1,0:T(8,128)(2,1)} %get-tuple-element.137.refs_0_, bf16[160,640]{1,0:T(8,128)(2,1)} %copy-done.27, bf16[160,640]{1,0:T(8,128)(2,1)} %copy-done.28, bf16[160,640]{1,0:T(8,128)(2,1)} %copy-done.29), custom_call_target="tpu_custom_call" | custom-call | tf_op jit(solution)/shard_map/unsort_0/pallas_call | solution.py:171
  294.6 3.7 %unsort_5.1.refs_4_ = bf16[2048,640]{1,0:T(8,128)(2,1)} custom-call(bf16[640,640]{1,0:T(8,128)(2,1)} %get-tuple-element.98.home_ref, bf16[160,384]{1,0:T(8,128)(2,1)} %get-tuple-element.141.refs_0_, bf16[160,384]{1,0:T(8,128)(2,1)} %copy-done.39, bf16[160,384]{1,0:T(8,128)(2,1)} %copy-done.40, ...), custom_call_target="tpu_custom_call", output_to_operand_aliasing={{}: (5, {})} | custom-call | tf_op jit(solution)/shard_map/unsort_5/pallas_call | solution.py:171
  300.8 3.4 collective-permute-done.23.refs_2_
  304.2 3.5 right_grads_1.1
  307.7 4.0 %collective-permute-start.25 = (bf16[2,16,32,128]{3,2,1,0:T(8,128)(2,1)}, bf16[2,16,32,128]{3,2,1,0:T(8,128)(2,1)S(1)}, u32[]{:S(2)}, u32[]{:S(2)}) collective-permute-start(bf16[2,16,32,128]{3,2,1,0:T(8,128)(2,1)} %get-tuple-element.165), channel_id=1, source_target_pairs={{0,8},{8,0},{16,24},{24,16},{1,9},{9,1},{17,25},{25,17},{2,10},{10... | collective-permute-start | bytes 786440 | tf_op jit(solution)/shard_map/ppermute | solution.py:363
  311.7 3.5 unsort_8.1.refs_4_
  317.7 4.4 %left_down.1 = bf16[8,256,512]{2,1,0:T(8,128)(2,1)} custom-call(bf16[8,256,512]{2,1,0:T(8,128)(2,1)} %all-to-all-done.8.in_ref, bf16[16,128,128]{2,1,0:T(8,128)(2,1)S(1)} %copy-done.7), custom_call_target="tpu_custom_call" | custom-call | tf_op jit(solution)/shard_map/left_down/pallas_call | solution.py:301
  322.2 4.5 %all-to-all-start.9 = ((bf16[8,256,512]{2,1,0:T(8,128)(2,1)}), bf16[8,256,512]{2,1,0:T(8,128)(2,1)}, u32[]{:S(2)}, u32[]{:S(2)}) async-start(bf16[8,256,512]{2,1,0:T(8,128)(2,1)} %left_down.1), calls=%async_computation.9 | async-start | bytes 4194304 | tf_op jit(solution)/shard_map/all_to_all | solution.py:709
  338.2 4.8 %unsort_11.1 = bf16[2048,640]{1,0:T(8,128)(2,1)} custom-call(bf16[640,640]{1,0:T(8,128)(2,1)} %get-tuple-element.98.home_ref, bf16[160,640]{1,0:T(8,128)(2,1)} %get-tuple-element.156.refs_0_, bf16[160,640]{1,0:T(8,128)(2,1)} %copy-done.30, bf16[160,640]{1,0:T(8,128)(2,1)} %copy-done.31, bf16[160,640]{1,0:T(8,128)(2,1)} %copy-done.32, ...), custom_call_target="tpu_custom_call", output_to_operand_aliasing={{}: (5, {})} | custom-call | tf_op jit(solution)/shard_map/unsort_11/pallas_call | solution.py:171
  347.2 4.1 %collective-permute-done.28 = bf16[1,16,32,128]{3,2,1,0:T(8,128)(2,1)S(1)} collective-permute-done((bf16[1,16,32,128]{3,2,1,0:T(8,128)(2,1)}, bf16[1,16,32,128]{3,2,1,0:T(8,128)(2,1)S(1)}, u32[]{:S(2)}, u32[]{:S(2)}) %collective-permute-start.28) | collective-permute-done | bytes 131104 | tf_op jit(solution)/shard_map/ppermute | solution.py:363
  (160 shorter events, 80.5 us)
Async XLA Ops:
  5.3 31.9 %all-to-all-start = ((bf16[8,256,512]{2,1,0:T(8,128)(2,1)}), bf16[8,256,512]{2,1,0:T(8,128)(2,1)S(1)}, u32[]{:S(2)}, u32[]{:S(2)}) async-start(bf16[8,256,512]{2,1,0:T(8,128)(2,1)} %send_cotangent.1), calls=%async_computation | async-start | bytes 4194304 | tf_op jit(solution)/shard_map/all_to_all | solution.py:709
  17.0 13.4 %collective-permute-start = (bf16[160,512]{1,0:T(8,128)(2,1)}, bf16[160,512]{1,0:T(8,128)(2,1)S(1)}, u32[]{:S(2)}, u32[]{:S(2)}) collective-permute-start(bf16[160,512]{1,0:T(8,128)(2,1)} %get-tuple-element.100), channel_id=1, source_target_pairs={{0,8},{8,0},{16,24},{24,16},{1,9},{9,1},{17,25},{25,17},{2,10},{10... | collective-permute-start | bytes 491528 | tf_op jit(solution)/shard_map/ppermute | solution.py:151
  18.6 15.2 %collective-permute-start.1 = (bf16[160,512]{1,0:T(8,128)(2,1)}, bf16[160,512]{1,0:T(8,128)(2,1)S(1)}, u32[]{:S(2)}, u32[]{:S(2)}) collective-permute-start(bf16[160,512]{1,0:T(8,128)(2,1)} %get-tuple-element.101), channel_id=1, source_target_pairs={{0,16},{8,24},{16,0},{24,8},{1,17},{9,25},{17,1},{25,9},{2,18},{10... | collective-permute-start | bytes 491528 | tf_op jit(solution)/shard_map/ppermute | solution.py:151
  21.1 12.6 %collective-permute-start.2 = (bf16[160,512]{1,0:T(8,128)(2,1)}, bf16[160,512]{1,0:T(8,128)(2,1)S(1)}, u32[]{:S(2)}, u32[]{:S(2)}) collective-permute-start(bf16[160,512]{1,0:T(8,128)(2,1)} %get-tuple-element.102), channel_id=1, source_target_pairs={{0,24},{8,16},{16,8},{24,0},{1,25},{9,17},{17,9},{25,1},{2,26},{10... | collective-permute-start | bytes 491528 | tf_op jit(solution)/shard_map/ppermute | solution.py:151
  40.5 30.3 %copy-start.4 = (bf16[16,128,128]{2,1,0:T(8,128)(2,1)S(1)}, bf16[16,128,128]{2,1,0:T(8,128)(2,1)}, u32[]{:S(2)}) copy-start(bf16[16,128,128]{2,1,0:T(8,128)(2,1)} %factor_ref.6) | copy-start | bytes 1572868
  40.5 30.3 %all-to-all-start.1 = ((bf16[8,256,512]{2,1,0:T(8,128)(2,1)}), bf16[8,256,512]{2,1,0:T(8,128)(2,1)S(1)}, u32[]{:S(2)}, u32[]{:S(2)}) async-start(bf16[8,256,512]{2,1,0:T(8,128)(2,1)} %left_back_down.1), calls=%async_computation.1 | async-start | bytes 4194304 | tf_op jit(solution)/shard_map/all_to_all | solution.py:709
  44.3 13.2 %collective-permute-start.3 = (bf16[160,768]{1,0:T(8,128)(2,1)}, bf16[160,768]{1,0:T(8,128)(2,1)S(1)}, u32[]{:S(2)}, u32[]{:S(2)}) collective-permute-start(bf16[160,768]{1,0:T(8,128)(2,1)} %get-tuple-element.104), channel_id=1, source_target_pairs={{0,8},{8,0},{16,24},{24,16},{1,9},{9,1},{17,25},{25,17},{2,10},{10... | collective-permute-start | bytes 737288 | tf_op jit(solution)/shard_map/ppermute | solution.py:151
  45.9 20.5 %collective-permute-start.4 = (bf16[160,768]{1,0:T(8,128)(2,1)}, bf16[160,768]{1,0:T(8,128)(2,1)S(1)}, u32[]{:S(2)}, u32[]{:S(2)}) collective-permute-start(bf16[160,768]{1,0:T(8,128)(2,1)} %get-tuple-element.105), channel_id=1, source_target_pairs={{0,16},{8,24},{16,0},{24,8},{1,17},{9,25},{17,1},{25,9},{2,18},{10... | collective-permute-start | bytes 737288 | tf_op jit(solution)/shard_map/ppermute | solution.py:151
  48.5 17.9 %collective-permute-start.5 = (bf16[160,768]{1,0:T(8,128)(2,1)}, bf16[160,768]{1,0:T(8,128)(2,1)S(1)}, u32[]{:S(2)}, u32[]{:S(2)}) collective-permute-start(bf16[160,768]{1,0:T(8,128)(2,1)} %get-tuple-element.106), channel_id=1, source_target_pairs={{0,24},{8,16},{16,8},{24,0},{1,25},{9,17},{17,9},{25,1},{2,26},{10... | collective-permute-start | bytes 737288 | tf_op jit(solution)/shard_map/ppermute | solution.py:151
  74.1 35.3 %all-to-all-start.2 = ((bf16[8,256,512]{2,1,0:T(8,128)(2,1)}), bf16[8,256,512]{2,1,0:T(8,128)(2,1)S(1)}, u32[]{:S(2)}, u32[]{:S(2)}) async-start(bf16[8,256,512]{2,1,0:T(8,128)(2,1)} %right_back_down.1), calls=%async_computation.2 | async-start | bytes 4194304 | tf_op jit(solution)/shard_map/all_to_all | solution.py:709
  77.7 13.2 %collective-permute-start.6 = (bf16[160,768]{1,0:T(8,128)(2,1)}, bf16[160,768]{1,0:T(8,128)(2,1)S(1)}, u32[]{:S(2)}, u32[]{:S(2)}) collective-permute-start(bf16[160,768]{1,0:T(8,128)(2,1)} %get-tuple-element.108), channel_id=1, source_target_pairs={{0,8},{8,0},{16,24},{24,16},{1,9},{9,1},{17,25},{25,17},{2,10},{10... | collective-permute-start | bytes 737288 | tf_op jit(solution)/shard_map/ppermute | solution.py:151
  79.3 20.5 %collective-permute-start.7 = (bf16[160,768]{1,0:T(8,128)(2,1)}, bf16[160,768]{1,0:T(8,128)(2,1)S(1)}, u32[]{:S(2)}, u32[]{:S(2)}) collective-permute-start(bf16[160,768]{1,0:T(8,128)(2,1)} %get-tuple-element.109), channel_id=1, source_target_pairs={{0,16},{8,24},{16,0},{24,8},{1,17},{9,25},{17,1},{25,9},{2,18},{10... | collective-permute-start | bytes 737288 | tf_op jit(solution)/shard_map/ppermute | solution.py:151
  81.9 17.9 %collective-permute-start.8 = (bf16[160,768]{1,0:T(8,128)(2,1)}, bf16[160,768]{1,0:T(8,128)(2,1)S(1)}, u32[]{:S(2)}, u32[]{:S(2)}) collective-permute-start(bf16[160,768]{1,0:T(8,128)(2,1)} %get-tuple-element.110), channel_id=1, source_target_pairs={{0,24},{8,16},{16,8},{24,0},{1,25},{9,17},{17,9},{25,1},{2,26},{10... | collective-permute-start | bytes 737288 | tf_op jit(solution)/shard_map/ppermute | solution.py:151
  109.4 42.4 %all-to-all-start.3 = ((bf16[8,512,384]{2,1,0:T(8,128)(2,1)}), bf16[8,512,384]{2,1,0:T(8,128)(2,1)}, u32[]{:S(2)}, u32[]{:S(2)}) async-start(bf16[8,512,384]{2,1,0:T(8,128)(2,1)} %get-tuple-element.120), calls=%async_computation.3 | async-start | bytes 6291456 | tf_op jit(solution)/shard_map/all_to_all | solution.py:709
  151.8 18.9 %all-to-all-start.4 = ((bf16[8,512,128]{2,1,0:T(8,128)(2,1)}), bf16[8,512,128]{2,1,0:T(8,128)(2,1)S(1)}, u32[]{:S(2)}, u32[]{:S(2)}) async-start(bf16[8,512,128]{2,1,0:T(8,128)(2,1)} %get-tuple-element.121), calls=%async_computation.4 | async-start | bytes 2097152 | tf_op jit(solution)/shard_map/all_to_all | solution.py:709
  178.6 30.5 %all-to-all-start.5 = ((bf16[8,256,512]{2,1,0:T(8,128)(2,1)}), bf16[8,256,512]{2,1,0:T(8,128)(2,1)S(1)}, u32[]{:S(2)}, u32[]{:S(2)}) async-start(bf16[8,256,512]{2,1,0:T(8,128)(2,1)} %get-tuple-element.130), calls=%async_computation.5 | async-start | bytes 4194304 | tf_op jit(solution)/shard_map/all_to_all | solution.py:709
  182.4 17.3 %collective-permute-start.9 = (bf16[32,32,128]{2,1,0:T(8,128)(2,1)}, bf16[32,32,128]{2,1,0:T(8,128)(2,1)S(1)}, u32[]{:S(2)}, u32[]{:S(2)}) collective-permute-start(bf16[32,32,128]{2,1,0:T(8,128)(2,1)} %get-tuple-element.132), channel_id=1, source_target_pairs={{0,8},{8,0},{16,24},{24,16},{1,9},{9,1},{17,25},{25,17},{2,10},{10... | collective-permute-start | bytes 786440 | tf_op jit(solution)/shard_map/ppermute | solution.py:151
  187.3 21.3 %collective-permute-start.10 = (bf16[32,32,128]{2,1,0:T(8,128)(2,1)S(1)}, bf16[32,32,128]{2,1,0:T(8,128)(2,1)S(1)}, u32[]{:S(2)}, u32[]{:S(2)}) collective-permute-start(bf16[32,32,128]{2,1,0:T(8,128)(2,1)S(1)} %copy-done.44), channel_id=1, source_target_pairs={{0,16},{8,24},{16,0},{24,8},{1,17},{9,25},{17,1},{25,9},{2,18},{10... | collective-permute-start | bytes 786440 | tf_op jit(solution)/shard_map/ppermute | solution.py:151
  188.4 20.2 %collective-permute-start.11 = (bf16[32,32,128]{2,1,0:T(8,128)(2,1)S(1)}, bf16[32,32,128]{2,1,0:T(8,128)(2,1)S(1)}, u32[]{:S(2)}, u32[]{:S(2)}) collective-permute-start(bf16[32,32,128]{2,1,0:T(8,128)(2,1)S(1)} %copy-done.43), channel_id=1, source_target_pairs={{0,24},{8,16},{16,8},{24,0},{1,25},{9,17},{17,9},{25,1},{2,26},{10... | collective-permute-start | bytes 786440 | tf_op jit(solution)/shard_map/ppermute | solution.py:151
  199.7 27.4 %copy-start.23 = (bf16[32,32,128]{2,1,0:T(8,128)(2,1)}, bf16[32,32,128]{2,1,0:T(8,128)(2,1)S(1)}, u32[]{:S(2)}) copy-start(bf16[32,32,128]{2,1,0:T(8,128)(2,1)S(1)} %collective-permute-done.9.refs_1_) | copy-start | bytes 786436
  208.6 18.5 %copy-start.25 = (bf16[32,32,128]{2,1,0:T(8,128)(2,1)}, bf16[32,32,128]{2,1,0:T(8,128)(2,1)S(1)}, u32[]{:S(2)}) copy-start(bf16[32,32,128]{2,1,0:T(8,128)(2,1)S(1)} %collective-permute-done.10.refs_2_) | copy-start | bytes 786436
  210.4 32.1 %all-to-all-start.6 = ((bf16[8,256,512]{2,1,0:T(8,128)(2,1)}), bf16[8,256,512]{2,1,0:T(8,128)(2,1)S(1)}, u32[]{:S(2)}, u32[]{:S(2)}) async-start(bf16[8,256,512]{2,1,0:T(8,128)(2,1)} %get-tuple-element.135), calls=%async_computation.6 | async-start | bytes 4194304 | tf_op jit(solution)/shard_map/all_to_all | solution.py:709
  219.6 16.9 %collective-permute-start.12 = (bf16[160,640]{1,0:T(8,128)(2,1)}, bf16[160,640]{1,0:T(8,128)(2,1)S(1)}, u32[]{:S(2)}, u32[]{:S(2)}) collective-permute-start(bf16[160,640]{1,0:T(8,128)(2,1)} %get-tuple-element.138), channel_id=1, source_target_pairs={{0,8},{8,0},{16,24},{24,16},{1,9},{9,1},{17,25},{25,17},{2,10},{10... | collective-permute-start | bytes 614408 | tf_op jit(solution)/shard_map/ppermute | solution.py:151
  224.6 17.8 %collective-permute-start.13 = (bf16[160,640]{1,0:T(8,128)(2,1)}, bf16[160,640]{1,0:T(8,128)(2,1)S(1)}, u32[]{:S(2)}, u32[]{:S(2)}) collective-permute-start(bf16[160,640]{1,0:T(8,128)(2,1)} %get-tuple-element.139), channel_id=1, source_target_pairs={{0,16},{8,24},{16,0},{24,8},{1,17},{9,25},{17,1},{25,9},{2,18},{10... | collective-permute-start | bytes 614408 | tf_op jit(solution)/shard_map/ppermute | solution.py:151
  225.7 16.7 %collective-permute-start.14 = (bf16[160,640]{1,0:T(8,128)(2,1)}, bf16[160,640]{1,0:T(8,128)(2,1)S(1)}, u32[]{:S(2)}, u32[]{:S(2)}) collective-permute-start(bf16[160,640]{1,0:T(8,128)(2,1)} %get-tuple-element.140), channel_id=1, source_target_pairs={{0,24},{8,16},{16,8},{24,0},{1,25},{9,17},{17,9},{25,1},{2,26},{10... | collective-permute-start | bytes 614408 | tf_op jit(solution)/shard_map/ppermute | solution.py:151
  236.5 41.9 %copy-start.27 = (bf16[160,640]{1,0:T(8,128)(2,1)}, bf16[160,640]{1,0:T(8,128)(2,1)S(1)}, u32[]{:S(2)}) copy-start(bf16[160,640]{1,0:T(8,128)(2,1)S(1)} %collective-permute-done.12.refs_1_) | copy-start | bytes 614404
  242.5 35.9 %copy-start.28 = (bf16[160,640]{1,0:T(8,128)(2,1)}, bf16[160,640]{1,0:T(8,128)(2,1)S(1)}, u32[]{:S(2)}) copy-start(bf16[160,640]{1,0:T(8,128)(2,1)S(1)} %collective-permute-done.13.refs_2_) | copy-start | bytes 614404
  242.5 35.9 %copy-start.29 = (bf16[160,640]{1,0:T(8,128)(2,1)}, bf16[160,640]{1,0:T(8,128)(2,1)S(1)}, u32[]{:S(2)}) copy-start(bf16[160,640]{1,0:T(8,128)(2,1)S(1)} %collective-permute-done.14.refs_3_) | copy-start | bytes 614404
  243.8 31.3 %all-to-all-start.7 = ((bf16[8,256,512]{2,1,0:T(8,128)(2,1)}), bf16[8,256,512]{2,1,0:T(8,128)(2,1)S(1)}, u32[]{:S(2)}, u32[]{:S(2)}) async-start(bf16[8,256,512]{2,1,0:T(8,128)(2,1)} %get-tuple-element.151), calls=%async_computation.7 | async-start | bytes 4194304 | tf_op jit(solution)/shard_map/all_to_all | solution.py:709
  248.0 13.3 %collective-permute-start.15 = (bf16[160,384]{1,0:T(8,128)(2,1)}, bf16[160,384]{1,0:T(8,128)(2,1)S(1)}, u32[]{:S(2)}, u32[]{:S(2)}) collective-permute-start(bf16[160,384]{1,0:T(8,128)(2,1)} %get-tuple-element.142), channel_id=1, source_target_pairs={{0,8},{8,0},{16,24},{24,16},{1,9},{9,1},{17,25},{25,17},{2,10},{10... | collective-permute-start | bytes 368648 | tf_op jit(solution)/shard_map/ppermute | solution.py:151
  251.9 16.1 %collective-permute-start.16 = (bf16[160,384]{1,0:T(8,128)(2,1)}, bf16[160,384]{1,0:T(8,128)(2,1)S(1)}, u32[]{:S(2)}, u32[]{:S(2)}) collective-permute-start(bf16[160,384]{1,0:T(8,128)(2,1)} %get-tuple-element.143), channel_id=1, source_target_pairs={{0,16},{8,24},{16,0},{24,8},{1,17},{9,25},{17,1},{25,9},{2,18},{10... | collective-permute-start | bytes 368648 | tf_op jit(solution)/shard_map/ppermute | solution.py:151
  253.0 15.1 %collective-permute-start.17 = (bf16[160,384]{1,0:T(8,128)(2,1)}, bf16[160,384]{1,0:T(8,128)(2,1)S(1)}, u32[]{:S(2)}, u32[]{:S(2)}) collective-permute-start(bf16[160,384]{1,0:T(8,128)(2,1)} %get-tuple-element.144), channel_id=1, source_target_pairs={{0,24},{8,16},{16,8},{24,0},{1,25},{9,17},{17,9},{25,1},{2,26},{10... | collective-permute-start | bytes 368648 | tf_op jit(solution)/shard_map/ppermute | solution.py:151
  258.2 9.8 %collective-permute-start.18 = (bf16[160,384]{1,0:T(8,128)(2,1)}, bf16[160,384]{1,0:T(8,128)(2,1)S(1)}, u32[]{:S(2)}, u32[]{:S(2)}) collective-permute-start(bf16[160,384]{1,0:T(8,128)(2,1)} %get-tuple-element.153), channel_id=1, source_target_pairs={{0,8},{8,0},{16,24},{24,16},{1,9},{9,1},{17,25},{25,17},{2,10},{10... | collective-permute-start | bytes 368648 | tf_op jit(solution)/shard_map/ppermute | solution.py:151
  259.3 15.8 %collective-permute-start.19 = (bf16[160,384]{1,0:T(8,128)(2,1)}, bf16[160,384]{1,0:T(8,128)(2,1)S(1)}, u32[]{:S(2)}, u32[]{:S(2)}) collective-permute-start(bf16[160,384]{1,0:T(8,128)(2,1)} %get-tuple-element.154), channel_id=1, source_target_pairs={{0,16},{8,24},{16,0},{24,8},{1,17},{9,25},{17,1},{25,9},{2,18},{10... | collective-permute-start | bytes 368648 | tf_op jit(solution)/shard_map/ppermute | solution.py:151
  261.3 13.8 %collective-permute-start.20 = (bf16[160,384]{1,0:T(8,128)(2,1)}, bf16[160,384]{1,0:T(8,128)(2,1)}, u32[]{:S(2)}, u32[]{:S(2)}) collective-permute-start(bf16[160,384]{1,0:T(8,128)(2,1)} %get-tuple-element.155), channel_id=1, source_target_pairs={{0,24},{8,16},{16,8},{24,0},{1,25},{9,17},{17,9},{25,1},{2,26},{10... | collective-permute-start | bytes 368648 | tf_op jit(solution)/shard_map/ppermute | solution.py:151
  278.4 39.3 %all-to-all-start.8 = ((bf16[8,256,512]{2,1,0:T(8,128)(2,1)}), bf16[8,256,512]{2,1,0:T(8,128)(2,1)}, u32[]{:S(2)}, u32[]{:S(2)}) async-start(bf16[8,256,512]{2,1,0:T(8,128)(2,1)} %right_down.1), calls=%async_computation.8 | async-start | bytes 4194304 | tf_op jit(solution)/shard_map/all_to_all | solution.py:709
  282.8 18.0 %collective-permute-start.22 = (bf16[160,640]{1,0:T(8,128)(2,1)}, bf16[160,640]{1,0:T(8,128)(2,1)S(1)}, u32[]{:S(2)}, u32[]{:S(2)}) collective-permute-start(bf16[160,640]{1,0:T(8,128)(2,1)} %get-tuple-element.157), channel_id=1, source_target_pairs={{0,8},{8,0},{16,24},{24,16},{1,9},{9,1},{17,25},{25,17},{2,10},{10... | collective-permute-start | bytes 614408 | tf_op jit(solution)/shard_map/ppermute | solution.py:151
  286.2 17.9 %collective-permute-start.23 = (bf16[160,640]{1,0:T(8,128)(2,1)}, bf16[160,640]{1,0:T(8,128)(2,1)S(1)}, u32[]{:S(2)}, u32[]{:S(2)}) collective-permute-start(bf16[160,640]{1,0:T(8,128)(2,1)} %get-tuple-element.158), channel_id=1, source_target_pairs={{0,16},{8,24},{16,0},{24,8},{1,17},{9,25},{17,1},{25,9},{2,18},{10... | collective-permute-start | bytes 614408 | tf_op jit(solution)/shard_map/ppermute | solution.py:151
  287.3 16.8 %collective-permute-start.24 = (bf16[160,640]{1,0:T(8,128)(2,1)}, bf16[160,640]{1,0:T(8,128)(2,1)S(1)}, u32[]{:S(2)}, u32[]{:S(2)}) collective-permute-start(bf16[160,640]{1,0:T(8,128)(2,1)} %get-tuple-element.159), channel_id=1, source_target_pairs={{0,24},{8,16},{16,8},{24,0},{1,25},{9,17},{17,9},{25,1},{2,26},{10... | collective-permute-start | bytes 614408 | tf_op jit(solution)/shard_map/ppermute | solution.py:151
  288.7 26.5 %collective-permute-start.21 = (bf16[2,16,32,128]{3,2,1,0:T(8,128)(2,1)}, bf16[2,16,32,128]{3,2,1,0:T(8,128)(2,1)S(1)}, u32[]{:S(2)}, u32[]{:S(2)}) collective-permute-start(bf16[2,16,32,128]{3,2,1,0:T(8,128)(2,1)} %get-tuple-element.149), channel_id=1, source_target_pairs={{0,8},{8,0},{16,24},{24,16},{1,9},{9,1},{17,25},{25,17},{2,10},{10... | collective-permute-start | bytes 786440 | tf_op jit(solution)/shard_map/ppermute | solution.py:363
  299.8 15.5 %collective-permute-start.26 = (bf16[2,16,32,128]{3,2,1,0:T(8,128)(2,1)}, bf16[2,16,32,128]{3,2,1,0:T(8,128)(2,1)S(1)}, u32[]{:S(2)}, u32[]{:S(2)}) collective-permute-start(bf16[2,16,32,128]{3,2,1,0:T(8,128)(2,1)} %get-tuple-element.163), channel_id=1, source_target_pairs={{0,8},{8,0},{16,24},{24,16},{1,9},{9,1},{17,25},{25,17},{2,10},{10... | collective-permute-start | bytes 786440 | tf_op jit(solution)/shard_map/ppermute | solution.py:363
  307.7 10.0 %collective-permute-start.25 = (bf16[2,16,32,128]{3,2,1,0:T(8,128)(2,1)}, bf16[2,16,32,128]{3,2,1,0:T(8,128)(2,1)S(1)}, u32[]{:S(2)}, u32[]{:S(2)}) collective-permute-start(bf16[2,16,32,128]{3,2,1,0:T(8,128)(2,1)} %get-tuple-element.165), channel_id=1, source_target_pairs={{0,8},{8,0},{16,24},{24,16},{1,9},{9,1},{17,25},{25,17},{2,10},{10... | collective-permute-start | bytes 786440 | tf_op jit(solution)/shard_map/ppermute | solution.py:363
  322.2 31.5 %all-to-all-start.9 = ((bf16[8,256,512]{2,1,0:T(8,128)(2,1)}), bf16[8,256,512]{2,1,0:T(8,128)(2,1)}, u32[]{:S(2)}, u32[]{:S(2)}) async-start(bf16[8,256,512]{2,1,0:T(8,128)(2,1)} %left_down.1), calls=%async_computation.9 | async-start | bytes 4194304 | tf_op jit(solution)/shard_map/all_to_all | solution.py:709
  329.8 13.2 %collective-permute-start.30 = (bf16[2,16,32,128]{3,2,1,0:T(8,128)(2,1)}, bf16[2,16,32,128]{3,2,1,0:T(8,128)(2,1)S(1)}, u32[]{:S(2)}, u32[]{:S(2)}) collective-permute-start(bf16[2,16,32,128]{3,2,1,0:T(8,128)(2,1)} %get-tuple-element.181), channel_id=1, source_target_pairs={{0,8},{8,0},{16,24},{24,16},{1,9},{9,1},{17,25},{25,17},{2,10},{10... | collective-permute-start | bytes 786440 | tf_op jit(solution)/shard_map/ppermute | solution.py:363
  334.0 17.3 %collective-permute-start.28 = (bf16[1,16,32,128]{3,2,1,0:T(8,128)(2,1)}, bf16[1,16,32,128]{3,2,1,0:T(8,128)(2,1)S(1)}, u32[]{:S(2)}, u32[]{:S(2)}) collective-permute-start(bf16[1,16,32,128]{3,2,1,0:T(8,128)(2,1)} %get-tuple-element.171), channel_id=1, source_target_pairs={{0,16},{8,24},{16,0},{24,8},{1,17},{9,25},{17,1},{25,9},{2,18},{10... | collective-permute-start | bytes 393224 | tf_op jit(solution)/shard_map/ppermute | solution.py:363
  335.3 21.0 %collective-permute-start.27 = (bf16[1,16,32,128]{3,2,1,0:T(8,128)(2,1)}, bf16[1,16,32,128]{3,2,1,0:T(8,128)(2,1)S(1)}, u32[]{:S(2)}, u32[]{:S(2)}) collective-permute-start(bf16[1,16,32,128]{3,2,1,0:T(8,128)(2,1)} %get-tuple-element.169), channel_id=1, source_target_pairs={{0,16},{8,24},{16,0},{24,8},{1,17},{9,25},{17,1},{25,9},{2,18},{10... | collective-permute-start | bytes 393224 | tf_op jit(solution)/shard_map/ppermute | solution.py:363
  336.9 21.4 %collective-permute-start.29 = (bf16[1,16,32,128]{3,2,1,0:T(8,128)(2,1)}, bf16[1,16,32,128]{3,2,1,0:T(8,128)(2,1)S(1)}, u32[]{:S(2)}, u32[]{:S(2)}) collective-permute-start(bf16[1,16,32,128]{3,2,1,0:T(8,128)(2,1)} %get-tuple-element.175), channel_id=1, source_target_pairs={{0,16},{8,24},{16,0},{24,8},{1,17},{9,25},{17,1},{25,9},{2,18},{10... | collective-permute-start | bytes 393224 | tf_op jit(solution)/shard_map/ppermute | solution.py:363
  345.6 15.4 %collective-permute-start.31 = (bf16[1,16,32,128]{3,2,1,0:T(8,128)(2,1)}, bf16[1,16,32,128]{3,2,1,0:T(8,128)(2,1)S(1)}, u32[]{:S(2)}, u32[]{:S(2)}) collective-permute-start(bf16[1,16,32,128]{3,2,1,0:T(8,128)(2,1)} %get-tuple-element.185), channel_id=1, source_target_pairs={{0,16},{8,24},{16,0},{24,8},{1,17},{9,25},{17,1},{25,9},{2,18},{10... | collective-permute-start | bytes 393224 | tf_op jit(solution)/shard_map/ppermute | solution.py:363
  (39 other events, 250.5 us)
